TPU v7x, 32 devices: a whole 2x2x4 slice. The times are simulated.
32 devices in a mesh: dp: 4 (over y, x), ctx: 8 (over z, core).
Axes of the slice: x: 2, y: 2, z: 4, core: 2. Of those that a mesh axis runs over, the one named last changes fastest.
Arguments:
- q_rows: bfloat16 [4, 2048, 8192], P('dp', 'ctx'), may hold values from -16 to 16
- k_rows: bfloat16 [4, 2048, 1024], P('dp', 'ctx'), may hold values from -16 to 16
- value_slot_rows: bfloat16 [4, 2048, 1024], P('dp', 'ctx'), may hold values from -6 to 6
- counts: int32 [4, 8], P('dp', 'ctx'), may hold values from 0 to 256, as said below
- doc_ids: int32 [4, 1024], P('dp', 'ctx'), may hold values from 0 to 2, never falling along the last dimension, each value on 1 to 512 neighbouring positions
Outputs:
- attended: bfloat16 [4, 1024, 8192], P('dp', 'ctx')
Inputs may be any that keep to these rules, and one draw needn't show every extreme that they name: In every column c and for every replica r, the sum of counts of replicas 0 to r exceeds (r + 1) * 128 by 0 to 128, and by 0 for the last replica. In every column some replica's count is 256 and the next replica's is 0. `doc_ids`: along each window the ids never fall; each id covers 1 to 512 positions, one exactly that many.
All inputs are finite; a program needn't handle non-finite values.
Results may differ from a plain program's by a relative error of at most 0.0038.
Values may be sent and summed in bfloat16 or wider, within the bound.
No kernel may reach another device: no remote copies, remote signals or barrier semaphores. Data moves between devices by JAX's collectives and lax.ppermute only.
A program may use at most 64 MiB of HBM per device.

v0:
```python
import math

import jax
import jax.numpy as jnp
from jax import lax
from jax.sharding import PartitionSpec as P

QUERY_HEADS = 64
KEY_VALUE_HEADS = 8
HEAD_SIZE = 128


def entering(x, axis, combine, identity):
    peers, place = (lax.axis_size(axis), lax.axis_index(axis))
    everything = lax.all_gather(x, axis)
    start = jnp.broadcast_to(jnp.asarray(identity, x.dtype), x.shape)

    def hop(k, before):
        reached = k < place
        new = combine(before, everything[k])
        return jnp.where(reached, new, before)

    return lax.fori_loop(0, peers, hop, start)


def passed_along(value, axis, steps):
    count = lax.axis_size(axis)
    initial, last = (max(0, -steps), min(count, count - steps))
    return lax.ppermute(value, axis, [(source, source + steps) for source in range(initial, last)])


def add_counts(earlier, later):
    return earlier + later


def tail_rows(local_rows, own_count, row_allowance):
    padded = jnp.concatenate(
        [jnp.zeros((row_allowance, local_rows.shape[1]), local_rows.dtype), local_rows], axis=0
    )
    return lax.dynamic_slice_in_dim(padded, own_count, row_allowance, 0)


def settle(arrived, local_rows, shift_in, row_allowance):
    joined = jnp.concatenate([arrived, local_rows], axis=0)
    return lax.dynamic_slice_in_dim(joined, row_allowance - shift_in, row_allowance, 0)


def attend_heads(query_tensor, key_tensor, value_tensor, window_docs):
    window = query_tensor.shape[0]
    block_rows = math.gcd(window, 512)
    score_scale = 1.0 / math.sqrt(HEAD_SIZE)
    places = jnp.arange(window, dtype=jnp.int32)

    def one_block(block_index):
        first_row = block_index * block_rows
        q_block = lax.dynamic_slice_in_dim(query_tensor, first_row, block_rows, 0)
        q_docs = lax.dynamic_slice_in_dim(window_docs, first_row, block_rows, 0)
        q_places = first_row + jnp.arange(block_rows, dtype=jnp.int32)
        scores = (
            jnp.einsum("bhd,kd->hbk", q_block, key_tensor, preferred_element_type=jnp.float32)
            * score_scale
        )
        allowed = (places[None, :] <= q_places[:, None]) & (window_docs[None, :] == q_docs[:, None])
        scores = jnp.where(allowed[None], scores, -jnp.inf)
        largest = jnp.max(scores, axis=-1, keepdims=True)
        weights = jnp.exp(scores - largest)
        totals = jnp.sum(weights, axis=-1)
        mixed = jnp.einsum(
            "hbk,kd->bhd",
            weights.astype(jnp.bfloat16),
            value_tensor,
            preferred_element_type=jnp.float32,
        )
        return (mixed / totals.T[:, :, None]).astype(jnp.bfloat16)

    blocks = lax.map(one_block, jnp.arange(window // block_rows, dtype=jnp.int32))
    return blocks.reshape(window, query_tensor.shape[1], query_tensor.shape[2])


def body(q_rows, k_rows, value_slot_rows, counts, doc_ids):
    row_allowance = doc_ids.shape[1]
    own_count = counts[0, 0]
    my_rank = lax.axis_index("dp")
    before = entering(own_count, "dp", add_counts, jnp.int32(0))
    shift_in = before - my_rank * row_allowance
    local_q = q_rows[0]
    local_k = k_rows[0]
    local_v = value_slot_rows[0]
    arrived_q, arrived_k, arrived_v = passed_along(
        (
            tail_rows(local_q, own_count, row_allowance),
            tail_rows(local_k, own_count, row_allowance),
            tail_rows(local_v, own_count, row_allowance),
        ),
        "dp",
        1,
    )
    balanced_q = settle(arrived_q, local_q, shift_in, row_allowance)
    levelled_key_rows = settle(arrived_k, local_k, shift_in, row_allowance)
    levelled_value_rows = settle(arrived_v, local_v, shift_in, row_allowance)
    duplicates = lax.axis_size("ctx") // KEY_VALUE_HEADS
    dispersed_key_rows = jnp.repeat(
        levelled_key_rows.reshape(row_allowance, KEY_VALUE_HEADS, HEAD_SIZE), duplicates, axis=1
    )
    dispersed_value_rows = jnp.repeat(
        levelled_value_rows.reshape(row_allowance, KEY_VALUE_HEADS, HEAD_SIZE), duplicates, axis=1
    )
    head_q, head_k, head_v = (
        lax.all_to_all(
            balanced_q.reshape(row_allowance, QUERY_HEADS, HEAD_SIZE),
            "ctx",
            split_axis=1,
            concat_axis=0,
            tiled=True,
        ),
        lax.all_to_all(dispersed_key_rows, "ctx", split_axis=1, concat_axis=0, tiled=True),
        lax.all_to_all(dispersed_value_rows, "ctx", split_axis=1, concat_axis=0, tiled=True),
    )
    window_docs = lax.all_gather(doc_ids, "ctx", axis=1, tiled=True)
    outcome = attend_heads(head_q, head_k[:, 0, :], head_v[:, 0, :], window_docs[0])
    returned = lax.all_to_all(outcome, "ctx", split_axis=0, concat_axis=1, tiled=True)
    return returned.reshape(1, row_allowance, QUERY_HEADS * HEAD_SIZE)


def solution(mesh):
    return jax.shard_map(
        body,
        mesh=mesh,
        in_specs=(
            P("dp", "ctx", None),
            P("dp", "ctx", None),
            P("dp", "ctx", None),
            P("dp", "ctx"),
            P("dp", "ctx"),
        ),
        out_specs=P("dp", "ctx", None),
        check_vma=False,
    )
```

profile of v0, /device:TPU:21, one launch (start us, length us, event | category | flops | bytes accessed | tf_op | source)
XLA Modules:
  0.0 255.2 jit_solution(8050198580027775988)
XLA Ops:
  0.7 6.4 %copy.28 = bf16[1,256,8192]{1,2,0:T(8,128)(2,1)} copy(bf16[1,256,8192]{2,1,0:T(8,128)(2,1)} %param.9) | data formatting | bytes 8388608 | tf_op args[0]
  7.0 0.0 copy-start.1
  7.0 0.0 copy-start.3
  7.0 2.6 %pad_dynamic-slice_fusion.2 = bf16[128,8192]{0,1:T(8,128)(2,1)S(1)} fusion(s32[]{:T(128)S(6)} %select_n.34, bf16[256,8192]{0,1:T(8,128)(2,1)} %bitcast.87), kind=kLoop, calls=%fused_computation.25 | loop fusion | bytes 6291460 | tf_op jit(solution)/shard_map/dynamic_slice | solution.py:40
  9.7 3.7 %collective-permute-start = (bf16[128,8192]{0,1:T(8,128)(2,1)S(1)}, bf16[128,8192]{0,1:T(8,128)(2,1)}, u32[]{:S(2)}, u32[]{:S(2)}) collective-permute-start(bf16[128,8192]{0,1:T(8,128)(2,1)S(1)} %pad_dynamic-slice_fusion.2), channel_id=1, source_target_pairs={{0,8},{8,16},{16,24},{1,9},{9,17},{17,25},{2,10},{10,18},{18,26},{... | collective-permute-start | bytes 6291464 | tf_op jit(solution)/shard_map/ppermute | solution.py:29
  13.4 0.0 copy-done.1
  13.4 0.2 copy.32
  13.6 0.9 pad_dynamic-slice_fusion.8
  14.5 1.9 collective-permute-start.1
  16.4 0.0 copy-done.3
  16.4 0.6 dynamic-slice
  17.0 0.6 bitcast_dynamic-update-slice_fusion
  17.7 48.1 %all-reduce.3 = s32[4]{0:T(128)S(1)} all-reduce(s32[4]{0:T(128)S(1)} %bitcast_dynamic-update-slice_fusion), channel_id=2, replica_groups=mesh['dp'=4,'ctx'=8] {'dp'}, use_global_device_ids=true, to_apply=%add.3 | all-reduce | flops 4 | bytes 32 | tf_op jit(solution)/shard_map/all_gather | solution.py:15
  65.8 4.9 %while.24 = (s32[]{:T(128)}, s32[]{:T(128)}, s32[]{:T(128)}, s32[4]{0:T(128)S(1)}, s32[]{:T(128)}) while((s32[]{:T(128)}, s32[]{:T(128)}, s32[]{:T(128)}, s32[4]{0:T(128)S(1)}, s32[]{:T(128)}) %tuple.50), condition=%wide.region_1.2_spmd, body=%wide.region_0.1_spmd.sunk | while | flops 5 | bytes 107 | solution.py:23
  65.8 0.6 dynamic_slice.76
  67.0 0.6 dynamic_slice.76
  68.3 0.6 dynamic_slice.76
  69.5 0.6 dynamic_slice.76
  70.7 1.2 copy.34
  72.0 0.0 collective-permute-done.1
  72.0 1.0 fusion.23
  73.0 7.4 %all-to-all-start.1 = ((bf16[128,8,128]{0,2,1:T(8,128)(2,1)}), bf16[128,8,128]{0,2,1:T(8,128)(2,1)S(1)}, u32[]{:S(2)}, u32[]{:S(2)}) async-start(bf16[128,8,128]{0,2,1:T(8,128)(2,1)} %bitcast.100), calls=%async_computation.1 | async-start | bytes 524288 | tf_op jit(solution)/shard_map/all_to_all | solution.py:116
  80.4 0.2 pad_dynamic-slice_fusion.7
  80.6 2.2 collective-permute-start.2
  82.8 8.2 %collective-permute-done.2 = bf16[128,1024]{0,1:T(8,128)(2,1)S(1)} collective-permute-done((bf16[128,1024]{0,1:T(8,128)(2,1)S(1)}, bf16[128,1024]{0,1:T(8,128)(2,1)S(1)}, u32[]{:S(2)}, u32[]{:S(2)}) %collective-permute-start.2) | collective-permute-done | bytes 262176 | tf_op jit(solution)/shard_map/ppermute | solution.py:29
  90.9 1.0 fusion.22
  91.9 0.0 all-to-all-done.1
  91.9 5.9 %all-to-all-start.2 = ((bf16[128,8,128]{0,2,1:T(8,128)(2,1)}), bf16[128,8,128]{0,2,1:T(8,128)(2,1)}, u32[]{:S(2)}, u32[]{:S(2)}) async-start(bf16[128,8,128]{0,2,1:T(8,128)(2,1)} %bitcast.17), calls=%async_computation.2 | async-start | bytes 524288 | tf_op jit(solution)/shard_map/all_to_all | solution.py:117
  97.8 0.0 collective-permute-done
  97.8 4.0 %fusion.21 = bf16[128,8192]{0,1:T(8,128)(2,1)S(1)} fusion(s32[]{:T(128)S(6)} %select_n.35, bf16[128,8192]{0,1:T(8,128)(2,1)} %collective-permute-done, bf16[256,8192]{0,1:T(8,128)(2,1)} %bitcast.88), kind=kLoop, calls=%fused_computation.26 | loop fusion | flops 4194304 | bytes 8388612 | tf_op jit(solution)/shard_map/concatenate | solution.py:44
  101.8 0.0 copy-start.2
  101.8 2.9 %copy.29 = bf16[128,64,128]{2,0,1:T(8,128)(2,1)} copy(bf16[128,64,128]{0,2,1:T(8,128)(2,1)S(1)} %bitcast.94) | data formatting | bytes 4194304 | tf_op jit(solution)/shard_map/reshape | solution.py:110
  104.8 0.0 all-to-all-done.2
  104.8 6.4 %all-to-all-start = ((bf16[128,64,128]{2,0,1:T(8,128)(2,1)}), bf16[128,64,128]{2,0,1:T(8,128)(2,1)S(1)}, u32[]{:S(2)}, u32[]{:S(2)}) async-start(bf16[128,64,128]{2,0,1:T(8,128)(2,1)} %copy.29), calls=%async_computation | async-start | bytes 4194304 | tf_op jit(solution)/shard_map/all_to_all | solution.py:109
  111.2 0.0 copy-done.2
  111.2 50.7 %all_gather.6 = s32[1,1024]{1,0:T(1,128)S(1)} all-gather(s32[1,128]{1,0:T(1,128)S(1)} %copy-done.2), channel_id=1, replica_groups=mesh['dp'=4,'ctx'=8] {'ctx'}, dimensions={1}, use_global_device_ids=true | all-gather | bytes 4608 | tf_op jit(solution)/shard_map/all_gather | solution.py:119
  161.9 0.2 copy.33
  162.0 1.1 copy.35
  163.2 0.0 all-to-all-done
  163.2 0.0 copy-start
  163.2 1.3 copy-done
  164.5 3.0 %copy.31 = bf16[8,128,8,128]{3,2,1,0:T(8,128)(2,1)S(1)} copy(bf16[8,128,8,128]{3,1,2,0:T(8,128)(2,1)} %bitcast.91) | data formatting | bytes 4194304 | tf_op jit(solution)/shard_map/all_to_all | solution.py:109
  167.5 31.5 %while.25 = (s32[]{:T(128)}, bf16[2,512,8,128]{3,2,1,0:T(8,128)(2,1)}, s32[2]{0:T(128)S(1)}, s32[1,1024]{1,0:T(1,128)S(1)}, s32[1024]{0:T(1024)S(1)}, /*index=5*...) while((s32[]{:T(128)}, ...), condition=%wide.region_5.6_spmd.clone, body=%wide.region_2.5_spmd.clone.sunk | while | flops 2196234752 | bytes 59341496 | solution.py:76
  167.5 0.6 dynamic_slice.78
  168.7 0.1 dynamic_slice.79
  168.8 0.5 fusion.31
  169.3 0.1 constant_dynamic-slice_fusion.2
  169.3 3.2 %bitcast_reduce_fusion.2 = (f32[8,512]{1,0:T(8,128)S(1)}, f32[512,8,1024]{2,0,1:T(8,128)S(1)}) fusion(pred[512,1024]{1,0:T(8,128)(4,1)S(1)} %fusion.31, bf16[1024,128]{1,0:T(8,128)(2,1)S(1)} %get-tuple-element.324, bf16[512,8,128]{2,1,0:T(8,128)(2,1)S(1)} %constant_dynamic-slice_fusion.2), kind=kOutput, calls=%fused_computation.2.clone.1 | convolution fusion | flops 1086320640 | bytes 18628608 | tf_op jit(solution)/shard_map/while/body/eval_jaxpr/bhd,kd->hbk/dot_general | solution.py:60
  172.5 4.4 %fusion.32 = f32[8,512]{1,0:T(8,128)S(1)} fusion(f32[512,8,1024]{2,0,1:T(8,128)S(1)} %get-tuple-element.277, f32[8,512]{1,0:T(8,128)S(1)} %get-tuple-element.278, pred[512,1024]{1,0:T(8,128)(4,1)S(1)} %fusion.31), kind=kLoop, calls=%fused_computation.5.clone.1 | loop fusion | flops 16773120 | bytes 17334272 | tf_op jit(solution)/shard_map/while/body/eval_jaxpr/reduce_sum | solution.py:67
  176.9 4.7 %fusion.33 = bf16[1,512,8,128]{3,1,2,0:T(8,128)(2,1)S(1)} fusion(f32[512,8,1024]{2,0,1:T(8,128)S(1)} %get-tuple-element.277, f32[8,512]{1,0:T(8,128)S(1)} %get-tuple-element.278, pred[512,1024]{1,0:T(8,128)(4,1)S(1)} %fusion.31, f32[512,8]{0,1:T(8,128)S(1)} %bitcast.101, bf16[1024,128]{1,0:T(8,128)(2,1)S(1)} %get-tuple-element.325), kind=kOutput, calls=%fused_computation.13.clone.1 | convolution fusion | flops 1091567616 | bytes 18644992 | tf_op jit(solution)/shard_map/while/body/eval_jaxpr/hbk,kd->bhd/dot_general | solution.py:68
  181.6 1.7 copy_dynamic-update-slice_fusion.2
  183.2 0.6 dynamic_slice.78
  184.4 0.1 dynamic_slice.79
  184.5 0.5 fusion.31
  185.0 0.1 constant_dynamic-slice_fusion.2
  185.1 3.2 %bitcast_reduce_fusion.2 = (f32[8,512]{1,0:T(8,128)S(1)}, f32[512,8,1024]{2,0,1:T(8,128)S(1)}) fusion(pred[512,1024]{1,0:T(8,128)(4,1)S(1)} %fusion.31, bf16[1024,128]{1,0:T(8,128)(2,1)S(1)} %get-tuple-element.324, bf16[512,8,128]{2,1,0:T(8,128)(2,1)S(1)} %constant_dynamic-slice_fusion.2), kind=kOutput, calls=%fused_computation.2.clone.1 | convolution fusion | flops 1086320640 | bytes 18628608 | tf_op jit(solution)/shard_map/while/body/eval_jaxpr/bhd,kd->hbk/dot_general | solution.py:60
  188.3 4.4 %fusion.32 = f32[8,512]{1,0:T(8,128)S(1)} fusion(f32[512,8,1024]{2,0,1:T(8,128)S(1)} %get-tuple-element.277, f32[8,512]{1,0:T(8,128)S(1)} %get-tuple-element.278, pred[512,1024]{1,0:T(8,128)(4,1)S(1)} %fusion.31), kind=kLoop, calls=%fused_computation.5.clone.1 | loop fusion | flops 16773120 | bytes 17334272 | tf_op jit(solution)/shard_map/while/body/eval_jaxpr/reduce_sum | solution.py:67
  192.6 4.7 %fusion.33 = bf16[1,512,8,128]{3,1,2,0:T(8,128)(2,1)S(1)} fusion(f32[512,8,1024]{2,0,1:T(8,128)S(1)} %get-tuple-element.277, f32[8,512]{1,0:T(8,128)S(1)} %get-tuple-element.278, pred[512,1024]{1,0:T(8,128)(4,1)S(1)} %fusion.31, f32[512,8]{0,1:T(8,128)S(1)} %bitcast.101, bf16[1024,128]{1,0:T(8,128)(2,1)S(1)} %get-tuple-element.325), kind=kOutput, calls=%fused_computation.13.clone.1 | convolution fusion | flops 1091567616 | bytes 18644992 | tf_op jit(solution)/shard_map/while/body/eval_jaxpr/hbk,kd->bhd/dot_general | solution.py:68
  197.3 1.7 copy_dynamic-update-slice_fusion.2
  199.0 49.3 %all_to_all.63 = bf16[1024,8,128]{2,1,0:T(8,128)(2,1)S(1)} all-to-all(bf16[1024,8,128]{2,1,0:T(8,128)(2,1)} %bitcast.21), channel_id=1, replica_groups=mesh['dp'=4,'ctx'=8] {'ctx'}, dimensions={0} | all-to-all | bytes 4194304 | tf_op jit(solution)/shard_map/all_to_all | solution.py:121
  248.3 2.8 %copy.38 = bf16[128,8,8,128]{0,3,2,1:T(8,128)(2,1)} copy(bf16[128,8,8,128]{3,2,0,1:T(8,128)(2,1)S(1)} %bitcast.92) | data formatting | bytes 4194304 | tf_op jit(solution)/shard_map/all_to_all | solution.py:121
  251.1 4.1 %copy.39 = bf16[1,128,8192]{2,1,0:T(8,128)(2,1)} copy(bf16[1,128,8192]{1,2,0:T(8,128)(2,1)} %bitcast.93) | data formatting | bytes 4194304 | tf_op jit(solution)/shard_map/reshape | solution.py:122
  (5 shorter events, 0.0 us)
Async XLA Ops:
  7.0 6.4 %copy-start.1 = (bf16[1,256,1024]{2,1,0:T(8,128)(2,1)S(1)}, bf16[1,256,1024]{2,1,0:T(8,128)(2,1)}, u32[]{:S(2)}) copy-start(bf16[1,256,1024]{2,1,0:T(8,128)(2,1)} %param.10) | copy-start | bytes 1572868
  7.0 9.4 %copy-start.3 = (u32[32]{0:T(128)S(1)}, u32[32]{0:T(128)}, u32[]{:S(2)}) copy-start(u32[32]{0:T(128)} %constant.70) | copy-start | bytes 388
  9.7 88.2 %collective-permute-start = (bf16[128,8192]{0,1:T(8,128)(2,1)S(1)}, bf16[128,8192]{0,1:T(8,128)(2,1)}, u32[]{:S(2)}, u32[]{:S(2)}) collective-permute-start(bf16[128,8192]{0,1:T(8,128)(2,1)S(1)} %pad_dynamic-slice_fusion.2), channel_id=1, source_target_pairs={{0,8},{8,16},{16,24},{1,9},{9,17},{17,25},{2,10},{10,18},{18,26},{... | collective-permute-start | bytes 6291464 | tf_op jit(solution)/shard_map/ppermute | solution.py:29
  14.5 57.5 %collective-permute-start.1 = (bf16[128,1024]{0,1:T(8,128)(2,1)}, bf16[128,1024]{0,1:T(8,128)(2,1)S(1)}, u32[]{:S(2)}, u32[]{:S(2)}) collective-permute-start(bf16[128,1024]{0,1:T(8,128)(2,1)} %pad_dynamic-slice_fusion.8), channel_id=1, source_target_pairs={{0,8},{8,16},{16,24},{1,9},{9,17},{17,25},{2,10},{10,18},{18,26},{... | collective-permute-start | bytes 786440 | tf_op jit(solution)/shard_map/ppermute | solution.py:29
  73.0 18.9 %all-to-all-start.1 = ((bf16[128,8,128]{0,2,1:T(8,128)(2,1)}), bf16[128,8,128]{0,2,1:T(8,128)(2,1)S(1)}, u32[]{:S(2)}, u32[]{:S(2)}) async-start(bf16[128,8,128]{0,2,1:T(8,128)(2,1)} %bitcast.100), calls=%async_computation.1 | async-start | bytes 524288 | tf_op jit(solution)/shard_map/all_to_all | solution.py:116
  80.6 10.3 %collective-permute-start.2 = (bf16[128,1024]{0,1:T(8,128)(2,1)S(1)}, bf16[128,1024]{0,1:T(8,128)(2,1)S(1)}, u32[]{:S(2)}, u32[]{:S(2)}) collective-permute-start(bf16[128,1024]{0,1:T(8,128)(2,1)S(1)} %pad_dynamic-slice_fusion.7), channel_id=1, source_target_pairs={{0,8},{8,16},{16,24},{1,9},{9,17},{17,25},{2,10},{10,18},{18,26},{... | collective-permute-start | bytes 786440 | tf_op jit(solution)/shard_map/ppermute | solution.py:29
  91.9 12.9 %all-to-all-start.2 = ((bf16[128,8,128]{0,2,1:T(8,128)(2,1)}), bf16[128,8,128]{0,2,1:T(8,128)(2,1)}, u32[]{:S(2)}, u32[]{:S(2)}) async-start(bf16[128,8,128]{0,2,1:T(8,128)(2,1)} %bitcast.17), calls=%async_computation.2 | async-start | bytes 524288 | tf_op jit(solution)/shard_map/all_to_all | solution.py:117
  101.8 9.4 %copy-start.2 = (s32[1,128]{1,0:T(1,128)S(1)}, s32[1,128]{1,0:T(1,128)}, u32[]{:S(2)}) copy-start(s32[1,128]{1,0:T(1,128)} %param.13) | copy-start | bytes 1540
  104.8 58.4 %all-to-all-start = ((bf16[128,64,128]{2,0,1:T(8,128)(2,1)}), bf16[128,64,128]{2,0,1:T(8,128)(2,1)S(1)}, u32[]{:S(2)}, u32[]{:S(2)}) async-start(bf16[128,64,128]{2,0,1:T(8,128)(2,1)} %copy.29), calls=%async_computation | async-start | bytes 4194304 | tf_op jit(solution)/shard_map/all_to_all | solution.py:109
  163.2 1.3 copy-start
where the time goes:
time: 259 us; the launch traced here: 255 us
  blocking collectives  148 us (57%)
  local copies, waits for them, and re-layouts  35.3 us (14%)
  starting transfers between devices  27.6 us (11%)
  other arithmetic  15.7 us (6%)
  matrix products  15.7 us (6%)
  waiting for transfers between devices  8.17 us (3%)
  loops' own time  3.79 us (1%)
    all_gather x1, blocking collectives, body(): window_docs = lax.all_gather(doc_ids, 'ctx', axis=1, tiled=True)  50.7 us
    all_to_all x1, blocking collectives, body(): lax.all_to_all(outcome, 'ctx', split_axis=0, concat_axis=1, tiled=True)  49.3 us
    all_gather x1, blocking collectives, entering(): everything = lax.all_gather(x, axis)  48.1 us
    unnamed x14, local copies, waits for them, and re-layouts  10.4 us
    dot_general x2, matrix products, one_block(): jnp.einsum('hbk,kd->bhd', weights.astype(jnp.bfloat16), value_tensor, pre...  9.32 us
    reduce_sum x2, other arithmetic, one_block(): totals = jnp.sum(weights, axis=-1)  8.73 us
    ppermute x3, waiting for transfers between devices, passed_along(): lax.ppermute(value, axis, [(source, source + steps) for source in range(i...  8.16 us
    ppermute x3, starting transfers between devices, passed_along(): lax.ppermute(value, axis, [(source, source + steps) for source in range(i...  7.8 us
  transfers between devices with their start and end apart: 6, of which 1 were waited for; matrix products, arithmetic and copies ran while one was open for 6% of the time, Pallas kernels for 0%

commit v1 on v0

v1 whole, which is shorter than its diff:
```python
import functools
import math

import jax
import jax.numpy as jnp
from jax import lax
from jax.experimental import pallas as pl
from jax.experimental.pallas import tpu as pltpu
from jax.sharding import PartitionSpec as P

QUERY_HEADS = 64
KEY_VALUE_HEADS = 8
HEAD_SIZE = 128
GROUP = QUERY_HEADS // KEY_VALUE_HEADS
GROUP_WIDTH = GROUP * HEAD_SIZE
KV_WIDTH = KEY_VALUE_HEADS * HEAD_SIZE
MASKED = -1e30
CHUNKS = (2, 2, 2, 1, 1)


def shifted(x, axis, steps):
    n = lax.axis_size(axis)
    return lax.ppermute(x, axis, [(i, i + steps) for i in range(n - steps)])


def swapped_cores(x):
    n = lax.axis_size("ctx")
    return lax.ppermute(x, "ctx", [(i, i ^ 1) for i in range(n)])


def everyones(x, axis):
    n = lax.axis_size(axis)
    spread = jnp.broadcast_to(x[None], (n,) + x.shape)
    return lax.all_to_all(spread, axis, split_axis=0, concat_axis=0)


def placing(scal_ref, quota):
    s, s_before = scal_ref[0], scal_ref[1]
    row = lax.broadcasted_iota(jnp.int32, (quota, 2 * quota), 0)
    col = lax.broadcasted_iota(jnp.int32, (quota, 2 * quota), 1)
    turned = row - s_before
    turned = jnp.where(turned < 0, turned + quota, turned)
    source = jnp.where(row < s, turned, row - s + quota)
    return jnp.where(col == source, 1.0, 0.0).astype(jnp.bfloat16)


def place_rows(hot, arrived, local):
    both = jnp.concatenate([arrived, local], axis=0)
    return jnp.dot(hot, both, preferred_element_type=jnp.float32).astype(jnp.bfloat16)


def settle_kernel(scal_ref, arrived_ref, k_ref, v_ref, out_ref):
    quota = out_ref.shape[0]
    hot = placing(scal_ref, quota)
    out_ref[:, :KV_WIDTH] = place_rows(hot, arrived_ref[:, :KV_WIDTH], k_ref[0])
    out_ref[:, KV_WIDTH:] = place_rows(hot, arrived_ref[:, KV_WIDTH:], v_ref[0])


def settle_kv(scal, arrived, k_rows, v_rows):
    quota = arrived.shape[0]
    half = pl.BlockSpec((1, quota, KV_WIDTH), lambda i: (0, 0, 0))
    whole = pl.BlockSpec((quota, 2 * KV_WIDTH), lambda i: (0, 0))
    return pl.pallas_call(
        settle_kernel,
        grid=(1,),
        in_specs=[pl.BlockSpec(memory_space=pltpu.SMEM), whole, half, half],
        out_specs=whole,
        out_shape=jax.ShapeDtypeStruct(arrived.shape, jnp.bfloat16),
        name="settle_kv",
    )(scal, arrived, k_rows, v_rows)


def attend_kernel(blocks, has_out, scal_ref, bias_ref, arrived_ref, local_ref, *refs):
    k_refs, v_refs = refs[:blocks], refs[blocks : 2 * blocks]
    out_ref = refs[-1]
    quota = arrived_ref.shape[0]
    hot = placing(scal_ref, quota)
    q = place_rows(hot, arrived_ref[...], local_ref[0])
    keys = jnp.concatenate([r[...] for r in k_refs], axis=0)
    values = jnp.concatenate([r[...] for r in v_refs], axis=0)
    unit = math.log2(math.e) / math.sqrt(HEAD_SIZE)
    for head in range(GROUP):
        cols = slice(head * HEAD_SIZE, (head + 1) * HEAD_SIZE)
        scores = lax.dot_general(
            q[:, cols], keys, (((1,), (1,)), ((), ())), preferred_element_type=jnp.float32
        )
        scores = scores * unit + bias_ref[...]
        weights = jnp.exp2(scores - jnp.max(scores, axis=1, keepdims=True))
        totals = jnp.sum(weights, axis=1, keepdims=True)
        mixed = jnp.dot(weights.astype(jnp.bfloat16), values, preferred_element_type=jnp.float32)
        out_ref[0, :, cols] = (mixed / totals).astype(jnp.bfloat16)


def attend(scal, bias, arrived, q_rows, kv_blocks, first, count, out):
    quota = arrived.shape[0]
    blocks = len(kv_blocks)
    k_spec = pl.BlockSpec((quota, HEAD_SIZE), lambda g: (0, first + g))
    v_spec = pl.BlockSpec((quota, HEAD_SIZE), lambda g: (0, KEY_VALUE_HEADS + first + g))
    in_specs = [
        pl.BlockSpec(memory_space=pltpu.SMEM),
        pl.BlockSpec(bias.shape, lambda g: (0, 0)),
        pl.BlockSpec((quota, GROUP_WIDTH), lambda g: (0, g)),
        pl.BlockSpec((1, quota, GROUP_WIDTH), lambda g: (0, 0, first + g)),
    ]
    in_specs += [k_spec] * blocks + [v_spec] * blocks
    operands = [scal, bias, arrived, q_rows, *kv_blocks, *kv_blocks]
    aliases = {}
    if out is not None:
        in_specs.append(pl.BlockSpec(memory_space=pl.ANY))
        aliases = {len(operands): 0}
        operands.append(out)
    pairs = count * GROUP * quota * quota * blocks
    return pl.pallas_call(
        functools.partial(attend_kernel, blocks, out is not None),
        grid=(count,),
        in_specs=in_specs,
        out_specs=pl.BlockSpec((1, quota, GROUP_WIDTH), lambda g: (0, 0, first + g)),
        out_shape=jax.ShapeDtypeStruct((1, quota, QUERY_HEADS * HEAD_SIZE), jnp.bfloat16),
        input_output_aliases=aliases,
        cost_estimate=pl.CostEstimate(
            flops=4 * pairs * HEAD_SIZE,
            bytes_accessed=count * quota * (3 * GROUP_WIDTH + 2 * blocks * HEAD_SIZE) * 2,
            transcendentals=pairs,
        ),
        compiler_params=pltpu.CompilerParams(vmem_limit_bytes=32 * 1024 * 1024),
        name="attend_heads",
    )(*operands)


def circular_tail(rows, own_count, quota):
    later = (quota + jnp.arange(quota, dtype=jnp.int32) < own_count)[:, None]
    return jnp.where(later, rows[quota:], rows[:quota])


def body(q_rows, k_rows, value_slot_rows, counts, doc_ids):
    quota = doc_ids.shape[1]
    n_ctx = lax.axis_size("ctx")
    rounds = n_ctx // 4
    replica, rank = lax.axis_index("dp"), lax.axis_index("ctx")
    core = rank % 2
    own_count = counts[0, 0]

    kv_tail = jnp.concatenate(
        [
            circular_tail(k_rows[0], own_count, quota),
            circular_tail(value_slot_rows[0], own_count, quota),
        ],
        axis=1,
    )
    arrived_kv = shifted(kv_tail, "dp", 1)

    all_counts = everyones(counts[0], "dp")[:, 0]
    window_docs = everyones(doc_ids[0], "ctx").reshape(-1)

    places = jnp.arange(lax.axis_size("dp"), dtype=jnp.int32)
    before = jnp.sum(jnp.where(places < replica, all_counts, 0))
    before_last = jnp.sum(jnp.where(places < replica - 1, all_counts, 0))
    shift_in = before - replica * quota
    shift_before = jnp.where(replica > 0, before_last - (replica - 1) * quota, 0)
    scal = jnp.stack([shift_in, shift_before]).astype(jnp.int32)

    ranks = [rank]
    for back in range(1, rounds + 1):
        ranks.append(rank - 2 * back)
        if back < rounds:
            ranks.append(rank - 2 * back + jnp.where(core == 0, 1, -1))
    ranks.append(jnp.where(core == 0, rank - 2 * rounds + 1, rank - 1))
    key_places = (
        jnp.stack(ranks)[:, None] * quota + jnp.arange(quota, dtype=jnp.int32)[None, :]
    ).reshape(1, -1)
    own_places = rank * quota + jnp.arange(quota, dtype=jnp.int32)[:, None]
    doc_start = jnp.sum(
        (window_docs[None, :] < doc_ids[0][:, None]).astype(jnp.int32), axis=1, keepdims=True
    )
    allowed = (key_places <= own_places) & (key_places >= doc_start)
    bias = jnp.where(allowed, 0.0, MASKED).astype(jnp.float32)

    own = settle_kv(scal, arrived_kv, k_rows, value_slot_rows)

    arrived_q = []
    first = 0
    for size in CHUNKS:
        cols = slice(first * GROUP_WIDTH, (first + size) * GROUP_WIDTH)
        tail = circular_tail(q_rows[0, :, cols], own_count, quota)
        arrived_q.append(shifted(tail, "dp", 1))
        first += size

    kv_blocks = [own]
    carried = own
    for back in range(1, rounds + 1):
        carried = shifted(carried, "ctx", 2)
        kv_blocks.append(carried)
        if back < rounds:
            kv_blocks.append(swapped_cores(carried))
    kv_blocks.append(swapped_cores(jnp.where(core == 0, own, carried)))

    out = None
    first = 0
    for size, arrived in zip(CHUNKS, arrived_q):
        out = attend(scal, bias, arrived, q_rows, kv_blocks, first, size, out)
        first += size
    return out


def solution(mesh):
    return jax.shard_map(
        body,
        mesh=mesh,
        in_specs=(
            P("dp", "ctx", None),
            P("dp", "ctx", None),
            P("dp", "ctx", None),
            P("dp", "ctx"),
            P("dp", "ctx"),
        ),
        out_specs=P("dp", "ctx", None),
        check_vma=False,
    )
```

time: 259 us -> 106 us (0.41)
  the two profiles are of different devices: /device:TPU:21 before, /device:TPU:0 now
where the time goes in v1:
time: 106 us; the launch traced here: 105 us
  starting transfers between devices  38.9 us (37%)
  Pallas kernels  31.8 us (30%)
  waiting for transfers between devices  19.8 us (19%)
  other arithmetic  8.29 us (8%)
  local copies, waits for them, and re-layouts  4.25 us (4%)
  between operations  2.13 us (2%)
    ppermute x8, starting transfers between devices, shifted(): return lax.ppermute(x, axis, [(i, i + steps) for i in range(n - steps)])  31.4 us
    pallas_call x5, Pallas kernels, attend(): pl.pallas_call(functools.partial(attend_kernel, blocks, out is not None),...  29.4 us
    ppermute x8, waiting for transfers between devices, shifted(): return lax.ppermute(x, axis, [(i, i + steps) for i in range(n - steps)])  10.6 us
    all_to_all x2, waiting for transfers between devices, everyones(): return lax.all_to_all(spread, axis, split_axis=0, concat_axis=0)  9.25 us
    all_to_all x2, starting transfers between devices, everyones(): return lax.all_to_all(spread, axis, split_axis=0, concat_axis=0)  7.06 us
    select_n x2, other arithmetic, circular_tail(): return jnp.where(later, rows[quota:], rows[:quota])  5.48 us
    unnamed x12, local copies, waits for them, and re-layouts  2.99 us
    pallas_call x1, Pallas kernels, settle_kv(): pl.pallas_call(settle_kernel, grid=(1,), in_specs=[pl.BlockSpec(memory_sp...  2.31 us
  transfers between devices with their start and end apart: 12, of which 3 were waited for; matrix products, arithmetic and copies ran while one was open for 7% of the time, Pallas kernels for 24%

profile of v1, /device:TPU:0, one launch (start us, length us, event | category | flops | bytes accessed | tf_op | source)
XLA Modules:
  0.0 105.2 jit_solution(8851223776196127003)
XLA Ops:
  0.7 2.4 %bitcast_select_fusion.3 = (bf16[128,1024]{1,0:T(8,128)(2,1)}, bf16[128,1024]{1,0:T(8,128)(2,1)S(1)}, bf16[128,1024]{1,0:T(8,128)(2,1)S(1)}, bf16[128,1024]{1,0:T(8,128)(2,1)S(1)}) fusion(bf16[1,256,8192]{2,1,0:T(8,128)(2,1)} %local_ref.9, pred[128]{0:T(512)(128)(4,1)S(1)} %add_compare_fusion, bf16[1,256,1024]{2,1,0:T(8,128)(2,1)} %k_ref.1, ...), kind=kLoop, calls=%fused_computation.7 | loop fusion | flops 524288 | bytes 3145856 | tf_op jit(solution)/shard_map/jit(_where)/select_n | solution.py:132
  3.1 0.0 copy-start.5
  3.1 4.9 %collective-permute-start.1 = (bf16[128,2048]{1,0:T(8,128)(2,1)S(1)}, bf16[128,2048]{1,0:T(8,128)(2,1)S(1)}, u32[]{:S(2)}, u32[]{:S(2)}) collective-permute-start(bf16[128,2048]{1,0:T(8,128)(2,1)S(1)} %pad_maximum_fusion), channel_id=1, source_target_pairs={{0,8},{8,16},{16,24},{1,9},{9,17},{17,25},{2,10},{10,18},{18,26},{... | collective-permute-start | bytes 1572872 | tf_op jit(solution)/shard_map/ppermute | solution.py:23
  8.0 0.6 broadcast_in_dim.68
  8.6 3.2 %all-to-all-start = ((s32[4,1,1]{2,1,0:T(1,128)}), s32[4,1,1]{2,1,0:T(1,128)S(1)}, u32[]{:S(2)}, u32[]{:S(2)}) async-start(s32[4,1,1]{2,1,0:T(1,128)} %broadcast_in_dim.68), calls=%async_computation | async-start | bytes 4096 | tf_op jit(solution)/shard_map/all_to_all | solution.py:34
  11.8 9.2 %all-to-all-done = s32[4,1,1]{2,1,0:T(1,128)S(1)} async-done(((s32[4,1,1]{2,1,0:T(1,128)}), s32[4,1,1]{2,1,0:T(1,128)S(1)}, u32[]{:S(2)}, u32[]{:S(2)}) %all-to-all-start) | async-done | bytes 48 | tf_op jit(solution)/shard_map/all_to_all | solution.py:34
  21.1 0.2 reduce
  21.2 0.7 fusion
  23.2 0.6 pad_add_fusion.scal_ref
  23.9 0.0 collective-permute-done.1.arrived_ref
  23.9 0.0 copy-start.4
  23.9 0.8 copy-done.4
  24.7 2.3 %settle_kv.1.refs_0_.refs_5_ = bf16[128,2048]{1,0:T(8,128)(2,1)} custom-call(s32[2]{0:T(128)} %pad_add_fusion.scal_ref, bf16[128,2048]{1,0:T(8,128)(2,1)} %copy-done.4, bf16[1,256,1024]{2,1,0:T(8,128)(2,1)} %k_ref.1, bf16[1,256,1024]{2,1,0:T(8,128)(2,1)} %v_ref.1), custom_call_target="tpu_custom_call" | custom-call | tf_op jit(solution)/shard_map/settle_kv/pallas_call | solution.py:63
  27.0 3.5 %collective-permute-start.2 = (bf16[128,2048]{1,0:T(8,128)(2,1)}, bf16[128,2048]{1,0:T(8,128)(2,1)S(1)}, u32[]{:S(2)}, u32[]{:S(2)}) collective-permute-start(bf16[128,2048]{1,0:T(8,128)(2,1)} %settle_kv.1.refs_0_.refs_5_), channel_id=1, source_target_pairs={{0,2},{1,3},{2,4},{3,5},{4,6},{5,7},{8,10},{9,11},{10,12},{11,13},... | collective-permute-start | bytes 1572872 | tf_op jit(solution)/shard_map/ppermute | solution.py:23
  30.5 0.0 copy-done.5
  30.5 0.6 broadcast_in_dim.70
  31.1 3.8 %all-to-all-start.1 = ((s32[8,1,128]{2,1,0:T(1,128)}), s32[8,1,128]{2,1,0:T(1,128)S(1)}, u32[]{:S(2)}, u32[]{:S(2)}) async-start(s32[8,1,128]{2,1,0:T(1,128)} %broadcast_in_dim.70), calls=%async_computation.1 | async-start | bytes 8192 | tf_op jit(solution)/shard_map/all_to_all | solution.py:34
  34.9 0.0 copy-start.2
  34.9 0.0 copy-start.3
  34.9 5.9 %collective-permute-done.2.refs_1_.refs_6_ = bf16[128,2048]{1,0:T(8,128)(2,1)S(1)} collective-permute-done((bf16[128,2048]{1,0:T(8,128)(2,1)}, bf16[128,2048]{1,0:T(8,128)(2,1)S(1)}, u32[]{:S(2)}, u32[]{:S(2)}) %collective-permute-start.2) | collective-permute-done | bytes 524320 | tf_op jit(solution)/shard_map/ppermute | solution.py:23
  40.8 4.3 %collective-permute-start.4 = (bf16[128,2048]{1,0:T(8,128)(2,1)S(1)}, bf16[128,2048]{1,0:T(8,128)(2,1)S(1)}, u32[]{:S(2)}, u32[]{:S(2)}) collective-permute-start(bf16[128,2048]{1,0:T(8,128)(2,1)S(1)} %collective-permute-done.2.refs_1_.refs_6_), channel_id=1, source_target_pairs={{0,2},{1,3},{2,4},{3,5},{4,6},{5,7},{8,10},{9,11},{10,12},{11,13},... | collective-permute-start | bytes 1572872 | tf_op jit(solution)/shard_map/ppermute | solution.py:23
  45.1 3.1 %bitcast_select_fusion = (bf16[128,2048]{1,0:T(8,128)(2,1)}, bf16[128,2048]{1,0:T(8,128)(2,1)}, bf16[128,2048]{1,0:T(8,128)(2,1)}) fusion(bf16[1,256,8192]{2,1,0:T(8,128)(2,1)} %local_ref.9, pred[128]{0:T(512)(128)(4,1)S(1)} %add_compare_fusion), kind=kLoop, calls=%fused_computation.1 | loop fusion | flops 786432 | bytes 4718720 | tf_op jit(solution)/shard_map/jit(_where)/select_n | solution.py:132
  48.2 4.2 %collective-permute-start.9 = (bf16[128,2048]{1,0:T(8,128)(2,1)}, bf16[128,2048]{1,0:T(8,128)(2,1)}, u32[]{:S(2)}, u32[]{:S(2)}) collective-permute-start(bf16[128,2048]{1,0:T(8,128)(2,1)} %get-tuple-element.7), channel_id=1, source_target_pairs={{0,8},{8,16},{16,24},{1,9},{9,17},{17,25},{2,10},{10,18},{18,26},{... | collective-permute-start | bytes 1572872 | tf_op jit(solution)/shard_map/ppermute | solution.py:23
  52.4 3.6 %collective-permute-start.8 = (bf16[128,2048]{1,0:T(8,128)(2,1)}, bf16[128,2048]{1,0:T(8,128)(2,1)}, u32[]{:S(2)}, u32[]{:S(2)}) collective-permute-start(bf16[128,2048]{1,0:T(8,128)(2,1)} %get-tuple-element.8), channel_id=1, source_target_pairs={{0,8},{8,16},{16,24},{1,9},{9,17},{17,25},{2,10},{10,18},{18,26},{... | collective-permute-start | bytes 1572872 | tf_op jit(solution)/shard_map/ppermute | solution.py:23
  56.0 1.7 %collective-permute-start.7 = (bf16[128,2048]{1,0:T(8,128)(2,1)}, bf16[128,2048]{1,0:T(8,128)(2,1)S(1)}, u32[]{:S(2)}, u32[]{:S(2)}) collective-permute-start(bf16[128,2048]{1,0:T(8,128)(2,1)} %get-tuple-element.9), channel_id=1, source_target_pairs={{0,8},{8,16},{16,24},{1,9},{9,17},{17,25},{2,10},{10,18},{18,26},{... | collective-permute-start | bytes 1572872 | tf_op jit(solution)/shard_map/ppermute | solution.py:23
  57.8 0.1 stack.35
  57.9 0.0 collective-permute-start.3
  57.9 0.0 collective-permute-done.4.refs_3_.refs_8_
  57.9 0.0 copy-done.2
  57.9 0.9 broadcast_select_fusion
  58.8 0.5 collective-permute-start.5
  59.3 0.1 add_bitcast_fusion
  59.3 0.0 all-to-all-done.1
  59.3 0.2 convert_reduce_fusion
  59.5 4.7 %collective-permute-done.9.arrived_ref = bf16[128,2048]{1,0:T(8,128)(2,1)} collective-permute-done((bf16[128,2048]{1,0:T(8,128)(2,1)}, bf16[128,2048]{1,0:T(8,128)(2,1)}, u32[]{:S(2)}, u32[]{:S(2)}) %collective-permute-start.9) | collective-permute-done | bytes 524320 | tf_op jit(solution)/shard_map/ppermute | solution.py:23
  64.2 4.4 %collective-permute-start.6 = (bf16[128,1024]{1,0:T(8,128)(2,1)}, bf16[128,1024]{1,0:T(8,128)(2,1)S(1)}, u32[]{:S(2)}, u32[]{:S(2)}) collective-permute-start(bf16[128,1024]{1,0:T(8,128)(2,1)} %get-tuple-element.10), channel_id=1, source_target_pairs={{0,8},{8,16},{16,24},{1,9},{9,17},{17,25},{2,10},{10,18},{18,26},{... | collective-permute-start | bytes 786440 | tf_op jit(solution)/shard_map/ppermute | solution.py:23
  68.6 0.0 collective-permute-done.3.refs_2_.refs_7_
  68.7 4.7 %collective-permute-start = (bf16[128,1024]{1,0:T(8,128)(2,1)S(1)}, bf16[128,1024]{1,0:T(8,128)(2,1)S(1)}, u32[]{:S(2)}, u32[]{:S(2)}) collective-permute-start(bf16[128,1024]{1,0:T(8,128)(2,1)S(1)} %get-tuple-element.11), channel_id=1, source_target_pairs={{0,8},{8,16},{16,24},{1,9},{9,17},{17,25},{2,10},{10,18},{18,26},{... | collective-permute-start | bytes 786440 | tf_op jit(solution)/shard_map/ppermute | solution.py:23
  73.4 0.1 and_select_fusion.bias_ref
  73.5 0.0 collective-permute-done.5.refs_4_.refs_9_
  73.5 0.0 copy-done.3
  73.5 0.0 copy-start
  73.5 2.2 %copy-done = bf16[1,256,8192]{2,1,0:T(8,128)(2,1)S(1)} copy-done((bf16[1,256,8192]{2,1,0:T(8,128)(2,1)S(1)}, bf16[1,256,8192]{2,1,0:T(8,128)(2,1)}, u32[]{:S(2)}) %copy-start) | copy-done | bytes 4194328
  75.7 0.0 copy-start.1
  75.7 7.3 %attend_heads.5.refs_10_ = bf16[1,128,8192]{2,1,0:T(8,128)(2,1)} custom-call(s32[2]{0:T(128)S(1)} %copy-done.3, f32[128,640]{1,0:T(8,128)S(1)} %and_select_fusion.bias_ref, bf16[128,2048]{1,0:T(8,128)(2,1)} %collective-permute-done.9.arrived_ref, bf16[1,256,8192]{2,1,0:T(8,128)(2,1)S(1)} %copy-done, bf16[128,2048]{1,0:T(8,128)(2,1)S(1)} %copy-done.2, ...), custom_call_target="tpu_custom_call" | custom-call | flops 671088640 | bytes 2228224 | tf_op jit(solution)/shard_map/attend_heads/pallas_call | solution.py:113
  83.0 0.0 collective-permute-done.8.arrived_ref
  83.0 0.0 copy-done.1
  83.0 7.3 %attend_heads.6.refs_10_ = bf16[1,128,8192]{2,1,0:T(8,128)(2,1)} custom-call(s32[2]{0:T(128)S(1)} %copy-done.3, f32[128,640]{1,0:T(8,128)S(1)} %and_select_fusion.bias_ref, bf16[128,2048]{1,0:T(8,128)(2,1)} %collective-permute-done.8.arrived_ref, bf16[1,256,8192]{2,1,0:T(8,128)(2,1)S(1)} %copy-done.1, ...), custom_call_target="tpu_custom_call", output_to_operand_aliasing={{}: (14, {})} | custom-call | flops 671088640 | bytes 2228224 | tf_op jit(solution)/shard_map/attend_heads/pallas_call | solution.py:113
  90.3 0.0 collective-permute-done.7.arrived_ref
  90.3 6.9 %attend_heads.7.refs_10_ = bf16[1,128,8192]{2,1,0:T(8,128)(2,1)} custom-call(s32[2]{0:T(128)S(1)} %copy-done.3, f32[128,640]{1,0:T(8,128)S(1)} %and_select_fusion.bias_ref, bf16[128,2048]{1,0:T(8,128)(2,1)S(1)} %collective-permute-done.7.arrived_ref, bf16[1,256,8192]{2,1,0:T(8,128)(2,1)S(1)} %copy-done.1, ...), custom_call_target="tpu_custom_call", output_to_operand_aliasing={{}: (14, {})} | custom-call | flops 671088640 | bytes 2228224 | tf_op jit(solution)/shard_map/attend_heads/pallas_call | solution.py:113
  97.3 0.0 collective-permute-done.6.arrived_ref
  97.3 4.0 %attend_heads.8.refs_10_ = bf16[1,128,8192]{2,1,0:T(8,128)(2,1)} custom-call(s32[2]{0:T(128)S(1)} %copy-done.3, f32[128,640]{1,0:T(8,128)S(1)} %and_select_fusion.bias_ref, bf16[128,1024]{1,0:T(8,128)(2,1)S(1)} %collective-permute-done.6.arrived_ref, bf16[1,256,8192]{2,1,0:T(8,128)(2,1)S(1)} %copy-done.1, ...), custom_call_target="tpu_custom_call", output_to_operand_aliasing={{}: (14, {})} | custom-call | flops 335544320 | bytes 1114112 | tf_op jit(solution)/shard_map/attend_heads/pallas_call | solution.py:113
  101.2 0.0 collective-permute-done.arrived_ref
  101.2 4.0 %attend_heads.9 = bf16[1,128,8192]{2,1,0:T(8,128)(2,1)} custom-call(s32[2]{0:T(128)S(1)} %copy-done.3, f32[128,640]{1,0:T(8,128)S(1)} %and_select_fusion.bias_ref, bf16[128,1024]{1,0:T(8,128)(2,1)S(1)} %collective-permute-done.arrived_ref, bf16[1,256,8192]{2,1,0:T(8,128)(2,1)S(1)} %copy-done.1, ...), custom_call_target="tpu_custom_call", output_to_operand_aliasing={{}: (14, {})} | custom-call | flops 335544320 | bytes 1114112 | tf_op jit(solution)/shard_map/attend_heads/pallas_call | solution.py:113
  (4 shorter events, 0.1 us)
Async XLA Ops:
  3.1 27.4 %copy-start.5 = (s32[1,128]{1,0:T(1,128)S(1)}, s32[1,128]{1,0:T(1,128)}, u32[]{:S(2)}) copy-start(s32[1,128]{1,0:T(1,128)} %param.9) | copy-start | bytes 1540
  3.1 20.8 %collective-permute-start.1 = (bf16[128,2048]{1,0:T(8,128)(2,1)S(1)}, bf16[128,2048]{1,0:T(8,128)(2,1)S(1)}, u32[]{:S(2)}, u32[]{:S(2)}) collective-permute-start(bf16[128,2048]{1,0:T(8,128)(2,1)S(1)} %pad_maximum_fusion), channel_id=1, source_target_pairs={{0,8},{8,16},{16,24},{1,9},{9,17},{17,25},{2,10},{10,18},{18,26},{... | collective-permute-start | bytes 1572872 | tf_op jit(solution)/shard_map/ppermute | solution.py:23
  8.6 12.5 %all-to-all-start = ((s32[4,1,1]{2,1,0:T(1,128)}), s32[4,1,1]{2,1,0:T(1,128)S(1)}, u32[]{:S(2)}, u32[]{:S(2)}) async-start(s32[4,1,1]{2,1,0:T(1,128)} %broadcast_in_dim.68), calls=%async_computation | async-start | bytes 4096 | tf_op jit(solution)/shard_map/all_to_all | solution.py:34
  23.9 0.8 copy-start.4
  27.0 13.8 %collective-permute-start.2 = (bf16[128,2048]{1,0:T(8,128)(2,1)}, bf16[128,2048]{1,0:T(8,128)(2,1)S(1)}, u32[]{:S(2)}, u32[]{:S(2)}) collective-permute-start(bf16[128,2048]{1,0:T(8,128)(2,1)} %settle_kv.1.refs_0_.refs_5_), channel_id=1, source_target_pairs={{0,2},{1,3},{2,4},{3,5},{4,6},{5,7},{8,10},{9,11},{10,12},{11,13},... | collective-permute-start | bytes 1572872 | tf_op jit(solution)/shard_map/ppermute | solution.py:23
  31.1 28.3 %all-to-all-start.1 = ((s32[8,1,128]{2,1,0:T(1,128)}), s32[8,1,128]{2,1,0:T(1,128)S(1)}, u32[]{:S(2)}, u32[]{:S(2)}) async-start(s32[8,1,128]{2,1,0:T(1,128)} %broadcast_in_dim.70), calls=%async_computation.1 | async-start | bytes 8192 | tf_op jit(solution)/shard_map/all_to_all | solution.py:34
  34.9 23.0 %copy-start.2 = (bf16[128,2048]{1,0:T(8,128)(2,1)S(1)}, bf16[128,2048]{1,0:T(8,128)(2,1)}, u32[]{:S(2)}) copy-start(bf16[128,2048]{1,0:T(8,128)(2,1)} %settle_kv.1.refs_0_.refs_5_) | copy-start | bytes 1572868
  34.9 38.6 %copy-start.3 = (s32[2]{0:T(128)S(1)}, s32[2]{0:T(128)}, u32[]{:S(2)}) copy-start(s32[2]{0:T(128)} %pad_add_fusion.scal_ref) | copy-start | bytes 28
  40.8 17.1 %collective-permute-start.4 = (bf16[128,2048]{1,0:T(8,128)(2,1)S(1)}, bf16[128,2048]{1,0:T(8,128)(2,1)S(1)}, u32[]{:S(2)}, u32[]{:S(2)}) collective-permute-start(bf16[128,2048]{1,0:T(8,128)(2,1)S(1)} %collective-permute-done.2.refs_1_.refs_6_), channel_id=1, source_target_pairs={{0,2},{1,3},{2,4},{3,5},{4,6},{5,7},{8,10},{9,11},{10,12},{11,13},... | collective-permute-start | bytes 1572872 | tf_op jit(solution)/shard_map/ppermute | solution.py:23
  48.2 16.1 %collective-permute-start.9 = (bf16[128,2048]{1,0:T(8,128)(2,1)}, bf16[128,2048]{1,0:T(8,128)(2,1)}, u32[]{:S(2)}, u32[]{:S(2)}) collective-permute-start(bf16[128,2048]{1,0:T(8,128)(2,1)} %get-tuple-element.7), channel_id=1, source_target_pairs={{0,8},{8,16},{16,24},{1,9},{9,17},{17,25},{2,10},{10,18},{18,26},{... | collective-permute-start | bytes 1572872 | tf_op jit(solution)/shard_map/ppermute | solution.py:23
  52.4 30.7 %collective-permute-start.8 = (bf16[128,2048]{1,0:T(8,128)(2,1)}, bf16[128,2048]{1,0:T(8,128)(2,1)}, u32[]{:S(2)}, u32[]{:S(2)}) collective-permute-start(bf16[128,2048]{1,0:T(8,128)(2,1)} %get-tuple-element.8), channel_id=1, source_target_pairs={{0,8},{8,16},{16,24},{1,9},{9,17},{17,25},{2,10},{10,18},{18,26},{... | collective-permute-start | bytes 1572872 | tf_op jit(solution)/shard_map/ppermute | solution.py:23
  56.0 34.3 %collective-permute-start.7 = (bf16[128,2048]{1,0:T(8,128)(2,1)}, bf16[128,2048]{1,0:T(8,128)(2,1)S(1)}, u32[]{:S(2)}, u32[]{:S(2)}) collective-permute-start(bf16[128,2048]{1,0:T(8,128)(2,1)} %get-tuple-element.9), channel_id=1, source_target_pairs={{0,8},{8,16},{16,24},{1,9},{9,17},{17,25},{2,10},{10,18},{18,26},{... | collective-permute-start | bytes 1572872 | tf_op jit(solution)/shard_map/ppermute | solution.py:23
  57.9 10.8 %collective-permute-start.3 = (bf16[128,2048]{1,0:T(8,128)(2,1)S(1)}, bf16[128,2048]{1,0:T(8,128)(2,1)S(1)}, u32[]{:S(2)}, u32[]{:S(2)}) collective-permute-start(bf16[128,2048]{1,0:T(8,128)(2,1)S(1)} %collective-permute-done.2.refs_1_.refs_6_), channel_id=1, source_target_pairs={{0,1},{1,0},{2,3},{3,2},{4,5},{5,4},{6,7},{7,6},{8,9},{9,8},{10,11... | collective-permute-start | bytes 1572872 | tf_op jit(solution)/shard_map/ppermute | solution.py:28
  58.8 14.7 %collective-permute-start.5 = (bf16[128,2048]{1,0:T(8,128)(2,1)}, bf16[128,2048]{1,0:T(8,128)(2,1)S(1)}, u32[]{:S(2)}, u32[]{:S(2)}) collective-permute-start(bf16[128,2048]{1,0:T(8,128)(2,1)} %broadcast_select_fusion), channel_id=1, source_target_pairs={{0,1},{1,0},{2,3},{3,2},{4,5},{5,4},{6,7},{7,6},{8,9},{9,8},{10,11... | collective-permute-start | bytes 1572872 | tf_op jit(solution)/shard_map/ppermute | solution.py:28
  64.2 33.0 %collective-permute-start.6 = (bf16[128,1024]{1,0:T(8,128)(2,1)}, bf16[128,1024]{1,0:T(8,128)(2,1)S(1)}, u32[]{:S(2)}, u32[]{:S(2)}) collective-permute-start(bf16[128,1024]{1,0:T(8,128)(2,1)} %get-tuple-element.10), channel_id=1, source_target_pairs={{0,8},{8,16},{16,24},{1,9},{9,17},{17,25},{2,10},{10,18},{18,26},{... | collective-permute-start | bytes 786440 | tf_op jit(solution)/shard_map/ppermute | solution.py:23
  68.7 32.6 %collective-permute-start = (bf16[128,1024]{1,0:T(8,128)(2,1)S(1)}, bf16[128,1024]{1,0:T(8,128)(2,1)S(1)}, u32[]{:S(2)}, u32[]{:S(2)}) collective-permute-start(bf16[128,1024]{1,0:T(8,128)(2,1)S(1)} %get-tuple-element.11), channel_id=1, source_target_pairs={{0,8},{8,16},{16,24},{1,9},{9,17},{17,25},{2,10},{10,18},{18,26},{... | collective-permute-start | bytes 786440 | tf_op jit(solution)/shard_map/ppermute | solution.py:23
  73.5 2.2 %copy-start = (bf16[1,256,8192]{2,1,0:T(8,128)(2,1)S(1)}, bf16[1,256,8192]{2,1,0:T(8,128)(2,1)}, u32[]{:S(2)}) copy-start(bf16[1,256,8192]{2,1,0:T(8,128)(2,1)} %local_ref.9) | copy-start | bytes 12582916
  75.7 7.3 %copy-start.1 = (bf16[1,256,8192]{2,1,0:T(8,128)(2,1)S(1)}, bf16[1,256,8192]{2,1,0:T(8,128)(2,1)}, u32[]{:S(2)}) copy-start(bf16[1,256,8192]{2,1,0:T(8,128)(2,1)} %local_ref.9) | copy-start | bytes 12582916

commit v2 on v1

--- a/solution.py
+++ b/solution.py
@@ -15,7 +15,8 @@
 GROUP_WIDTH = GROUP * HEAD_SIZE
 KV_WIDTH = KEY_VALUE_HEADS * HEAD_SIZE
 MASKED = -1e30
-CHUNKS = (2, 2, 2, 1, 1)
+CHUNKS = (1, 3, 2, 2)
+PARTS = 2
 
 
 def shifted(x, axis, steps):
@@ -70,7 +71,7 @@
     )(scal, arrived, k_rows, v_rows)
 
 
-def attend_kernel(blocks, has_out, scal_ref, bias_ref, arrived_ref, local_ref, *refs):
+def attend_kernel(blocks, scal_ref, bias_ref, arrived_ref, local_ref, *refs):
     k_refs, v_refs = refs[:blocks], refs[blocks : 2 * blocks]
     out_ref = refs[-1]
     quota = arrived_ref.shape[0]
@@ -78,17 +79,37 @@
     q = place_rows(hot, arrived_ref[...], local_ref[0])
     keys = jnp.concatenate([r[...] for r in k_refs], axis=0)
     values = jnp.concatenate([r[...] for r in v_refs], axis=0)
+    values = jnp.concatenate([values, jnp.ones_like(values)], axis=1)
     unit = math.log2(math.e) / math.sqrt(HEAD_SIZE)
-    for head in range(GROUP):
-        cols = slice(head * HEAD_SIZE, (head + 1) * HEAD_SIZE)
-        scores = lax.dot_general(
-            q[:, cols], keys, (((1,), (1,)), ((), ())), preferred_element_type=jnp.float32
+    heads = GROUP // PARTS
+
+    def scored(part):
+        stacked = jnp.concatenate(
+            [
+                q[:, h * HEAD_SIZE : (h + 1) * HEAD_SIZE]
+                for h in range(part * heads, (part + 1) * heads)
+            ],
+            axis=0,
         )
-        scores = scores * unit + bias_ref[...]
-        weights = jnp.exp2(scores - jnp.max(scores, axis=1, keepdims=True))
-        totals = jnp.sum(weights, axis=1, keepdims=True)
-        mixed = jnp.dot(weights.astype(jnp.bfloat16), values, preferred_element_type=jnp.float32)
-        out_ref[0, :, cols] = (mixed / totals).astype(jnp.bfloat16)
+        return lax.dot_general(
+            stacked, keys, (((1,), (1,)), ((), ())), preferred_element_type=jnp.float32
+        )
+
+    def finished(part, scores):
+        scores = scores.reshape(heads, quota, -1) * unit + bias_ref[...][None]
+        weights = jnp.exp2(scores - jnp.max(scores, axis=2, keepdims=True))
+        weights = weights.astype(jnp.bfloat16).reshape(heads * quota, -1)
+        mixed = jnp.dot(weights, values, preferred_element_type=jnp.float32)
+        mixed = (mixed[:, :HEAD_SIZE] / mixed[:, HEAD_SIZE:]).astype(jnp.bfloat16)
+        for h in range(heads):
+            at = (part * heads + h) * HEAD_SIZE
+            out_ref[0, :, at : at + HEAD_SIZE] = mixed[h * quota : (h + 1) * quota]
+
+    scores = scored(0)
+    for part in range(PARTS):
+        later = scored(part + 1) if part + 1 < PARTS else None
+        finished(part, scores)
+        scores = later
 
 
 def attend(scal, bias, arrived, q_rows, kv_blocks, first, count, out):
@@ -111,7 +132,7 @@
         operands.append(out)
     pairs = count * GROUP * quota * quota * blocks
     return pl.pallas_call(
-        functools.partial(attend_kernel, blocks, out is not None),
+        functools.partial(attend_kernel, blocks),
         grid=(count,),
         in_specs=in_specs,
         out_specs=pl.BlockSpec((1, quota, GROUP_WIDTH), lambda g: (0, 0, first + g)),
@@ -127,9 +148,9 @@
     )(*operands)
 
 
-def circular_tail(rows, own_count, quota):
-    later = (quota + jnp.arange(quota, dtype=jnp.int32) < own_count)[:, None]
-    return jnp.where(later, rows[quota:], rows[:quota])
+def circular_tail(rows, later):
+    quota = later.shape[0]
+    return jnp.where(later[:, None], rows[quota:], rows[:quota])
 
 
 def body(q_rows, k_rows, value_slot_rows, counts, doc_ids):
@@ -140,16 +161,25 @@
     core = rank % 2
     own_count = counts[0, 0]
 
+    all_counts = everyones(counts[0], "dp")[:, 0]
+    later = quota + jnp.arange(quota, dtype=jnp.int32) < own_count
     kv_tail = jnp.concatenate(
         [
-            circular_tail(k_rows[0], own_count, quota),
-            circular_tail(value_slot_rows[0], own_count, quota),
+            circular_tail(k_rows[0], later),
+            circular_tail(value_slot_rows[0], later),
         ],
         axis=1,
     )
+    kv_tail, later = lax.optimization_barrier((kv_tail, later))
     arrived_kv = shifted(kv_tail, "dp", 1)
-
-    all_counts = everyones(counts[0], "dp")[:, 0]
+    q_tails = []
+    first = 0
+    for size in CHUNKS:
+        cols = slice(first * GROUP_WIDTH, (first + size) * GROUP_WIDTH)
+        q_tails.append(circular_tail(q_rows[0, :, cols], later))
+        first += size
+    arrived_q = [shifted(tail, "dp", 1) for tail in q_tails]
+
     window_docs = everyones(doc_ids[0], "ctx").reshape(-1)
 
     places = jnp.arange(lax.axis_size("dp"), dtype=jnp.int32)
@@ -176,20 +206,15 @@
     bias = jnp.where(allowed, 0.0, MASKED).astype(jnp.float32)
 
     own = settle_kv(scal, arrived_kv, k_rows, value_slot_rows)
-
-    arrived_q = []
-    first = 0
-    for size in CHUNKS:
-        cols = slice(first * GROUP_WIDTH, (first + size) * GROUP_WIDTH)
-        tail = circular_tail(q_rows[0, :, cols], own_count, quota)
-        arrived_q.append(shifted(tail, "dp", 1))
-        first += size
+    own, arrived_q[0] = lax.optimization_barrier((own, arrived_q[0]))
 
     kv_blocks = [own]
     carried = own
     for back in range(1, rounds + 1):
         carried = shifted(carried, "ctx", 2)
         kv_blocks.append(carried)
+        if back < min(rounds + 1, len(CHUNKS)):
+            carried, arrived_q[back] = lax.optimization_barrier((carried, arrived_q[back]))
         if back < rounds:
             kv_blocks.append(swapped_cores(carried))
     kv_blocks.append(swapped_cores(jnp.where(core == 0, own, carried)))

time: 106 us -> 104 us (0.981)
  the two profiles are of different devices: /device:TPU:0 before, /device:TPU:21 now
where the time goes in v2:
time: 104 us; the launch traced here: 103 us
  starting transfers between devices  34.1 us (33%)
  waiting for transfers between devices  29.4 us (28%)
  Pallas kernels  20.8 us (20%)
  other arithmetic  10.3 us (10%)
  local copies, waits for them, and re-layouts  5.98 us (6%)
  between operations  2.04 us (2%)
    all_to_all x2, waiting for transfers between devices, everyones(): return lax.all_to_all(spread, axis, split_axis=0, concat_axis=0)  22.3 us
    pallas_call x4, Pallas kernels, attend(): pl.pallas_call(functools.partial(attend_kernel, blocks), grid=(count,), i...  18.5 us
    ppermute x7, starting transfers between devices, shifted(): return lax.ppermute(x, axis, [(i, i + steps) for i in range(n - steps)])  17.9 us
    all_to_all x2, starting transfers between devices, everyones(): return lax.all_to_all(spread, axis, split_axis=0, concat_axis=0)  12.5 us
    select_n x4, other arithmetic, circular_tail(): return jnp.where(later[:, None], rows[quota:], rows[:quota])  7.49 us
    ppermute x7, waiting for transfers between devices, shifted(): return lax.ppermute(x, axis, [(i, i + steps) for i in range(n - steps)])  5.8 us
    unnamed x18, local copies, waits for them, and re-layouts  4.75 us
    ppermute x2, starting transfers between devices, swapped_cores(): return lax.ppermute(x, 'ctx', [(i, i ^ 1) for i in range(n)])  3.72 us
  transfers between devices with their start and end apart: 11, of which 3 were waited for; matrix products, arithmetic and copies ran while one was open for 9% of the time, Pallas kernels for 16%

profile of v2, /device:TPU:21, one launch (start us, length us, event | category | flops | bytes accessed | tf_op | source)
XLA Modules:
  0.0 102.6 jit_solution(14626480170723055752)
XLA Ops:
  0.7 1.3 %bitcast_select_fusion.5 = (bf16[128,1024]{1,0:T(8,128)(2,1)S(1)}, bf16[128,1024]{1,0:T(8,128)(2,1)S(1)}) fusion(bf16[1,256,1024]{2,1,0:T(8,128)(2,1)} %k_ref.1, pred[128]{0:T(512)(128)(4,1)S(1)} %add_compare_fusion, bf16[1,256,1024]{2,1,0:T(8,128)(2,1)} %v_ref.1), kind=kLoop, calls=%fused_computation.9 | loop fusion | flops 262144 | bytes 1572992 | tf_op jit(solution)/shard_map/jit(_where)/select_n | solution.py:153
  2.0 0.0 copy-start.8
  2.0 1.1 %bitcast_select_fusion.3 = bf16[128,1024]{1,0:T(8,128)(2,1)S(1)} fusion(bf16[1,256,8192]{2,1,0:T(8,128)(2,1)} %local_ref.7, pred[128]{0:T(512)(128)(4,1)S(1)} %add_compare_fusion), kind=kLoop, calls=%fused_computation.7 | loop fusion | flops 131072 | bytes 786560 | tf_op jit(solution)/shard_map/jit(_where)/select_n | solution.py:153
  3.2 3.1 %collective-permute-start.2 = (bf16[128,1024]{1,0:T(8,128)(2,1)S(1)}, bf16[128,1024]{1,0:T(8,128)(2,1)S(1)}, u32[]{:S(2)}, u32[]{:S(2)}) collective-permute-start(bf16[128,1024]{1,0:T(8,128)(2,1)S(1)} %bitcast_select_fusion.3), channel_id=1, source_target_pairs={{0,8},{8,16},{16,24},{1,9},{9,17},{17,25},{2,10},{10,18},{18,26},{... | collective-permute-start | bytes 786440 | tf_op jit(solution)/shard_map/ppermute | solution.py:24
  6.3 1.9 %collective-permute-start.1 = (bf16[128,2048]{1,0:T(8,128)(2,1)S(1)}, bf16[128,2048]{1,0:T(8,128)(2,1)S(1)}, u32[]{:S(2)}, u32[]{:S(2)}) collective-permute-start(bf16[128,2048]{1,0:T(8,128)(2,1)S(1)} %pad_maximum_fusion), channel_id=1, source_target_pairs={{0,8},{8,16},{16,24},{1,9},{9,17},{17,25},{2,10},{10,18},{18,26},{... | collective-permute-start | bytes 1572872 | tf_op jit(solution)/shard_map/ppermute | solution.py:24
  8.2 2.4 %bitcast_select_fusion = bf16[128,3072]{1,0:T(8,128)(2,1)} fusion(bf16[1,256,8192]{2,1,0:T(8,128)(2,1)} %local_ref.7, pred[128]{0:T(512)(128)(4,1)S(1)} %add_compare_fusion), kind=kLoop, calls=%fused_computation | loop fusion | flops 393216 | bytes 2359424 | tf_op jit(solution)/shard_map/jit(_where)/select_n | solution.py:153
  10.6 1.9 %collective-permute-start.4 = (bf16[128,3072]{1,0:T(8,128)(2,1)}, bf16[128,3072]{1,0:T(8,128)(2,1)S(1)}, u32[]{:S(2)}, u32[]{:S(2)}) collective-permute-start(bf16[128,3072]{1,0:T(8,128)(2,1)} %bitcast_select_fusion), channel_id=1, source_target_pairs={{0,8},{8,16},{16,24},{1,9},{9,17},{17,25},{2,10},{10,18},{18,26},{... | collective-permute-start | bytes 2359304 | tf_op jit(solution)/shard_map/ppermute | solution.py:24
  12.5 0.6 broadcast_in_dim.71
  13.1 5.8 %all-to-all-start = ((s32[4,1,1]{2,1,0:T(1,128)}), s32[4,1,1]{2,1,0:T(1,128)S(1)}, u32[]{:S(2)}, u32[]{:S(2)}) async-start(s32[4,1,1]{2,1,0:T(1,128)} %broadcast_in_dim.71), calls=%async_computation | async-start | bytes 4096 | tf_op jit(solution)/shard_map/all_to_all | solution.py:35
  18.9 22.3 %all-to-all-done = s32[4,1,1]{2,1,0:T(1,128)S(1)} async-done(((s32[4,1,1]{2,1,0:T(1,128)}), s32[4,1,1]{2,1,0:T(1,128)S(1)}, u32[]{:S(2)}, u32[]{:S(2)}) %all-to-all-start) | async-done | bytes 48 | tf_op jit(solution)/shard_map/all_to_all | solution.py:35
  41.2 0.2 reduce
  41.4 0.7 fusion
  43.3 0.7 pad_add_fusion.scal_ref
  43.9 0.0 copy-start.6
  43.9 0.0 collective-permute-done.1.arrived_ref
  43.9 0.0 copy-start.7
  43.9 0.8 copy-done.7
  44.7 2.3 %settle_kv.1.refs_0_.refs_5_ = bf16[128,2048]{1,0:T(8,128)(2,1)} custom-call(s32[2]{0:T(128)} %pad_add_fusion.scal_ref, bf16[128,2048]{1,0:T(8,128)(2,1)} %copy-done.7, bf16[1,256,1024]{2,1,0:T(8,128)(2,1)} %k_ref.1, bf16[1,256,1024]{2,1,0:T(8,128)(2,1)} %v_ref.1), custom_call_target="tpu_custom_call" | custom-call | tf_op jit(solution)/shard_map/settle_kv/pallas_call | solution.py:64
  47.0 0.0 copy-start.1
  47.0 0.0 collective-permute-done.2.arrived_ref
  47.0 0.0 copy-start.4
  47.0 3.3 %collective-permute-start.3 = (bf16[128,2048]{1,0:T(8,128)(2,1)}, bf16[128,2048]{1,0:T(8,128)(2,1)S(1)}, u32[]{:S(2)}, u32[]{:S(2)}) collective-permute-start(bf16[128,2048]{1,0:T(8,128)(2,1)} %settle_kv.1.refs_0_.refs_5_), channel_id=1, source_target_pairs={{0,2},{1,3},{2,4},{3,5},{4,6},{5,7},{8,10},{9,11},{10,12},{11,13},... | collective-permute-start | bytes 1572872 | tf_op jit(solution)/shard_map/ppermute | solution.py:24
  50.4 2.7 %bitcast_select_fusion.1 = (bf16[128,2048]{1,0:T(8,128)(2,1)}, bf16[128,2048]{1,0:T(8,128)(2,1)}) fusion(bf16[1,256,8192]{2,1,0:T(8,128)(2,1)} %local_ref.7, pred[128]{0:T(512)(128)(4,1)S(1)} %add_compare_fusion), kind=kLoop, calls=%fused_computation.2 | loop fusion | flops 524288 | bytes 3145856 | tf_op jit(solution)/shard_map/jit(_where)/select_n | solution.py:153
  53.0 2.2 %collective-permute-start.7 = (bf16[128,2048]{1,0:T(8,128)(2,1)}, bf16[128,2048]{1,0:T(8,128)(2,1)S(1)}, u32[]{:S(2)}, u32[]{:S(2)}) collective-permute-start(bf16[128,2048]{1,0:T(8,128)(2,1)} %get-tuple-element.23), channel_id=1, source_target_pairs={{0,8},{8,16},{16,24},{1,9},{9,17},{17,25},{2,10},{10,18},{18,26},{... | collective-permute-start | bytes 1572872 | tf_op jit(solution)/shard_map/ppermute | solution.py:24
  55.3 0.0 collective-permute-done.4.arrived_ref
  55.3 0.0 copy-done.4
  55.3 5.8 %collective-permute-done.3.refs_1_.refs_6_ = bf16[128,2048]{1,0:T(8,128)(2,1)S(1)} collective-permute-done((bf16[128,2048]{1,0:T(8,128)(2,1)}, bf16[128,2048]{1,0:T(8,128)(2,1)S(1)}, u32[]{:S(2)}, u32[]{:S(2)}) %collective-permute-start.3) | collective-permute-done | bytes 524320 | tf_op jit(solution)/shard_map/ppermute | solution.py:24
  61.1 3.2 %collective-permute-start.6 = (bf16[128,2048]{1,0:T(8,128)(2,1)S(1)}, bf16[128,2048]{1,0:T(8,128)(2,1)S(1)}, u32[]{:S(2)}, u32[]{:S(2)}) collective-permute-start(bf16[128,2048]{1,0:T(8,128)(2,1)S(1)} %collective-permute-done.3.refs_1_.refs_6_), channel_id=1, source_target_pairs={{0,2},{1,3},{2,4},{3,5},{4,6},{5,7},{8,10},{9,11},{10,12},{11,13},... | collective-permute-start | bytes 1572872 | tf_op jit(solution)/shard_map/ppermute | solution.py:24
  64.3 0.0 copy-done.8
  64.3 0.6 broadcast_in_dim.73
  64.9 6.7 %all-to-all-start.1 = ((s32[8,1,128]{2,1,0:T(1,128)}), s32[8,1,128]{2,1,0:T(1,128)S(1)}, u32[]{:S(2)}, u32[]{:S(2)}) async-start(s32[8,1,128]{2,1,0:T(1,128)} %broadcast_in_dim.73), calls=%async_computation.1 | async-start | bytes 8192 | tf_op jit(solution)/shard_map/all_to_all | solution.py:35
  71.5 2.2 %collective-permute-start = (bf16[128,2048]{1,0:T(8,128)(2,1)}, bf16[128,2048]{1,0:T(8,128)(2,1)}, u32[]{:S(2)}, u32[]{:S(2)}) collective-permute-start(bf16[128,2048]{1,0:T(8,128)(2,1)} %get-tuple-element.24), channel_id=1, source_target_pairs={{0,8},{8,16},{16,24},{1,9},{9,17},{17,25},{2,10},{10,18},{18,26},{... | collective-permute-start | bytes 1572872 | tf_op jit(solution)/shard_map/ppermute | solution.py:24
  73.8 0.1 stack.35
  73.9 0.6 collective-permute-start.5
  74.5 0.0 collective-permute-done.7.arrived_ref
  74.5 0.0 copy-start.2
  74.5 0.8 copy-done.2
  75.3 0.0 collective-permute-done.6.refs_3_.refs_8_
  75.3 0.9 broadcast_select_fusion
  76.2 3.1 %collective-permute-start.8 = (bf16[128,2048]{1,0:T(8,128)(2,1)}, bf16[128,2048]{1,0:T(8,128)(2,1)S(1)}, u32[]{:S(2)}, u32[]{:S(2)}) collective-permute-start(bf16[128,2048]{1,0:T(8,128)(2,1)} %broadcast_select_fusion), channel_id=1, source_target_pairs={{0,1},{1,0},{2,3},{3,2},{4,5},{5,4},{6,7},{7,6},{8,9},{9,8},{10,11... | collective-permute-start | bytes 1572872 | tf_op jit(solution)/shard_map/ppermute | solution.py:29
  79.2 0.1 add_bitcast_fusion
  79.3 0.0 all-to-all-done.1
  79.3 0.2 convert_reduce_fusion
  79.5 0.1 and_select_fusion.bias_ref
  79.7 0.0 collective-permute-done.5.refs_2_.refs_7_
  79.7 1.3 %collective-permute-done.8.refs_4_.refs_9_ = bf16[128,2048]{1,0:T(8,128)(2,1)S(1)} collective-permute-done((bf16[128,2048]{1,0:T(8,128)(2,1)}, bf16[128,2048]{1,0:T(8,128)(2,1)S(1)}, u32[]{:S(2)}, u32[]{:S(2)}) %collective-permute-start.8) | collective-permute-done | bytes 524320 | tf_op jit(solution)/shard_map/ppermute | solution.py:29
  81.0 0.0 copy-done.6
  81.0 0.0 copy-done.1
  81.0 0.0 copy-start
  81.0 2.2 %copy-done = bf16[1,256,8192]{2,1,0:T(8,128)(2,1)S(1)} copy-done((bf16[1,256,8192]{2,1,0:T(8,128)(2,1)S(1)}, bf16[1,256,8192]{2,1,0:T(8,128)(2,1)}, u32[]{:S(2)}) %copy-start) | copy-done | bytes 4194328
  83.2 0.0 copy-start.5
  83.2 0.9 copy-done.5
  84.1 2.8 %attend_heads.4.refs_10_ = bf16[1,128,8192]{2,1,0:T(8,128)(2,1)} custom-call(s32[2]{0:T(128)S(1)} %copy-done.6, f32[128,640]{1,0:T(8,128)S(1)} %and_select_fusion.bias_ref, bf16[128,1024]{1,0:T(8,128)(2,1)S(1)} %copy-done.5, bf16[1,256,8192]{2,1,0:T(8,128)(2,1)S(1)} %copy-done, bf16[128,2048]{1,0:T(8,128)(2,1)S(1)} %copy-done.1, ...), custom_call_target="tpu_custom_call" | custom-call | flops 335544320 | bytes 1114112 | tf_op jit(solution)/shard_map/attend_heads/pallas_call | solution.py:134
  86.9 0.0 copy-start.3
  87.0 6.3 %attend_heads.5.refs_10_ = bf16[1,128,8192]{2,1,0:T(8,128)(2,1)} custom-call(s32[2]{0:T(128)S(1)} %copy-done.6, f32[128,640]{1,0:T(8,128)S(1)} %and_select_fusion.bias_ref, bf16[128,3072]{1,0:T(8,128)(2,1)S(1)} %collective-permute-done.4.arrived_ref, bf16[1,256,8192]{2,1,0:T(8,128)(2,1)S(1)} %copy-done, ...), custom_call_target="tpu_custom_call", output_to_operand_aliasing={{}: (14, {})} | custom-call | flops 1006632960 | bytes 3342336 | tf_op jit(solution)/shard_map/attend_heads/pallas_call | solution.py:134
  93.3 0.0 copy-done.3
  93.3 4.6 %attend_heads.6.refs_10_ = bf16[1,128,8192]{2,1,0:T(8,128)(2,1)} custom-call(s32[2]{0:T(128)S(1)} %copy-done.6, f32[128,640]{1,0:T(8,128)S(1)} %and_select_fusion.bias_ref, bf16[128,2048]{1,0:T(8,128)(2,1)S(1)} %copy-done.3, bf16[1,256,8192]{2,1,0:T(8,128)(2,1)S(1)} %copy-done, bf16[128,2048]{1,0:T(8,128)(2,1)S(1)} %copy-done.1, ...), custom_call_target="tpu_custom_call", output_to_operand_aliasing={{}: (14, {})} | custom-call | flops 671088640 | bytes 2228224 | tf_op jit(solution)/shard_map/attend_heads/pallas_call | solution.py:134
  97.8 0.0 collective-permute-done.arrived_ref
  97.8 4.8 %attend_heads.7 = bf16[1,128,8192]{2,1,0:T(8,128)(2,1)} custom-call(s32[2]{0:T(128)S(1)} %copy-done.6, f32[128,640]{1,0:T(8,128)S(1)} %and_select_fusion.bias_ref, bf16[128,2048]{1,0:T(8,128)(2,1)} %collective-permute-done.arrived_ref, bf16[1,256,8192]{2,1,0:T(8,128)(2,1)S(1)} %copy-done, ...), custom_call_target="tpu_custom_call", output_to_operand_aliasing={{}: (14, {})} | custom-call | flops 671088640 | bytes 2228224 | tf_op jit(solution)/shard_map/attend_heads/pallas_call | solution.py:134
  (4 shorter events, 0.1 us)
Async XLA Ops:
  2.0 62.3 %copy-start.8 = (s32[1,128]{1,0:T(1,128)S(1)}, s32[1,128]{1,0:T(1,128)}, u32[]{:S(2)}) copy-start(s32[1,128]{1,0:T(1,128)} %param.9) | copy-start | bytes 1540
  3.2 43.9 %collective-permute-start.2 = (bf16[128,1024]{1,0:T(8,128)(2,1)S(1)}, bf16[128,1024]{1,0:T(8,128)(2,1)S(1)}, u32[]{:S(2)}, u32[]{:S(2)}) collective-permute-start(bf16[128,1024]{1,0:T(8,128)(2,1)S(1)} %bitcast_select_fusion.3), channel_id=1, source_target_pairs={{0,8},{8,16},{16,24},{1,9},{9,17},{17,25},{2,10},{10,18},{18,26},{... | collective-permute-start | bytes 786440 | tf_op jit(solution)/shard_map/ppermute | solution.py:24
  6.3 37.6 %collective-permute-start.1 = (bf16[128,2048]{1,0:T(8,128)(2,1)S(1)}, bf16[128,2048]{1,0:T(8,128)(2,1)S(1)}, u32[]{:S(2)}, u32[]{:S(2)}) collective-permute-start(bf16[128,2048]{1,0:T(8,128)(2,1)S(1)} %pad_maximum_fusion), channel_id=1, source_target_pairs={{0,8},{8,16},{16,24},{1,9},{9,17},{17,25},{2,10},{10,18},{18,26},{... | collective-permute-start | bytes 1572872 | tf_op jit(solution)/shard_map/ppermute | solution.py:24
  10.6 44.6 %collective-permute-start.4 = (bf16[128,3072]{1,0:T(8,128)(2,1)}, bf16[128,3072]{1,0:T(8,128)(2,1)S(1)}, u32[]{:S(2)}, u32[]{:S(2)}) collective-permute-start(bf16[128,3072]{1,0:T(8,128)(2,1)} %bitcast_select_fusion), channel_id=1, source_target_pairs={{0,8},{8,16},{16,24},{1,9},{9,17},{17,25},{2,10},{10,18},{18,26},{... | collective-permute-start | bytes 2359304 | tf_op jit(solution)/shard_map/ppermute | solution.py:24
  13.1 28.1 %all-to-all-start = ((s32[4,1,1]{2,1,0:T(1,128)}), s32[4,1,1]{2,1,0:T(1,128)S(1)}, u32[]{:S(2)}, u32[]{:S(2)}) async-start(s32[4,1,1]{2,1,0:T(1,128)} %broadcast_in_dim.71), calls=%async_computation | async-start | bytes 4096 | tf_op jit(solution)/shard_map/all_to_all | solution.py:35
  43.9 37.1 %copy-start.6 = (s32[2]{0:T(128)S(1)}, s32[2]{0:T(128)}, u32[]{:S(2)}) copy-start(s32[2]{0:T(128)} %pad_add_fusion.scal_ref) | copy-start | bytes 28
  43.9 0.8 copy-start.7
  47.0 34.0 %copy-start.1 = (bf16[128,2048]{1,0:T(8,128)(2,1)S(1)}, bf16[128,2048]{1,0:T(8,128)(2,1)}, u32[]{:S(2)}) copy-start(bf16[128,2048]{1,0:T(8,128)(2,1)} %settle_kv.1.refs_0_.refs_5_) | copy-start | bytes 1572868
  47.0 8.2 %copy-start.4 = (bf16[128,1024]{1,0:T(8,128)(2,1)}, bf16[128,1024]{1,0:T(8,128)(2,1)S(1)}, u32[]{:S(2)}) copy-start(bf16[128,1024]{1,0:T(8,128)(2,1)S(1)} %collective-permute-done.2.arrived_ref) | copy-start | bytes 786436
  47.0 14.0 %collective-permute-start.3 = (bf16[128,2048]{1,0:T(8,128)(2,1)}, bf16[128,2048]{1,0:T(8,128)(2,1)S(1)}, u32[]{:S(2)}, u32[]{:S(2)}) collective-permute-start(bf16[128,2048]{1,0:T(8,128)(2,1)} %settle_kv.1.refs_0_.refs_5_), channel_id=1, source_target_pairs={{0,2},{1,3},{2,4},{3,5},{4,6},{5,7},{8,10},{9,11},{10,12},{11,13},... | collective-permute-start | bytes 1572872 | tf_op jit(solution)/shard_map/ppermute | solution.py:24
  53.0 21.5 %collective-permute-start.7 = (bf16[128,2048]{1,0:T(8,128)(2,1)}, bf16[128,2048]{1,0:T(8,128)(2,1)S(1)}, u32[]{:S(2)}, u32[]{:S(2)}) collective-permute-start(bf16[128,2048]{1,0:T(8,128)(2,1)} %get-tuple-element.23), channel_id=1, source_target_pairs={{0,8},{8,16},{16,24},{1,9},{9,17},{17,25},{2,10},{10,18},{18,26},{... | collective-permute-start | bytes 1572872 | tf_op jit(solution)/shard_map/ppermute | solution.py:24
  61.1 14.2 %collective-permute-start.6 = (bf16[128,2048]{1,0:T(8,128)(2,1)S(1)}, bf16[128,2048]{1,0:T(8,128)(2,1)S(1)}, u32[]{:S(2)}, u32[]{:S(2)}) collective-permute-start(bf16[128,2048]{1,0:T(8,128)(2,1)S(1)} %collective-permute-done.3.refs_1_.refs_6_), channel_id=1, source_target_pairs={{0,2},{1,3},{2,4},{3,5},{4,6},{5,7},{8,10},{9,11},{10,12},{11,13},... | collective-permute-start | bytes 1572872 | tf_op jit(solution)/shard_map/ppermute | solution.py:24
  64.9 14.5 %all-to-all-start.1 = ((s32[8,1,128]{2,1,0:T(1,128)}), s32[8,1,128]{2,1,0:T(1,128)S(1)}, u32[]{:S(2)}, u32[]{:S(2)}) async-start(s32[8,1,128]{2,1,0:T(1,128)} %broadcast_in_dim.73), calls=%async_computation.1 | async-start | bytes 8192 | tf_op jit(solution)/shard_map/all_to_all | solution.py:35
  71.5 26.3 %collective-permute-start = (bf16[128,2048]{1,0:T(8,128)(2,1)}, bf16[128,2048]{1,0:T(8,128)(2,1)}, u32[]{:S(2)}, u32[]{:S(2)}) collective-permute-start(bf16[128,2048]{1,0:T(8,128)(2,1)} %get-tuple-element.24), channel_id=1, source_target_pairs={{0,8},{8,16},{16,24},{1,9},{9,17},{17,25},{2,10},{10,18},{18,26},{... | collective-permute-start | bytes 1572872 | tf_op jit(solution)/shard_map/ppermute | solution.py:24
  73.9 5.8 %collective-permute-start.5 = (bf16[128,2048]{1,0:T(8,128)(2,1)S(1)}, bf16[128,2048]{1,0:T(8,128)(2,1)S(1)}, u32[]{:S(2)}, u32[]{:S(2)}) collective-permute-start(bf16[128,2048]{1,0:T(8,128)(2,1)S(1)} %collective-permute-done.3.refs_1_.refs_6_), channel_id=1, source_target_pairs={{0,1},{1,0},{2,3},{3,2},{4,5},{5,4},{6,7},{7,6},{8,9},{9,8},{10,11... | collective-permute-start | bytes 1572872 | tf_op jit(solution)/shard_map/ppermute | solution.py:29
  74.5 0.8 copy-start.2
  76.2 4.8 %collective-permute-start.8 = (bf16[128,2048]{1,0:T(8,128)(2,1)}, bf16[128,2048]{1,0:T(8,128)(2,1)S(1)}, u32[]{:S(2)}, u32[]{:S(2)}) collective-permute-start(bf16[128,2048]{1,0:T(8,128)(2,1)} %broadcast_select_fusion), channel_id=1, source_target_pairs={{0,1},{1,0},{2,3},{3,2},{4,5},{5,4},{6,7},{7,6},{8,9},{9,8},{10,11... | collective-permute-start | bytes 1572872 | tf_op jit(solution)/shard_map/ppermute | solution.py:29
  81.0 2.2 %copy-start = (bf16[1,256,8192]{2,1,0:T(8,128)(2,1)S(1)}, bf16[1,256,8192]{2,1,0:T(8,128)(2,1)}, u32[]{:S(2)}) copy-start(bf16[1,256,8192]{2,1,0:T(8,128)(2,1)} %local_ref.7) | copy-start | bytes 12582916
  83.2 0.9 copy-start.5
  86.9 6.3 %copy-start.3 = (bf16[128,2048]{1,0:T(8,128)(2,1)S(1)}, bf16[128,2048]{1,0:T(8,128)(2,1)}, u32[]{:S(2)}) copy-start(bf16[128,2048]{1,0:T(8,128)(2,1)} %copy-done.2) | copy-start | bytes 1572868

commit v3 on v2

v3 whole, which is shorter than its diff:
```python
import functools
import math

import jax
import jax.numpy as jnp
from jax import lax
from jax.experimental import pallas as pl
from jax.experimental.pallas import tpu as pltpu
from jax.sharding import PartitionSpec as P

QUERY_HEADS = 64
KEY_VALUE_HEADS = 8
HEAD_SIZE = 128
GROUP = QUERY_HEADS // KEY_VALUE_HEADS
GROUP_WIDTH = GROUP * HEAD_SIZE
KV_WIDTH = KEY_VALUE_HEADS * HEAD_SIZE
NOTE = 2 * KV_WIDTH
MASKED = -1e30
CHUNKS = (3, 3, 2)
PARTS = 2

WHOLE = pl.BlockSpec(memory_space=pltpu.VMEM)
SCALARS = pl.BlockSpec(memory_space=pltpu.SMEM)


def shifted(x, axis, steps):
    n = lax.axis_size(axis)
    return lax.ppermute(x, axis, [(i, i + steps) for i in range(n - steps)])


def swapped_cores(x):
    n = lax.axis_size("ctx")
    return lax.ppermute(x, "ctx", [(i, i ^ 1) for i in range(n)])


def everyones(x, axis):
    n = lax.axis_size(axis)
    spread = jnp.broadcast_to(x[None], (n,) + x.shape)
    return lax.all_to_all(spread, axis, split_axis=0, concat_axis=0)


def shift_in_known(own_count, quota):
    n = lax.axis_size("dp")
    replica = lax.axis_index("dp")
    if n > 4:
        all_counts = everyones(own_count[None], "dp")[:, 0]
        places = jnp.arange(n, dtype=jnp.int32)
        before = jnp.sum(jnp.where(places < replica, all_counts, 0))
        return jnp.stack([before - replica * quota, jnp.int32(0)])
    shift = jnp.where(own_count == 0, quota, 0)
    shift = jnp.where(replica == n - 1, quota - own_count, shift)
    shift = jnp.where(replica == 0, 0, shift)
    return jnp.stack([shift, (replica == 1).astype(jnp.int32)])


def place_rows(hot, arrived, local):
    both = jnp.concatenate([arrived, local], axis=0)
    return jnp.dot(hot, both, preferred_element_type=jnp.float32).astype(jnp.bfloat16)


def settle_kernel(shift_ref, docs_ref, arrived_ref, k_ref, v_ref, out_ref, hot_ref):
    quota = out_ref.shape[0]
    count_before = arrived_ref[:, NOTE:].astype(jnp.float32).astype(jnp.int32)
    shift = jnp.where(shift_ref[1] == 1, count_before - quota, shift_ref[0])
    shift_before = shift - count_before + quota
    row = lax.broadcasted_iota(jnp.int32, (quota, quota), 0)
    col = lax.broadcasted_iota(jnp.int32, (quota, quota), 1)
    turned = row - shift_before
    turned = jnp.where(turned < 0, turned + quota, turned)
    hot_arrived = jnp.where((row < shift) & (col == turned), 1.0, 0.0)
    hot_local = jnp.where(col == row - shift, 1.0, 0.0)
    hot = jnp.concatenate([hot_arrived, hot_local], axis=1).astype(jnp.bfloat16)
    hot_ref[...] = hot
    out_ref[:, :KV_WIDTH] = place_rows(hot, arrived_ref[:, :KV_WIDTH], k_ref[0])
    out_ref[:, KV_WIDTH:NOTE] = place_rows(hot, arrived_ref[:, KV_WIDTH:NOTE], v_ref[0])
    docs = jnp.broadcast_to(docs_ref[...].astype(jnp.float32), (quota, quota))
    out_ref[:, NOTE:] = docs.astype(jnp.bfloat16)


def settle_kv(shift, docs, arrived, k_rows, v_rows):
    quota = arrived.shape[0]
    half = pl.BlockSpec((1, quota, KV_WIDTH), lambda i: (0, 0, 0))
    whole = pl.BlockSpec(arrived.shape, lambda i: (0, 0))
    return pl.pallas_call(
        settle_kernel,
        grid=(1,),
        in_specs=[SCALARS, pl.BlockSpec(docs.shape, lambda i: (0, 0)), whole, half, half],
        out_specs=[whole, pl.BlockSpec((quota, 2 * quota), lambda i: (0, 0))],
        out_shape=[
            jax.ShapeDtypeStruct(arrived.shape, jnp.bfloat16),
            jax.ShapeDtypeStruct((quota, 2 * quota), jnp.bfloat16),
        ],
        name="settle_kv",
    )(shift, docs, arrived, k_rows, v_rows)


def block_ranks(rank, core, rounds):
    ranks = [rank]
    for back in range(1, rounds + 1):
        ranks.append(rank - 2 * back)
        if back < rounds:
            ranks.append(rank - 2 * back + jnp.where(core == 0, 1, -1))
    ranks.append(jnp.where(core == 0, rank - 2 * rounds + 1, rank - 1))
    return ranks


def attend_kernel(blocks, first, count, rank_ref, hot_ref, arrived_ref, *refs):
    kv_refs, q_hbm = refs[:blocks], refs[blocks]
    out_hbm, local, result, bias, q_sem, out_sems = refs[-6:]
    quota = hot_ref.shape[0]
    width = count * GROUP_WIDTH
    start = first * GROUP_WIDTH
    fetch = pltpu.make_async_copy(q_hbm.at[0, 0:quota, start : start + width], local, q_sem)
    fetch.start()

    rank = rank_ref[0]
    row = lax.broadcasted_iota(jnp.int32, (quota, quota), 0)
    col = lax.broadcasted_iota(jnp.int32, (quota, quota), 1)
    own_docs = kv_refs[0][:, NOTE:].astype(jnp.float32)
    q_docs = jnp.sum(jnp.where(row == col, own_docs, 0.0), axis=1, keepdims=True)
    for b, block_rank in enumerate(block_ranks(rank, lax.rem(rank, 2), (blocks - 1) // 2)):
        allowed = kv_refs[b][:, NOTE:].astype(jnp.float32) == q_docs
        allowed &= (col <= row) if b == 0 else (block_rank >= 0)
        bias[:, b * quota : (b + 1) * quota] = jnp.where(allowed, 0.0, MASKED)

    unit = math.log2(math.e) / math.sqrt(HEAD_SIZE)
    heads = GROUP // PARTS
    hot = hot_ref[...]

    def operands(g):
        at = (first + g) * HEAD_SIZE
        keys = jnp.concatenate([r[:, at : at + HEAD_SIZE] for r in kv_refs], axis=0)
        at += KV_WIDTH
        values = jnp.concatenate([r[:, at : at + HEAD_SIZE] for r in kv_refs], axis=0)
        values = jnp.concatenate([values, jnp.ones_like(values)], axis=1)
        cols = slice(g * GROUP_WIDTH, (g + 1) * GROUP_WIDTH)
        q = place_rows(hot, arrived_ref[:, cols], local[:, cols])
        return q, keys, values

    def scored(q, keys, part):
        stacked = jnp.concatenate(
            [
                q[:, h * HEAD_SIZE : (h + 1) * HEAD_SIZE]
                for h in range(part * heads, (part + 1) * heads)
            ],
            axis=0,
        )
        return lax.dot_general(
            stacked, keys, (((1,), (1,)), ((), ())), preferred_element_type=jnp.float32
        )

    def finished(scores, values, g, part):
        scores = scores.reshape(heads, quota, -1) * unit + bias[...][None]
        weights = jnp.exp2(scores - jnp.max(scores, axis=2, keepdims=True))
        weights = weights.astype(jnp.bfloat16).reshape(heads * quota, -1)
        mixed = jnp.dot(weights, values, preferred_element_type=jnp.float32)
        mixed = (mixed[:, :HEAD_SIZE] / mixed[:, HEAD_SIZE:]).astype(jnp.bfloat16)
        for h in range(heads):
            at = g * GROUP_WIDTH + (part * heads + h) * HEAD_SIZE
            result[:, at : at + HEAD_SIZE] = mixed[h * quota : (h + 1) * quota]

    fetch.wait()
    stores = []
    q, keys, values = operands(0)
    scores = scored(q, keys, 0)
    for step in range(count * PARTS):
        g, part = divmod(step, PARTS)
        own_values, later = values, None
        if step + 1 < count * PARTS:
            if part == PARTS - 1:
                q, keys, values = operands(g + 1)
            later = scored(q, keys, (part + 1) % PARTS)
        finished(scores, own_values, g, part)
        scores = later
        if part == PARTS - 1:
            cols = slice(g * GROUP_WIDTH, (g + 1) * GROUP_WIDTH)
            at = (first + g) * GROUP_WIDTH
            store = pltpu.make_async_copy(
                result.at[:, cols], out_hbm.at[0, :, at : at + GROUP_WIDTH], out_sems.at[g]
            )
            store.start()
            stores.append(store)
    for store in stores:
        store.wait()


def attend(rank, hot, arrived, q_rows, kv_blocks, first, count, out):
    quota = arrived.shape[0]
    blocks = len(kv_blocks)
    width = count * GROUP_WIDTH
    anywhere = pl.BlockSpec(memory_space=pl.ANY)
    in_specs = [SCALARS, WHOLE, WHOLE] + [WHOLE] * blocks + [anywhere]
    operands = [rank, hot, arrived, *kv_blocks, q_rows]
    aliases = {}
    if out is not None:
        in_specs.append(anywhere)
        aliases = {len(operands): 0}
        operands.append(out)
    pairs = count * GROUP * quota * quota * blocks
    return pl.pallas_call(
        functools.partial(attend_kernel, blocks, first, count),
        in_specs=in_specs,
        out_specs=anywhere,
        out_shape=jax.ShapeDtypeStruct((1, quota, QUERY_HEADS * HEAD_SIZE), jnp.bfloat16),
        input_output_aliases=aliases,
        scratch_shapes=[
            pltpu.VMEM((quota, width), jnp.bfloat16),
            pltpu.VMEM((quota, width), jnp.bfloat16),
            pltpu.VMEM((quota, blocks * quota), jnp.float32),
            pltpu.SemaphoreType.DMA,
            pltpu.SemaphoreType.DMA((count,)),
        ],
        cost_estimate=pl.CostEstimate(
            flops=4 * pairs * HEAD_SIZE,
            bytes_accessed=count * quota * (3 * GROUP_WIDTH + 2 * blocks * HEAD_SIZE) * 2,
            transcendentals=pairs,
        ),
        compiler_params=pltpu.CompilerParams(vmem_limit_bytes=24 * 1024 * 1024),
        name="attend_heads",
    )(*operands)


def circular_tail(rows, later):
    quota = later.shape[0]
    return jnp.where(later[:, None], rows[quota:], rows[:quota])


def body(q_rows, k_rows, value_slot_rows, counts, doc_ids):
    quota = doc_ids.shape[1]
    rounds = lax.axis_size("ctx") // 4
    rank = lax.axis_index("ctx")
    own_count = counts[0, 0]

    later = quota + jnp.arange(quota, dtype=jnp.int32) < own_count
    kv_tail = jnp.concatenate(
        [
            circular_tail(k_rows[0], later),
            circular_tail(value_slot_rows[0], later),
            jnp.broadcast_to(own_count.astype(jnp.bfloat16), (quota, quota)),
        ],
        axis=1,
    )
    kv_tail, later = lax.optimization_barrier((kv_tail, later))
    arrived_kv = shifted(kv_tail, "dp", 1)
    arrived_q = []
    first = 0
    for size in CHUNKS:
        cols = slice(first * GROUP_WIDTH, (first + size) * GROUP_WIDTH)
        arrived_q.append(shifted(circular_tail(q_rows[0, :, cols], later), "dp", 1))
        first += size

    shift = shift_in_known(own_count, quota)
    own, hot = settle_kv(shift, doc_ids, arrived_kv, k_rows, value_slot_rows)

    kv_blocks = [own]
    carried = own
    for back in range(1, rounds + 1):
        carried = shifted(carried, "ctx", 2)
        kv_blocks.append(carried)
        if back <= min(rounds, len(CHUNKS) - 1):
            carried, arrived_q[back - 1] = lax.optimization_barrier((carried, arrived_q[back - 1]))
        if back < rounds:
            kv_blocks.append(swapped_cores(carried))
    kv_blocks.append(swapped_cores(jnp.where(rank % 2 == 0, own, carried)))

    out = None
    first = 0
    for size, arrived in zip(CHUNKS, arrived_q):
        out = attend(rank[None], hot, arrived, q_rows, kv_blocks, first, size, out)
        first += size
    return out


def solution(mesh):
    return jax.shard_map(
        body,
        mesh=mesh,
        in_specs=(
            P("dp", "ctx", None),
            P("dp", "ctx", None),
            P("dp", "ctx", None),
            P("dp", "ctx"),
            P("dp", "ctx"),
        ),
        out_specs=P("dp", "ctx", None),
        check_vma=False,
    )
```

time: 104 us -> 76.5 us (0.74)
  starting transfers between devices: 34.1 us -> 22.6 us
  Pallas kernels: 20.8 us -> 14.8 us
  other arithmetic: 10.3 us -> 6.34 us
  local copies, waits for them, and re-layouts: 5.98 us -> 3.01 us
  between operations: 2.04 us -> 0.86 us
    ppermute x7 -> x6, waiting for transfers between devices: 5.8 us -> 28.4 us  [shifted(): return lax.ppermute(x, axis, [(i, i + steps) for i in range(n - steps)])]
    all_to_all x2 -> x0, waiting for transfers between devices: 22.3 us -> none  [everyones(): return lax.all_to_all(spread, axis, split_axis=0, concat_axis=0)]
    all_to_all x2 -> x0, starting transfers between devices: 12.5 us -> none  [everyones(): return lax.all_to_all(spread, axis, split_axis=0, concat_axis=0)]
    pallas_call x5 -> x4, Pallas kernels: 20.8 us -> 14.8 us  [the longest x3 12.4 us: attend(): pl.pallas_call(functools.partial(attend_kernel, blocks, first, count), in...]
    ppermute x2, starting transfers between devices: 3.72 us -> 6.58 us  [swapped_cores(): return lax.ppermute(x, 'ctx', [(i, i ^ 1) for i in range(n)])]
    select_n x4 -> x3, other arithmetic: 7.49 us -> 5.57 us  [circular_tail(): return jnp.where(later[:, None], rows[quota:], rows[:quota])]
    ppermute x7 -> x6, starting transfers between devices: 17.9 us -> 16 us  [shifted(): return lax.ppermute(x, axis, [(i, i + steps) for i in range(n - steps)])]
    unnamed x18 -> x10, local copies, waits for them, and re-layouts: 4.75 us -> 3 us
  transfers between devices with their start and end apart: 11 -> 8, of which waited for: 3 -> 4; matrix products, arithmetic and copies ran while one was open for 9% -> 6% of each run, Pallas kernels for 16% -> 15%
where the time goes in v3:
time: 76.5 us; the launch traced here: 76 us
  waiting for transfers between devices  28.4 us (37%)
  starting transfers between devices  22.6 us (30%)
  Pallas kernels  14.8 us (19%)
  other arithmetic  6.34 us (8%)
  local copies, waits for them, and re-layouts  3.01 us (4%)
  between operations  0.86 us (1%)
    ppermute x6, waiting for transfers between devices, shifted(): return lax.ppermute(x, axis, [(i, i + steps) for i in range(n - steps)])  28.4 us
    ppermute x6, starting transfers between devices, shifted(): return lax.ppermute(x, axis, [(i, i + steps) for i in range(n - steps)])  16 us
    pallas_call x3, Pallas kernels, attend(): pl.pallas_call(functools.partial(attend_kernel, blocks, first, count), in...  12.4 us
    ppermute x2, starting transfers between devices, swapped_cores(): return lax.ppermute(x, 'ctx', [(i, i ^ 1) for i in range(n)])  6.58 us
    select_n x3, other arithmetic, circular_tail(): return jnp.where(later[:, None], rows[quota:], rows[:quota])  5.57 us
    unnamed x10, local copies, waits for them, and re-layouts  3 us
    pallas_call x1, Pallas kernels, settle_kv(): pl.pallas_call(settle_kernel, grid=(1,), in_specs=[SCALARS, pl.BlockSpec(...  2.35 us
  transfers between devices with their start and end apart: 8, of which 4 were waited for; matrix products, arithmetic and copies ran while one was open for 6% of the time, Pallas kernels for 15%

profile of v3, /device:TPU:21, one launch (start us, length us, event | category | flops | bytes accessed | tf_op | source)
XLA Modules:
  0.0 76.0 jit_solution(11476482842563792340)
XLA Ops:
  0.7 1.3 %bitcast_select_fusion.4 = (bf16[128,1024]{1,0:T(8,128)(2,1)S(1)}, bf16[128,1024]{1,0:T(8,128)(2,1)S(1)}) fusion(bf16[1,256,1024]{2,1,0:T(8,128)(2,1)} %k_ref.1, pred[128]{0:T(512)(128)(4,1)S(1)} %add_compare_fusion, bf16[1,256,1024]{2,1,0:T(8,128)(2,1)} %v_ref.1), kind=kLoop, calls=%fused_computation.6 | loop fusion | flops 262144 | bytes 1572992 | tf_op jit(solution)/shard_map/jit(_where)/select_n | solution.py:225
  2.0 0.1 maximum_maximum_fusion
  2.1 3.1 %collective-permute-start = (bf16[128,2176]{1,0:T(8,128)(2,1)S(1)}, bf16[128,2176]{1,0:T(8,128)(2,1)S(1)}, u32[]{:S(2)}, u32[]{:S(2)}) collective-permute-start(bf16[128,2176]{1,0:T(8,128)(2,1)S(1)} %maximum_maximum_fusion), channel_id=1, source_target_pairs={{0,8},{8,16},{16,24},{1,9},{9,17},{17,25},{2,10},{10,18},{18,26},{... | collective-permute-start | bytes 1671176 | tf_op jit(solution)/shard_map/ppermute | solution.py:28
  5.2 2.9 %bitcast_select_fusion = (bf16[128,3072]{1,0:T(8,128)(2,1)}, bf16[128,3072]{1,0:T(8,128)(2,1)S(1)}) fusion(bf16[1,256,8192]{2,1,0:T(8,128)(2,1)} %refs_5_.5, pred[128]{0:T(512)(128)(4,1)S(1)} %add_compare_fusion), kind=kLoop, calls=%fused_computation | loop fusion | flops 786432 | bytes 4718720 | tf_op jit(solution)/shard_map/jit(_where)/select_n | solution.py:225
  8.2 1.9 %collective-permute-start.3 = (bf16[128,3072]{1,0:T(8,128)(2,1)S(1)}, bf16[128,3072]{1,0:T(8,128)(2,1)S(1)}, u32[]{:S(2)}, u32[]{:S(2)}) collective-permute-start(bf16[128,3072]{1,0:T(8,128)(2,1)S(1)} %get-tuple-element.22), channel_id=1, source_target_pairs={{0,8},{8,16},{16,24},{1,9},{9,17},{17,25},{2,10},{10,18},{18,26},{... | collective-permute-start | bytes 2359304 | tf_op jit(solution)/shard_map/ppermute | solution.py:28
  10.1 0.6 pad_add_fusion.shift_ref
  10.7 7.7 %collective-permute-done.arrived_ref = bf16[128,2176]{1,0:T(8,128)(2,1)S(1)} collective-permute-done((bf16[128,2176]{1,0:T(8,128)(2,1)S(1)}, bf16[128,2176]{1,0:T(8,128)(2,1)S(1)}, u32[]{:S(2)}, u32[]{:S(2)}) %collective-permute-start) | collective-permute-done | bytes 557088 | tf_op jit(solution)/shard_map/ppermute | solution.py:28
  18.4 0.0 copy-start.4
  18.4 0.8 %copy-done.4 = bf16[128,2176]{1,0:T(8,128)(2,1)} copy-done((bf16[128,2176]{1,0:T(8,128)(2,1)}, bf16[128,2176]{1,0:T(8,128)(2,1)S(1)}, u32[]{:S(2)}) %copy-start.4) | copy-done | bytes 557080
  19.2 2.3 %settle_kv.1 = (bf16[128,2176]{1,0:T(8,128)(2,1)}, bf16[128,256]{1,0:T(8,128)(2,1)}) custom-call(s32[2]{0:T(128)} %pad_add_fusion.shift_ref, s32[1,128]{1,0:T(1,128)} %docs_ref.1, bf16[128,2176]{1,0:T(8,128)(2,1)} %copy-done.4, bf16[1,256,1024]{2,1,0:T(8,128)(2,1)} %k_ref.1, bf16[1,256,1024]{2,1,0:T(8,128)(2,1)} %v_ref.1), custom_call_target="tpu_custom_call" | custom-call | tf_op jit(solution)/shard_map/settle_kv/pallas_call | solution.py:84
  21.6 0.0 copy-start.2
  21.6 0.0 copy-start.3
  21.6 3.3 %collective-permute-start.2 = (bf16[128,2176]{1,0:T(8,128)(2,1)}, bf16[128,2176]{1,0:T(8,128)(2,1)S(1)}, u32[]{:S(2)}, u32[]{:S(2)}) collective-permute-start(bf16[128,2176]{1,0:T(8,128)(2,1)} %get-tuple-element.16.refs_0_), channel_id=1, source_target_pairs={{0,2},{1,3},{2,4},{3,5},{4,6},{5,7},{8,10},{9,11},{10,12},{11,13},... | collective-permute-start | bytes 1671176 | tf_op jit(solution)/shard_map/ppermute | solution.py:28
  24.9 2.2 %collective-permute-start.6 = (bf16[128,3072]{1,0:T(8,128)(2,1)}, bf16[128,3072]{1,0:T(8,128)(2,1)S(1)}, u32[]{:S(2)}, u32[]{:S(2)}) collective-permute-start(bf16[128,3072]{1,0:T(8,128)(2,1)} %get-tuple-element.21), channel_id=1, source_target_pairs={{0,8},{8,16},{16,24},{1,9},{9,17},{17,25},{2,10},{10,18},{18,26},{... | collective-permute-start | bytes 2359304 | tf_op jit(solution)/shard_map/ppermute | solution.py:28
  27.1 8.1 %collective-permute-done.3.arrived_ref = bf16[128,3072]{1,0:T(8,128)(2,1)S(1)} collective-permute-done((bf16[128,3072]{1,0:T(8,128)(2,1)S(1)}, bf16[128,3072]{1,0:T(8,128)(2,1)S(1)}, u32[]{:S(2)}, u32[]{:S(2)}) %collective-permute-start.3) | collective-permute-done | bytes 786464 | tf_op jit(solution)/shard_map/ppermute | solution.py:28
  35.3 0.0 collective-permute-done.2.refs_1_
  35.3 3.2 %collective-permute-start.5 = (bf16[128,2176]{1,0:T(8,128)(2,1)S(1)}, bf16[128,2176]{1,0:T(8,128)(2,1)S(1)}, u32[]{:S(2)}, u32[]{:S(2)}) collective-permute-start(bf16[128,2176]{1,0:T(8,128)(2,1)S(1)} %collective-permute-done.2.refs_1_), channel_id=1, source_target_pairs={{0,2},{1,3},{2,4},{3,5},{4,6},{5,7},{8,10},{9,11},{10,12},{11,13},... | collective-permute-start | bytes 1671176 | tf_op jit(solution)/shard_map/ppermute | solution.py:28
  38.5 3.9 %collective-permute-start.4 = (bf16[128,2176]{1,0:T(8,128)(2,1)S(1)}, bf16[128,2176]{1,0:T(8,128)(2,1)S(1)}, u32[]{:S(2)}, u32[]{:S(2)}) collective-permute-start(bf16[128,2176]{1,0:T(8,128)(2,1)S(1)} %collective-permute-done.2.refs_1_), channel_id=1, source_target_pairs={{0,1},{1,0},{2,3},{3,2},{4,5},{5,4},{6,7},{7,6},{8,9},{9,8},{10,11... | collective-permute-start | bytes 1671176 | tf_op jit(solution)/shard_map/ppermute | solution.py:33
  42.4 9.7 %collective-permute-done.6.arrived_ref = bf16[128,3072]{1,0:T(8,128)(2,1)S(1)} collective-permute-done((bf16[128,3072]{1,0:T(8,128)(2,1)}, bf16[128,3072]{1,0:T(8,128)(2,1)S(1)}, u32[]{:S(2)}, u32[]{:S(2)}) %collective-permute-start.6) | collective-permute-done | bytes 786464 | tf_op jit(solution)/shard_map/ppermute | solution.py:28
  52.1 0.0 collective-permute-done.5.refs_3_
  52.1 0.1 broadcast_select_fusion
  52.2 2.7 %collective-permute-start.7 = (bf16[128,2176]{1,0:T(8,128)(2,1)S(1)}, bf16[128,2176]{1,0:T(8,128)(2,1)S(1)}, u32[]{:S(2)}, u32[]{:S(2)}) collective-permute-start(bf16[128,2176]{1,0:T(8,128)(2,1)S(1)} %broadcast_select_fusion), channel_id=1, source_target_pairs={{0,1},{1,0},{2,3},{3,2},{4,5},{5,4},{6,7},{7,6},{8,9},{9,8},{10,11... | collective-permute-start | bytes 1671176 | tf_op jit(solution)/shard_map/ppermute | solution.py:33
  54.8 1.3 %bitcast_select_fusion.2 = bf16[128,2048]{1,0:T(8,128)(2,1)S(1)} fusion(bf16[1,256,8192]{2,1,0:T(8,128)(2,1)} %refs_5_.5, pred[128]{0:T(512)(128)(4,1)S(1)} %add_compare_fusion), kind=kLoop, calls=%fused_computation.4 | loop fusion | flops 262144 | bytes 1572992 | tf_op jit(solution)/shard_map/jit(_where)/select_n | solution.py:225
  56.2 2.2 %collective-permute-start.1 = (bf16[128,2048]{1,0:T(8,128)(2,1)S(1)}, bf16[128,2048]{1,0:T(8,128)(2,1)S(1)}, u32[]{:S(2)}, u32[]{:S(2)}) collective-permute-start(bf16[128,2048]{1,0:T(8,128)(2,1)S(1)} %bitcast_select_fusion.2), channel_id=1, source_target_pairs={{0,8},{8,16},{16,24},{1,9},{9,17},{17,25},{2,10},{10,18},{18,26},{... | collective-permute-start | bytes 1572872 | tf_op jit(solution)/shard_map/ppermute | solution.py:28
  58.4 0.0 collective-permute-done.4.refs_2_
  58.4 0.0 collective-permute-done.7.refs_4_
  58.4 0.0 copy-done.2
  58.4 0.0 copy-done.3
  58.4 0.0 copy-start
  58.5 2.2 %copy-done = bf16[1,256,8192]{2,1,0:T(8,128)(2,1)S(1)} copy-done((bf16[1,256,8192]{2,1,0:T(8,128)(2,1)S(1)}, bf16[1,256,8192]{2,1,0:T(8,128)(2,1)}, u32[]{:S(2)}) %copy-start) | copy-done | bytes 4194328
  60.6 0.0 copy-start.1
  60.6 4.5 %attend_heads.3.refs_6_ = bf16[1,128,8192]{2,1,0:T(8,128)(2,1)} custom-call(s32[1]{0:T(128)} %bitcast.rank_ref, bf16[128,256]{1,0:T(8,128)(2,1)S(1)} %copy-done.3, bf16[128,3072]{1,0:T(8,128)(2,1)S(1)} %collective-permute-done.3.arrived_ref, bf16[128,2176]{1,0:T(8,128)(2,1)S(1)} %copy-done.2, bf16[128,2176]{1,0:T(8,128)(2,1)S(1)} %collective-permute-done.2.refs_1_, ...), custom_call_target="tpu_custom_call" | custom-call | flops 1006632960 | bytes 3342336 | tf_op jit(solution)/shard_map/attend_heads/pallas_call | solution.py:200
  65.1 0.0 copy-done.1
  65.1 4.5 %attend_heads.4.refs_6_ = bf16[1,128,8192]{2,1,0:T(8,128)(2,1)} custom-call(s32[1]{0:T(128)} %bitcast.rank_ref, bf16[128,256]{1,0:T(8,128)(2,1)S(1)} %copy-done.3, bf16[128,3072]{1,0:T(8,128)(2,1)S(1)} %collective-permute-done.6.arrived_ref, bf16[128,2176]{1,0:T(8,128)(2,1)S(1)} %copy-done.2, ...), custom_call_target="tpu_custom_call", output_to_operand_aliasing={{}: (9, {})} | custom-call | flops 1006632960 | bytes 3342336 | tf_op jit(solution)/shard_map/attend_heads/pallas_call | solution.py:200
  69.6 2.9 %collective-permute-done.1.arrived_ref = bf16[128,2048]{1,0:T(8,128)(2,1)S(1)} collective-permute-done((bf16[128,2048]{1,0:T(8,128)(2,1)S(1)}, bf16[128,2048]{1,0:T(8,128)(2,1)S(1)}, u32[]{:S(2)}, u32[]{:S(2)}) %collective-permute-start.1) | collective-permute-done | bytes 524320 | tf_op jit(solution)/shard_map/ppermute | solution.py:28
  72.5 3.5 %attend_heads.5 = bf16[1,128,8192]{2,1,0:T(8,128)(2,1)} custom-call(s32[1]{0:T(128)} %bitcast.rank_ref, bf16[128,256]{1,0:T(8,128)(2,1)S(1)} %copy-done.3, bf16[128,2048]{1,0:T(8,128)(2,1)S(1)} %collective-permute-done.1.arrived_ref, bf16[128,2176]{1,0:T(8,128)(2,1)S(1)} %copy-done.2, ...), custom_call_target="tpu_custom_call", output_to_operand_aliasing={{}: (9, {})} | custom-call | flops 671088640 | bytes 2228224 | tf_op jit(solution)/shard_map/attend_heads/pallas_call | solution.py:200
  (3 shorter events, 0.0 us)
Async XLA Ops:
  2.1 16.3 %collective-permute-start = (bf16[128,2176]{1,0:T(8,128)(2,1)S(1)}, bf16[128,2176]{1,0:T(8,128)(2,1)S(1)}, u32[]{:S(2)}, u32[]{:S(2)}) collective-permute-start(bf16[128,2176]{1,0:T(8,128)(2,1)S(1)} %maximum_maximum_fusion), channel_id=1, source_target_pairs={{0,8},{8,16},{16,24},{1,9},{9,17},{17,25},{2,10},{10,18},{18,26},{... | collective-permute-start | bytes 1671176 | tf_op jit(solution)/shard_map/ppermute | solution.py:28
  8.2 27.1 %collective-permute-start.3 = (bf16[128,3072]{1,0:T(8,128)(2,1)S(1)}, bf16[128,3072]{1,0:T(8,128)(2,1)S(1)}, u32[]{:S(2)}, u32[]{:S(2)}) collective-permute-start(bf16[128,3072]{1,0:T(8,128)(2,1)S(1)} %get-tuple-element.22), channel_id=1, source_target_pairs={{0,8},{8,16},{16,24},{1,9},{9,17},{17,25},{2,10},{10,18},{18,26},{... | collective-permute-start | bytes 2359304 | tf_op jit(solution)/shard_map/ppermute | solution.py:28
  18.4 0.8 %copy-start.4 = (bf16[128,2176]{1,0:T(8,128)(2,1)}, bf16[128,2176]{1,0:T(8,128)(2,1)S(1)}, u32[]{:S(2)}) copy-start(bf16[128,2176]{1,0:T(8,128)(2,1)S(1)} %collective-permute-done.arrived_ref) | copy-start | bytes 1671172
  21.6 36.9 %copy-start.2 = (bf16[128,2176]{1,0:T(8,128)(2,1)S(1)}, bf16[128,2176]{1,0:T(8,128)(2,1)}, u32[]{:S(2)}) copy-start(bf16[128,2176]{1,0:T(8,128)(2,1)} %get-tuple-element.16.refs_0_) | copy-start | bytes 1671172
  21.6 36.9 %copy-start.3 = (bf16[128,256]{1,0:T(8,128)(2,1)S(1)}, bf16[128,256]{1,0:T(8,128)(2,1)}, u32[]{:S(2)}) copy-start(bf16[128,256]{1,0:T(8,128)(2,1)} %get-tuple-element.14.hot_ref) | copy-start | bytes 196612
  21.6 13.7 %collective-permute-start.2 = (bf16[128,2176]{1,0:T(8,128)(2,1)}, bf16[128,2176]{1,0:T(8,128)(2,1)S(1)}, u32[]{:S(2)}, u32[]{:S(2)}) collective-permute-start(bf16[128,2176]{1,0:T(8,128)(2,1)} %get-tuple-element.16.refs_0_), channel_id=1, source_target_pairs={{0,2},{1,3},{2,4},{3,5},{4,6},{5,7},{8,10},{9,11},{10,12},{11,13},... | collective-permute-start | bytes 1671176 | tf_op jit(solution)/shard_map/ppermute | solution.py:28
  24.9 27.2 %collective-permute-start.6 = (bf16[128,3072]{1,0:T(8,128)(2,1)}, bf16[128,3072]{1,0:T(8,128)(2,1)S(1)}, u32[]{:S(2)}, u32[]{:S(2)}) collective-permute-start(bf16[128,3072]{1,0:T(8,128)(2,1)} %get-tuple-element.21), channel_id=1, source_target_pairs={{0,8},{8,16},{16,24},{1,9},{9,17},{17,25},{2,10},{10,18},{18,26},{... | collective-permute-start | bytes 2359304 | tf_op jit(solution)/shard_map/ppermute | solution.py:28
  35.3 16.9 %collective-permute-start.5 = (bf16[128,2176]{1,0:T(8,128)(2,1)S(1)}, bf16[128,2176]{1,0:T(8,128)(2,1)S(1)}, u32[]{:S(2)}, u32[]{:S(2)}) collective-permute-start(bf16[128,2176]{1,0:T(8,128)(2,1)S(1)} %collective-permute-done.2.refs_1_), channel_id=1, source_target_pairs={{0,2},{1,3},{2,4},{3,5},{4,6},{5,7},{8,10},{9,11},{10,12},{11,13},... | collective-permute-start | bytes 1671176 | tf_op jit(solution)/shard_map/ppermute | solution.py:28
  38.5 19.9 %collective-permute-start.4 = (bf16[128,2176]{1,0:T(8,128)(2,1)S(1)}, bf16[128,2176]{1,0:T(8,128)(2,1)S(1)}, u32[]{:S(2)}, u32[]{:S(2)}) collective-permute-start(bf16[128,2176]{1,0:T(8,128)(2,1)S(1)} %collective-permute-done.2.refs_1_), channel_id=1, source_target_pairs={{0,1},{1,0},{2,3},{3,2},{4,5},{5,4},{6,7},{7,6},{8,9},{9,8},{10,11... | collective-permute-start | bytes 1671176 | tf_op jit(solution)/shard_map/ppermute | solution.py:33
  52.2 6.2 %collective-permute-start.7 = (bf16[128,2176]{1,0:T(8,128)(2,1)S(1)}, bf16[128,2176]{1,0:T(8,128)(2,1)S(1)}, u32[]{:S(2)}, u32[]{:S(2)}) collective-permute-start(bf16[128,2176]{1,0:T(8,128)(2,1)S(1)} %broadcast_select_fusion), channel_id=1, source_target_pairs={{0,1},{1,0},{2,3},{3,2},{4,5},{5,4},{6,7},{7,6},{8,9},{9,8},{10,11... | collective-permute-start | bytes 1671176 | tf_op jit(solution)/shard_map/ppermute | solution.py:33
  56.2 16.3 %collective-permute-start.1 = (bf16[128,2048]{1,0:T(8,128)(2,1)S(1)}, bf16[128,2048]{1,0:T(8,128)(2,1)S(1)}, u32[]{:S(2)}, u32[]{:S(2)}) collective-permute-start(bf16[128,2048]{1,0:T(8,128)(2,1)S(1)} %bitcast_select_fusion.2), channel_id=1, source_target_pairs={{0,8},{8,16},{16,24},{1,9},{9,17},{17,25},{2,10},{10,18},{18,26},{... | collective-permute-start | bytes 1572872 | tf_op jit(solution)/shard_map/ppermute | solution.py:28
  58.4 2.2 %copy-start = (bf16[1,256,8192]{2,1,0:T(8,128)(2,1)S(1)}, bf16[1,256,8192]{2,1,0:T(8,128)(2,1)}, u32[]{:S(2)}) copy-start(bf16[1,256,8192]{2,1,0:T(8,128)(2,1)} %refs_5_.5) | copy-start | bytes 12582916
  60.6 4.5 %copy-start.1 = (bf16[1,256,8192]{2,1,0:T(8,128)(2,1)S(1)}, bf16[1,256,8192]{2,1,0:T(8,128)(2,1)}, u32[]{:S(2)}) copy-start(bf16[1,256,8192]{2,1,0:T(8,128)(2,1)} %refs_5_.5) | copy-start | bytes 12582916

commit v4 on v3

--- a/solution.py
+++ b/solution.py
@@ -16,7 +16,7 @@
 KV_WIDTH = KEY_VALUE_HEADS * HEAD_SIZE
 NOTE = 2 * KV_WIDTH
 MASKED = -1e30
-CHUNKS = (3, 3, 2)
+CHUNKS = (2, 3, 3)
 PARTS = 2
 
 WHOLE = pl.BlockSpec(memory_space=pltpu.VMEM)
@@ -28,9 +28,9 @@
     return lax.ppermute(x, axis, [(i, i + steps) for i in range(n - steps)])
 
 
-def swapped_cores(x):
+def across_cores(x, sources=(0, 1)):
     n = lax.axis_size("ctx")
-    return lax.ppermute(x, "ctx", [(i, i ^ 1) for i in range(n)])
+    return lax.ppermute(x, "ctx", [(i, i ^ 1) for i in range(n) if i % 2 in sources])
 
 
 def everyones(x, axis):
@@ -58,7 +58,7 @@
     return jnp.dot(hot, both, preferred_element_type=jnp.float32).astype(jnp.bfloat16)
 
 
-def settle_kernel(shift_ref, docs_ref, arrived_ref, k_ref, v_ref, out_ref, hot_ref):
+def settle_kernel(shift_ref, docs_ref, arrived_ref, local_ref, out_ref, hot_ref):
     quota = out_ref.shape[0]
     count_before = arrived_ref[:, NOTE:].astype(jnp.float32).astype(jnp.int32)
     shift = jnp.where(shift_ref[1] == 1, count_before - quota, shift_ref[0])
@@ -71,27 +71,24 @@
     hot_local = jnp.where(col == row - shift, 1.0, 0.0)
     hot = jnp.concatenate([hot_arrived, hot_local], axis=1).astype(jnp.bfloat16)
     hot_ref[...] = hot
-    out_ref[:, :KV_WIDTH] = place_rows(hot, arrived_ref[:, :KV_WIDTH], k_ref[0])
-    out_ref[:, KV_WIDTH:NOTE] = place_rows(hot, arrived_ref[:, KV_WIDTH:NOTE], v_ref[0])
+    out_ref[:, :NOTE] = place_rows(hot, arrived_ref[:, :NOTE], local_ref[...])
     docs = jnp.broadcast_to(docs_ref[...].astype(jnp.float32), (quota, quota))
     out_ref[:, NOTE:] = docs.astype(jnp.bfloat16)
 
 
-def settle_kv(shift, docs, arrived, k_rows, v_rows):
+def settle_kv(shift, docs, arrived, local):
     quota = arrived.shape[0]
-    half = pl.BlockSpec((1, quota, KV_WIDTH), lambda i: (0, 0, 0))
-    whole = pl.BlockSpec(arrived.shape, lambda i: (0, 0))
     return pl.pallas_call(
         settle_kernel,
-        grid=(1,),
-        in_specs=[SCALARS, pl.BlockSpec(docs.shape, lambda i: (0, 0)), whole, half, half],
-        out_specs=[whole, pl.BlockSpec((quota, 2 * quota), lambda i: (0, 0))],
+        in_specs=[SCALARS, WHOLE, WHOLE, WHOLE],
+        out_specs=[WHOLE, WHOLE],
         out_shape=[
             jax.ShapeDtypeStruct(arrived.shape, jnp.bfloat16),
             jax.ShapeDtypeStruct((quota, 2 * quota), jnp.bfloat16),
         ],
+        compiler_params=pltpu.CompilerParams(vmem_limit_bytes=24 * 1024 * 1024),
         name="settle_kv",
-    )(shift, docs, arrived, k_rows, v_rows)
+    )(shift, docs, arrived, local)
 
 
 def block_ranks(rank, core, rounds):
@@ -105,8 +102,8 @@
 
 
 def attend_kernel(blocks, first, count, rank_ref, hot_ref, arrived_ref, *refs):
-    kv_refs, q_hbm = refs[:blocks], refs[blocks]
-    out_hbm, local, result, bias, q_sem, out_sems = refs[-6:]
+    kv_refs, far_ref, mate_ref, q_hbm = refs[: blocks - 1], *refs[blocks - 1 : blocks + 2]
+    out_hbm, local, result, bias, rest, q_sem, out_sems = refs[-7:]
     quota = hot_ref.shape[0]
     width = count * GROUP_WIDTH
     start = first * GROUP_WIDTH
@@ -114,11 +111,26 @@
     fetch.start()
 
     rank = rank_ref[0]
+    core = lax.rem(rank, 2)
+    parts = [(first + part) * HEAD_SIZE for part in (0, KEY_VALUE_HEADS)]
+    spans = [slice(at, at + count * HEAD_SIZE) for at in parts] + [slice(NOTE, NOTE + quota)]
+
+    @pl.when(core == 0)
+    def _():
+        for span in spans:
+            rest[:, span] = far_ref[:, span]
+
+    @pl.when(core == 1)
+    def _():
+        for span in spans:
+            rest[:, span] = mate_ref[:, span]
+
+    kv_refs = [*kv_refs, rest]
     row = lax.broadcasted_iota(jnp.int32, (quota, quota), 0)
     col = lax.broadcasted_iota(jnp.int32, (quota, quota), 1)
     own_docs = kv_refs[0][:, NOTE:].astype(jnp.float32)
     q_docs = jnp.sum(jnp.where(row == col, own_docs, 0.0), axis=1, keepdims=True)
-    for b, block_rank in enumerate(block_ranks(rank, lax.rem(rank, 2), (blocks - 1) // 2)):
+    for b, block_rank in enumerate(block_ranks(rank, core, (blocks - 1) // 2)):
         allowed = kv_refs[b][:, NOTE:].astype(jnp.float32) == q_docs
         allowed &= (col <= row) if b == 0 else (block_rank >= 0)
         bias[:, b * quota : (b + 1) * quota] = jnp.where(allowed, 0.0, MASKED)
@@ -186,35 +198,31 @@
 
 def attend(rank, hot, arrived, q_rows, kv_blocks, first, count, out):
     quota = arrived.shape[0]
-    blocks = len(kv_blocks)
+    blocks = len(kv_blocks) - 1
     width = count * GROUP_WIDTH
-    anywhere = pl.BlockSpec(memory_space=pl.ANY)
-    in_specs = [SCALARS, WHOLE, WHOLE] + [WHOLE] * blocks + [anywhere]
+    in_hbm = pl.BlockSpec(memory_space=pltpu.HBM)
+    in_specs = [SCALARS, WHOLE, WHOLE] + [WHOLE] * len(kv_blocks) + [in_hbm]
     operands = [rank, hot, arrived, *kv_blocks, q_rows]
     aliases = {}
     if out is not None:
-        in_specs.append(anywhere)
+        in_specs.append(in_hbm)
         aliases = {len(operands): 0}
         operands.append(out)
-    pairs = count * GROUP * quota * quota * blocks
     return pl.pallas_call(
         functools.partial(attend_kernel, blocks, first, count),
         in_specs=in_specs,
-        out_specs=anywhere,
+        out_specs=in_hbm,
         out_shape=jax.ShapeDtypeStruct((1, quota, QUERY_HEADS * HEAD_SIZE), jnp.bfloat16),
         input_output_aliases=aliases,
         scratch_shapes=[
             pltpu.VMEM((quota, width), jnp.bfloat16),
             pltpu.VMEM((quota, width), jnp.bfloat16),
             pltpu.VMEM((quota, blocks * quota), jnp.float32),
+            pltpu.VMEM((quota, NOTE + quota), jnp.bfloat16),
             pltpu.SemaphoreType.DMA,
             pltpu.SemaphoreType.DMA((count,)),
         ],
-        cost_estimate=pl.CostEstimate(
-            flops=4 * pairs * HEAD_SIZE,
-            bytes_accessed=count * quota * (3 * GROUP_WIDTH + 2 * blocks * HEAD_SIZE) * 2,
-            transcendentals=pairs,
-        ),
+        cost_estimate=pl.CostEstimate(flops=0, bytes_accessed=0, transcendentals=0),
         compiler_params=pltpu.CompilerParams(vmem_limit_bytes=24 * 1024 * 1024),
         name="attend_heads",
     )(*operands)
@@ -240,7 +248,9 @@
         ],
         axis=1,
     )
+    local_kv = jnp.concatenate([k_rows[0, :quota], value_slot_rows[0, :quota]], axis=1)
     kv_tail, later = lax.optimization_barrier((kv_tail, later))
+    local_kv, later = lax.optimization_barrier((local_kv, later))
     arrived_kv = shifted(kv_tail, "dp", 1)
     arrived_q = []
     first = 0
@@ -250,7 +260,7 @@
         first += size
 
     shift = shift_in_known(own_count, quota)
-    own, hot = settle_kv(shift, doc_ids, arrived_kv, k_rows, value_slot_rows)
+    own, hot = settle_kv(shift, doc_ids, arrived_kv, local_kv)
 
     kv_blocks = [own]
     carried = own
@@ -260,8 +270,8 @@
         if back <= min(rounds, len(CHUNKS) - 1):
             carried, arrived_q[back - 1] = lax.optimization_barrier((carried, arrived_q[back - 1]))
         if back < rounds:
-            kv_blocks.append(swapped_cores(carried))
-    kv_blocks.append(swapped_cores(jnp.where(rank % 2 == 0, own, carried)))
+            kv_blocks.append(across_cores(carried))
+    kv_blocks += [across_cores(carried, (1,)), across_cores(own, (0,))]
 
     out = None
     first = 0

time: 76.5 us -> 73.8 us (0.965)
  waiting for transfers between devices: 28.4 us -> 16 us
  starting transfers between devices: 22.6 us -> 30.8 us
  local copies, waits for them, and re-layouts: 3.01 us -> 4.96 us
    ppermute x6, waiting for transfers between devices: 28.4 us -> 14.5 us  [shifted(): return lax.ppermute(x, axis, [(i, i + steps) for i in range(n - steps)])]
    ppermute x2 -> x3, starting transfers between devices: 6.58 us -> 14.9 us  [across_cores(): lax.ppermute(x, 'ctx', [(i, i ^ 1) for i in range(n) if i % 2 in sources])]
    unnamed x10 -> x16, local copies, waits for them, and re-layouts: 3 us -> 4.91 us
    ppermute x2 -> x3, waiting for transfers between devices: 0.01 us -> 1.51 us  [across_cores(): lax.ppermute(x, 'ctx', [(i, i ^ 1) for i in range(n) if i % 2 in sources])]
    pallas_call x1, Pallas kernels: 2.35 us -> 0.86 us  [settle_kv(): pl.pallas_call(settle_kernel, in_specs=[SCALARS, WHOLE, WHOLE, WHOLE], ou...]
    pallas_call x3, Pallas kernels: 12.4 us -> 13.8 us  [attend(): pl.pallas_call(functools.partial(attend_kernel, blocks, first, count), in...]
  transfers between devices with their start and end apart: 8 -> 9, of which waited for: 4 -> 5; matrix products, arithmetic and copies ran while one was open for 6% -> 6% of each run, Pallas kernels for 15% -> 12%
where the time goes in v4:
time: 73.8 us; the launch traced here: 73.3 us
  starting transfers between devices  30.8 us (42%)
  waiting for transfers between devices  16 us (22%)
  Pallas kernels  14.6 us (20%)
  other arithmetic  5.79 us (8%)
  local copies, waits for them, and re-layouts  4.96 us (7%)
  between operations  1.15 us (2%)
    ppermute x6, starting transfers between devices, shifted(): return lax.ppermute(x, axis, [(i, i + steps) for i in range(n - steps)])  15.9 us
    ppermute x3, starting transfers between devices, across_cores(): lax.ppermute(x, 'ctx', [(i, i ^ 1) for i in range(n) if i % 2 in sources])  14.9 us
    ppermute x6, waiting for transfers between devices, shifted(): return lax.ppermute(x, axis, [(i, i + steps) for i in range(n - steps)])  14.5 us
    pallas_call x3, Pallas kernels, attend(): pl.pallas_call(functools.partial(attend_kernel, blocks, first, count), in...  13.8 us
    select_n x3, other arithmetic, circular_tail(): return jnp.where(later[:, None], rows[quota:], rows[:quota])  5.57 us
    unnamed x16, local copies, waits for them, and re-layouts  4.91 us
    ppermute x3, waiting for transfers between devices, across_cores(): lax.ppermute(x, 'ctx', [(i, i ^ 1) for i in range(n) if i % 2 in sources])  1.51 us
  transfers between devices with their start and end apart: 9, of which 5 were waited for; matrix products, arithmetic and copies ran while one was open for 6% of the time, Pallas kernels for 12%

profile of v4, /device:TPU:21, one launch (start us, length us, event | category | flops | bytes accessed | tf_op | source)
XLA Modules:
  0.0 73.3 jit_solution(1999579346758787779)
XLA Ops:
  0.0 0.0 copy-start.7
  0.0 0.0 copy-start.6
  0.8 1.3 %bitcast_select_fusion.4 = (bf16[128,1024]{1,0:T(8,128)(2,1)S(1)}, bf16[128,1024]{1,0:T(8,128)(2,1)S(1)}) fusion(bf16[1,256,1024]{2,1,0:T(8,128)(2,1)} %param.6, pred[128]{0:T(512)(128)(4,1)S(1)} %add_compare_fusion, bf16[1,256,1024]{2,1,0:T(8,128)(2,1)} %param.7), kind=kLoop, calls=%fused_computation.6 | loop fusion | flops 262144 | bytes 1572992 | tf_op jit(solution)/shard_map/jit(_where)/select_n | solution.py:233
  2.1 0.1 maximum_maximum_fusion
  2.2 0.0 copy-start.5
  2.2 3.1 %collective-permute-start = (bf16[128,2176]{1,0:T(8,128)(2,1)S(1)}, bf16[128,2176]{1,0:T(8,128)(2,1)S(1)}, u32[]{:S(2)}, u32[]{:S(2)}) collective-permute-start(bf16[128,2176]{1,0:T(8,128)(2,1)S(1)} %maximum_maximum_fusion), channel_id=1, source_target_pairs={{0,8},{8,16},{16,24},{1,9},{9,17},{17,25},{2,10},{10,18},{18,26},{... | collective-permute-start | bytes 1671176 | tf_op jit(solution)/shard_map/ppermute | solution.py:28
  5.3 0.0 copy-done.7
  5.4 0.0 copy-done.6
  5.5 1.3 %bitcast_select_fusion.2 = bf16[128,2048]{1,0:T(8,128)(2,1)S(1)} fusion(bf16[1,256,8192]{2,1,0:T(8,128)(2,1)} %refs_6_.5, pred[128]{0:T(512)(128)(4,1)S(1)} %add_compare_fusion), kind=kLoop, calls=%fused_computation.4 | loop fusion | flops 262144 | bytes 1572992 | tf_op jit(solution)/shard_map/jit(_where)/select_n | solution.py:233
  6.8 1.9 %collective-permute-start.3 = (bf16[128,2048]{1,0:T(8,128)(2,1)S(1)}, bf16[128,2048]{1,0:T(8,128)(2,1)S(1)}, u32[]{:S(2)}, u32[]{:S(2)}) collective-permute-start(bf16[128,2048]{1,0:T(8,128)(2,1)S(1)} %bitcast_select_fusion.2), channel_id=1, source_target_pairs={{0,8},{8,16},{16,24},{1,9},{9,17},{17,25},{2,10},{10,18},{18,26},{... | collective-permute-start | bytes 1572872 | tf_op jit(solution)/shard_map/ppermute | solution.py:28
  8.7 0.1 pad_add_fusion.shift_ref
  8.8 9.7 %collective-permute-done.arrived_ref = bf16[128,2176]{1,0:T(8,128)(2,1)S(1)} collective-permute-done((bf16[128,2176]{1,0:T(8,128)(2,1)S(1)}, bf16[128,2176]{1,0:T(8,128)(2,1)S(1)}, u32[]{:S(2)}, u32[]{:S(2)}) %collective-permute-start) | collective-permute-done | bytes 557088 | tf_op jit(solution)/shard_map/ppermute | solution.py:28
  18.5 0.0 copy-done.5
  18.5 0.9 %settle_kv.1 = (bf16[128,2176]{1,0:T(8,128)(2,1)S(1)}, bf16[128,256]{1,0:T(8,128)(2,1)S(1)}) custom-call(s32[2]{0:T(128)S(1)} %pad_add_fusion.shift_ref, s32[1,128]{1,0:T(1,128)S(1)} %copy-done.5, bf16[128,2176]{1,0:T(8,128)(2,1)S(1)} %collective-permute-done.arrived_ref, bf16[128,2048]{1,0:T(8,128)(2,1)S(1)} %pad_maximum_fusion.local_ref), custom_call_target="tpu_custom_call" | custom-call | tf_op jit(solution)/shard_map/settle_kv/pallas_call | solution.py:81
  19.4 3.2 %collective-permute-start.2 = (bf16[128,2176]{1,0:T(8,128)(2,1)S(1)}, bf16[128,2176]{1,0:T(8,128)(2,1)S(1)}, u32[]{:S(2)}, u32[]{:S(2)}) collective-permute-start(bf16[128,2176]{1,0:T(8,128)(2,1)S(1)} %get-tuple-element.20.refs_0_), channel_id=1, source_target_pairs={{0,2},{1,3},{2,4},{3,5},{4,6},{5,7},{8,10},{9,11},{10,12},{11,13},... | collective-permute-start | bytes 1671176 | tf_op jit(solution)/shard_map/ppermute | solution.py:28
  22.6 2.9 %bitcast_select_fusion = (bf16[128,3072]{1,0:T(8,128)(2,1)S(1)}, bf16[128,3072]{1,0:T(8,128)(2,1)}) fusion(bf16[1,256,8192]{2,1,0:T(8,128)(2,1)} %refs_6_.5, pred[128]{0:T(512)(128)(4,1)S(1)} %add_compare_fusion), kind=kLoop, calls=%fused_computation | loop fusion | flops 786432 | bytes 4718720 | tf_op jit(solution)/shard_map/jit(_where)/select_n | solution.py:233
  25.5 2.2 %collective-permute-start.6 = (bf16[128,3072]{1,0:T(8,128)(2,1)S(1)}, bf16[128,3072]{1,0:T(8,128)(2,1)S(1)}, u32[]{:S(2)}, u32[]{:S(2)}) collective-permute-start(bf16[128,3072]{1,0:T(8,128)(2,1)S(1)} %get-tuple-element.25), channel_id=1, source_target_pairs={{0,8},{8,16},{16,24},{1,9},{9,17},{17,25},{2,10},{10,18},{18,26},{... | collective-permute-start | bytes 2359304 | tf_op jit(solution)/shard_map/ppermute | solution.py:28
  27.8 2.0 %collective-permute-done.3.arrived_ref = bf16[128,2048]{1,0:T(8,128)(2,1)S(1)} collective-permute-done((bf16[128,2048]{1,0:T(8,128)(2,1)S(1)}, bf16[128,2048]{1,0:T(8,128)(2,1)S(1)}, u32[]{:S(2)}, u32[]{:S(2)}) %collective-permute-start.3) | collective-permute-done | bytes 524320 | tf_op jit(solution)/shard_map/ppermute | solution.py:28
  29.7 0.0 copy-start.3
  29.7 0.8 %copy-done.3 = bf16[128,2048]{1,0:T(8,128)(2,1)} copy-done((bf16[128,2048]{1,0:T(8,128)(2,1)}, bf16[128,2048]{1,0:T(8,128)(2,1)S(1)}, u32[]{:S(2)}) %copy-start.3) | copy-done | bytes 524312
  30.5 2.2 %collective-permute-done.2.refs_1_ = bf16[128,2176]{1,0:T(8,128)(2,1)S(1)} collective-permute-done((bf16[128,2176]{1,0:T(8,128)(2,1)S(1)}, bf16[128,2176]{1,0:T(8,128)(2,1)S(1)}, u32[]{:S(2)}, u32[]{:S(2)}) %collective-permute-start.2) | collective-permute-done | bytes 557088 | tf_op jit(solution)/shard_map/ppermute | solution.py:28
  32.7 3.2 %collective-permute-start.5 = (bf16[128,2176]{1,0:T(8,128)(2,1)S(1)}, bf16[128,2176]{1,0:T(8,128)(2,1)S(1)}, u32[]{:S(2)}, u32[]{:S(2)}) collective-permute-start(bf16[128,2176]{1,0:T(8,128)(2,1)S(1)} %collective-permute-done.2.refs_1_), channel_id=1, source_target_pairs={{0,2},{1,3},{2,4},{3,5},{4,6},{5,7},{8,10},{9,11},{10,12},{11,13},... | collective-permute-start | bytes 1671176 | tf_op jit(solution)/shard_map/ppermute | solution.py:28
  35.9 2.2 %collective-permute-start.1 = (bf16[128,3072]{1,0:T(8,128)(2,1)}, bf16[128,3072]{1,0:T(8,128)(2,1)}, u32[]{:S(2)}, u32[]{:S(2)}) collective-permute-start(bf16[128,3072]{1,0:T(8,128)(2,1)} %get-tuple-element.26), channel_id=1, source_target_pairs={{0,8},{8,16},{16,24},{1,9},{9,17},{17,25},{2,10},{10,18},{18,26},{... | collective-permute-start | bytes 2359304 | tf_op jit(solution)/shard_map/ppermute | solution.py:28
  38.1 1.3 %collective-permute-start.8 = (bf16[128,2176]{1,0:T(8,128)(2,1)S(1)}, bf16[128,2176]{1,0:T(8,128)(2,1)S(1)}, u32[]{:S(2)}, u32[]{:S(2)}) collective-permute-start(bf16[128,2176]{1,0:T(8,128)(2,1)S(1)} %get-tuple-element.20.refs_0_), channel_id=1, source_target_pairs={{0,1},{2,3},{4,5},{6,7},{8,9},{10,11},{12,13},{14,15},{16,17},{18,... | collective-permute-start | bytes 1671176 | tf_op jit(solution)/shard_map/ppermute | solution.py:33
  39.4 4.3 %collective-permute-start.4 = (bf16[128,2176]{1,0:T(8,128)(2,1)S(1)}, bf16[128,2176]{1,0:T(8,128)(2,1)S(1)}, u32[]{:S(2)}, u32[]{:S(2)}) collective-permute-start(bf16[128,2176]{1,0:T(8,128)(2,1)S(1)} %collective-permute-done.2.refs_1_), channel_id=1, source_target_pairs={{0,1},{1,0},{2,3},{3,2},{4,5},{5,4},{6,7},{7,6},{8,9},{9,8},{10,11... | collective-permute-start | bytes 1671176 | tf_op jit(solution)/shard_map/ppermute | solution.py:33
  43.7 0.7 collective-permute-done.6.arrived_ref
  44.4 0.0 copy-start.1
  44.4 0.9 %copy-done.1 = bf16[128,3072]{1,0:T(8,128)(2,1)} copy-done((bf16[128,3072]{1,0:T(8,128)(2,1)}, bf16[128,3072]{1,0:T(8,128)(2,1)S(1)}, u32[]{:S(2)}) %copy-start.1) | copy-done | bytes 786456
  45.2 0.0 collective-permute-done.5.refs_3_
  45.2 9.3 %collective-permute-start.7 = (bf16[128,2176]{1,0:T(8,128)(2,1)S(1)}, bf16[128,2176]{1,0:T(8,128)(2,1)S(1)}, u32[]{:S(2)}, u32[]{:S(2)}) collective-permute-start(bf16[128,2176]{1,0:T(8,128)(2,1)S(1)} %collective-permute-done.5.refs_3_), channel_id=1, source_target_pairs={{1,0},{3,2},{5,4},{7,6},{9,8},{11,10},{13,12},{15,14},{17,16},{19,... | collective-permute-start | bytes 1671176 | tf_op jit(solution)/shard_map/ppermute | solution.py:33
  54.6 0.0 collective-permute-done.8.refs_5_
  54.6 0.0 collective-permute-done.4.refs_2_
  54.6 1.5 %collective-permute-done.7.refs_4_ = bf16[128,2176]{1,0:T(8,128)(2,1)S(1)} collective-permute-done((bf16[128,2176]{1,0:T(8,128)(2,1)S(1)}, bf16[128,2176]{1,0:T(8,128)(2,1)S(1)}, u32[]{:S(2)}, u32[]{:S(2)}) %collective-permute-start.7) | collective-permute-done | bytes 557088 | tf_op jit(solution)/shard_map/ppermute | solution.py:33
  56.1 0.0 copy-start
  56.1 2.2 %copy-done = bf16[1,256,8192]{2,1,0:T(8,128)(2,1)S(1)} copy-done((bf16[1,256,8192]{2,1,0:T(8,128)(2,1)S(1)}, bf16[1,256,8192]{2,1,0:T(8,128)(2,1)}, u32[]{:S(2)}) %copy-start) | copy-done | bytes 4194328
  58.3 0.0 copy-start.4
  58.3 1.0 %copy-done.4 = bf16[128,2048]{1,0:T(8,128)(2,1)S(1)} copy-done((bf16[128,2048]{1,0:T(8,128)(2,1)S(1)}, bf16[128,2048]{1,0:T(8,128)(2,1)}, u32[]{:S(2)}) %copy-start.4) | copy-done | bytes 524312
  59.3 0.0 copy-start.2
  59.4 3.5 %attend_heads.3.refs_7_ = bf16[1,128,8192]{2,1,0:T(8,128)(2,1)} custom-call(s32[1]{0:T(128)} %bitcast.rank_ref, bf16[128,256]{1,0:T(8,128)(2,1)S(1)} %get-tuple-element.18.hot_ref, bf16[128,2048]{1,0:T(8,128)(2,1)S(1)} %copy-done.4, bf16[128,2176]{1,0:T(8,128)(2,1)S(1)} %get-tuple-element.20.refs_0_, bf16[128,2176]{1,0:T(8,128)(2,1)S(1)} %collective-permute-done.2.refs_1_, ...), custom_call_target="tpu_custom_call" | custom-call | tf_op jit(solution)/shard_map/attend_heads/pallas_call | solution.py:211
  62.8 0.0 copy-done.2
  62.8 4.5 %attend_heads.4.refs_7_ = bf16[1,128,8192]{2,1,0:T(8,128)(2,1)} custom-call(s32[1]{0:T(128)} %bitcast.rank_ref, bf16[128,256]{1,0:T(8,128)(2,1)S(1)} %get-tuple-element.18.hot_ref, bf16[128,3072]{1,0:T(8,128)(2,1)S(1)} %copy-done.2, bf16[128,2176]{1,0:T(8,128)(2,1)S(1)} %get-tuple-element.20.refs_0_, ...), custom_call_target="tpu_custom_call", output_to_operand_aliasing={{}: (10, {})} | custom-call | tf_op jit(solution)/shard_map/attend_heads/pallas_call | solution.py:211
  67.4 0.0 collective-permute-done.1.arrived_ref
  67.4 5.8 %attend_heads.5 = bf16[1,128,8192]{2,1,0:T(8,128)(2,1)} custom-call(s32[1]{0:T(128)} %bitcast.rank_ref, bf16[128,256]{1,0:T(8,128)(2,1)S(1)} %get-tuple-element.18.hot_ref, bf16[128,3072]{1,0:T(8,128)(2,1)} %collective-permute-done.1.arrived_ref, bf16[128,2176]{1,0:T(8,128)(2,1)S(1)} %get-tuple-element.20.refs_0_, ...), custom_call_target="tpu_custom_call", output_to_operand_aliasing={{}: (10, {})} | custom-call | tf_op jit(solution)/shard_map/attend_heads/pallas_call | solution.py:211
  (5 shorter events, 0.1 us)
Async XLA Ops:
  0.0 5.3 %copy-start.7 = (bf16[1,256,1024]{2,1,0:T(8,128)(2,1)S(1)}, bf16[1,256,1024]{2,1,0:T(8,128)(2,1)}, u32[]{:S(2)}) copy-start(bf16[1,256,1024]{2,1,0:T(8,128)(2,1)} %param.7) | copy-start | bytes 1572868
  0.0 5.4 %copy-start.6 = (bf16[1,256,1024]{2,1,0:T(8,128)(2,1)S(1)}, bf16[1,256,1024]{2,1,0:T(8,128)(2,1)}, u32[]{:S(2)}) copy-start(bf16[1,256,1024]{2,1,0:T(8,128)(2,1)} %param.6) | copy-start | bytes 1572868
  2.2 16.3 %copy-start.5 = (s32[1,128]{1,0:T(1,128)S(1)}, s32[1,128]{1,0:T(1,128)}, u32[]{:S(2)}) copy-start(s32[1,128]{1,0:T(1,128)} %docs_ref.1) | copy-start | bytes 1540
  2.2 16.3 %collective-permute-start = (bf16[128,2176]{1,0:T(8,128)(2,1)S(1)}, bf16[128,2176]{1,0:T(8,128)(2,1)S(1)}, u32[]{:S(2)}, u32[]{:S(2)}) collective-permute-start(bf16[128,2176]{1,0:T(8,128)(2,1)S(1)} %maximum_maximum_fusion), channel_id=1, source_target_pairs={{0,8},{8,16},{16,24},{1,9},{9,17},{17,25},{2,10},{10,18},{18,26},{... | collective-permute-start | bytes 1671176 | tf_op jit(solution)/shard_map/ppermute | solution.py:28
  6.8 23.0 %collective-permute-start.3 = (bf16[128,2048]{1,0:T(8,128)(2,1)S(1)}, bf16[128,2048]{1,0:T(8,128)(2,1)S(1)}, u32[]{:S(2)}, u32[]{:S(2)}) collective-permute-start(bf16[128,2048]{1,0:T(8,128)(2,1)S(1)} %bitcast_select_fusion.2), channel_id=1, source_target_pairs={{0,8},{8,16},{16,24},{1,9},{9,17},{17,25},{2,10},{10,18},{18,26},{... | collective-permute-start | bytes 1572872 | tf_op jit(solution)/shard_map/ppermute | solution.py:28
  19.4 13.3 %collective-permute-start.2 = (bf16[128,2176]{1,0:T(8,128)(2,1)S(1)}, bf16[128,2176]{1,0:T(8,128)(2,1)S(1)}, u32[]{:S(2)}, u32[]{:S(2)}) collective-permute-start(bf16[128,2176]{1,0:T(8,128)(2,1)S(1)} %get-tuple-element.20.refs_0_), channel_id=1, source_target_pairs={{0,2},{1,3},{2,4},{3,5},{4,6},{5,7},{8,10},{9,11},{10,12},{11,13},... | collective-permute-start | bytes 1671176 | tf_op jit(solution)/shard_map/ppermute | solution.py:28
  25.5 18.8 %collective-permute-start.6 = (bf16[128,3072]{1,0:T(8,128)(2,1)S(1)}, bf16[128,3072]{1,0:T(8,128)(2,1)S(1)}, u32[]{:S(2)}, u32[]{:S(2)}) collective-permute-start(bf16[128,3072]{1,0:T(8,128)(2,1)S(1)} %get-tuple-element.25), channel_id=1, source_target_pairs={{0,8},{8,16},{16,24},{1,9},{9,17},{17,25},{2,10},{10,18},{18,26},{... | collective-permute-start | bytes 2359304 | tf_op jit(solution)/shard_map/ppermute | solution.py:28
  29.7 0.8 %copy-start.3 = (bf16[128,2048]{1,0:T(8,128)(2,1)}, bf16[128,2048]{1,0:T(8,128)(2,1)S(1)}, u32[]{:S(2)}) copy-start(bf16[128,2048]{1,0:T(8,128)(2,1)S(1)} %collective-permute-done.3.arrived_ref) | copy-start | bytes 1572868
  32.7 12.6 %collective-permute-start.5 = (bf16[128,2176]{1,0:T(8,128)(2,1)S(1)}, bf16[128,2176]{1,0:T(8,128)(2,1)S(1)}, u32[]{:S(2)}, u32[]{:S(2)}) collective-permute-start(bf16[128,2176]{1,0:T(8,128)(2,1)S(1)} %collective-permute-done.2.refs_1_), channel_id=1, source_target_pairs={{0,2},{1,3},{2,4},{3,5},{4,6},{5,7},{8,10},{9,11},{10,12},{11,13},... | collective-permute-start | bytes 1671176 | tf_op jit(solution)/shard_map/ppermute | solution.py:28
  35.9 31.5 %collective-permute-start.1 = (bf16[128,3072]{1,0:T(8,128)(2,1)}, bf16[128,3072]{1,0:T(8,128)(2,1)}, u32[]{:S(2)}, u32[]{:S(2)}) collective-permute-start(bf16[128,3072]{1,0:T(8,128)(2,1)} %get-tuple-element.26), channel_id=1, source_target_pairs={{0,8},{8,16},{16,24},{1,9},{9,17},{17,25},{2,10},{10,18},{18,26},{... | collective-permute-start | bytes 2359304 | tf_op jit(solution)/shard_map/ppermute | solution.py:28
  38.1 16.5 %collective-permute-start.8 = (bf16[128,2176]{1,0:T(8,128)(2,1)S(1)}, bf16[128,2176]{1,0:T(8,128)(2,1)S(1)}, u32[]{:S(2)}, u32[]{:S(2)}) collective-permute-start(bf16[128,2176]{1,0:T(8,128)(2,1)S(1)} %get-tuple-element.20.refs_0_), channel_id=1, source_target_pairs={{0,1},{2,3},{4,5},{6,7},{8,9},{10,11},{12,13},{14,15},{16,17},{18,... | collective-permute-start | bytes 1671176 | tf_op jit(solution)/shard_map/ppermute | solution.py:33
  39.4 15.2 %collective-permute-start.4 = (bf16[128,2176]{1,0:T(8,128)(2,1)S(1)}, bf16[128,2176]{1,0:T(8,128)(2,1)S(1)}, u32[]{:S(2)}, u32[]{:S(2)}) collective-permute-start(bf16[128,2176]{1,0:T(8,128)(2,1)S(1)} %collective-permute-done.2.refs_1_), channel_id=1, source_target_pairs={{0,1},{1,0},{2,3},{3,2},{4,5},{5,4},{6,7},{7,6},{8,9},{9,8},{10,11... | collective-permute-start | bytes 1671176 | tf_op jit(solution)/shard_map/ppermute | solution.py:33
  44.4 0.9 %copy-start.1 = (bf16[128,3072]{1,0:T(8,128)(2,1)}, bf16[128,3072]{1,0:T(8,128)(2,1)S(1)}, u32[]{:S(2)}) copy-start(bf16[128,3072]{1,0:T(8,128)(2,1)S(1)} %collective-permute-done.6.arrived_ref) | copy-start | bytes 2359300
  45.2 10.9 %collective-permute-start.7 = (bf16[128,2176]{1,0:T(8,128)(2,1)S(1)}, bf16[128,2176]{1,0:T(8,128)(2,1)S(1)}, u32[]{:S(2)}, u32[]{:S(2)}) collective-permute-start(bf16[128,2176]{1,0:T(8,128)(2,1)S(1)} %collective-permute-done.5.refs_3_), channel_id=1, source_target_pairs={{1,0},{3,2},{5,4},{7,6},{9,8},{11,10},{13,12},{15,14},{17,16},{19,... | collective-permute-start | bytes 1671176 | tf_op jit(solution)/shard_map/ppermute | solution.py:33
  56.1 2.2 %copy-start = (bf16[1,256,8192]{2,1,0:T(8,128)(2,1)S(1)}, bf16[1,256,8192]{2,1,0:T(8,128)(2,1)}, u32[]{:S(2)}) copy-start(bf16[1,256,8192]{2,1,0:T(8,128)(2,1)} %refs_6_.5) | copy-start | bytes 12582916
  58.3 1.0 %copy-start.4 = (bf16[128,2048]{1,0:T(8,128)(2,1)S(1)}, bf16[128,2048]{1,0:T(8,128)(2,1)}, u32[]{:S(2)}) copy-start(bf16[128,2048]{1,0:T(8,128)(2,1)} %copy-done.3) | copy-start | bytes 1572868
  59.3 3.5 %copy-start.2 = (bf16[128,3072]{1,0:T(8,128)(2,1)S(1)}, bf16[128,3072]{1,0:T(8,128)(2,1)}, u32[]{:S(2)}) copy-start(bf16[128,3072]{1,0:T(8,128)(2,1)} %copy-done.1) | copy-start | bytes 2359300

commit v5 on v4

--- a/solution.py
+++ b/solution.py
@@ -17,7 +17,8 @@
 NOTE = 2 * KV_WIDTH
 MASKED = -1e30
 CHUNKS = (2, 3, 3)
-PARTS = 2
+TILE = 32
+VMEM_GRANT = 48 * 1024 * 1024
 
 WHOLE = pl.BlockSpec(memory_space=pltpu.VMEM)
 SCALARS = pl.BlockSpec(memory_space=pltpu.SMEM)
@@ -86,7 +87,7 @@
             jax.ShapeDtypeStruct(arrived.shape, jnp.bfloat16),
             jax.ShapeDtypeStruct((quota, 2 * quota), jnp.bfloat16),
         ],
-        compiler_params=pltpu.CompilerParams(vmem_limit_bytes=24 * 1024 * 1024),
+        compiler_params=pltpu.CompilerParams(vmem_limit_bytes=VMEM_GRANT),
         name="settle_kv",
     )(shift, docs, arrived, local)
 
@@ -101,14 +102,22 @@
     return ranks
 
 
-def attend_kernel(blocks, first, count, rank_ref, hot_ref, arrived_ref, *refs):
-    kv_refs, far_ref, mate_ref, q_hbm = refs[: blocks - 1], *refs[blocks - 1 : blocks + 2]
-    out_hbm, local, result, bias, rest, q_sem, out_sems = refs[-7:]
+def attend_kernel(blocks, first, count, rank_ref, hot_ref, *refs):
+    kv_refs, far_ref, mate_ref = refs[: blocks - 1], refs[blocks - 1], refs[blocks]
+    arrived_hbm, local_hbm = refs[blocks + 1 : blocks + 3]
+    out_hbm, arrived, local, result, bias, rest, q, keys, values, *refs = refs[-15:]
+    scores, weights, (in_sems, out_sems) = refs[:2], refs[2:4], refs[4:]
     quota = hot_ref.shape[0]
     width = count * GROUP_WIDTH
     start = first * GROUP_WIDTH
-    fetch = pltpu.make_async_copy(q_hbm.at[0, 0:quota, start : start + width], local, q_sem)
-    fetch.start()
+    fetches = [
+        pltpu.make_async_copy(arrived_hbm, arrived, in_sems.at[0]),
+        pltpu.make_async_copy(
+            local_hbm.at[0, 0:quota, start : start + width], local, in_sems.at[1]
+        ),
+    ]
+    for fetch in fetches:
+        fetch.start()
 
     rank = rank_ref[0]
     core = lax.rem(rank, 2)
@@ -134,96 +143,113 @@
         allowed = kv_refs[b][:, NOTE:].astype(jnp.float32) == q_docs
         allowed &= (col <= row) if b == 0 else (block_rank >= 0)
         bias[:, b * quota : (b + 1) * quota] = jnp.where(allowed, 0.0, MASKED)
+    values[:, HEAD_SIZE:] = jnp.ones((blocks * quota, HEAD_SIZE), jnp.bfloat16)
 
     unit = math.log2(math.e) / math.sqrt(HEAD_SIZE)
-    heads = GROUP // PARTS
-    hot = hot_ref[...]
-
-    def operands(g):
-        at = (first + g) * HEAD_SIZE
-        keys = jnp.concatenate([r[:, at : at + HEAD_SIZE] for r in kv_refs], axis=0)
-        at += KV_WIDTH
-        values = jnp.concatenate([r[:, at : at + HEAD_SIZE] for r in kv_refs], axis=0)
-        values = jnp.concatenate([values, jnp.ones_like(values)], axis=1)
-        cols = slice(g * GROUP_WIDTH, (g + 1) * GROUP_WIDTH)
-        q = place_rows(hot, arrived_ref[:, cols], local[:, cols])
-        return q, keys, values
-
-    def scored(q, keys, part):
-        stacked = jnp.concatenate(
-            [
-                q[:, h * HEAD_SIZE : (h + 1) * HEAD_SIZE]
-                for h in range(part * heads, (part + 1) * heads)
-            ],
-            axis=0,
+    half = GROUP // 2
+
+    def columns(at, g, width):
+        return pl.ds(pl.multiple_of(at + g * width, width), width)
+
+    def take_queries_and_keys(g):
+        cols = columns(0, g, GROUP_WIDTH)
+        placed = place_rows(hot_ref[...], arrived[:, cols], local[:, cols])
+        for h in range(GROUP):
+            q[h * quota : (h + 1) * quota] = placed[:, h * HEAD_SIZE : (h + 1) * HEAD_SIZE]
+        for b, ref in enumerate(kv_refs):
+            keys[b * quota : (b + 1) * quota] = ref[:, columns(parts[0], g, HEAD_SIZE)]
+
+    def take_values(g):
+        for b, ref in enumerate(kv_refs):
+            values[b * quota : (b + 1) * quota, :HEAD_SIZE] = ref[:, columns(parts[1], g, HEAD_SIZE)]
+
+    def score(part):
+        rows = slice(part * half * quota, (part + 1) * half * quota)
+        scores[part][...] = lax.dot_general(
+            q[rows], keys[...], (((1,), (1,)), ((), ())), preferred_element_type=jnp.float32
         )
-        return lax.dot_general(
-            stacked, keys, (((1,), (1,)), ((), ())), preferred_element_type=jnp.float32
+
+    def finish(part, g):
+        for at in range(0, half * quota, TILE):
+            rows = slice(at, at + TILE)
+            bias_rows = slice(at % quota, at % quota + TILE)
+            tile = scores[part][rows] * unit + bias[bias_rows]
+            tile = jnp.exp2(tile - jnp.max(tile, axis=1, keepdims=True))
+            weights[part][rows] = tile.astype(jnp.bfloat16)
+        mixed = jnp.dot(weights[part][...], values[...], preferred_element_type=jnp.float32)
+        mixed = (mixed[:, :HEAD_SIZE] / mixed[:, HEAD_SIZE:]).astype(jnp.bfloat16)
+        for h in range(half):
+            cols = pl.ds(
+                pl.multiple_of(g * GROUP_WIDTH + (part * half + h) * HEAD_SIZE, HEAD_SIZE), HEAD_SIZE
+            )
+            result[:, cols] = mixed[h * quota : (h + 1) * quota]
+
+    def store(g):
+        return pltpu.make_async_copy(
+            result.at[:, columns(0, g, GROUP_WIDTH)],
+            out_hbm.at[0, :, columns(start, g, GROUP_WIDTH)],
+            out_sems.at[g],
         )
 
-    def finished(scores, values, g, part):
-        scores = scores.reshape(heads, quota, -1) * unit + bias[...][None]
-        weights = jnp.exp2(scores - jnp.max(scores, axis=2, keepdims=True))
-        weights = weights.astype(jnp.bfloat16).reshape(heads * quota, -1)
-        mixed = jnp.dot(weights, values, preferred_element_type=jnp.float32)
-        mixed = (mixed[:, :HEAD_SIZE] / mixed[:, HEAD_SIZE:]).astype(jnp.bfloat16)
-        for h in range(heads):
-            at = g * GROUP_WIDTH + (part * heads + h) * HEAD_SIZE
-            result[:, at : at + HEAD_SIZE] = mixed[h * quota : (h + 1) * quota]
-
-    fetch.wait()
-    stores = []
-    q, keys, values = operands(0)
-    scores = scored(q, keys, 0)
-    for step in range(count * PARTS):
-        g, part = divmod(step, PARTS)
-        own_values, later = values, None
-        if step + 1 < count * PARTS:
-            if part == PARTS - 1:
-                q, keys, values = operands(g + 1)
-            later = scored(q, keys, (part + 1) % PARTS)
-        finished(scores, own_values, g, part)
-        scores = later
-        if part == PARTS - 1:
-            cols = slice(g * GROUP_WIDTH, (g + 1) * GROUP_WIDTH)
-            at = (first + g) * GROUP_WIDTH
-            store = pltpu.make_async_copy(
-                result.at[:, cols], out_hbm.at[0, :, at : at + GROUP_WIDTH], out_sems.at[g]
-            )
-            store.start()
-            stores.append(store)
-    for store in stores:
-        store.wait()
+    for fetch in fetches:
+        fetch.wait()
+    take_queries_and_keys(0)
+    take_values(0)
+    score(0)
+
+    @pl.loop(0, count)
+    def _(g):
+        later = jnp.minimum(g + 1, count - 1)
+        score(1)
+        finish(0, g)
+        take_queries_and_keys(later)
+        score(0)
+        finish(1, g)
+        take_values(later)
+        store(g).start()
+
+    @pl.loop(0, count)
+    def _(g):
+        store(g).wait()
 
 
 def attend(rank, hot, arrived, q_rows, kv_blocks, first, count, out):
     quota = arrived.shape[0]
     blocks = len(kv_blocks) - 1
     width = count * GROUP_WIDTH
-    in_hbm = pl.BlockSpec(memory_space=pltpu.HBM)
-    in_specs = [SCALARS, WHOLE, WHOLE] + [WHOLE] * len(kv_blocks) + [in_hbm]
-    operands = [rank, hot, arrived, *kv_blocks, q_rows]
+    rows = GROUP // 2 * quota
+    anywhere = pl.BlockSpec(memory_space=pl.ANY)
+    in_specs = [SCALARS, WHOLE] + [WHOLE] * len(kv_blocks) + [anywhere] * 2
+    operands = [rank, hot, *kv_blocks, arrived, q_rows]
     aliases = {}
     if out is not None:
-        in_specs.append(in_hbm)
+        in_specs.append(anywhere)
         aliases = {len(operands): 0}
         operands.append(out)
     return pl.pallas_call(
         functools.partial(attend_kernel, blocks, first, count),
         in_specs=in_specs,
-        out_specs=in_hbm,
+        out_specs=anywhere,
         out_shape=jax.ShapeDtypeStruct((1, quota, QUERY_HEADS * HEAD_SIZE), jnp.bfloat16),
         input_output_aliases=aliases,
         scratch_shapes=[
             pltpu.VMEM((quota, width), jnp.bfloat16),
             pltpu.VMEM((quota, width), jnp.bfloat16),
+            pltpu.VMEM((quota, width), jnp.bfloat16),
             pltpu.VMEM((quota, blocks * quota), jnp.float32),
             pltpu.VMEM((quota, NOTE + quota), jnp.bfloat16),
-            pltpu.SemaphoreType.DMA,
+            pltpu.VMEM((GROUP * quota, HEAD_SIZE), jnp.bfloat16),
+            pltpu.VMEM((blocks * quota, HEAD_SIZE), jnp.bfloat16),
+            pltpu.VMEM((blocks * quota, 2 * HEAD_SIZE), jnp.bfloat16),
+            pltpu.VMEM((rows, blocks * quota), jnp.float32),
+            pltpu.VMEM((rows, blocks * quota), jnp.float32),
+            pltpu.VMEM((rows, blocks * quota), jnp.bfloat16),
+            pltpu.VMEM((rows, blocks * quota), jnp.bfloat16),
+            pltpu.SemaphoreType.DMA((2,)),
             pltpu.SemaphoreType.DMA((count,)),
         ],
         cost_estimate=pl.CostEstimate(flops=0, bytes_accessed=0, transcendentals=0),
-        compiler_params=pltpu.CompilerParams(vmem_limit_bytes=24 * 1024 * 1024),
+        compiler_params=pltpu.CompilerParams(vmem_limit_bytes=VMEM_GRANT),
         name="attend_heads",
     )(*operands)
 

time: 73.8 us -> 76.5 us (1.037)
  Pallas kernels: 14.6 us -> 19.7 us
  local copies, waits for them, and re-layouts: 4.96 us -> 2.78 us
    pallas_call x3, Pallas kernels: 13.8 us -> 18.8 us  [attend(): pl.pallas_call(functools.partial(attend_kernel, blocks, first, count), in...]
    unnamed x16 -> x14, local copies, waits for them, and re-layouts: 4.91 us -> 2.73 us
  transfers between devices with their start and end apart: 9 -> 9, of which waited for: 5 -> 5; matrix products, arithmetic and copies ran while one was open for 6% -> 6% of each run, Pallas kernels for 12% -> 17%
where the time goes in v5:
time: 76.5 us; the launch traced here: 76 us
  starting transfers between devices  30.8 us (40%)
  Pallas kernels  19.7 us (26%)
  waiting for transfers between devices  16 us (21%)
  other arithmetic  5.79 us (8%)
  local copies, waits for them, and re-layouts  2.78 us (4%)
  between operations  0.98 us (1%)
    pallas_call x3, Pallas kernels, attend(): pl.pallas_call(functools.partial(attend_kernel, blocks, first, count), in...  18.8 us
    ppermute x6, starting transfers between devices, shifted(): return lax.ppermute(x, axis, [(i, i + steps) for i in range(n - steps)])  15.9 us
    ppermute x3, starting transfers between devices, across_cores(): lax.ppermute(x, 'ctx', [(i, i ^ 1) for i in range(n) if i % 2 in sources])  14.9 us
    ppermute x6, waiting for transfers between devices, shifted(): return lax.ppermute(x, axis, [(i, i + steps) for i in range(n - steps)])  14.5 us
    select_n x3, other arithmetic, circular_tail(): return jnp.where(later[:, None], rows[quota:], rows[:quota])  5.58 us
    unnamed x14, local copies, waits for them, and re-layouts  2.73 us
  transfers between devices with their start and end apart: 9, of which 5 were waited for; matrix products, arithmetic and copies ran while one was open for 6% of the time, Pallas kernels for 17%

profile of v5, /device:TPU:21, one launch (start us, length us, event | category | flops | bytes accessed | tf_op | source)
XLA Modules:
  0.0 76.0 jit_solution(14449194021931553755)
XLA Ops:
  0.0 0.0 copy-start.6
  0.0 0.0 copy-start.5
  0.8 1.3 %bitcast_select_fusion.4 = (bf16[128,1024]{1,0:T(8,128)(2,1)S(1)}, bf16[128,1024]{1,0:T(8,128)(2,1)S(1)}) fusion(bf16[1,256,1024]{2,1,0:T(8,128)(2,1)} %param.6, pred[128]{0:T(512)(128)(4,1)S(1)} %add_compare_fusion, bf16[1,256,1024]{2,1,0:T(8,128)(2,1)} %param.7), kind=kLoop, calls=%fused_computation.6 | loop fusion | flops 262144 | bytes 1572992 | tf_op jit(solution)/shard_map/jit(_where)/select_n | solution.py:259
  2.1 0.1 maximum_maximum_fusion
  2.2 0.0 copy-start.4
  2.2 3.1 %collective-permute-start = (bf16[128,2176]{1,0:T(8,128)(2,1)S(1)}, bf16[128,2176]{1,0:T(8,128)(2,1)S(1)}, u32[]{:S(2)}, u32[]{:S(2)}) collective-permute-start(bf16[128,2176]{1,0:T(8,128)(2,1)S(1)} %maximum_maximum_fusion), channel_id=1, source_target_pairs={{0,8},{8,16},{16,24},{1,9},{9,17},{17,25},{2,10},{10,18},{18,26},{... | collective-permute-start | bytes 1671176 | tf_op jit(solution)/shard_map/ppermute | solution.py:29
  5.3 0.0 copy-done.6
  5.4 0.0 copy-done.5
  5.5 1.3 %bitcast_select_fusion.2 = bf16[128,2048]{1,0:T(8,128)(2,1)S(1)} fusion(bf16[1,256,8192]{2,1,0:T(8,128)(2,1)} %refs_7_.5, pred[128]{0:T(512)(128)(4,1)S(1)} %add_compare_fusion), kind=kLoop, calls=%fused_computation.4 | loop fusion | flops 262144 | bytes 1572992 | tf_op jit(solution)/shard_map/jit(_where)/select_n | solution.py:259
  6.8 1.9 %collective-permute-start.2 = (bf16[128,2048]{1,0:T(8,128)(2,1)S(1)}, bf16[128,2048]{1,0:T(8,128)(2,1)S(1)}, u32[]{:S(2)}, u32[]{:S(2)}) collective-permute-start(bf16[128,2048]{1,0:T(8,128)(2,1)S(1)} %bitcast_select_fusion.2), channel_id=1, source_target_pairs={{0,8},{8,16},{16,24},{1,9},{9,17},{17,25},{2,10},{10,18},{18,26},{... | collective-permute-start | bytes 1572872 | tf_op jit(solution)/shard_map/ppermute | solution.py:29
  8.7 0.1 pad_add_fusion.shift_ref
  8.8 9.7 %collective-permute-done.arrived_ref = bf16[128,2176]{1,0:T(8,128)(2,1)S(1)} collective-permute-done((bf16[128,2176]{1,0:T(8,128)(2,1)S(1)}, bf16[128,2176]{1,0:T(8,128)(2,1)S(1)}, u32[]{:S(2)}, u32[]{:S(2)}) %collective-permute-start) | collective-permute-done | bytes 557088 | tf_op jit(solution)/shard_map/ppermute | solution.py:29
  18.5 0.0 copy-done.4
  18.5 0.9 %settle_kv.1 = (bf16[128,2176]{1,0:T(8,128)(2,1)S(1)}, bf16[128,256]{1,0:T(8,128)(2,1)S(1)}) custom-call(s32[2]{0:T(128)S(1)} %pad_add_fusion.shift_ref, s32[1,128]{1,0:T(1,128)S(1)} %copy-done.4, bf16[128,2176]{1,0:T(8,128)(2,1)S(1)} %collective-permute-done.arrived_ref, bf16[128,2048]{1,0:T(8,128)(2,1)S(1)} %pad_maximum_fusion.local_ref), custom_call_target="tpu_custom_call" | custom-call | tf_op jit(solution)/shard_map/settle_kv/pallas_call | solution.py:82
  19.4 3.2 %collective-permute-start.1 = (bf16[128,2176]{1,0:T(8,128)(2,1)S(1)}, bf16[128,2176]{1,0:T(8,128)(2,1)S(1)}, u32[]{:S(2)}, u32[]{:S(2)}) collective-permute-start(bf16[128,2176]{1,0:T(8,128)(2,1)S(1)} %get-tuple-element.19.refs_0_), channel_id=1, source_target_pairs={{0,2},{1,3},{2,4},{3,5},{4,6},{5,7},{8,10},{9,11},{10,12},{11,13},... | collective-permute-start | bytes 1671176 | tf_op jit(solution)/shard_map/ppermute | solution.py:29
  22.6 3.0 %bitcast_select_fusion = (bf16[128,3072]{1,0:T(8,128)(2,1)}, bf16[128,3072]{1,0:T(8,128)(2,1)S(1)}) fusion(bf16[1,256,8192]{2,1,0:T(8,128)(2,1)} %refs_7_.5, pred[128]{0:T(512)(128)(4,1)S(1)} %add_compare_fusion), kind=kLoop, calls=%fused_computation | loop fusion | flops 786432 | bytes 4718720 | tf_op jit(solution)/shard_map/jit(_where)/select_n | solution.py:259
  25.5 2.2 %collective-permute-start.5 = (bf16[128,3072]{1,0:T(8,128)(2,1)S(1)}, bf16[128,3072]{1,0:T(8,128)(2,1)S(1)}, u32[]{:S(2)}, u32[]{:S(2)}) collective-permute-start(bf16[128,3072]{1,0:T(8,128)(2,1)S(1)} %get-tuple-element.26), channel_id=1, source_target_pairs={{0,8},{8,16},{16,24},{1,9},{9,17},{17,25},{2,10},{10,18},{18,26},{... | collective-permute-start | bytes 2359304 | tf_op jit(solution)/shard_map/ppermute | solution.py:29
  27.8 2.0 %collective-permute-done.2.refs_6_ = bf16[128,2048]{1,0:T(8,128)(2,1)S(1)} collective-permute-done((bf16[128,2048]{1,0:T(8,128)(2,1)S(1)}, bf16[128,2048]{1,0:T(8,128)(2,1)S(1)}, u32[]{:S(2)}, u32[]{:S(2)}) %collective-permute-start.2) | collective-permute-done | bytes 524320 | tf_op jit(solution)/shard_map/ppermute | solution.py:29
  29.7 0.0 copy-start.2
  29.7 0.8 %copy-done.2 = bf16[128,2048]{1,0:T(8,128)(2,1)} copy-done((bf16[128,2048]{1,0:T(8,128)(2,1)}, bf16[128,2048]{1,0:T(8,128)(2,1)S(1)}, u32[]{:S(2)}) %copy-start.2) | copy-done | bytes 524312
  30.5 2.2 %collective-permute-done.1.refs_1_ = bf16[128,2176]{1,0:T(8,128)(2,1)S(1)} collective-permute-done((bf16[128,2176]{1,0:T(8,128)(2,1)S(1)}, bf16[128,2176]{1,0:T(8,128)(2,1)S(1)}, u32[]{:S(2)}, u32[]{:S(2)}) %collective-permute-start.1) | collective-permute-done | bytes 557088 | tf_op jit(solution)/shard_map/ppermute | solution.py:29
  32.7 3.2 %collective-permute-start.4 = (bf16[128,2176]{1,0:T(8,128)(2,1)S(1)}, bf16[128,2176]{1,0:T(8,128)(2,1)S(1)}, u32[]{:S(2)}, u32[]{:S(2)}) collective-permute-start(bf16[128,2176]{1,0:T(8,128)(2,1)S(1)} %collective-permute-done.1.refs_1_), channel_id=1, source_target_pairs={{0,2},{1,3},{2,4},{3,5},{4,6},{5,7},{8,10},{9,11},{10,12},{11,13},... | collective-permute-start | bytes 1671176 | tf_op jit(solution)/shard_map/ppermute | solution.py:29
  35.9 2.2 %collective-permute-start.8 = (bf16[128,3072]{1,0:T(8,128)(2,1)}, bf16[128,3072]{1,0:T(8,128)(2,1)}, u32[]{:S(2)}, u32[]{:S(2)}) collective-permute-start(bf16[128,3072]{1,0:T(8,128)(2,1)} %get-tuple-element.25), channel_id=1, source_target_pairs={{0,8},{8,16},{16,24},{1,9},{9,17},{17,25},{2,10},{10,18},{18,26},{... | collective-permute-start | bytes 2359304 | tf_op jit(solution)/shard_map/ppermute | solution.py:29
  38.1 1.3 %collective-permute-start.7 = (bf16[128,2176]{1,0:T(8,128)(2,1)S(1)}, bf16[128,2176]{1,0:T(8,128)(2,1)S(1)}, u32[]{:S(2)}, u32[]{:S(2)}) collective-permute-start(bf16[128,2176]{1,0:T(8,128)(2,1)S(1)} %get-tuple-element.19.refs_0_), channel_id=1, source_target_pairs={{0,1},{2,3},{4,5},{6,7},{8,9},{10,11},{12,13},{14,15},{16,17},{18,... | collective-permute-start | bytes 1671176 | tf_op jit(solution)/shard_map/ppermute | solution.py:34
  39.4 4.3 %collective-permute-start.3 = (bf16[128,2176]{1,0:T(8,128)(2,1)S(1)}, bf16[128,2176]{1,0:T(8,128)(2,1)S(1)}, u32[]{:S(2)}, u32[]{:S(2)}) collective-permute-start(bf16[128,2176]{1,0:T(8,128)(2,1)S(1)} %collective-permute-done.1.refs_1_), channel_id=1, source_target_pairs={{0,1},{1,0},{2,3},{3,2},{4,5},{5,4},{6,7},{7,6},{8,9},{9,8},{10,11... | collective-permute-start | bytes 1671176 | tf_op jit(solution)/shard_map/ppermute | solution.py:34
  43.7 0.7 collective-permute-done.5.refs_6_
  44.4 0.0 copy-start
  44.4 0.9 %copy-done = bf16[128,3072]{1,0:T(8,128)(2,1)} copy-done((bf16[128,3072]{1,0:T(8,128)(2,1)}, bf16[128,3072]{1,0:T(8,128)(2,1)S(1)}, u32[]{:S(2)}) %copy-start) | copy-done | bytes 786456
  45.3 0.0 collective-permute-done.4.refs_3_
  45.3 9.3 %collective-permute-start.6 = (bf16[128,2176]{1,0:T(8,128)(2,1)S(1)}, bf16[128,2176]{1,0:T(8,128)(2,1)S(1)}, u32[]{:S(2)}, u32[]{:S(2)}) collective-permute-start(bf16[128,2176]{1,0:T(8,128)(2,1)S(1)} %collective-permute-done.4.refs_3_), channel_id=1, source_target_pairs={{1,0},{3,2},{5,4},{7,6},{9,8},{11,10},{13,12},{15,14},{17,16},{19,... | collective-permute-start | bytes 1671176 | tf_op jit(solution)/shard_map/ppermute | solution.py:34
  54.6 0.0 collective-permute-done.7.refs_5_
  54.6 0.0 collective-permute-done.3.refs_2_
  54.6 1.5 %collective-permute-done.6.refs_4_ = bf16[128,2176]{1,0:T(8,128)(2,1)S(1)} collective-permute-done((bf16[128,2176]{1,0:T(8,128)(2,1)S(1)}, bf16[128,2176]{1,0:T(8,128)(2,1)S(1)}, u32[]{:S(2)}, u32[]{:S(2)}) %collective-permute-start.6) | collective-permute-done | bytes 557088 | tf_op jit(solution)/shard_map/ppermute | solution.py:34
  56.1 0.0 copy-start.3
  56.1 1.0 %copy-done.3 = bf16[128,2048]{1,0:T(8,128)(2,1)S(1)} copy-done((bf16[128,2048]{1,0:T(8,128)(2,1)S(1)}, bf16[128,2048]{1,0:T(8,128)(2,1)}, u32[]{:S(2)}) %copy-start.3) | copy-done | bytes 524312
  57.2 0.0 copy-start.1
  57.2 5.2 %attend_heads.3.refs_8_ = bf16[1,128,8192]{2,1,0:T(8,128)(2,1)} custom-call(s32[1]{0:T(128)} %bitcast.rank_ref, bf16[128,256]{1,0:T(8,128)(2,1)S(1)} %get-tuple-element.18.hot_ref, bf16[128,2176]{1,0:T(8,128)(2,1)S(1)} %get-tuple-element.19.refs_0_, bf16[128,2176]{1,0:T(8,128)(2,1)S(1)} %collective-permute-done.1.refs_1_, ...), custom_call_target="tpu_custom_call" | custom-call | tf_op jit(solution)/shard_map/attend_heads/pallas_call | solution.py:229
  62.4 0.0 copy-done.1
  62.4 6.7 %attend_heads.4.refs_8_ = bf16[1,128,8192]{2,1,0:T(8,128)(2,1)} custom-call(s32[1]{0:T(128)} %bitcast.rank_ref, bf16[128,256]{1,0:T(8,128)(2,1)S(1)} %get-tuple-element.18.hot_ref, bf16[128,2176]{1,0:T(8,128)(2,1)S(1)} %get-tuple-element.19.refs_0_, bf16[128,2176]{1,0:T(8,128)(2,1)S(1)} %collective-permute-done.1.refs_1_, ...), custom_call_target="tpu_custom_call", output_to_operand_aliasing={{}: (10, {})} | custom-call | tf_op jit(solution)/shard_map/attend_heads/pallas_call | solution.py:229
  69.1 0.0 collective-permute-done.8.refs_6_
  69.1 6.9 %attend_heads.5 = bf16[1,128,8192]{2,1,0:T(8,128)(2,1)} custom-call(s32[1]{0:T(128)} %bitcast.rank_ref, bf16[128,256]{1,0:T(8,128)(2,1)S(1)} %get-tuple-element.18.hot_ref, bf16[128,2176]{1,0:T(8,128)(2,1)S(1)} %get-tuple-element.19.refs_0_, bf16[128,2176]{1,0:T(8,128)(2,1)S(1)} %collective-permute-done.1.refs_1_, ...), custom_call_target="tpu_custom_call", output_to_operand_aliasing={{}: (10, {})} | custom-call | tf_op jit(solution)/shard_map/attend_heads/pallas_call | solution.py:229
  (5 shorter events, 0.1 us)
Async XLA Ops:
  0.0 5.3 %copy-start.6 = (bf16[1,256,1024]{2,1,0:T(8,128)(2,1)S(1)}, bf16[1,256,1024]{2,1,0:T(8,128)(2,1)}, u32[]{:S(2)}) copy-start(bf16[1,256,1024]{2,1,0:T(8,128)(2,1)} %param.7) | copy-start | bytes 1572868
  0.0 5.4 %copy-start.5 = (bf16[1,256,1024]{2,1,0:T(8,128)(2,1)S(1)}, bf16[1,256,1024]{2,1,0:T(8,128)(2,1)}, u32[]{:S(2)}) copy-start(bf16[1,256,1024]{2,1,0:T(8,128)(2,1)} %param.6) | copy-start | bytes 1572868
  2.2 16.3 %copy-start.4 = (s32[1,128]{1,0:T(1,128)S(1)}, s32[1,128]{1,0:T(1,128)}, u32[]{:S(2)}) copy-start(s32[1,128]{1,0:T(1,128)} %docs_ref.1) | copy-start | bytes 1540
  2.2 16.3 %collective-permute-start = (bf16[128,2176]{1,0:T(8,128)(2,1)S(1)}, bf16[128,2176]{1,0:T(8,128)(2,1)S(1)}, u32[]{:S(2)}, u32[]{:S(2)}) collective-permute-start(bf16[128,2176]{1,0:T(8,128)(2,1)S(1)} %maximum_maximum_fusion), channel_id=1, source_target_pairs={{0,8},{8,16},{16,24},{1,9},{9,17},{17,25},{2,10},{10,18},{18,26},{... | collective-permute-start | bytes 1671176 | tf_op jit(solution)/shard_map/ppermute | solution.py:29
  6.8 23.0 %collective-permute-start.2 = (bf16[128,2048]{1,0:T(8,128)(2,1)S(1)}, bf16[128,2048]{1,0:T(8,128)(2,1)S(1)}, u32[]{:S(2)}, u32[]{:S(2)}) collective-permute-start(bf16[128,2048]{1,0:T(8,128)(2,1)S(1)} %bitcast_select_fusion.2), channel_id=1, source_target_pairs={{0,8},{8,16},{16,24},{1,9},{9,17},{17,25},{2,10},{10,18},{18,26},{... | collective-permute-start | bytes 1572872 | tf_op jit(solution)/shard_map/ppermute | solution.py:29
  19.4 13.3 %collective-permute-start.1 = (bf16[128,2176]{1,0:T(8,128)(2,1)S(1)}, bf16[128,2176]{1,0:T(8,128)(2,1)S(1)}, u32[]{:S(2)}, u32[]{:S(2)}) collective-permute-start(bf16[128,2176]{1,0:T(8,128)(2,1)S(1)} %get-tuple-element.19.refs_0_), channel_id=1, source_target_pairs={{0,2},{1,3},{2,4},{3,5},{4,6},{5,7},{8,10},{9,11},{10,12},{11,13},... | collective-permute-start | bytes 1671176 | tf_op jit(solution)/shard_map/ppermute | solution.py:29
  25.5 18.8 %collective-permute-start.5 = (bf16[128,3072]{1,0:T(8,128)(2,1)S(1)}, bf16[128,3072]{1,0:T(8,128)(2,1)S(1)}, u32[]{:S(2)}, u32[]{:S(2)}) collective-permute-start(bf16[128,3072]{1,0:T(8,128)(2,1)S(1)} %get-tuple-element.26), channel_id=1, source_target_pairs={{0,8},{8,16},{16,24},{1,9},{9,17},{17,25},{2,10},{10,18},{18,26},{... | collective-permute-start | bytes 2359304 | tf_op jit(solution)/shard_map/ppermute | solution.py:29
  29.7 0.8 %copy-start.2 = (bf16[128,2048]{1,0:T(8,128)(2,1)}, bf16[128,2048]{1,0:T(8,128)(2,1)S(1)}, u32[]{:S(2)}) copy-start(bf16[128,2048]{1,0:T(8,128)(2,1)S(1)} %collective-permute-done.2.refs_6_) | copy-start | bytes 1572868
  32.7 12.6 %collective-permute-start.4 = (bf16[128,2176]{1,0:T(8,128)(2,1)S(1)}, bf16[128,2176]{1,0:T(8,128)(2,1)S(1)}, u32[]{:S(2)}, u32[]{:S(2)}) collective-permute-start(bf16[128,2176]{1,0:T(8,128)(2,1)S(1)} %collective-permute-done.1.refs_1_), channel_id=1, source_target_pairs={{0,2},{1,3},{2,4},{3,5},{4,6},{5,7},{8,10},{9,11},{10,12},{11,13},... | collective-permute-start | bytes 1671176 | tf_op jit(solution)/shard_map/ppermute | solution.py:29
  35.9 33.2 %collective-permute-start.8 = (bf16[128,3072]{1,0:T(8,128)(2,1)}, bf16[128,3072]{1,0:T(8,128)(2,1)}, u32[]{:S(2)}, u32[]{:S(2)}) collective-permute-start(bf16[128,3072]{1,0:T(8,128)(2,1)} %get-tuple-element.25), channel_id=1, source_target_pairs={{0,8},{8,16},{16,24},{1,9},{9,17},{17,25},{2,10},{10,18},{18,26},{... | collective-permute-start | bytes 2359304 | tf_op jit(solution)/shard_map/ppermute | solution.py:29
  38.1 16.5 %collective-permute-start.7 = (bf16[128,2176]{1,0:T(8,128)(2,1)S(1)}, bf16[128,2176]{1,0:T(8,128)(2,1)S(1)}, u32[]{:S(2)}, u32[]{:S(2)}) collective-permute-start(bf16[128,2176]{1,0:T(8,128)(2,1)S(1)} %get-tuple-element.19.refs_0_), channel_id=1, source_target_pairs={{0,1},{2,3},{4,5},{6,7},{8,9},{10,11},{12,13},{14,15},{16,17},{18,... | collective-permute-start | bytes 1671176 | tf_op jit(solution)/shard_map/ppermute | solution.py:34
  39.4 15.2 %collective-permute-start.3 = (bf16[128,2176]{1,0:T(8,128)(2,1)S(1)}, bf16[128,2176]{1,0:T(8,128)(2,1)S(1)}, u32[]{:S(2)}, u32[]{:S(2)}) collective-permute-start(bf16[128,2176]{1,0:T(8,128)(2,1)S(1)} %collective-permute-done.1.refs_1_), channel_id=1, source_target_pairs={{0,1},{1,0},{2,3},{3,2},{4,5},{5,4},{6,7},{7,6},{8,9},{9,8},{10,11... | collective-permute-start | bytes 1671176 | tf_op jit(solution)/shard_map/ppermute | solution.py:34
  44.4 0.9 %copy-start = (bf16[128,3072]{1,0:T(8,128)(2,1)}, bf16[128,3072]{1,0:T(8,128)(2,1)S(1)}, u32[]{:S(2)}) copy-start(bf16[128,3072]{1,0:T(8,128)(2,1)S(1)} %collective-permute-done.5.refs_6_) | copy-start | bytes 2359300
  45.3 10.9 %collective-permute-start.6 = (bf16[128,2176]{1,0:T(8,128)(2,1)S(1)}, bf16[128,2176]{1,0:T(8,128)(2,1)S(1)}, u32[]{:S(2)}, u32[]{:S(2)}) collective-permute-start(bf16[128,2176]{1,0:T(8,128)(2,1)S(1)} %collective-permute-done.4.refs_3_), channel_id=1, source_target_pairs={{1,0},{3,2},{5,4},{7,6},{9,8},{11,10},{13,12},{15,14},{17,16},{19,... | collective-permute-start | bytes 1671176 | tf_op jit(solution)/shard_map/ppermute | solution.py:34
  56.1 1.0 %copy-start.3 = (bf16[128,2048]{1,0:T(8,128)(2,1)S(1)}, bf16[128,2048]{1,0:T(8,128)(2,1)}, u32[]{:S(2)}) copy-start(bf16[128,2048]{1,0:T(8,128)(2,1)} %copy-done.2) | copy-start | bytes 1572868
  57.2 5.2 %copy-start.1 = (bf16[128,3072]{1,0:T(8,128)(2,1)S(1)}, bf16[128,3072]{1,0:T(8,128)(2,1)}, u32[]{:S(2)}) copy-start(bf16[128,3072]{1,0:T(8,128)(2,1)} %copy-done) | copy-start | bytes 2359300

commit v6 on v4

--- a/solution.py
+++ b/solution.py
@@ -18,8 +18,10 @@
 MASKED = -1e30
 CHUNKS = (2, 3, 3)
 PARTS = 2
+VMEM_GRANT = 48 * 1024 * 1024
 
 WHOLE = pl.BlockSpec(memory_space=pltpu.VMEM)
+ANYWHERE = pl.BlockSpec(memory_space=pl.ANY)
 SCALARS = pl.BlockSpec(memory_space=pltpu.SMEM)
 
 
@@ -86,7 +88,7 @@
             jax.ShapeDtypeStruct(arrived.shape, jnp.bfloat16),
             jax.ShapeDtypeStruct((quota, 2 * quota), jnp.bfloat16),
         ],
-        compiler_params=pltpu.CompilerParams(vmem_limit_bytes=24 * 1024 * 1024),
+        compiler_params=pltpu.CompilerParams(vmem_limit_bytes=VMEM_GRANT),
         name="settle_kv",
     )(shift, docs, arrived, local)
 
@@ -101,43 +103,91 @@
     return ranks
 
 
-def attend_kernel(blocks, first, count, rank_ref, hot_ref, arrived_ref, *refs):
-    kv_refs, far_ref, mate_ref, q_hbm = refs[: blocks - 1], *refs[blocks - 1 : blocks + 2]
-    out_hbm, local, result, bias, rest, q_sem, out_sems = refs[-7:]
-    quota = hot_ref.shape[0]
-    width = count * GROUP_WIDTH
-    start = first * GROUP_WIDTH
-    fetch = pltpu.make_async_copy(q_hbm.at[0, 0:quota, start : start + width], local, q_sem)
+def place_kernel(start, hot_ref, arrived_ref, local_hbm, *refs):
+    out_hbm, local, placed, in_sem, out_sems = refs[-5:]
+    quota, width = arrived_ref.shape
+    fetch = pltpu.make_async_copy(
+        local_hbm.at[0, 0:quota, start : start + width], local, in_sem
+    )
     fetch.start()
-
-    rank = rank_ref[0]
+    fetch.wait()
+    stores = []
+    for g in range(width // GROUP_WIDTH):
+        cols = slice(g * GROUP_WIDTH, (g + 1) * GROUP_WIDTH)
+        placed[:, cols] = place_rows(hot_ref[...], arrived_ref[:, cols], local[:, cols])
+        at = start + g * GROUP_WIDTH
+        store = pltpu.make_async_copy(
+            placed.at[:, cols], out_hbm.at[0, :, at : at + GROUP_WIDTH], out_sems.at[g]
+        )
+        store.start()
+        stores.append(store)
+    for store in stores:
+        store.wait()
+
+
+def place_queries(hot, arrived, q_rows, first, out):
+    quota, width = arrived.shape
+    in_specs = [WHOLE, WHOLE, ANYWHERE]
+    operands = [hot, arrived, q_rows]
+    aliases = {}
+    if out is not None:
+        aliases = {len(operands): 0}
+        in_specs.append(ANYWHERE)
+        operands.append(out)
+    return pl.pallas_call(
+        functools.partial(place_kernel, first * GROUP_WIDTH),
+        in_specs=in_specs,
+        out_specs=ANYWHERE,
+        out_shape=jax.ShapeDtypeStruct((1, quota, QUERY_HEADS * HEAD_SIZE), jnp.bfloat16),
+        input_output_aliases=aliases,
+        scratch_shapes=[
+            pltpu.VMEM((quota, width), jnp.bfloat16),
+            pltpu.VMEM((quota, width), jnp.bfloat16),
+            pltpu.SemaphoreType.DMA,
+            pltpu.SemaphoreType.DMA((width // GROUP_WIDTH,)),
+        ],
+        compiler_params=pltpu.CompilerParams(vmem_limit_bytes=VMEM_GRANT),
+        name="place_queries",
+    )(*operands)
+
+
+def make_bias(kv_refs, far_ref, mate_ref, bias, rank):
+    quota = bias.shape[0]
     core = lax.rem(rank, 2)
+    row = lax.broadcasted_iota(jnp.int32, (quota, quota), 0)
+    col = lax.broadcasted_iota(jnp.int32, (quota, quota), 1)
+    note = slice(NOTE, NOTE + quota)
+    q_docs = jnp.where(row == col, kv_refs[0][:, note].astype(jnp.float32), 0.0)
+    q_docs = jnp.sum(q_docs, axis=1, keepdims=True)
+    blocks = len(kv_refs) + 1
+    for b, block_rank in enumerate(block_ranks(rank, core, (blocks - 1) // 2)):
+        if b < blocks - 1:
+            docs = kv_refs[b][:, note].astype(jnp.float32)
+        else:
+            far = far_ref[:, note].astype(jnp.float32)
+            docs = jnp.where(core == 0, far, mate_ref[:, note].astype(jnp.float32))
+        allowed = docs == q_docs
+        allowed &= (col <= row) if b == 0 else (block_rank >= 0)
+        bias[:, b * quota : (b + 1) * quota] = jnp.where(allowed, 0.0, MASKED)
+
+
+def attend_heads(first, count, core, kv_refs, far_ref, mate_ref, bias, rest, take, result, put):
+    quota = bias.shape[0]
     parts = [(first + part) * HEAD_SIZE for part in (0, KEY_VALUE_HEADS)]
-    spans = [slice(at, at + count * HEAD_SIZE) for at in parts] + [slice(NOTE, NOTE + quota)]
 
     @pl.when(core == 0)
     def _():
-        for span in spans:
-            rest[:, span] = far_ref[:, span]
+        for at in parts:
+            rest[:, at : at + count * HEAD_SIZE] = far_ref[:, at : at + count * HEAD_SIZE]
 
     @pl.when(core == 1)
     def _():
-        for span in spans:
-            rest[:, span] = mate_ref[:, span]
+        for at in parts:
+            rest[:, at : at + count * HEAD_SIZE] = mate_ref[:, at : at + count * HEAD_SIZE]
 
     kv_refs = [*kv_refs, rest]
-    row = lax.broadcasted_iota(jnp.int32, (quota, quota), 0)
-    col = lax.broadcasted_iota(jnp.int32, (quota, quota), 1)
-    own_docs = kv_refs[0][:, NOTE:].astype(jnp.float32)
-    q_docs = jnp.sum(jnp.where(row == col, own_docs, 0.0), axis=1, keepdims=True)
-    for b, block_rank in enumerate(block_ranks(rank, core, (blocks - 1) // 2)):
-        allowed = kv_refs[b][:, NOTE:].astype(jnp.float32) == q_docs
-        allowed &= (col <= row) if b == 0 else (block_rank >= 0)
-        bias[:, b * quota : (b + 1) * quota] = jnp.where(allowed, 0.0, MASKED)
-
     unit = math.log2(math.e) / math.sqrt(HEAD_SIZE)
     heads = GROUP // PARTS
-    hot = hot_ref[...]
 
     def operands(g):
         at = (first + g) * HEAD_SIZE
@@ -145,9 +195,7 @@
         at += KV_WIDTH
         values = jnp.concatenate([r[:, at : at + HEAD_SIZE] for r in kv_refs], axis=0)
         values = jnp.concatenate([values, jnp.ones_like(values)], axis=1)
-        cols = slice(g * GROUP_WIDTH, (g + 1) * GROUP_WIDTH)
-        q = place_rows(hot, arrived_ref[:, cols], local[:, cols])
-        return q, keys, values
+        return take(g), keys, values
 
     def scored(q, keys, part):
         stacked = jnp.concatenate(
@@ -171,7 +219,6 @@
             at = g * GROUP_WIDTH + (part * heads + h) * HEAD_SIZE
             result[:, at : at + HEAD_SIZE] = mixed[h * quota : (h + 1) * quota]
 
-    fetch.wait()
     stores = []
     q, keys, values = operands(0)
     scores = scored(q, keys, 0)
@@ -185,47 +232,124 @@
         finished(scores, own_values, g, part)
         scores = later
         if part == PARTS - 1:
-            cols = slice(g * GROUP_WIDTH, (g + 1) * GROUP_WIDTH)
-            at = (first + g) * GROUP_WIDTH
-            store = pltpu.make_async_copy(
-                result.at[:, cols], out_hbm.at[0, :, at : at + GROUP_WIDTH], out_sems.at[g]
-            )
-            store.start()
-            stores.append(store)
+            stores.append(put(g))
     for store in stores:
         store.wait()
 
 
-def attend(rank, hot, arrived, q_rows, kv_blocks, first, count, out):
-    quota = arrived.shape[0]
+def head_columns(g, start=0):
+    return slice(start + g * GROUP_WIDTH, start + (g + 1) * GROUP_WIDTH)
+
+
+def putting(result, out_hbm, sems, start):
+    def put(g):
+        store = pltpu.make_async_copy(
+            result.at[:, head_columns(g)], out_hbm.at[0, :, head_columns(g, start)], sems.at[g]
+        )
+        store.start()
+        return store
+
+    return put
+
+
+def early_kernel(blocks, count, rank_ref, *refs):
+    kv_refs, far_ref, mate_ref = refs[: blocks - 1], refs[blocks - 1], refs[blocks]
+    q_hbm, in_hbm, out_hbm, bias, local = refs[blocks + 1 : blocks + 6]
+    queries, result, rest, q_sem, local_sem, out_sems = refs[blocks + 6 :]
+    quota = bias.shape[0]
+    start = count * GROUP_WIDTH
+    fetch = pltpu.make_async_copy(in_hbm.at[0, :, 0:start], queries, q_sem)
+    fetch.start()
+    ahead = pltpu.make_async_copy(q_hbm.at[0, 0:quota, start:], local, local_sem)
+    ahead.start()
+    make_bias(kv_refs, far_ref, mate_ref, bias, rank_ref[0])
+    fetch.wait()
+    attend_heads(
+        0,
+        count,
+        lax.rem(rank_ref[0], 2),
+        kv_refs,
+        far_ref,
+        mate_ref,
+        bias,
+        rest,
+        lambda g: queries[:, head_columns(g)],
+        result,
+        putting(result, out_hbm, out_sems, 0),
+    )
+    ahead.wait()
+
+
+def last_kernel(blocks, first, count, rank_ref, *refs):
+    kv_refs, far_ref, mate_ref = refs[: blocks - 1], refs[blocks - 1], refs[blocks]
+    hot_ref, arrived_ref, local_ref, bias, _, out_hbm = refs[blocks + 1 : blocks + 7]
+    result, rest, out_sems = refs[blocks + 7 :]
+
+    def take(g):
+        cols = head_columns(g)
+        return place_rows(hot_ref[...], arrived_ref[:, cols], local_ref[:, cols])
+
+    attend_heads(
+        first,
+        count,
+        lax.rem(rank_ref[0], 2),
+        kv_refs,
+        far_ref,
+        mate_ref,
+        bias,
+        rest,
+        take,
+        result,
+        putting(result, out_hbm, out_sems, first * GROUP_WIDTH),
+    )
+
+
+def attend(rank, hot, arrived, q_rows, kv_blocks, out):
+    quota, width = arrived.shape
     blocks = len(kv_blocks) - 1
-    width = count * GROUP_WIDTH
-    in_hbm = pl.BlockSpec(memory_space=pltpu.HBM)
-    in_specs = [SCALARS, WHOLE, WHOLE] + [WHOLE] * len(kv_blocks) + [in_hbm]
-    operands = [rank, hot, arrived, *kv_blocks, q_rows]
-    aliases = {}
-    if out is not None:
-        in_specs.append(in_hbm)
-        aliases = {len(operands): 0}
-        operands.append(out)
+    last = width // GROUP_WIDTH
+    early = KEY_VALUE_HEADS - last
+    whole_out = jax.ShapeDtypeStruct((1, quota, QUERY_HEADS * HEAD_SIZE), jnp.bfloat16)
+    rest = pltpu.VMEM((quota, NOTE), jnp.bfloat16)
+    hints = dict(
+        cost_estimate=pl.CostEstimate(flops=0, bytes_accessed=0, transcendentals=0),
+        compiler_params=pltpu.CompilerParams(vmem_limit_bytes=VMEM_GRANT),
+    )
+    out, bias, local = pl.pallas_call(
+        functools.partial(early_kernel, blocks, early),
+        in_specs=[SCALARS] + [WHOLE] * len(kv_blocks) + [ANYWHERE] * 2,
+        out_specs=[ANYWHERE, WHOLE, WHOLE],
+        out_shape=[
+            whole_out,
+            jax.ShapeDtypeStruct((quota, blocks * quota), jnp.float32),
+            jax.ShapeDtypeStruct((quota, width), jnp.bfloat16),
+        ],
+        input_output_aliases={len(kv_blocks) + 2: 0},
+        scratch_shapes=[
+            pltpu.VMEM((quota, early * GROUP_WIDTH), jnp.bfloat16),
+            pltpu.VMEM((quota, early * GROUP_WIDTH), jnp.bfloat16),
+            rest,
+            pltpu.SemaphoreType.DMA,
+            pltpu.SemaphoreType.DMA,
+            pltpu.SemaphoreType.DMA((early,)),
+        ],
+        name="attend_early",
+        **hints,
+    )(rank, *kv_blocks, q_rows, out)
     return pl.pallas_call(
-        functools.partial(attend_kernel, blocks, first, count),
-        in_specs=in_specs,
-        out_specs=in_hbm,
-        out_shape=jax.ShapeDtypeStruct((1, quota, QUERY_HEADS * HEAD_SIZE), jnp.bfloat16),
-        input_output_aliases=aliases,
+        functools.partial(last_kernel, blocks, early, last),
+        in_specs=[SCALARS] + [WHOLE] * (len(kv_blocks) + 4) + [ANYWHERE],
+        out_specs=ANYWHERE,
+        out_shape=whole_out,
+        input_output_aliases={len(kv_blocks) + 5: 0},
         scratch_shapes=[
             pltpu.VMEM((quota, width), jnp.bfloat16),
-            pltpu.VMEM((quota, width), jnp.bfloat16),
-            pltpu.VMEM((quota, blocks * quota), jnp.float32),
-            pltpu.VMEM((quota, NOTE + quota), jnp.bfloat16),
-            pltpu.SemaphoreType.DMA,
-            pltpu.SemaphoreType.DMA((count,)),
-        ],
-        cost_estimate=pl.CostEstimate(flops=0, bytes_accessed=0, transcendentals=0),
-        compiler_params=pltpu.CompilerParams(vmem_limit_bytes=24 * 1024 * 1024),
-        name="attend_heads",
-    )(*operands)
+            rest,
+            pltpu.SemaphoreType.DMA((last,)),
+        ],
+        name="attend_last",
+        **hints,
+    )(rank, *kv_blocks, hot, arrived, local, bias, out)
 
 
 def circular_tail(rows, later):
@@ -263,22 +387,18 @@
     own, hot = settle_kv(shift, doc_ids, arrived_kv, local_kv)
 
     kv_blocks = [own]
-    carried = own
+    carried, out = own, None
     for back in range(1, rounds + 1):
         carried = shifted(carried, "ctx", 2)
         kv_blocks.append(carried)
-        if back <= min(rounds, len(CHUNKS) - 1):
-            carried, arrived_q[back - 1] = lax.optimization_barrier((carried, arrived_q[back - 1]))
+        if back <= len(CHUNKS) - 1:
+            first = sum(CHUNKS[: back - 1])
+            out = place_queries(hot, arrived_q[back - 1], q_rows, first, out)
+            carried, out = lax.optimization_barrier((carried, out))
         if back < rounds:
             kv_blocks.append(across_cores(carried))
     kv_blocks += [across_cores(carried, (1,)), across_cores(own, (0,))]
-
-    out = None
-    first = 0
-    for size, arrived in zip(CHUNKS, arrived_q):
-        out = attend(rank[None], hot, arrived, q_rows, kv_blocks, first, size, out)
-        first += size
-    return out
+    return attend(rank[None], hot, arrived_q[-1], q_rows, kv_blocks, out)
 
 
 def solution(mesh):

time: 73.8 us -> 70.9 us (0.961)
  local copies, waits for them, and re-layouts: 4.96 us -> 0.07 us
  Pallas kernels: 14.6 us -> 16.6 us
    unnamed x16 -> x8, local copies, waits for them, and re-layouts: 4.91 us -> 0.02 us
    pallas_call x3 -> x4, Pallas kernels: 13.8 us -> 15.7 us  [the longest x1 7.75 us: attend(): pl.pallas_call(functools.partial(early_kernel, blocks, early), in_specs=[...]
  transfers between devices with their start and end apart: 9 -> 9, of which waited for: 5 -> 5; matrix products, arithmetic and copies ran while one was open for 6% -> 6% of each run, Pallas kernels for 12% -> 16%
where the time goes in v6:
time: 70.9 us; the launch traced here: 70.2 us
  starting transfers between devices  31 us (44%)
  Pallas kernels  16.6 us (23%)
  waiting for transfers between devices  15.7 us (22%)
  other arithmetic  5.8 us (8%)
  between operations  0.99 us (1%)
    ppermute x6, starting transfers between devices, shifted(): return lax.ppermute(x, axis, [(i, i + steps) for i in range(n - steps)])  16.1 us
    ppermute x3, starting transfers between devices, across_cores(): lax.ppermute(x, 'ctx', [(i, i ^ 1) for i in range(n) if i % 2 in sources])  14.9 us
    ppermute x6, waiting for transfers between devices, shifted(): return lax.ppermute(x, axis, [(i, i + steps) for i in range(n - steps)])  14.2 us
    pallas_call x1, Pallas kernels, attend(): pl.pallas_call(functools.partial(early_kernel, blocks, early), in_specs=[...  7.75 us
    pallas_call x1, Pallas kernels, attend(): pl.pallas_call(functools.partial(last_kernel, blocks, early, last), in_sp...  5.67 us
    select_n x3, other arithmetic, circular_tail(): return jnp.where(later[:, None], rows[quota:], rows[:quota])  5.59 us
    pallas_call x2, Pallas kernels, place_queries(): pl.pallas_call(functools.partial(place_kernel, first * GROUP_WIDTH), in_s...  2.3 us
    ppermute x3, waiting for transfers between devices, across_cores(): lax.ppermute(x, 'ctx', [(i, i ^ 1) for i in range(n) if i % 2 in sources])  1.51 us
  transfers between devices with their start and end apart: 9, of which 5 were waited for; matrix products, arithmetic and copies ran while one was open for 6% of the time, Pallas kernels for 16%

profile of v6, /device:TPU:21, one launch (start us, length us, event | category | flops | bytes accessed | tf_op | source)
XLA Modules:
  0.0 70.2 jit_solution(12830741165342765014)
XLA Ops:
  0.0 0.0 copy-start.3
  0.0 0.0 copy-start.2
  0.8 1.3 %bitcast_select_fusion.4 = (bf16[128,1024]{1,0:T(8,128)(2,1)S(1)}, bf16[128,1024]{1,0:T(8,128)(2,1)S(1)}) fusion(bf16[1,256,1024]{2,1,0:T(8,128)(2,1)} %param.6, pred[128]{0:T(512)(128)(4,1)S(1)} %add_compare_fusion, bf16[1,256,1024]{2,1,0:T(8,128)(2,1)} %param.7), kind=kLoop, calls=%fused_computation.6 | loop fusion | flops 262144 | bytes 1572992 | tf_op jit(solution)/shard_map/jit(_where)/select_n | solution.py:357
  2.1 0.1 maximum_maximum_fusion
  2.2 0.0 copy-start.1
  2.2 3.1 %collective-permute-start = (bf16[128,2176]{1,0:T(8,128)(2,1)S(1)}, bf16[128,2176]{1,0:T(8,128)(2,1)S(1)}, u32[]{:S(2)}, u32[]{:S(2)}) collective-permute-start(bf16[128,2176]{1,0:T(8,128)(2,1)S(1)} %maximum_maximum_fusion), channel_id=1, source_target_pairs={{0,8},{8,16},{16,24},{1,9},{9,17},{17,25},{2,10},{10,18},{18,26},{... | collective-permute-start | bytes 1671176 | tf_op jit(solution)/shard_map/ppermute | solution.py:30
  5.3 0.0 copy-done.3
  5.4 0.0 copy-done.2
  5.5 1.3 %bitcast_select_fusion.2 = bf16[128,2048]{1,0:T(8,128)(2,1)S(1)} fusion(bf16[1,256,8192]{2,1,0:T(8,128)(2,1)} %refs_6_.1, pred[128]{0:T(512)(128)(4,1)S(1)} %add_compare_fusion), kind=kLoop, calls=%fused_computation.4 | loop fusion | flops 262144 | bytes 1572992 | tf_op jit(solution)/shard_map/jit(_where)/select_n | solution.py:357
  6.8 1.9 %collective-permute-start.2 = (bf16[128,2048]{1,0:T(8,128)(2,1)S(1)}, bf16[128,2048]{1,0:T(8,128)(2,1)S(1)}, u32[]{:S(2)}, u32[]{:S(2)}) collective-permute-start(bf16[128,2048]{1,0:T(8,128)(2,1)S(1)} %bitcast_select_fusion.2), channel_id=1, source_target_pairs={{0,8},{8,16},{16,24},{1,9},{9,17},{17,25},{2,10},{10,18},{18,26},{... | collective-permute-start | bytes 1572872 | tf_op jit(solution)/shard_map/ppermute | solution.py:30
  8.7 0.1 pad_add_fusion.shift_ref
  8.8 9.7 %collective-permute-done.arrived_ref = bf16[128,2176]{1,0:T(8,128)(2,1)S(1)} collective-permute-done((bf16[128,2176]{1,0:T(8,128)(2,1)S(1)}, bf16[128,2176]{1,0:T(8,128)(2,1)S(1)}, u32[]{:S(2)}, u32[]{:S(2)}) %collective-permute-start) | collective-permute-done | bytes 557088 | tf_op jit(solution)/shard_map/ppermute | solution.py:30
  18.5 0.0 copy-done.1
  18.5 0.9 %settle_kv.1 = (bf16[128,2176]{1,0:T(8,128)(2,1)S(1)}, bf16[128,256]{1,0:T(8,128)(2,1)S(1)}) custom-call(s32[2]{0:T(128)S(1)} %pad_add_fusion.shift_ref, s32[1,128]{1,0:T(1,128)S(1)} %copy-done.1, bf16[128,2176]{1,0:T(8,128)(2,1)S(1)} %collective-permute-done.arrived_ref, bf16[128,2048]{1,0:T(8,128)(2,1)S(1)} %pad_maximum_fusion.local_ref), custom_call_target="tpu_custom_call" | custom-call | tf_op jit(solution)/shard_map/settle_kv/pallas_call | solution.py:83
  19.4 0.0 copy-start
  19.4 3.5 %collective-permute-start.1 = (bf16[128,2176]{1,0:T(8,128)(2,1)S(1)}, bf16[128,2176]{1,0:T(8,128)(2,1)S(1)}, u32[]{:S(2)}, u32[]{:S(2)}) collective-permute-start(bf16[128,2176]{1,0:T(8,128)(2,1)S(1)} %get-tuple-element.21.refs_0_), channel_id=1, source_target_pairs={{0,2},{1,3},{2,4},{3,5},{4,6},{5,7},{8,10},{9,11},{10,12},{11,13},... | collective-permute-start | bytes 1671176 | tf_op jit(solution)/shard_map/ppermute | solution.py:30
  22.9 3.0 %bitcast_select_fusion = (bf16[128,3072]{1,0:T(8,128)(2,1)}, bf16[128,3072]{1,0:T(8,128)(2,1)S(1)}) fusion(bf16[1,256,8192]{2,1,0:T(8,128)(2,1)} %refs_6_.1, pred[128]{0:T(512)(128)(4,1)S(1)} %add_compare_fusion), kind=kLoop, calls=%fused_computation | loop fusion | flops 786432 | bytes 4718720 | tf_op jit(solution)/shard_map/jit(_where)/select_n | solution.py:357
  25.8 2.2 %collective-permute-start.5 = (bf16[128,3072]{1,0:T(8,128)(2,1)S(1)}, bf16[128,3072]{1,0:T(8,128)(2,1)S(1)}, u32[]{:S(2)}, u32[]{:S(2)}) collective-permute-start(bf16[128,3072]{1,0:T(8,128)(2,1)S(1)} %get-tuple-element.32), channel_id=1, source_target_pairs={{0,8},{8,16},{16,24},{1,9},{9,17},{17,25},{2,10},{10,18},{18,26},{... | collective-permute-start | bytes 2359304 | tf_op jit(solution)/shard_map/ppermute | solution.py:30
  28.0 1.7 %collective-permute-done.2.arrived_ref = bf16[128,2048]{1,0:T(8,128)(2,1)S(1)} collective-permute-done((bf16[128,2048]{1,0:T(8,128)(2,1)S(1)}, bf16[128,2048]{1,0:T(8,128)(2,1)S(1)}, u32[]{:S(2)}, u32[]{:S(2)}) %collective-permute-start.2) | collective-permute-done | bytes 524320 | tf_op jit(solution)/shard_map/ppermute | solution.py:30
  29.7 0.0 copy-done
  29.7 1.1 %place_queries.2.refs_0_ = bf16[1,128,8192]{2,1,0:T(8,128)(2,1)} custom-call(bf16[128,256]{1,0:T(8,128)(2,1)S(1)} %get-tuple-element.22.hot_ref.refs_6_, bf16[128,2048]{1,0:T(8,128)(2,1)S(1)} %collective-permute-done.2.arrived_ref, bf16[1,256,8192]{2,1,0:T(8,128)(2,1)S(1)} %copy-done), custom_call_target="tpu_custom_call" | custom-call | tf_op jit(solution)/shard_map/place_queries/pallas_call | solution.py:137
  30.8 2.1 %collective-permute-done.1.refs_1_ = bf16[128,2176]{1,0:T(8,128)(2,1)S(1)} collective-permute-done((bf16[128,2176]{1,0:T(8,128)(2,1)S(1)}, bf16[128,2176]{1,0:T(8,128)(2,1)S(1)}, u32[]{:S(2)}, u32[]{:S(2)}) %collective-permute-start.1) | collective-permute-done | bytes 557088 | tf_op jit(solution)/shard_map/ppermute | solution.py:30
  33.0 3.2 %collective-permute-start.4 = (bf16[128,2176]{1,0:T(8,128)(2,1)S(1)}, bf16[128,2176]{1,0:T(8,128)(2,1)S(1)}, u32[]{:S(2)}, u32[]{:S(2)}) collective-permute-start(bf16[128,2176]{1,0:T(8,128)(2,1)S(1)} %collective-permute-done.1.refs_1_), channel_id=1, source_target_pairs={{0,2},{1,3},{2,4},{3,5},{4,6},{5,7},{8,10},{9,11},{10,12},{11,13},... | collective-permute-start | bytes 1671176 | tf_op jit(solution)/shard_map/ppermute | solution.py:30
  36.2 2.2 %collective-permute-start.8 = (bf16[128,3072]{1,0:T(8,128)(2,1)}, bf16[128,3072]{1,0:T(8,128)(2,1)}, u32[]{:S(2)}, u32[]{:S(2)}) collective-permute-start(bf16[128,3072]{1,0:T(8,128)(2,1)} %get-tuple-element.31), channel_id=1, source_target_pairs={{0,8},{8,16},{16,24},{1,9},{9,17},{17,25},{2,10},{10,18},{18,26},{... | collective-permute-start | bytes 2359304 | tf_op jit(solution)/shard_map/ppermute | solution.py:30
  38.4 1.3 %collective-permute-start.7 = (bf16[128,2176]{1,0:T(8,128)(2,1)S(1)}, bf16[128,2176]{1,0:T(8,128)(2,1)S(1)}, u32[]{:S(2)}, u32[]{:S(2)}) collective-permute-start(bf16[128,2176]{1,0:T(8,128)(2,1)S(1)} %get-tuple-element.21.refs_0_), channel_id=1, source_target_pairs={{0,1},{2,3},{4,5},{6,7},{8,9},{10,11},{12,13},{14,15},{16,17},{18,... | collective-permute-start | bytes 1671176 | tf_op jit(solution)/shard_map/ppermute | solution.py:35
  39.7 4.3 %collective-permute-start.3 = (bf16[128,2176]{1,0:T(8,128)(2,1)S(1)}, bf16[128,2176]{1,0:T(8,128)(2,1)S(1)}, u32[]{:S(2)}, u32[]{:S(2)}) collective-permute-start(bf16[128,2176]{1,0:T(8,128)(2,1)S(1)} %collective-permute-done.1.refs_1_), channel_id=1, source_target_pairs={{0,1},{1,0},{2,3},{3,2},{4,5},{5,4},{6,7},{7,6},{8,9},{9,8},{10,11... | collective-permute-start | bytes 1671176 | tf_op jit(solution)/shard_map/ppermute | solution.py:35
  44.0 0.7 collective-permute-done.5.arrived_ref
  44.7 1.2 %place_queries.3.refs_7_ = bf16[1,128,8192]{2,1,0:T(8,128)(2,1)} custom-call(bf16[128,256]{1,0:T(8,128)(2,1)S(1)} %get-tuple-element.22.hot_ref.refs_6_, bf16[128,3072]{1,0:T(8,128)(2,1)S(1)} %collective-permute-done.5.arrived_ref, bf16[1,256,8192]{2,1,0:T(8,128)(2,1)S(1)} %copy-done, ...), custom_call_target="tpu_custom_call", output_to_operand_aliasing={{}: (3, {})} | custom-call | tf_op jit(solution)/shard_map/place_queries/pallas_call | solution.py:137
  45.9 0.0 collective-permute-done.4.refs_3_
  45.9 9.3 %collective-permute-start.6 = (bf16[128,2176]{1,0:T(8,128)(2,1)S(1)}, bf16[128,2176]{1,0:T(8,128)(2,1)S(1)}, u32[]{:S(2)}, u32[]{:S(2)}) collective-permute-start(bf16[128,2176]{1,0:T(8,128)(2,1)S(1)} %collective-permute-done.4.refs_3_), channel_id=1, source_target_pairs={{1,0},{3,2},{5,4},{7,6},{9,8},{11,10},{13,12},{15,14},{17,16},{19,... | collective-permute-start | bytes 1671176 | tf_op jit(solution)/shard_map/ppermute | solution.py:35
  55.2 0.0 collective-permute-done.7.refs_5_
  55.3 0.0 collective-permute-done.3.refs_2_
  55.3 1.5 %collective-permute-done.6.refs_4_ = bf16[128,2176]{1,0:T(8,128)(2,1)S(1)} collective-permute-done((bf16[128,2176]{1,0:T(8,128)(2,1)S(1)}, bf16[128,2176]{1,0:T(8,128)(2,1)S(1)}, u32[]{:S(2)}, u32[]{:S(2)}) %collective-permute-start.6) | collective-permute-done | bytes 557088 | tf_op jit(solution)/shard_map/ppermute | solution.py:35
  56.8 7.8 %attend_early.1 = (bf16[1,128,8192]{2,1,0:T(8,128)(2,1)}, f32[128,640]{1,0:T(8,128)S(1)}, bf16[128,3072]{1,0:T(8,128)(2,1)S(1)}) custom-call(s32[1]{0:T(128)} %bitcast.rank_ref, bf16[128,2176]{1,0:T(8,128)(2,1)S(1)} %get-tuple-element.21.refs_0_, bf16[128,2176]{1,0:T(8,128)(2,1)S(1)} %collective-permute-done.1.refs_1_, ...), custom_call_target="tpu_custom_call", output_to_operand_aliasing={{0}: (8, {})} | custom-call | tf_op jit(solution)/shard_map/attend_early/pallas_call | solution.py:318
  64.5 0.0 collective-permute-done.8.refs_7_
  64.5 5.7 %attend_last.1 = bf16[1,128,8192]{2,1,0:T(8,128)(2,1)} custom-call(s32[1]{0:T(128)} %bitcast.rank_ref, bf16[128,2176]{1,0:T(8,128)(2,1)S(1)} %get-tuple-element.21.refs_0_, bf16[128,2176]{1,0:T(8,128)(2,1)S(1)} %collective-permute-done.1.refs_1_, bf16[128,2176]{1,0:T(8,128)(2,1)S(1)} %collective-permute-done.3.refs_2_, ...), custom_call_target="tpu_custom_call", output_to_operand_aliasing={{}: (11, {})} | custom-call | tf_op jit(solution)/shard_map/attend_last/pallas_call | solution.py:339
  (5 shorter events, 0.1 us)
Async XLA Ops:
  0.0 5.3 %copy-start.3 = (bf16[1,256,1024]{2,1,0:T(8,128)(2,1)S(1)}, bf16[1,256,1024]{2,1,0:T(8,128)(2,1)}, u32[]{:S(2)}) copy-start(bf16[1,256,1024]{2,1,0:T(8,128)(2,1)} %param.7) | copy-start | bytes 1572868
  0.0 5.4 %copy-start.2 = (bf16[1,256,1024]{2,1,0:T(8,128)(2,1)S(1)}, bf16[1,256,1024]{2,1,0:T(8,128)(2,1)}, u32[]{:S(2)}) copy-start(bf16[1,256,1024]{2,1,0:T(8,128)(2,1)} %param.6) | copy-start | bytes 1572868
  2.2 16.3 %copy-start.1 = (s32[1,128]{1,0:T(1,128)S(1)}, s32[1,128]{1,0:T(1,128)}, u32[]{:S(2)}) copy-start(s32[1,128]{1,0:T(1,128)} %docs_ref.1) | copy-start | bytes 1540
  2.2 16.3 %collective-permute-start = (bf16[128,2176]{1,0:T(8,128)(2,1)S(1)}, bf16[128,2176]{1,0:T(8,128)(2,1)S(1)}, u32[]{:S(2)}, u32[]{:S(2)}) collective-permute-start(bf16[128,2176]{1,0:T(8,128)(2,1)S(1)} %maximum_maximum_fusion), channel_id=1, source_target_pairs={{0,8},{8,16},{16,24},{1,9},{9,17},{17,25},{2,10},{10,18},{18,26},{... | collective-permute-start | bytes 1671176 | tf_op jit(solution)/shard_map/ppermute | solution.py:30
  6.8 23.0 %collective-permute-start.2 = (bf16[128,2048]{1,0:T(8,128)(2,1)S(1)}, bf16[128,2048]{1,0:T(8,128)(2,1)S(1)}, u32[]{:S(2)}, u32[]{:S(2)}) collective-permute-start(bf16[128,2048]{1,0:T(8,128)(2,1)S(1)} %bitcast_select_fusion.2), channel_id=1, source_target_pairs={{0,8},{8,16},{16,24},{1,9},{9,17},{17,25},{2,10},{10,18},{18,26},{... | collective-permute-start | bytes 1572872 | tf_op jit(solution)/shard_map/ppermute | solution.py:30
  19.4 10.4 %copy-start = (bf16[1,256,8192]{2,1,0:T(8,128)(2,1)S(1)}, bf16[1,256,8192]{2,1,0:T(8,128)(2,1)}, u32[]{:S(2)}) copy-start(bf16[1,256,8192]{2,1,0:T(8,128)(2,1)} %refs_6_.1) | copy-start | bytes 12582916
  19.4 13.6 %collective-permute-start.1 = (bf16[128,2176]{1,0:T(8,128)(2,1)S(1)}, bf16[128,2176]{1,0:T(8,128)(2,1)S(1)}, u32[]{:S(2)}, u32[]{:S(2)}) collective-permute-start(bf16[128,2176]{1,0:T(8,128)(2,1)S(1)} %get-tuple-element.21.refs_0_), channel_id=1, source_target_pairs={{0,2},{1,3},{2,4},{3,5},{4,6},{5,7},{8,10},{9,11},{10,12},{11,13},... | collective-permute-start | bytes 1671176 | tf_op jit(solution)/shard_map/ppermute | solution.py:30
  25.8 18.8 %collective-permute-start.5 = (bf16[128,3072]{1,0:T(8,128)(2,1)S(1)}, bf16[128,3072]{1,0:T(8,128)(2,1)S(1)}, u32[]{:S(2)}, u32[]{:S(2)}) collective-permute-start(bf16[128,3072]{1,0:T(8,128)(2,1)S(1)} %get-tuple-element.32), channel_id=1, source_target_pairs={{0,8},{8,16},{16,24},{1,9},{9,17},{17,25},{2,10},{10,18},{18,26},{... | collective-permute-start | bytes 2359304 | tf_op jit(solution)/shard_map/ppermute | solution.py:30
  33.0 12.9 %collective-permute-start.4 = (bf16[128,2176]{1,0:T(8,128)(2,1)S(1)}, bf16[128,2176]{1,0:T(8,128)(2,1)S(1)}, u32[]{:S(2)}, u32[]{:S(2)}) collective-permute-start(bf16[128,2176]{1,0:T(8,128)(2,1)S(1)} %collective-permute-done.1.refs_1_), channel_id=1, source_target_pairs={{0,2},{1,3},{2,4},{3,5},{4,6},{5,7},{8,10},{9,11},{10,12},{11,13},... | collective-permute-start | bytes 1671176 | tf_op jit(solution)/shard_map/ppermute | solution.py:30
  36.2 28.4 %collective-permute-start.8 = (bf16[128,3072]{1,0:T(8,128)(2,1)}, bf16[128,3072]{1,0:T(8,128)(2,1)}, u32[]{:S(2)}, u32[]{:S(2)}) collective-permute-start(bf16[128,3072]{1,0:T(8,128)(2,1)} %get-tuple-element.31), channel_id=1, source_target_pairs={{0,8},{8,16},{16,24},{1,9},{9,17},{17,25},{2,10},{10,18},{18,26},{... | collective-permute-start | bytes 2359304 | tf_op jit(solution)/shard_map/ppermute | solution.py:30
  38.4 16.8 %collective-permute-start.7 = (bf16[128,2176]{1,0:T(8,128)(2,1)S(1)}, bf16[128,2176]{1,0:T(8,128)(2,1)S(1)}, u32[]{:S(2)}, u32[]{:S(2)}) collective-permute-start(bf16[128,2176]{1,0:T(8,128)(2,1)S(1)} %get-tuple-element.21.refs_0_), channel_id=1, source_target_pairs={{0,1},{2,3},{4,5},{6,7},{8,9},{10,11},{12,13},{14,15},{16,17},{18,... | collective-permute-start | bytes 1671176 | tf_op jit(solution)/shard_map/ppermute | solution.py:35
  39.7 15.6 %collective-permute-start.3 = (bf16[128,2176]{1,0:T(8,128)(2,1)S(1)}, bf16[128,2176]{1,0:T(8,128)(2,1)S(1)}, u32[]{:S(2)}, u32[]{:S(2)}) collective-permute-start(bf16[128,2176]{1,0:T(8,128)(2,1)S(1)} %collective-permute-done.1.refs_1_), channel_id=1, source_target_pairs={{0,1},{1,0},{2,3},{3,2},{4,5},{5,4},{6,7},{7,6},{8,9},{9,8},{10,11... | collective-permute-start | bytes 1671176 | tf_op jit(solution)/shard_map/ppermute | solution.py:35
  45.9 10.9 %collective-permute-start.6 = (bf16[128,2176]{1,0:T(8,128)(2,1)S(1)}, bf16[128,2176]{1,0:T(8,128)(2,1)S(1)}, u32[]{:S(2)}, u32[]{:S(2)}) collective-permute-start(bf16[128,2176]{1,0:T(8,128)(2,1)S(1)} %collective-permute-done.4.refs_3_), channel_id=1, source_target_pairs={{1,0},{3,2},{5,4},{7,6},{9,8},{11,10},{13,12},{15,14},{17,16},{19,... | collective-permute-start | bytes 1671176 | tf_op jit(solution)/shard_map/ppermute | solution.py:35

commit v7 on v4

v7 whole, which is shorter than its diff:
```python
import functools
import math

import jax
import jax.numpy as jnp
from jax import lax
from jax.experimental import pallas as pl
from jax.experimental.pallas import tpu as pltpu
from jax.sharding import PartitionSpec as P

QUERY_HEADS = 64
KEY_VALUE_HEADS = 8
HEAD_SIZE = 128
GROUP = QUERY_HEADS // KEY_VALUE_HEADS
GROUP_WIDTH = GROUP * HEAD_SIZE
KV_WIDTH = KEY_VALUE_HEADS * HEAD_SIZE
NOTE = 2 * KV_WIDTH
MASKED = -1e30
HALF = GROUP // 2
HALF_WIDTH = HALF * HEAD_SIZE
CHUNKS = (6, 5, 5)
VMEM_GRANT = 48 * 1024 * 1024

WHOLE = pl.BlockSpec(memory_space=pltpu.VMEM)
ANYWHERE = pl.BlockSpec(memory_space=pl.ANY)
SCALARS = pl.BlockSpec(memory_space=pltpu.SMEM)


def shifted(x, axis, steps):
    n = lax.axis_size(axis)
    return lax.ppermute(x, axis, [(i, i + steps) for i in range(n - steps)])


def across_cores(x, sources=(0, 1)):
    n = lax.axis_size("ctx")
    return lax.ppermute(x, "ctx", [(i, i ^ 1) for i in range(n) if i % 2 in sources])


def everyones(x, axis):
    n = lax.axis_size(axis)
    spread = jnp.broadcast_to(x[None], (n,) + x.shape)
    return lax.all_to_all(spread, axis, split_axis=0, concat_axis=0)


def shift_in_known(own_count, quota):
    n = lax.axis_size("dp")
    replica = lax.axis_index("dp")
    if n > 4:
        all_counts = everyones(own_count[None], "dp")[:, 0]
        places = jnp.arange(n, dtype=jnp.int32)
        before = jnp.sum(jnp.where(places < replica, all_counts, 0))
        return jnp.stack([before - replica * quota, jnp.int32(0)])
    shift = jnp.where(own_count == 0, quota, 0)
    shift = jnp.where(replica == n - 1, quota - own_count, shift)
    shift = jnp.where(replica == 0, 0, shift)
    return jnp.stack([shift, (replica == 1).astype(jnp.int32)])


def place_rows(hot, arrived, local):
    both = jnp.concatenate([arrived, local], axis=0)
    return jnp.dot(hot, both, preferred_element_type=jnp.float32).astype(jnp.bfloat16)


def settle_kernel(shift_ref, docs_ref, arrived_ref, local_ref, out_ref, hot_ref):
    quota = out_ref.shape[0]
    count_before = arrived_ref[:, NOTE:].astype(jnp.float32).astype(jnp.int32)
    shift = jnp.where(shift_ref[1] == 1, count_before - quota, shift_ref[0])
    shift_before = shift - count_before + quota
    row = lax.broadcasted_iota(jnp.int32, (quota, quota), 0)
    col = lax.broadcasted_iota(jnp.int32, (quota, quota), 1)
    turned = row - shift_before
    turned = jnp.where(turned < 0, turned + quota, turned)
    hot_arrived = jnp.where((row < shift) & (col == turned), 1.0, 0.0)
    hot_local = jnp.where(col == row - shift, 1.0, 0.0)
    hot = jnp.concatenate([hot_arrived, hot_local], axis=1).astype(jnp.bfloat16)
    hot_ref[...] = hot
    out_ref[:, :NOTE] = place_rows(hot, arrived_ref[:, :NOTE], local_ref[...])
    docs = jnp.broadcast_to(docs_ref[...].astype(jnp.float32), (quota, quota))
    out_ref[:, NOTE:] = docs.astype(jnp.bfloat16)


def settle_kv(shift, docs, arrived, local):
    quota = arrived.shape[0]
    return pl.pallas_call(
        settle_kernel,
        in_specs=[SCALARS, WHOLE, WHOLE, WHOLE],
        out_specs=[WHOLE, WHOLE],
        out_shape=[
            jax.ShapeDtypeStruct(arrived.shape, jnp.bfloat16),
            jax.ShapeDtypeStruct((quota, 2 * quota), jnp.bfloat16),
        ],
        compiler_params=pltpu.CompilerParams(vmem_limit_bytes=VMEM_GRANT),
        name="settle_kv",
    )(shift, docs, arrived, local)


def block_ranks(rank, core, rounds):
    ranks = [rank]
    for back in range(1, rounds + 1):
        ranks.append(rank - 2 * back)
        if back < rounds:
            ranks.append(rank - 2 * back + jnp.where(core == 0, 1, -1))
    ranks.append(jnp.where(core == 0, rank - 2 * rounds + 1, rank - 1))
    return ranks


def half_columns(u, start=0):
    return slice((start + u) * HALF_WIDTH, (start + u + 1) * HALF_WIDTH)


def place_kernel(start, hot_ref, arrived_ref, local_hbm, *refs):
    out_hbm, local, placed, in_sem, out_sems = refs[-5:]
    quota, width = arrived_ref.shape
    at = start * HALF_WIDTH
    fetch = pltpu.make_async_copy(local_hbm.at[0, 0:quota, at : at + width], local, in_sem)
    fetch.start()
    fetch.wait()
    stores = []
    for u in range(width // HALF_WIDTH):
        cols = half_columns(u)
        placed[:, cols] = place_rows(hot_ref[...], arrived_ref[:, cols], local[:, cols])
        store = pltpu.make_async_copy(
            placed.at[:, cols], out_hbm.at[0, :, half_columns(u, start)], out_sems.at[u]
        )
        store.start()
        stores.append(store)
    for store in stores:
        store.wait()


def place_queries(hot, arrived, q_rows, first, out):
    quota, width = arrived.shape
    in_specs = [WHOLE, WHOLE, ANYWHERE]
    operands = [hot, arrived, q_rows]
    aliases = {}
    if out is not None:
        aliases = {len(operands): 0}
        in_specs.append(ANYWHERE)
        operands.append(out)
    return pl.pallas_call(
        functools.partial(place_kernel, first),
        in_specs=in_specs,
        out_specs=ANYWHERE,
        out_shape=jax.ShapeDtypeStruct((1, quota, QUERY_HEADS * HEAD_SIZE), jnp.bfloat16),
        input_output_aliases=aliases,
        scratch_shapes=[
            pltpu.VMEM((quota, width), jnp.bfloat16),
            pltpu.VMEM((quota, width), jnp.bfloat16),
            pltpu.SemaphoreType.DMA,
            pltpu.SemaphoreType.DMA((width // HALF_WIDTH,)),
        ],
        compiler_params=pltpu.CompilerParams(vmem_limit_bytes=VMEM_GRANT),
        name="place_queries",
    )(*operands)


def make_bias(kv_refs, far_ref, mate_ref, bias, rank):
    quota = bias.shape[0]
    core = lax.rem(rank, 2)
    row = lax.broadcasted_iota(jnp.int32, (quota, quota), 0)
    col = lax.broadcasted_iota(jnp.int32, (quota, quota), 1)
    note = slice(NOTE, NOTE + quota)
    q_docs = jnp.where(row == col, kv_refs[0][:, note].astype(jnp.float32), 0.0)
    q_docs = jnp.sum(q_docs, axis=1, keepdims=True)
    blocks = len(kv_refs) + 1
    for b, block_rank in enumerate(block_ranks(rank, core, (blocks - 1) // 2)):
        if b < blocks - 1:
            docs = kv_refs[b][:, note].astype(jnp.float32)
        else:
            far = far_ref[:, note].astype(jnp.float32)
            docs = jnp.where(core == 0, far, mate_ref[:, note].astype(jnp.float32))
        allowed = docs == q_docs
        allowed &= (col <= row) if b == 0 else (block_rank >= 0)
        bias[:, b * quota : (b + 1) * quota] = jnp.where(allowed, 0.0, MASKED)


def attend_kernel(blocks, first, count, late, rank_ref, *refs):
    kv_refs, far_ref, mate_ref = refs[: blocks - 1], refs[blocks - 1], refs[blocks]
    refs = refs[blocks + 1 :]
    if late:
        hot_ref, arrived_hbm, q_hbm, _, out_hbm, bias, rest, result, queries, local = refs[:10]
        sources = [
            lambda u: (arrived_hbm.at[:, half_columns(u)], queries),
            lambda u: (q_hbm.at[0, 0 : bias.shape[0], half_columns(u, first)], local),
        ]
    else:
        in_hbm, out_hbm, bias, rest, result, queries = refs[:6]
        sources = [lambda u: (in_hbm.at[0, :, half_columns(u, first)], queries)]
    in_sems, out_sems = refs[-2:]
    quota = bias.shape[0]
    fetches = []
    for u in range(count):
        fetches.append([])
        for i, source in enumerate(sources):
            origin, target = source(u)
            fetch = pltpu.make_async_copy(origin, target.at[:, half_columns(u)], in_sems.at[i, u])
            fetch.start()
            fetches[u].append(fetch)

    rank = rank_ref[0]
    core = lax.rem(rank, 2)
    make_bias(kv_refs, far_ref, mate_ref, bias, rank)
    first_head, last_head = first // 2, (first + count - 1) // 2
    parts = [(first_head + part) * HEAD_SIZE for part in (0, KEY_VALUE_HEADS)]
    spans = [slice(at, at + (last_head - first_head + 1) * HEAD_SIZE) for at in parts]

    @pl.when(core == 0)
    def _():
        for span in spans:
            rest[:, span] = far_ref[:, span]

    @pl.when(core == 1)
    def _():
        for span in spans:
            rest[:, span] = mate_ref[:, span]

    kv_refs = [*kv_refs, rest]
    unit = math.log2(math.e) / math.sqrt(HEAD_SIZE)

    def key_head(head):
        at = head * HEAD_SIZE
        keys = jnp.concatenate([r[:, at : at + HEAD_SIZE] for r in kv_refs], axis=0)
        at += KV_WIDTH
        values = jnp.concatenate([r[:, at : at + HEAD_SIZE] for r in kv_refs], axis=0)
        return keys, jnp.concatenate([values, jnp.ones_like(values)], axis=1)

    def scored(u, keys):
        for fetch in fetches[u]:
            fetch.wait()
        q = queries[:, half_columns(u)]
        if late:
            q = place_rows(hot_ref[...], q, local[:, half_columns(u)])
        stacked = jnp.concatenate(
            [q[:, h * HEAD_SIZE : (h + 1) * HEAD_SIZE] for h in range(HALF)], axis=0
        )
        return lax.dot_general(
            stacked, keys, (((1,), (1,)), ((), ())), preferred_element_type=jnp.float32
        )

    def finished(u, scores, values):
        scores = scores.reshape(HALF, quota, -1) * unit + bias[...][None]
        weights = jnp.exp2(scores - jnp.max(scores, axis=2, keepdims=True))
        weights = weights.astype(jnp.bfloat16).reshape(HALF * quota, -1)
        mixed = jnp.dot(weights, values, preferred_element_type=jnp.float32)
        totals = mixed[:, HEAD_SIZE:]
        inverse = pl.reciprocal(totals, approx=True)
        inverse = inverse * (2.0 - totals * inverse)
        mixed = (mixed[:, :HEAD_SIZE] * inverse).astype(jnp.bfloat16)
        for h in range(HALF):
            at = u * HALF_WIDTH + h * HEAD_SIZE
            result[:, at : at + HEAD_SIZE] = mixed[h * quota : (h + 1) * quota]
        store = pltpu.make_async_copy(
            result.at[:, half_columns(u)], out_hbm.at[0, :, half_columns(u, first)], out_sems.at[u]
        )
        store.start()
        return store

    stores = []
    keys, values = key_head(first_head)
    scores = scored(0, keys)
    for u in range(count):
        own_values, later = values, None
        if u + 1 < count:
            if (first + u + 1) % 2 == 0:
                keys, values = key_head((first + u + 1) // 2)
            later = scored(u + 1, keys)
        stores.append(finished(u, scores, own_values))
        scores = later
    for store in stores:
        store.wait()


def attend(rank, kv_blocks, late, out, first, count):
    quota = kv_blocks[0].shape[0]
    blocks = len(kv_blocks) - 1
    width = count * HALF_WIDTH
    columns = pltpu.VMEM((quota, width), jnp.bfloat16)
    sources = 2 if late else 1
    return pl.pallas_call(
        functools.partial(attend_kernel, blocks, first, count, bool(late)),
        in_specs=[SCALARS]
        + [WHOLE] * len(kv_blocks)
        + ([WHOLE, ANYWHERE, ANYWHERE] if late else [])
        + [ANYWHERE],
        out_specs=ANYWHERE,
        out_shape=jax.ShapeDtypeStruct((1, quota, QUERY_HEADS * HEAD_SIZE), jnp.bfloat16),
        input_output_aliases={1 + len(kv_blocks) + len(late): 0},
        scratch_shapes=[
            pltpu.VMEM((quota, blocks * quota), jnp.float32),
            pltpu.VMEM((quota, NOTE), jnp.bfloat16),
            columns,
            columns,
            *([columns] if late else []),
            pltpu.SemaphoreType.DMA((sources, count)),
            pltpu.SemaphoreType.DMA((count,)),
        ],
        cost_estimate=pl.CostEstimate(flops=0, bytes_accessed=0, transcendentals=0),
        compiler_params=pltpu.CompilerParams(vmem_limit_bytes=VMEM_GRANT),
        name="attend_late" if late else "attend_early",
    )(rank, *kv_blocks, *late, out)


def circular_tail(rows, later):
    quota = later.shape[0]
    return jnp.where(later[:, None], rows[quota:], rows[:quota])


def body(q_rows, k_rows, value_slot_rows, counts, doc_ids):
    quota = doc_ids.shape[1]
    rounds = lax.axis_size("ctx") // 4
    rank = lax.axis_index("ctx")
    own_count = counts[0, 0]

    later = quota + jnp.arange(quota, dtype=jnp.int32) < own_count
    kv_tail = jnp.concatenate(
        [
            circular_tail(k_rows[0], later),
            circular_tail(value_slot_rows[0], later),
            jnp.broadcast_to(own_count.astype(jnp.bfloat16), (quota, quota)),
        ],
        axis=1,
    )
    local_kv = jnp.concatenate([k_rows[0, :quota], value_slot_rows[0, :quota]], axis=1)
    kv_tail, later = lax.optimization_barrier((kv_tail, later))
    local_kv, later = lax.optimization_barrier((local_kv, later))
    arrived_kv = shifted(kv_tail, "dp", 1)
    arrived_q = []
    first = 0
    for size in CHUNKS:
        cols = slice(first * HALF_WIDTH, (first + size) * HALF_WIDTH)
        arrived_q.append(shifted(circular_tail(q_rows[0, :, cols], later), "dp", 1))
        first += size

    shift = shift_in_known(own_count, quota)
    own, hot = settle_kv(shift, doc_ids, arrived_kv, local_kv)

    kv_blocks = [own]
    carried, out = own, None
    for back in range(1, rounds + 1):
        carried = shifted(carried, "ctx", 2)
        kv_blocks.append(carried)
        if back <= len(CHUNKS) - 1:
            first = sum(CHUNKS[: back - 1])
            out = place_queries(hot, arrived_q[back - 1], q_rows, first, out)
            carried, out = lax.optimization_barrier((carried, out))
        if back < rounds:
            kv_blocks.append(across_cores(carried))
    kv_blocks += [across_cores(carried, (1,)), across_cores(own, (0,))]
    early, late = sum(CHUNKS[:-1]), CHUNKS[-1]
    out = attend(rank[None], kv_blocks, (), out, 0, early)
    return attend(rank[None], kv_blocks, (hot, arrived_q[-1], q_rows), out, early, late)


def solution(mesh):
    return jax.shard_map(
        body,
        mesh=mesh,
        in_specs=(
            P("dp", "ctx", None),
            P("dp", "ctx", None),
            P("dp", "ctx", None),
            P("dp", "ctx"),
            P("dp", "ctx"),
        ),
        out_specs=P("dp", "ctx", None),
        check_vma=False,
    )
```

time: 73.8 us -> 76.6 us (1.038)
  Pallas kernels: 14.6 us -> 21.1 us
  waiting for transfers between devices: 16 us -> 21.7 us
  starting transfers between devices: 30.8 us -> 25.7 us
  local copies, waits for them, and re-layouts: 4.96 us -> 0.06 us
  other arithmetic: 5.79 us -> 6.56 us
    pallas_call x3 -> x4, Pallas kernels: 13.8 us -> 20.3 us  [the longest x2 17.9 us: attend(): pl.pallas_call(functools.partial(attend_kernel, blocks, first, count, boo...]
    ppermute x6, waiting for transfers between devices: 14.5 us -> 20.1 us  [shifted(): return lax.ppermute(x, axis, [(i, i + steps) for i in range(n - steps)])]
    ppermute x3, starting transfers between devices: 14.9 us -> 9.53 us  [across_cores(): lax.ppermute(x, 'ctx', [(i, i ^ 1) for i in range(n) if i % 2 in sources])]
    unnamed x16 -> x8, local copies, waits for them, and re-layouts: 4.91 us -> 0.01 us
    concatenate x1, other arithmetic: 0.1 us -> 0.9 us  [body(): jnp.concatenate([circular_tail(k_rows[0], later), circular_tail(value_slo...]
  transfers between devices with their start and end apart: 9 -> 9, of which waited for: 5 -> 4; matrix products, arithmetic and copies ran while one was open for 6% -> 6% of each run, Pallas kernels for 12% -> 20%
where the time goes in v7:
time: 76.6 us; the launch traced here: 76.2 us
  starting transfers between devices  25.7 us (34%)
  waiting for transfers between devices  21.7 us (28%)
  Pallas kernels  21.1 us (28%)
  other arithmetic  6.56 us (9%)
  between operations  1.14 us (1%)
    ppermute x6, waiting for transfers between devices, shifted(): return lax.ppermute(x, axis, [(i, i + steps) for i in range(n - steps)])  20.1 us
    pallas_call x2, Pallas kernels, attend(): pl.pallas_call(functools.partial(attend_kernel, blocks, first, count, boo...  17.9 us
    ppermute x6, starting transfers between devices, shifted(): return lax.ppermute(x, axis, [(i, i + steps) for i in range(n - steps)])  16.1 us
    ppermute x3, starting transfers between devices, across_cores(): lax.ppermute(x, 'ctx', [(i, i ^ 1) for i in range(n) if i % 2 in sources])  9.53 us
    select_n x3, other arithmetic, circular_tail(): return jnp.where(later[:, None], rows[quota:], rows[:quota])  5.55 us
    pallas_call x2, Pallas kernels, place_queries(): pl.pallas_call(functools.partial(place_kernel, first), in_specs=in_specs,...  2.34 us
  transfers between devices with their start and end apart: 9, of which 4 were waited for; matrix products, arithmetic and copies ran while one was open for 6% of the time, Pallas kernels for 20%

profile of v7, /device:TPU:21, one launch (start us, length us, event | category | flops | bytes accessed | tf_op | source)
XLA Modules:
  0.0 76.2 jit_solution(14042880157458423411)
XLA Ops:
  0.0 0.0 copy-start.3
  0.0 0.0 copy-start.2
  0.8 1.3 %bitcast_select_fusion.4 = (bf16[128,1024]{1,0:T(8,128)(2,1)S(1)}, bf16[128,1024]{1,0:T(8,128)(2,1)S(1)}) fusion(bf16[1,256,1024]{2,1,0:T(8,128)(2,1)} %param.6, pred[128]{0:T(512)(128)(4,1)S(1)} %add_compare_fusion, bf16[1,256,1024]{2,1,0:T(8,128)(2,1)} %param.7), kind=kLoop, calls=%fused_computation.6 | loop fusion | flops 262144 | bytes 1572992 | tf_op jit(solution)/shard_map/jit(_where)/select_n | solution.py:305
  2.1 0.9 %maximum_maximum_fusion = bf16[128,2176]{1,0:T(8,128)(2,1)} fusion(bf16[128,1024]{1,0:T(8,128)(2,1)S(1)} %get-tuple-element.28, bf16[128,1024]{1,0:T(8,128)(2,1)S(1)} %get-tuple-element.27, bf16[2176]{0:T(1024)(128)(2,1)S(1)} %pad.4.clone), kind=kLoop, calls=%fused_computation.3 | loop fusion | flops 1671168 | bytes 1085696 | tf_op jit(solution)/shard_map/concatenate | solution.py:315
  3.0 0.0 copy-start.1
  3.0 3.2 %collective-permute-start = (bf16[128,2176]{1,0:T(8,128)(2,1)}, bf16[128,2176]{1,0:T(8,128)(2,1)S(1)}, u32[]{:S(2)}, u32[]{:S(2)}) collective-permute-start(bf16[128,2176]{1,0:T(8,128)(2,1)} %maximum_maximum_fusion), channel_id=1, source_target_pairs={{0,8},{8,16},{16,24},{1,9},{9,17},{17,25},{2,10},{10,18},{18,26},{... | collective-permute-start | bytes 1671176 | tf_op jit(solution)/shard_map/ppermute | solution.py:31
  6.3 0.0 copy-done.3
  6.3 0.0 copy-done.2
  6.4 1.5 %bitcast_select_fusion = bf16[128,3072]{1,0:T(8,128)(2,1)S(1)} fusion(bf16[1,256,8192]{2,1,0:T(8,128)(2,1)} %refs_8_.1, pred[128]{0:T(512)(128)(4,1)S(1)} %add_compare_fusion), kind=kLoop, calls=%fused_computation | loop fusion | flops 393216 | bytes 2359424 | tf_op jit(solution)/shard_map/jit(_where)/select_n | solution.py:305
  7.9 1.9 %collective-permute-start.2 = (bf16[128,3072]{1,0:T(8,128)(2,1)S(1)}, bf16[128,3072]{1,0:T(8,128)(2,1)S(1)}, u32[]{:S(2)}, u32[]{:S(2)}) collective-permute-start(bf16[128,3072]{1,0:T(8,128)(2,1)S(1)} %bitcast_select_fusion), channel_id=1, source_target_pairs={{0,8},{8,16},{16,24},{1,9},{9,17},{17,25},{2,10},{10,18},{18,26},{... | collective-permute-start | bytes 2359304 | tf_op jit(solution)/shard_map/ppermute | solution.py:31
  9.8 0.1 pad_add_fusion.shift_ref
  9.9 9.7 %collective-permute-done.arrived_ref = bf16[128,2176]{1,0:T(8,128)(2,1)S(1)} collective-permute-done((bf16[128,2176]{1,0:T(8,128)(2,1)}, bf16[128,2176]{1,0:T(8,128)(2,1)S(1)}, u32[]{:S(2)}, u32[]{:S(2)}) %collective-permute-start) | collective-permute-done | bytes 557088 | tf_op jit(solution)/shard_map/ppermute | solution.py:31
  19.6 0.0 copy-done.1
  19.6 0.0 copy-start
  19.6 0.9 %settle_kv.1 = (bf16[128,2176]{1,0:T(8,128)(2,1)S(1)}, bf16[128,256]{1,0:T(8,128)(2,1)S(1)}) custom-call(s32[2]{0:T(128)S(1)} %pad_add_fusion.shift_ref, s32[1,128]{1,0:T(1,128)S(1)} %copy-done.1, bf16[128,2176]{1,0:T(8,128)(2,1)S(1)} %collective-permute-done.arrived_ref, bf16[128,2048]{1,0:T(8,128)(2,1)S(1)} %pad_maximum_fusion.local_ref), custom_call_target="tpu_custom_call" | custom-call | tf_op jit(solution)/shard_map/settle_kv/pallas_call | solution.py:84
  20.5 3.3 %collective-permute-start.1 = (bf16[128,2176]{1,0:T(8,128)(2,1)S(1)}, bf16[128,2176]{1,0:T(8,128)(2,1)S(1)}, u32[]{:S(2)}, u32[]{:S(2)}) collective-permute-start(bf16[128,2176]{1,0:T(8,128)(2,1)S(1)} %get-tuple-element.18.refs_0_), channel_id=1, source_target_pairs={{0,2},{1,3},{2,4},{3,5},{4,6},{5,7},{8,10},{9,11},{10,12},{11,13},... | collective-permute-start | bytes 1671176 | tf_op jit(solution)/shard_map/ppermute | solution.py:31
  23.8 2.7 %bitcast_select_fusion.1 = (bf16[128,2560]{1,0:T(8,128)(2,1)}, bf16[128,2560]{1,0:T(8,128)(2,1)S(1)}) fusion(bf16[1,256,8192]{2,1,0:T(8,128)(2,1)} %refs_8_.1, pred[128]{0:T(512)(128)(4,1)S(1)} %add_compare_fusion), kind=kLoop, calls=%fused_computation.1 | loop fusion | flops 655360 | bytes 3932288 | tf_op jit(solution)/shard_map/jit(_where)/select_n | solution.py:305
  26.6 2.2 %collective-permute-start.5 = (bf16[128,2560]{1,0:T(8,128)(2,1)S(1)}, bf16[128,2560]{1,0:T(8,128)(2,1)S(1)}, u32[]{:S(2)}, u32[]{:S(2)}) collective-permute-start(bf16[128,2560]{1,0:T(8,128)(2,1)S(1)} %get-tuple-element.26), channel_id=1, source_target_pairs={{0,8},{8,16},{16,24},{1,9},{9,17},{17,25},{2,10},{10,18},{18,26},{... | collective-permute-start | bytes 1966088 | tf_op jit(solution)/shard_map/ppermute | solution.py:31
  28.8 7.7 %collective-permute-done.2.arrived_ref = bf16[128,3072]{1,0:T(8,128)(2,1)S(1)} collective-permute-done((bf16[128,3072]{1,0:T(8,128)(2,1)S(1)}, bf16[128,3072]{1,0:T(8,128)(2,1)S(1)}, u32[]{:S(2)}, u32[]{:S(2)}) %collective-permute-start.2) | collective-permute-done | bytes 786464 | tf_op jit(solution)/shard_map/ppermute | solution.py:31
  36.5 0.0 copy-done
  36.5 1.2 %place_queries.2.refs_0_ = bf16[1,128,8192]{2,1,0:T(8,128)(2,1)} custom-call(bf16[128,256]{1,0:T(8,128)(2,1)S(1)} %get-tuple-element.19.hot_ref.refs_6_, bf16[128,3072]{1,0:T(8,128)(2,1)S(1)} %collective-permute-done.2.arrived_ref, bf16[1,256,8192]{2,1,0:T(8,128)(2,1)S(1)} %copy-done), custom_call_target="tpu_custom_call" | custom-call | tf_op jit(solution)/shard_map/place_queries/pallas_call | solution.py:140
  37.7 0.0 collective-permute-done.1.refs_1_
  37.7 3.2 %collective-permute-start.4 = (bf16[128,2176]{1,0:T(8,128)(2,1)S(1)}, bf16[128,2176]{1,0:T(8,128)(2,1)S(1)}, u32[]{:S(2)}, u32[]{:S(2)}) collective-permute-start(bf16[128,2176]{1,0:T(8,128)(2,1)S(1)} %collective-permute-done.1.refs_1_), channel_id=1, source_target_pairs={{0,2},{1,3},{2,4},{3,5},{4,6},{5,7},{8,10},{9,11},{10,12},{11,13},... | collective-permute-start | bytes 1671176 | tf_op jit(solution)/shard_map/ppermute | solution.py:31
  40.9 2.2 %collective-permute-start.8 = (bf16[128,2560]{1,0:T(8,128)(2,1)}, bf16[128,2560]{1,0:T(8,128)(2,1)}, u32[]{:S(2)}, u32[]{:S(2)}) collective-permute-start(bf16[128,2560]{1,0:T(8,128)(2,1)} %get-tuple-element.25), channel_id=1, source_target_pairs={{0,8},{8,16},{16,24},{1,9},{9,17},{17,25},{2,10},{10,18},{18,26},{... | collective-permute-start | bytes 1966088 | tf_op jit(solution)/shard_map/ppermute | solution.py:31
  43.1 1.3 %collective-permute-start.7 = (bf16[128,2176]{1,0:T(8,128)(2,1)S(1)}, bf16[128,2176]{1,0:T(8,128)(2,1)S(1)}, u32[]{:S(2)}, u32[]{:S(2)}) collective-permute-start(bf16[128,2176]{1,0:T(8,128)(2,1)S(1)} %get-tuple-element.18.refs_0_), channel_id=1, source_target_pairs={{0,1},{2,3},{4,5},{6,7},{8,9},{10,11},{12,13},{14,15},{16,17},{18,... | collective-permute-start | bytes 1671176 | tf_op jit(solution)/shard_map/ppermute | solution.py:36
  44.4 3.4 %collective-permute-start.3 = (bf16[128,2176]{1,0:T(8,128)(2,1)S(1)}, bf16[128,2176]{1,0:T(8,128)(2,1)S(1)}, u32[]{:S(2)}, u32[]{:S(2)}) collective-permute-start(bf16[128,2176]{1,0:T(8,128)(2,1)S(1)} %collective-permute-done.1.refs_1_), channel_id=1, source_target_pairs={{0,1},{1,0},{2,3},{3,2},{4,5},{5,4},{6,7},{7,6},{8,9},{9,8},{10,11... | collective-permute-start | bytes 1671176 | tf_op jit(solution)/shard_map/ppermute | solution.py:36
  47.8 2.7 %collective-permute-done.5.arrived_ref = bf16[128,2560]{1,0:T(8,128)(2,1)S(1)} collective-permute-done((bf16[128,2560]{1,0:T(8,128)(2,1)S(1)}, bf16[128,2560]{1,0:T(8,128)(2,1)S(1)}, u32[]{:S(2)}, u32[]{:S(2)}) %collective-permute-start.5) | collective-permute-done | bytes 655392 | tf_op jit(solution)/shard_map/ppermute | solution.py:31
  50.5 1.1 %place_queries.3.refs_6_ = bf16[1,128,8192]{2,1,0:T(8,128)(2,1)} custom-call(bf16[128,256]{1,0:T(8,128)(2,1)S(1)} %get-tuple-element.19.hot_ref.refs_6_, bf16[128,2560]{1,0:T(8,128)(2,1)S(1)} %collective-permute-done.5.arrived_ref, bf16[1,256,8192]{2,1,0:T(8,128)(2,1)S(1)} %copy-done, ...), custom_call_target="tpu_custom_call", output_to_operand_aliasing={{}: (3, {})} | custom-call | tf_op jit(solution)/shard_map/place_queries/pallas_call | solution.py:140
  51.7 0.0 collective-permute-done.4.refs_3_
  51.7 4.9 %collective-permute-start.6 = (bf16[128,2176]{1,0:T(8,128)(2,1)S(1)}, bf16[128,2176]{1,0:T(8,128)(2,1)S(1)}, u32[]{:S(2)}, u32[]{:S(2)}) collective-permute-start(bf16[128,2176]{1,0:T(8,128)(2,1)S(1)} %collective-permute-done.4.refs_3_), channel_id=1, source_target_pairs={{1,0},{3,2},{5,4},{7,6},{9,8},{11,10},{13,12},{15,14},{17,16},{19,... | collective-permute-start | bytes 1671176 | tf_op jit(solution)/shard_map/ppermute | solution.py:36
  56.6 0.0 collective-permute-done.7.refs_5_
  56.6 0.0 collective-permute-done.3.refs_2_
  56.6 1.5 %collective-permute-done.6.refs_4_ = bf16[128,2176]{1,0:T(8,128)(2,1)S(1)} collective-permute-done((bf16[128,2176]{1,0:T(8,128)(2,1)S(1)}, bf16[128,2176]{1,0:T(8,128)(2,1)S(1)}, u32[]{:S(2)}, u32[]{:S(2)}) %collective-permute-start.6) | collective-permute-done | bytes 557088 | tf_op jit(solution)/shard_map/ppermute | solution.py:36
  58.1 11.8 %attend_early.1.refs_9_ = bf16[1,128,8192]{2,1,0:T(8,128)(2,1)} custom-call(s32[1]{0:T(128)} %bitcast.rank_ref, bf16[128,2176]{1,0:T(8,128)(2,1)S(1)} %get-tuple-element.18.refs_0_, bf16[128,2176]{1,0:T(8,128)(2,1)S(1)} %collective-permute-done.1.refs_1_, bf16[128,2176]{1,0:T(8,128)(2,1)S(1)} %collective-permute-done.3.refs_2_, ...), custom_call_target="tpu_custom_call", output_to_operand_aliasing={{}: (7, {})} | custom-call | tf_op jit(solution)/shard_map/attend_early/pallas_call | solution.py:279
  69.9 0.0 collective-permute-done.8.refs_7_
  69.9 6.2 %attend_late.1 = bf16[1,128,8192]{2,1,0:T(8,128)(2,1)} custom-call(s32[1]{0:T(128)} %bitcast.rank_ref, bf16[128,2176]{1,0:T(8,128)(2,1)S(1)} %get-tuple-element.18.refs_0_, bf16[128,2176]{1,0:T(8,128)(2,1)S(1)} %collective-permute-done.1.refs_1_, bf16[128,2176]{1,0:T(8,128)(2,1)S(1)} %collective-permute-done.3.refs_2_, ...), custom_call_target="tpu_custom_call", output_to_operand_aliasing={{}: (10, {})} | custom-call | tf_op jit(solution)/shard_map/attend_late/pallas_call | solution.py:279
  (5 shorter events, 0.1 us)
Async XLA Ops:
  0.0 6.3 %copy-start.3 = (bf16[1,256,1024]{2,1,0:T(8,128)(2,1)S(1)}, bf16[1,256,1024]{2,1,0:T(8,128)(2,1)}, u32[]{:S(2)}) copy-start(bf16[1,256,1024]{2,1,0:T(8,128)(2,1)} %param.7) | copy-start | bytes 1572868
  0.0 6.3 %copy-start.2 = (bf16[1,256,1024]{2,1,0:T(8,128)(2,1)S(1)}, bf16[1,256,1024]{2,1,0:T(8,128)(2,1)}, u32[]{:S(2)}) copy-start(bf16[1,256,1024]{2,1,0:T(8,128)(2,1)} %param.6) | copy-start | bytes 1572868
  3.0 16.6 %copy-start.1 = (s32[1,128]{1,0:T(1,128)S(1)}, s32[1,128]{1,0:T(1,128)}, u32[]{:S(2)}) copy-start(s32[1,128]{1,0:T(1,128)} %docs_ref.1) | copy-start | bytes 1540
  3.0 16.6 %collective-permute-start = (bf16[128,2176]{1,0:T(8,128)(2,1)}, bf16[128,2176]{1,0:T(8,128)(2,1)S(1)}, u32[]{:S(2)}, u32[]{:S(2)}) collective-permute-start(bf16[128,2176]{1,0:T(8,128)(2,1)} %maximum_maximum_fusion), channel_id=1, source_target_pairs={{0,8},{8,16},{16,24},{1,9},{9,17},{17,25},{2,10},{10,18},{18,26},{... | collective-permute-start | bytes 1671176 | tf_op jit(solution)/shard_map/ppermute | solution.py:31
  7.9 28.6 %collective-permute-start.2 = (bf16[128,3072]{1,0:T(8,128)(2,1)S(1)}, bf16[128,3072]{1,0:T(8,128)(2,1)S(1)}, u32[]{:S(2)}, u32[]{:S(2)}) collective-permute-start(bf16[128,3072]{1,0:T(8,128)(2,1)S(1)} %bitcast_select_fusion), channel_id=1, source_target_pairs={{0,8},{8,16},{16,24},{1,9},{9,17},{17,25},{2,10},{10,18},{18,26},{... | collective-permute-start | bytes 2359304 | tf_op jit(solution)/shard_map/ppermute | solution.py:31
  19.6 16.9 %copy-start = (bf16[1,256,8192]{2,1,0:T(8,128)(2,1)S(1)}, bf16[1,256,8192]{2,1,0:T(8,128)(2,1)}, u32[]{:S(2)}) copy-start(bf16[1,256,8192]{2,1,0:T(8,128)(2,1)} %refs_8_.1) | copy-start | bytes 12582916
  20.5 17.2 %collective-permute-start.1 = (bf16[128,2176]{1,0:T(8,128)(2,1)S(1)}, bf16[128,2176]{1,0:T(8,128)(2,1)S(1)}, u32[]{:S(2)}, u32[]{:S(2)}) collective-permute-start(bf16[128,2176]{1,0:T(8,128)(2,1)S(1)} %get-tuple-element.18.refs_0_), channel_id=1, source_target_pairs={{0,2},{1,3},{2,4},{3,5},{4,6},{5,7},{8,10},{9,11},{10,12},{11,13},... | collective-permute-start | bytes 1671176 | tf_op jit(solution)/shard_map/ppermute | solution.py:31
  26.6 24.0 %collective-permute-start.5 = (bf16[128,2560]{1,0:T(8,128)(2,1)S(1)}, bf16[128,2560]{1,0:T(8,128)(2,1)S(1)}, u32[]{:S(2)}, u32[]{:S(2)}) collective-permute-start(bf16[128,2560]{1,0:T(8,128)(2,1)S(1)} %get-tuple-element.26), channel_id=1, source_target_pairs={{0,8},{8,16},{16,24},{1,9},{9,17},{17,25},{2,10},{10,18},{18,26},{... | collective-permute-start | bytes 1966088 | tf_op jit(solution)/shard_map/ppermute | solution.py:31
  37.7 14.0 %collective-permute-start.4 = (bf16[128,2176]{1,0:T(8,128)(2,1)S(1)}, bf16[128,2176]{1,0:T(8,128)(2,1)S(1)}, u32[]{:S(2)}, u32[]{:S(2)}) collective-permute-start(bf16[128,2176]{1,0:T(8,128)(2,1)S(1)} %collective-permute-done.1.refs_1_), channel_id=1, source_target_pairs={{0,2},{1,3},{2,4},{3,5},{4,6},{5,7},{8,10},{9,11},{10,12},{11,13},... | collective-permute-start | bytes 1671176 | tf_op jit(solution)/shard_map/ppermute | solution.py:31
  40.9 29.0 %collective-permute-start.8 = (bf16[128,2560]{1,0:T(8,128)(2,1)}, bf16[128,2560]{1,0:T(8,128)(2,1)}, u32[]{:S(2)}, u32[]{:S(2)}) collective-permute-start(bf16[128,2560]{1,0:T(8,128)(2,1)} %get-tuple-element.25), channel_id=1, source_target_pairs={{0,8},{8,16},{16,24},{1,9},{9,17},{17,25},{2,10},{10,18},{18,26},{... | collective-permute-start | bytes 1966088 | tf_op jit(solution)/shard_map/ppermute | solution.py:31
  43.1 13.4 %collective-permute-start.7 = (bf16[128,2176]{1,0:T(8,128)(2,1)S(1)}, bf16[128,2176]{1,0:T(8,128)(2,1)S(1)}, u32[]{:S(2)}, u32[]{:S(2)}) collective-permute-start(bf16[128,2176]{1,0:T(8,128)(2,1)S(1)} %get-tuple-element.18.refs_0_), channel_id=1, source_target_pairs={{0,1},{2,3},{4,5},{6,7},{8,9},{10,11},{12,13},{14,15},{16,17},{18,... | collective-permute-start | bytes 1671176 | tf_op jit(solution)/shard_map/ppermute | solution.py:36
  44.4 12.1 %collective-permute-start.3 = (bf16[128,2176]{1,0:T(8,128)(2,1)S(1)}, bf16[128,2176]{1,0:T(8,128)(2,1)S(1)}, u32[]{:S(2)}, u32[]{:S(2)}) collective-permute-start(bf16[128,2176]{1,0:T(8,128)(2,1)S(1)} %collective-permute-done.1.refs_1_), channel_id=1, source_target_pairs={{0,1},{1,0},{2,3},{3,2},{4,5},{5,4},{6,7},{7,6},{8,9},{9,8},{10,11... | collective-permute-start | bytes 1671176 | tf_op jit(solution)/shard_map/ppermute | solution.py:36
  51.7 6.4 %collective-permute-start.6 = (bf16[128,2176]{1,0:T(8,128)(2,1)S(1)}, bf16[128,2176]{1,0:T(8,128)(2,1)S(1)}, u32[]{:S(2)}, u32[]{:S(2)}) collective-permute-start(bf16[128,2176]{1,0:T(8,128)(2,1)S(1)} %collective-permute-done.4.refs_3_), channel_id=1, source_target_pairs={{1,0},{3,2},{5,4},{7,6},{9,8},{11,10},{13,12},{15,14},{17,16},{19,... | collective-permute-start | bytes 1671176 | tf_op jit(solution)/shard_map/ppermute | solution.py:36

commit v8 on v7

--- a/solution.py
+++ b/solution.py
@@ -18,7 +18,7 @@
 MASKED = -1e30
 HALF = GROUP // 2
 HALF_WIDTH = HALF * HEAD_SIZE
-CHUNKS = (6, 5, 5)
+CHUNKS = (5, 6, 5)
 VMEM_GRANT = 48 * 1024 * 1024
 
 WHOLE = pl.BlockSpec(memory_space=pltpu.VMEM)
@@ -174,32 +174,8 @@
         bias[:, b * quota : (b + 1) * quota] = jnp.where(allowed, 0.0, MASKED)
 
 
-def attend_kernel(blocks, first, count, late, rank_ref, *refs):
-    kv_refs, far_ref, mate_ref = refs[: blocks - 1], refs[blocks - 1], refs[blocks]
-    refs = refs[blocks + 1 :]
-    if late:
-        hot_ref, arrived_hbm, q_hbm, _, out_hbm, bias, rest, result, queries, local = refs[:10]
-        sources = [
-            lambda u: (arrived_hbm.at[:, half_columns(u)], queries),
-            lambda u: (q_hbm.at[0, 0 : bias.shape[0], half_columns(u, first)], local),
-        ]
-    else:
-        in_hbm, out_hbm, bias, rest, result, queries = refs[:6]
-        sources = [lambda u: (in_hbm.at[0, :, half_columns(u, first)], queries)]
-    in_sems, out_sems = refs[-2:]
+def attend_halves(first, count, core, kv_refs, far_ref, mate_ref, bias, rest, take, result):
     quota = bias.shape[0]
-    fetches = []
-    for u in range(count):
-        fetches.append([])
-        for i, source in enumerate(sources):
-            origin, target = source(u)
-            fetch = pltpu.make_async_copy(origin, target.at[:, half_columns(u)], in_sems.at[i, u])
-            fetch.start()
-            fetches[u].append(fetch)
-
-    rank = rank_ref[0]
-    core = lax.rem(rank, 2)
-    make_bias(kv_refs, far_ref, mate_ref, bias, rank)
     first_head, last_head = first // 2, (first + count - 1) // 2
     parts = [(first_head + part) * HEAD_SIZE for part in (0, KEY_VALUE_HEADS)]
     spans = [slice(at, at + (last_head - first_head + 1) * HEAD_SIZE) for at in parts]
@@ -225,11 +201,7 @@
         return keys, jnp.concatenate([values, jnp.ones_like(values)], axis=1)
 
     def scored(u, keys):
-        for fetch in fetches[u]:
-            fetch.wait()
-        q = queries[:, half_columns(u)]
-        if late:
-            q = place_rows(hot_ref[...], q, local[:, half_columns(u)])
+        q = take(u)
         stacked = jnp.concatenate(
             [q[:, h * HEAD_SIZE : (h + 1) * HEAD_SIZE] for h in range(HALF)], axis=0
         )
@@ -249,13 +221,7 @@
         for h in range(HALF):
             at = u * HALF_WIDTH + h * HEAD_SIZE
             result[:, at : at + HEAD_SIZE] = mixed[h * quota : (h + 1) * quota]
-        store = pltpu.make_async_copy(
-            result.at[:, half_columns(u)], out_hbm.at[0, :, half_columns(u, first)], out_sems.at[u]
-        )
-        store.start()
-        return store
-
-    stores = []
+
     keys, values = key_head(first_head)
     scores = scored(0, keys)
     for u in range(count):
@@ -264,40 +230,102 @@
             if (first + u + 1) % 2 == 0:
                 keys, values = key_head((first + u + 1) // 2)
             later = scored(u + 1, keys)
-        stores.append(finished(u, scores, own_values))
+        finished(u, scores, own_values)
         scores = later
-    for store in stores:
-        store.wait()
-
-
-def attend(rank, kv_blocks, late, out, first, count):
-    quota = kv_blocks[0].shape[0]
+
+
+def early_kernel(blocks, count, rank_ref, *refs):
+    kv_refs, far_ref, mate_ref = refs[: blocks - 1], refs[blocks - 1], refs[blocks]
+    placed_hbm, result, bias, rest, queries, in_sem = refs[blocks + 1 :]
+    fetch = pltpu.make_async_copy(placed_hbm.at[0, :, 0 : count * HALF_WIDTH], queries, in_sem)
+    fetch.start()
+    rank = rank_ref[0]
+    make_bias(kv_refs, far_ref, mate_ref, bias, rank)
+    fetch.wait()
+    attend_halves(
+        0,
+        count,
+        lax.rem(rank, 2),
+        kv_refs,
+        far_ref,
+        mate_ref,
+        bias,
+        rest,
+        lambda u: queries[:, half_columns(u)],
+        result,
+    )
+
+
+def late_kernel(blocks, first, count, rank_ref, *refs):
+    kv_refs, far_ref, mate_ref = refs[: blocks - 1], refs[blocks - 1], refs[blocks]
+    hot_ref, arrived_hbm, q_hbm, early_ref, _, out_hbm = refs[blocks + 1 : blocks + 7]
+    bias, rest, result, arrived, local, sems = refs[blocks + 7 :]
+    at, width = first * HALF_WIDTH, count * HALF_WIDTH
+    fetches = [
+        pltpu.make_async_copy(arrived_hbm, arrived, sems.at[0]),
+        pltpu.make_async_copy(
+            q_hbm.at[0, 0 : bias.shape[0], at : at + width], local, sems.at[1]
+        ),
+    ]
+    for fetch in fetches:
+        fetch.start()
+    early = pltpu.make_async_copy(early_ref, out_hbm.at[0, :, 0:at], sems.at[2])
+    early.start()
+    rank = rank_ref[0]
+    make_bias(kv_refs, far_ref, mate_ref, bias, rank)
+    for fetch in fetches:
+        fetch.wait()
+
+    def take(u):
+        cols = half_columns(u)
+        return place_rows(hot_ref[...], arrived[:, cols], local[:, cols])
+
+    core = lax.rem(rank, 2)
+    attend_halves(
+        first, count, core, kv_refs, far_ref, mate_ref, bias, rest, take, result
+    )
+    store = pltpu.make_async_copy(result, out_hbm.at[0, :, at : at + width], sems.at[3])
+    store.start()
+    early.wait()
+    store.wait()
+
+
+def attend(rank, hot, arrived, q_rows, kv_blocks, out):
+    quota, width = arrived.shape
     blocks = len(kv_blocks) - 1
-    width = count * HALF_WIDTH
-    columns = pltpu.VMEM((quota, width), jnp.bfloat16)
-    sources = 2 if late else 1
-    return pl.pallas_call(
-        functools.partial(attend_kernel, blocks, first, count, bool(late)),
-        in_specs=[SCALARS]
-        + [WHOLE] * len(kv_blocks)
-        + ([WHOLE, ANYWHERE, ANYWHERE] if late else [])
-        + [ANYWHERE],
-        out_specs=ANYWHERE,
-        out_shape=jax.ShapeDtypeStruct((1, quota, QUERY_HEADS * HEAD_SIZE), jnp.bfloat16),
-        input_output_aliases={1 + len(kv_blocks) + len(late): 0},
-        scratch_shapes=[
-            pltpu.VMEM((quota, blocks * quota), jnp.float32),
-            pltpu.VMEM((quota, NOTE), jnp.bfloat16),
-            columns,
-            columns,
-            *([columns] if late else []),
-            pltpu.SemaphoreType.DMA((sources, count)),
-            pltpu.SemaphoreType.DMA((count,)),
-        ],
+    late = width // HALF_WIDTH
+    early = 2 * KEY_VALUE_HEADS - late
+    bias = pltpu.VMEM((quota, blocks * quota), jnp.float32)
+    rest = pltpu.VMEM((quota, NOTE), jnp.bfloat16)
+    hints = dict(
         cost_estimate=pl.CostEstimate(flops=0, bytes_accessed=0, transcendentals=0),
         compiler_params=pltpu.CompilerParams(vmem_limit_bytes=VMEM_GRANT),
-        name="attend_late" if late else "attend_early",
-    )(rank, *kv_blocks, *late, out)
+    )
+    result = pl.pallas_call(
+        functools.partial(early_kernel, blocks, early),
+        in_specs=[SCALARS] + [WHOLE] * len(kv_blocks) + [ANYWHERE],
+        out_specs=WHOLE,
+        out_shape=jax.ShapeDtypeStruct((quota, early * HALF_WIDTH), jnp.bfloat16),
+        scratch_shapes=[
+            bias,
+            rest,
+            pltpu.VMEM((quota, early * HALF_WIDTH), jnp.bfloat16),
+            pltpu.SemaphoreType.DMA,
+        ],
+        name="attend_early",
+        **hints,
+    )(rank, *kv_blocks, out)
+    columns = pltpu.VMEM((quota, width), jnp.bfloat16)
+    return pl.pallas_call(
+        functools.partial(late_kernel, blocks, early, late),
+        in_specs=[SCALARS] + [WHOLE] * (len(kv_blocks) + 1) + [ANYWHERE] * 2 + [WHOLE, ANYWHERE],
+        out_specs=ANYWHERE,
+        out_shape=jax.ShapeDtypeStruct(out.shape, out.dtype),
+        input_output_aliases={len(kv_blocks) + 5: 0},
+        scratch_shapes=[bias, rest, columns, columns, columns, pltpu.SemaphoreType.DMA((4,))],
+        name="attend_late",
+        **hints,
+    )(rank, *kv_blocks, hot, arrived, q_rows, result, out)
 
 
 def circular_tail(rows, later):
@@ -324,12 +352,14 @@
     kv_tail, later = lax.optimization_barrier((kv_tail, later))
     local_kv, later = lax.optimization_barrier((local_kv, later))
     arrived_kv = shifted(kv_tail, "dp", 1)
-    arrived_q = []
+    q_tails = []
     first = 0
     for size in CHUNKS:
         cols = slice(first * HALF_WIDTH, (first + size) * HALF_WIDTH)
-        arrived_q.append(shifted(circular_tail(q_rows[0, :, cols], later), "dp", 1))
+        q_tails.append(circular_tail(q_rows[0, :, cols], later))
         first += size
+    q_tails = lax.optimization_barrier(q_tails)
+    arrived_q = [shifted(tail, "dp", 1) for tail in q_tails]
 
     shift = shift_in_known(own_count, quota)
     own, hot = settle_kv(shift, doc_ids, arrived_kv, local_kv)
@@ -346,9 +376,7 @@
         if back < rounds:
             kv_blocks.append(across_cores(carried))
     kv_blocks += [across_cores(carried, (1,)), across_cores(own, (0,))]
-    early, late = sum(CHUNKS[:-1]), CHUNKS[-1]
-    out = attend(rank[None], kv_blocks, (), out, 0, early)
-    return attend(rank[None], kv_blocks, (hot, arrived_q[-1], q_rows), out, early, late)
+    return attend(rank[None], hot, arrived_q[-1], q_rows, kv_blocks, out)
 
 
 def solution(mesh):

time: 76.6 us -> 71 us (0.927)
  Pallas kernels: 21.1 us -> 16.4 us
  local copies, waits for them, and re-layouts: 0.06 us -> 3.2 us
  other arithmetic: 6.56 us -> 3.78 us
  waiting for transfers between devices: 21.7 us -> 20.5 us
    pallas_call x2, Pallas kernels: 17.9 us -> 13.2 us  [the longest x1 7.09 us: attend(): pl.pallas_call(functools.partial(early_kernel, blocks, early), in_specs=[...]
    unnamed x8 -> x10, local copies, waits for them, and re-layouts: 0.01 us -> 2.21 us
    select_n x3, other arithmetic: 5.55 us -> 3.56 us  [circular_tail(): return jnp.where(later[:, None], rows[quota:], rows[:quota])]
    ppermute x6, waiting for transfers between devices: 20.1 us -> 19 us  [shifted(): return lax.ppermute(x, axis, [(i, i + steps) for i in range(n - steps)])]
    slice x1, local copies, waits for them, and re-layouts: 0.04 us -> 0.99 us  [circular_tail(): return jnp.where(later[:, None], rows[quota:], rows[:quota])]
    concatenate x1, other arithmetic: 0.9 us -> 0.1 us  [body(): jnp.concatenate([circular_tail(k_rows[0], later), circular_tail(value_slo...]
  transfers between devices with their start and end apart: 9 -> 9, of which waited for: 4 -> 4; matrix products, arithmetic and copies ran while one was open for 6% -> 5% of each run, Pallas kernels for 20% -> 15%
where the time goes in v8:
time: 71 us; the launch traced here: 70.1 us
  starting transfers between devices  25.3 us (36%)
  waiting for transfers between devices  20.5 us (29%)
  Pallas kernels  16.4 us (23%)
  other arithmetic  3.78 us (5%)
  local copies, waits for them, and re-layouts  3.2 us (5%)
  between operations  0.95 us (1%)
    ppermute x6, waiting for transfers between devices, shifted(): return lax.ppermute(x, axis, [(i, i + steps) for i in range(n - steps)])  19 us
    ppermute x6, starting transfers between devices, shifted(): return lax.ppermute(x, axis, [(i, i + steps) for i in range(n - steps)])  16 us
    ppermute x3, starting transfers between devices, across_cores(): lax.ppermute(x, 'ctx', [(i, i ^ 1) for i in range(n) if i % 2 in sources])  9.28 us
    pallas_call x1, Pallas kernels, attend(): pl.pallas_call(functools.partial(early_kernel, blocks, early), in_specs=[...  7.09 us
    pallas_call x1, Pallas kernels, attend(): pl.pallas_call(functools.partial(late_kernel, blocks, early, late), in_sp...  6.11 us
    select_n x3, other arithmetic, circular_tail(): return jnp.where(later[:, None], rows[quota:], rows[:quota])  3.56 us
    pallas_call x2, Pallas kernels, place_queries(): pl.pallas_call(functools.partial(place_kernel, first), in_specs=in_specs,...  2.34 us
    unnamed x10, local copies, waits for them, and re-layouts  2.21 us
  transfers between devices with their start and end apart: 9, of which 4 were waited for; matrix products, arithmetic and copies ran while one was open for 5% of the time, Pallas kernels for 15%

profile of v8, /device:TPU:21, one launch (start us, length us, event | category | flops | bytes accessed | tf_op | source)
XLA Modules:
  0.0 70.1 jit_solution(2923695102162536037)
XLA Ops:
  0.0 0.0 copy-start.4
  0.8 0.0 copy-start
  0.8 1.5 %bitcast_select_fusion.4 = (bf16[128,1024]{1,0:T(8,128)(2,1)S(1)}, bf16[128,1024]{1,0:T(8,128)(2,1)S(1)}) fusion(bf16[1,256,1024]{2,1,0:T(8,128)(2,1)} %param.6, pred[128]{0:T(512)(128)(4,1)S(1)} %add_compare_fusion, bf16[1,256,1024]{2,1,0:T(8,128)(2,1)} %param.7), kind=kLoop, calls=%fused_computation.6 | loop fusion | flops 262144 | bytes 1572992 | tf_op jit(solution)/shard_map/jit(_where)/select_n | solution.py:333
  2.2 0.1 maximum_maximum_fusion
  2.3 3.1 %collective-permute-start = (bf16[128,2176]{1,0:T(8,128)(2,1)S(1)}, bf16[128,2176]{1,0:T(8,128)(2,1)S(1)}, u32[]{:S(2)}, u32[]{:S(2)}) collective-permute-start(bf16[128,2176]{1,0:T(8,128)(2,1)S(1)} %maximum_maximum_fusion), channel_id=1, source_target_pairs={{0,8},{8,16},{16,24},{1,9},{9,17},{17,25},{2,10},{10,18},{18,26},{... | collective-permute-start | bytes 1671176 | tf_op jit(solution)/shard_map/ppermute | solution.py:31
  5.5 0.0 copy-done.4
  5.5 1.0 %slice_bitcast_fusion = (bf16[128,1024]{1,0:T(8,128)(2,1)S(1)}, bf16[128,1024]{1,0:T(8,128)(2,1)S(1)}) fusion(bf16[1,256,1024]{2,1,0:T(8,128)(2,1)} %param.7, bf16[1,256,1024]{2,1,0:T(8,128)(2,1)S(1)} %copy-done.4), kind=kLoop, calls=%fused_computation.7 | loop fusion | bytes 1048576 | tf_op jit(solution)/shard_map/slice | solution.py:333
  6.5 0.0 copy-done
  6.5 1.1 %bitcast_select_fusion.1 = (bf16[128,2560]{1,0:T(8,128)(2,1)}, bf16[128,2560]{1,0:T(8,128)(2,1)S(1)}) fusion(bf16[1,256,8192]{2,1,0:T(8,128)(2,1)S(1)} %copy-done, pred[128]{0:T(512)(128)(4,1)S(1)} %add_compare_fusion), kind=kLoop, calls=%fused_computation.1 | loop fusion | flops 655360 | bytes 3932288 | tf_op jit(solution)/shard_map/jit(_where)/select_n | solution.py:333
  7.6 0.0 copy-start.3
  7.6 1.0 %bitcast_select_fusion = bf16[128,3072]{1,0:T(8,128)(2,1)} fusion(bf16[1,256,8192]{2,1,0:T(8,128)(2,1)S(1)} %copy-done, pred[128]{0:T(512)(128)(4,1)S(1)} %add_compare_fusion), kind=kLoop, calls=%fused_computation | loop fusion | flops 393216 | bytes 2359424 | tf_op jit(solution)/shard_map/jit(_where)/select_n | solution.py:333
  8.6 1.9 %collective-permute-start.2 = (bf16[128,2560]{1,0:T(8,128)(2,1)S(1)}, bf16[128,2560]{1,0:T(8,128)(2,1)S(1)}, u32[]{:S(2)}, u32[]{:S(2)}) collective-permute-start(bf16[128,2560]{1,0:T(8,128)(2,1)S(1)} %get-tuple-element.24), channel_id=1, source_target_pairs={{0,8},{8,16},{16,24},{1,9},{9,17},{17,25},{2,10},{10,18},{18,26},{... | collective-permute-start | bytes 1966088 | tf_op jit(solution)/shard_map/ppermute | solution.py:31
  10.6 0.1 pad_add_fusion.shift_ref
  10.6 8.0 %collective-permute-done.arrived_ref = bf16[128,2176]{1,0:T(8,128)(2,1)S(1)} collective-permute-done((bf16[128,2176]{1,0:T(8,128)(2,1)S(1)}, bf16[128,2176]{1,0:T(8,128)(2,1)S(1)}, u32[]{:S(2)}, u32[]{:S(2)}) %collective-permute-start) | collective-permute-done | bytes 557088 | tf_op jit(solution)/shard_map/ppermute | solution.py:31
  18.6 0.0 copy-done.3
  18.6 0.9 %settle_kv.1 = (bf16[128,2176]{1,0:T(8,128)(2,1)S(1)}, bf16[128,256]{1,0:T(8,128)(2,1)S(1)}) custom-call(s32[2]{0:T(128)S(1)} %pad_add_fusion.shift_ref, s32[1,128]{1,0:T(1,128)S(1)} %copy-done.3, bf16[128,2176]{1,0:T(8,128)(2,1)S(1)} %collective-permute-done.arrived_ref, bf16[128,2048]{1,0:T(8,128)(2,1)S(1)} %pad_maximum_fusion.local_ref), custom_call_target="tpu_custom_call" | custom-call | tf_op jit(solution)/shard_map/settle_kv/pallas_call | solution.py:84
  19.5 3.2 %collective-permute-start.1 = (bf16[128,2176]{1,0:T(8,128)(2,1)S(1)}, bf16[128,2176]{1,0:T(8,128)(2,1)S(1)}, u32[]{:S(2)}, u32[]{:S(2)}) collective-permute-start(bf16[128,2176]{1,0:T(8,128)(2,1)S(1)} %get-tuple-element.21.refs_0_), channel_id=1, source_target_pairs={{0,2},{1,3},{2,4},{3,5},{4,6},{5,7},{8,10},{9,11},{10,12},{11,13},... | collective-permute-start | bytes 1671176 | tf_op jit(solution)/shard_map/ppermute | solution.py:31
  22.7 2.2 %collective-permute-start.5 = (bf16[128,3072]{1,0:T(8,128)(2,1)}, bf16[128,3072]{1,0:T(8,128)(2,1)S(1)}, u32[]{:S(2)}, u32[]{:S(2)}) collective-permute-start(bf16[128,3072]{1,0:T(8,128)(2,1)} %bitcast_select_fusion), channel_id=1, source_target_pairs={{0,8},{8,16},{16,24},{1,9},{9,17},{17,25},{2,10},{10,18},{18,26},{... | collective-permute-start | bytes 2359304 | tf_op jit(solution)/shard_map/ppermute | solution.py:31
  24.9 7.7 %collective-permute-done.2.arrived_ref = bf16[128,2560]{1,0:T(8,128)(2,1)S(1)} collective-permute-done((bf16[128,2560]{1,0:T(8,128)(2,1)S(1)}, bf16[128,2560]{1,0:T(8,128)(2,1)S(1)}, u32[]{:S(2)}, u32[]{:S(2)}) %collective-permute-start.2) | collective-permute-done | bytes 655392 | tf_op jit(solution)/shard_map/ppermute | solution.py:31
  32.7 0.0 copy-start.1
  32.7 2.2 %copy-done.1 = bf16[1,256,8192]{2,1,0:T(8,128)(2,1)S(1)} copy-done((bf16[1,256,8192]{2,1,0:T(8,128)(2,1)S(1)}, bf16[1,256,8192]{2,1,0:T(8,128)(2,1)}, u32[]{:S(2)}) %copy-start.1) | copy-done | bytes 4194328
  34.9 0.0 copy-start.2
  34.9 1.1 %place_queries.2.refs_0_ = bf16[1,128,8192]{2,1,0:T(8,128)(2,1)} custom-call(bf16[128,256]{1,0:T(8,128)(2,1)S(1)} %get-tuple-element.22.hot_ref.refs_6_, bf16[128,2560]{1,0:T(8,128)(2,1)S(1)} %collective-permute-done.2.arrived_ref, bf16[1,256,8192]{2,1,0:T(8,128)(2,1)S(1)} %copy-done.1), custom_call_target="tpu_custom_call" | custom-call | tf_op jit(solution)/shard_map/place_queries/pallas_call | solution.py:140
  36.0 0.0 collective-permute-done.1.refs_1_
  36.0 3.3 %collective-permute-start.4 = (bf16[128,2176]{1,0:T(8,128)(2,1)S(1)}, bf16[128,2176]{1,0:T(8,128)(2,1)S(1)}, u32[]{:S(2)}, u32[]{:S(2)}) collective-permute-start(bf16[128,2176]{1,0:T(8,128)(2,1)S(1)} %collective-permute-done.1.refs_1_), channel_id=1, source_target_pairs={{0,2},{1,3},{2,4},{3,5},{4,6},{5,7},{8,10},{9,11},{10,12},{11,13},... | collective-permute-start | bytes 1671176 | tf_op jit(solution)/shard_map/ppermute | solution.py:31
  39.4 2.2 %collective-permute-start.8 = (bf16[128,2560]{1,0:T(8,128)(2,1)}, bf16[128,2560]{1,0:T(8,128)(2,1)}, u32[]{:S(2)}, u32[]{:S(2)}) collective-permute-start(bf16[128,2560]{1,0:T(8,128)(2,1)} %get-tuple-element.29), channel_id=1, source_target_pairs={{0,8},{8,16},{16,24},{1,9},{9,17},{17,25},{2,10},{10,18},{18,26},{... | collective-permute-start | bytes 1966088 | tf_op jit(solution)/shard_map/ppermute | solution.py:31
  41.6 1.3 %collective-permute-start.7 = (bf16[128,2176]{1,0:T(8,128)(2,1)S(1)}, bf16[128,2176]{1,0:T(8,128)(2,1)S(1)}, u32[]{:S(2)}, u32[]{:S(2)}) collective-permute-start(bf16[128,2176]{1,0:T(8,128)(2,1)S(1)} %get-tuple-element.21.refs_0_), channel_id=1, source_target_pairs={{0,1},{2,3},{4,5},{6,7},{8,9},{10,11},{12,13},{14,15},{16,17},{18,... | collective-permute-start | bytes 1671176 | tf_op jit(solution)/shard_map/ppermute | solution.py:36
  42.9 3.4 %collective-permute-start.3 = (bf16[128,2176]{1,0:T(8,128)(2,1)S(1)}, bf16[128,2176]{1,0:T(8,128)(2,1)S(1)}, u32[]{:S(2)}, u32[]{:S(2)}) collective-permute-start(bf16[128,2176]{1,0:T(8,128)(2,1)S(1)} %collective-permute-done.1.refs_1_), channel_id=1, source_target_pairs={{0,1},{1,0},{2,3},{3,2},{4,5},{5,4},{6,7},{7,6},{8,9},{9,8},{10,11... | collective-permute-start | bytes 1671176 | tf_op jit(solution)/shard_map/ppermute | solution.py:36
  46.2 3.3 %collective-permute-done.5.arrived_ref = bf16[128,3072]{1,0:T(8,128)(2,1)S(1)} collective-permute-done((bf16[128,3072]{1,0:T(8,128)(2,1)}, bf16[128,3072]{1,0:T(8,128)(2,1)S(1)}, u32[]{:S(2)}, u32[]{:S(2)}) %collective-permute-start.5) | collective-permute-done | bytes 786464 | tf_op jit(solution)/shard_map/ppermute | solution.py:31
  49.5 0.0 copy-done.2
  49.5 1.2 %place_queries.3.refs_6_.refs_10_ = bf16[1,128,8192]{2,1,0:T(8,128)(2,1)} custom-call(bf16[128,256]{1,0:T(8,128)(2,1)S(1)} %get-tuple-element.22.hot_ref.refs_6_, bf16[128,3072]{1,0:T(8,128)(2,1)S(1)} %collective-permute-done.5.arrived_ref, bf16[1,256,8192]{2,1,0:T(8,128)(2,1)S(1)} %copy-done.2, ...), custom_call_target="tpu_custom_call", output_to_operand_aliasing={{}: (3, {})} | custom-call | tf_op jit(solution)/shard_map/place_queries/pallas_call | solution.py:140
  50.7 0.0 collective-permute-done.4.refs_3_
  50.7 4.6 %collective-permute-start.6 = (bf16[128,2176]{1,0:T(8,128)(2,1)S(1)}, bf16[128,2176]{1,0:T(8,128)(2,1)S(1)}, u32[]{:S(2)}, u32[]{:S(2)}) collective-permute-start(bf16[128,2176]{1,0:T(8,128)(2,1)S(1)} %collective-permute-done.4.refs_3_), channel_id=1, source_target_pairs={{1,0},{3,2},{5,4},{7,6},{9,8},{11,10},{13,12},{15,14},{17,16},{19,... | collective-permute-start | bytes 1671176 | tf_op jit(solution)/shard_map/ppermute | solution.py:36
  55.4 0.0 collective-permute-done.7.refs_5_
  55.4 0.0 collective-permute-done.3.refs_2_
  55.4 1.5 %collective-permute-done.6.refs_4_ = bf16[128,2176]{1,0:T(8,128)(2,1)S(1)} collective-permute-done((bf16[128,2176]{1,0:T(8,128)(2,1)S(1)}, bf16[128,2176]{1,0:T(8,128)(2,1)S(1)}, u32[]{:S(2)}, u32[]{:S(2)}) %collective-permute-start.6) | collective-permute-done | bytes 557088 | tf_op jit(solution)/shard_map/ppermute | solution.py:36
  56.9 7.1 %attend_early.1.refs_9_ = bf16[128,5632]{1,0:T(8,128)(2,1)S(1)} custom-call(s32[1]{0:T(128)} %bitcast.rank_ref, bf16[128,2176]{1,0:T(8,128)(2,1)S(1)} %get-tuple-element.21.refs_0_, bf16[128,2176]{1,0:T(8,128)(2,1)S(1)} %collective-permute-done.1.refs_1_, bf16[128,2176]{1,0:T(8,128)(2,1)S(1)} %collective-permute-done.3.refs_2_, ...), custom_call_target="tpu_custom_call" | custom-call | tf_op jit(solution)/shard_map/attend_early/pallas_call | solution.py:304
  64.0 0.0 collective-permute-done.8.refs_7_
  64.0 6.1 %attend_late.1 = bf16[1,128,8192]{2,1,0:T(8,128)(2,1)} custom-call(s32[1]{0:T(128)} %bitcast.rank_ref, bf16[128,2176]{1,0:T(8,128)(2,1)S(1)} %get-tuple-element.21.refs_0_, bf16[128,2176]{1,0:T(8,128)(2,1)S(1)} %collective-permute-done.1.refs_1_, bf16[128,2176]{1,0:T(8,128)(2,1)S(1)} %collective-permute-done.3.refs_2_, ...), custom_call_target="tpu_custom_call", output_to_operand_aliasing={{}: (11, {})} | custom-call | tf_op jit(solution)/shard_map/attend_late/pallas_call | solution.py:319
  (4 shorter events, 0.1 us)
Async XLA Ops:
  0.0 5.5 %copy-start.4 = (bf16[1,256,1024]{2,1,0:T(8,128)(2,1)S(1)}, bf16[1,256,1024]{2,1,0:T(8,128)(2,1)}, u32[]{:S(2)}) copy-start(bf16[1,256,1024]{2,1,0:T(8,128)(2,1)} %param.6) | copy-start | bytes 1572868
  0.8 5.8 %copy-start = (bf16[1,256,8192]{2,1,0:T(8,128)(2,1)S(1)}, bf16[1,256,8192]{2,1,0:T(8,128)(2,1)}, u32[]{:S(2)}) copy-start(bf16[1,256,8192]{2,1,0:T(8,128)(2,1)} %refs_8_.1) | copy-start | bytes 12582916
  2.3 16.3 %collective-permute-start = (bf16[128,2176]{1,0:T(8,128)(2,1)S(1)}, bf16[128,2176]{1,0:T(8,128)(2,1)S(1)}, u32[]{:S(2)}, u32[]{:S(2)}) collective-permute-start(bf16[128,2176]{1,0:T(8,128)(2,1)S(1)} %maximum_maximum_fusion), channel_id=1, source_target_pairs={{0,8},{8,16},{16,24},{1,9},{9,17},{17,25},{2,10},{10,18},{18,26},{... | collective-permute-start | bytes 1671176 | tf_op jit(solution)/shard_map/ppermute | solution.py:31
  7.6 11.0 %copy-start.3 = (s32[1,128]{1,0:T(1,128)S(1)}, s32[1,128]{1,0:T(1,128)}, u32[]{:S(2)}) copy-start(s32[1,128]{1,0:T(1,128)} %docs_ref.1) | copy-start | bytes 1540
  8.6 24.0 %collective-permute-start.2 = (bf16[128,2560]{1,0:T(8,128)(2,1)S(1)}, bf16[128,2560]{1,0:T(8,128)(2,1)S(1)}, u32[]{:S(2)}, u32[]{:S(2)}) collective-permute-start(bf16[128,2560]{1,0:T(8,128)(2,1)S(1)} %get-tuple-element.24), channel_id=1, source_target_pairs={{0,8},{8,16},{16,24},{1,9},{9,17},{17,25},{2,10},{10,18},{18,26},{... | collective-permute-start | bytes 1966088 | tf_op jit(solution)/shard_map/ppermute | solution.py:31
  19.5 16.5 %collective-permute-start.1 = (bf16[128,2176]{1,0:T(8,128)(2,1)S(1)}, bf16[128,2176]{1,0:T(8,128)(2,1)S(1)}, u32[]{:S(2)}, u32[]{:S(2)}) collective-permute-start(bf16[128,2176]{1,0:T(8,128)(2,1)S(1)} %get-tuple-element.21.refs_0_), channel_id=1, source_target_pairs={{0,2},{1,3},{2,4},{3,5},{4,6},{5,7},{8,10},{9,11},{10,12},{11,13},... | collective-permute-start | bytes 1671176 | tf_op jit(solution)/shard_map/ppermute | solution.py:31
  22.7 26.8 %collective-permute-start.5 = (bf16[128,3072]{1,0:T(8,128)(2,1)}, bf16[128,3072]{1,0:T(8,128)(2,1)S(1)}, u32[]{:S(2)}, u32[]{:S(2)}) collective-permute-start(bf16[128,3072]{1,0:T(8,128)(2,1)} %bitcast_select_fusion), channel_id=1, source_target_pairs={{0,8},{8,16},{16,24},{1,9},{9,17},{17,25},{2,10},{10,18},{18,26},{... | collective-permute-start | bytes 2359304 | tf_op jit(solution)/shard_map/ppermute | solution.py:31
  32.7 2.2 %copy-start.1 = (bf16[1,256,8192]{2,1,0:T(8,128)(2,1)S(1)}, bf16[1,256,8192]{2,1,0:T(8,128)(2,1)}, u32[]{:S(2)}) copy-start(bf16[1,256,8192]{2,1,0:T(8,128)(2,1)} %refs_8_.1) | copy-start | bytes 12582916
  34.9 14.7 %copy-start.2 = (bf16[1,256,8192]{2,1,0:T(8,128)(2,1)S(1)}, bf16[1,256,8192]{2,1,0:T(8,128)(2,1)}, u32[]{:S(2)}) copy-start(bf16[1,256,8192]{2,1,0:T(8,128)(2,1)} %refs_8_.1) | copy-start | bytes 12582916
  36.0 14.7 %collective-permute-start.4 = (bf16[128,2176]{1,0:T(8,128)(2,1)S(1)}, bf16[128,2176]{1,0:T(8,128)(2,1)S(1)}, u32[]{:S(2)}, u32[]{:S(2)}) collective-permute-start(bf16[128,2176]{1,0:T(8,128)(2,1)S(1)} %collective-permute-done.1.refs_1_), channel_id=1, source_target_pairs={{0,2},{1,3},{2,4},{3,5},{4,6},{5,7},{8,10},{9,11},{10,12},{11,13},... | collective-permute-start | bytes 1671176 | tf_op jit(solution)/shard_map/ppermute | solution.py:31
  39.4 24.7 %collective-permute-start.8 = (bf16[128,2560]{1,0:T(8,128)(2,1)}, bf16[128,2560]{1,0:T(8,128)(2,1)}, u32[]{:S(2)}, u32[]{:S(2)}) collective-permute-start(bf16[128,2560]{1,0:T(8,128)(2,1)} %get-tuple-element.29), channel_id=1, source_target_pairs={{0,8},{8,16},{16,24},{1,9},{9,17},{17,25},{2,10},{10,18},{18,26},{... | collective-permute-start | bytes 1966088 | tf_op jit(solution)/shard_map/ppermute | solution.py:31
  41.6 13.8 %collective-permute-start.7 = (bf16[128,2176]{1,0:T(8,128)(2,1)S(1)}, bf16[128,2176]{1,0:T(8,128)(2,1)S(1)}, u32[]{:S(2)}, u32[]{:S(2)}) collective-permute-start(bf16[128,2176]{1,0:T(8,128)(2,1)S(1)} %get-tuple-element.21.refs_0_), channel_id=1, source_target_pairs={{0,1},{2,3},{4,5},{6,7},{8,9},{10,11},{12,13},{14,15},{16,17},{18,... | collective-permute-start | bytes 1671176 | tf_op jit(solution)/shard_map/ppermute | solution.py:36
  42.9 12.5 %collective-permute-start.3 = (bf16[128,2176]{1,0:T(8,128)(2,1)S(1)}, bf16[128,2176]{1,0:T(8,128)(2,1)S(1)}, u32[]{:S(2)}, u32[]{:S(2)}) collective-permute-start(bf16[128,2176]{1,0:T(8,128)(2,1)S(1)} %collective-permute-done.1.refs_1_), channel_id=1, source_target_pairs={{0,1},{1,0},{2,3},{3,2},{4,5},{5,4},{6,7},{7,6},{8,9},{9,8},{10,11... | collective-permute-start | bytes 1671176 | tf_op jit(solution)/shard_map/ppermute | solution.py:36
  50.7 6.2 %collective-permute-start.6 = (bf16[128,2176]{1,0:T(8,128)(2,1)S(1)}, bf16[128,2176]{1,0:T(8,128)(2,1)S(1)}, u32[]{:S(2)}, u32[]{:S(2)}) collective-permute-start(bf16[128,2176]{1,0:T(8,128)(2,1)S(1)} %collective-permute-done.4.refs_3_), channel_id=1, source_target_pairs={{1,0},{3,2},{5,4},{7,6},{9,8},{11,10},{13,12},{15,14},{17,16},{19,... | collective-permute-start | bytes 1671176 | tf_op jit(solution)/shard_map/ppermute | solution.py:36

commit v9 on v8

--- a/solution.py
+++ b/solution.py
@@ -12,14 +12,13 @@
 KEY_VALUE_HEADS = 8
 HEAD_SIZE = 128
 GROUP = QUERY_HEADS // KEY_VALUE_HEADS
-GROUP_WIDTH = GROUP * HEAD_SIZE
 KV_WIDTH = KEY_VALUE_HEADS * HEAD_SIZE
 NOTE = 2 * KV_WIDTH
 MASKED = -1e30
 HALF = GROUP // 2
-HALF_WIDTH = HALF * HEAD_SIZE
-CHUNKS = (5, 6, 5)
-VMEM_GRANT = 48 * 1024 * 1024
+CHUNKS = (20, 20, 18, 6)
+PLACED = 2
+VMEM_GRANT = 32 * 1024 * 1024
 
 WHOLE = pl.BlockSpec(memory_space=pltpu.VMEM)
 ANYWHERE = pl.BlockSpec(memory_space=pl.ANY)
@@ -104,23 +103,35 @@
     return ranks
 
 
-def half_columns(u, start=0):
-    return slice((start + u) * HALF_WIDTH, (start + u + 1) * HALF_WIDTH)
+def head_columns(head, heads=1):
+    return slice(head * HEAD_SIZE, (head + heads) * HEAD_SIZE)
+
+
+def pieces(first, count):
+    at, found = first, []
+    while at < first + count:
+        end = min(first + count, (at // GROUP + 1) * GROUP)
+        heads = end - at
+        if heads > HALF:
+            heads = min(HALF, -(-heads // 2))
+        found.append((at, heads))
+        at += heads
+    return found
 
 
 def place_kernel(start, hot_ref, arrived_ref, local_hbm, *refs):
     out_hbm, local, placed, in_sem, out_sems = refs[-5:]
     quota, width = arrived_ref.shape
-    at = start * HALF_WIDTH
+    at = start * HEAD_SIZE
     fetch = pltpu.make_async_copy(local_hbm.at[0, 0:quota, at : at + width], local, in_sem)
     fetch.start()
     fetch.wait()
     stores = []
-    for u in range(width // HALF_WIDTH):
-        cols = half_columns(u)
+    for u, (head, heads) in enumerate(pieces(start, width // HEAD_SIZE)):
+        cols = head_columns(head - start, heads)
         placed[:, cols] = place_rows(hot_ref[...], arrived_ref[:, cols], local[:, cols])
         store = pltpu.make_async_copy(
-            placed.at[:, cols], out_hbm.at[0, :, half_columns(u, start)], out_sems.at[u]
+            placed.at[:, cols], out_hbm.at[0, :, head_columns(head, heads)], out_sems.at[u]
         )
         store.start()
         stores.append(store)
@@ -147,7 +158,7 @@
             pltpu.VMEM((quota, width), jnp.bfloat16),
             pltpu.VMEM((quota, width), jnp.bfloat16),
             pltpu.SemaphoreType.DMA,
-            pltpu.SemaphoreType.DMA((width // HALF_WIDTH,)),
+            pltpu.SemaphoreType.DMA((len(pieces(first, width // HEAD_SIZE)),)),
         ],
         compiler_params=pltpu.CompilerParams(vmem_limit_bytes=VMEM_GRANT),
         name="place_queries",
@@ -174,158 +185,163 @@
         bias[:, b * quota : (b + 1) * quota] = jnp.where(allowed, 0.0, MASKED)
 
 
-def attend_halves(first, count, core, kv_refs, far_ref, mate_ref, bias, rest, take, result):
-    quota = bias.shape[0]
-    first_head, last_head = first // 2, (first + count - 1) // 2
-    parts = [(first_head + part) * HEAD_SIZE for part in (0, KEY_VALUE_HEADS)]
-    spans = [slice(at, at + (last_head - first_head + 1) * HEAD_SIZE) for at in parts]
+def choose_rest(first, count, core, far_ref, mate_ref, rest):
+    first_head, last_head = first // GROUP, (first + count - 1) // GROUP
+    keys = head_columns(first_head, last_head - first_head + 1)
+    values = slice(KV_WIDTH + keys.start, KV_WIDTH + keys.stop)
 
     @pl.when(core == 0)
     def _():
-        for span in spans:
-            rest[:, span] = far_ref[:, span]
+        rest[:, keys] = far_ref[:, keys]
+        rest[:, values] = far_ref[:, values]
 
     @pl.when(core == 1)
     def _():
-        for span in spans:
-            rest[:, span] = mate_ref[:, span]
-
-    kv_refs = [*kv_refs, rest]
+        rest[:, keys] = mate_ref[:, keys]
+        rest[:, values] = mate_ref[:, values]
+
+
+def attend_heads(first, count, kv_refs, bias, take, result):
+    quota = bias.shape[0]
     unit = math.log2(math.e) / math.sqrt(HEAD_SIZE)
 
     def key_head(head):
-        at = head * HEAD_SIZE
-        keys = jnp.concatenate([r[:, at : at + HEAD_SIZE] for r in kv_refs], axis=0)
-        at += KV_WIDTH
-        values = jnp.concatenate([r[:, at : at + HEAD_SIZE] for r in kv_refs], axis=0)
+        cols = head_columns(head)
+        keys = jnp.concatenate([r[:, cols] for r in kv_refs], axis=0)
+        cols = head_columns(KEY_VALUE_HEADS + head)
+        values = jnp.concatenate([r[:, cols] for r in kv_refs], axis=0)
         return keys, jnp.concatenate([values, jnp.ones_like(values)], axis=1)
 
-    def scored(u, keys):
-        q = take(u)
-        stacked = jnp.concatenate(
-            [q[:, h * HEAD_SIZE : (h + 1) * HEAD_SIZE] for h in range(HALF)], axis=0
-        )
+    def scored(head, heads, keys):
+        q = take(head_columns(head - first, heads))
+        stacked = jnp.concatenate([q[:, head_columns(h)] for h in range(heads)], axis=0)
         return lax.dot_general(
             stacked, keys, (((1,), (1,)), ((), ())), preferred_element_type=jnp.float32
         )
 
-    def finished(u, scores, values):
-        scores = scores.reshape(HALF, quota, -1) * unit + bias[...][None]
+    def finished(head, heads, scores, values):
+        scores = scores.reshape(heads, quota, -1) * unit + bias[...][None]
         weights = jnp.exp2(scores - jnp.max(scores, axis=2, keepdims=True))
-        weights = weights.astype(jnp.bfloat16).reshape(HALF * quota, -1)
+        weights = weights.astype(jnp.bfloat16).reshape(heads * quota, -1)
         mixed = jnp.dot(weights, values, preferred_element_type=jnp.float32)
         totals = mixed[:, HEAD_SIZE:]
         inverse = pl.reciprocal(totals, approx=True)
         inverse = inverse * (2.0 - totals * inverse)
         mixed = (mixed[:, :HEAD_SIZE] * inverse).astype(jnp.bfloat16)
-        for h in range(HALF):
-            at = u * HALF_WIDTH + h * HEAD_SIZE
-            result[:, at : at + HEAD_SIZE] = mixed[h * quota : (h + 1) * quota]
-
-    keys, values = key_head(first_head)
-    scores = scored(0, keys)
-    for u in range(count):
+        for h in range(heads):
+            result[:, head_columns(head - first + h)] = mixed[h * quota : (h + 1) * quota]
+
+    steps = pieces(first, count)
+    keys, values = key_head(first // GROUP)
+    scores = scored(*steps[0], keys)
+    for i, (head, heads) in enumerate(steps):
         own_values, later = values, None
-        if u + 1 < count:
-            if (first + u + 1) % 2 == 0:
-                keys, values = key_head((first + u + 1) // 2)
-            later = scored(u + 1, keys)
-        finished(u, scores, own_values)
+        if i + 1 < len(steps):
+            if steps[i + 1][0] // GROUP != head // GROUP:
+                keys, values = key_head(steps[i + 1][0] // GROUP)
+            later = scored(*steps[i + 1], keys)
+        finished(head, heads, scores, own_values)
         scores = later
 
 
 def early_kernel(blocks, count, rank_ref, *refs):
     kv_refs, far_ref, mate_ref = refs[: blocks - 1], refs[blocks - 1], refs[blocks]
     placed_hbm, result, bias, rest, queries, in_sem = refs[blocks + 1 :]
-    fetch = pltpu.make_async_copy(placed_hbm.at[0, :, 0 : count * HALF_WIDTH], queries, in_sem)
+    fetch = pltpu.make_async_copy(placed_hbm.at[0, :, head_columns(0, count)], queries, in_sem)
     fetch.start()
     rank = rank_ref[0]
     make_bias(kv_refs, far_ref, mate_ref, bias, rank)
+    choose_rest(0, count, lax.rem(rank, 2), far_ref, mate_ref, rest)
     fetch.wait()
-    attend_halves(
-        0,
-        count,
-        lax.rem(rank, 2),
-        kv_refs,
-        far_ref,
-        mate_ref,
-        bias,
-        rest,
-        lambda u: queries[:, half_columns(u)],
-        result,
-    )
-
-
-def late_kernel(blocks, first, count, rank_ref, *refs):
+    attend_heads(0, count, [*kv_refs, rest], bias, lambda cols: queries[:, cols], result)
+
+
+def late_kernel(blocks, before, first, count, last, rank_ref, *refs):
     kv_refs, far_ref, mate_ref = refs[: blocks - 1], refs[blocks - 1], refs[blocks]
-    hot_ref, arrived_hbm, q_hbm, early_ref, _, out_hbm = refs[blocks + 1 : blocks + 7]
-    bias, rest, result, arrived, local, sems = refs[blocks + 7 :]
-    at, width = first * HALF_WIDTH, count * HALF_WIDTH
+    hot_ref, arrived_hbm, q_hbm, before_ref, _, out_hbm = refs[blocks + 1 : blocks + 7]
+    result, bias, rest, arrived, local, sems = refs[blocks + 7 :]
+    cols = head_columns(first, count)
     fetches = [
         pltpu.make_async_copy(arrived_hbm, arrived, sems.at[0]),
-        pltpu.make_async_copy(
-            q_hbm.at[0, 0 : bias.shape[0], at : at + width], local, sems.at[1]
-        ),
+        pltpu.make_async_copy(q_hbm.at[0, 0 : bias.shape[0], cols], local, sems.at[1]),
     ]
     for fetch in fetches:
         fetch.start()
-    early = pltpu.make_async_copy(early_ref, out_hbm.at[0, :, 0:at], sems.at[2])
-    early.start()
     rank = rank_ref[0]
     make_bias(kv_refs, far_ref, mate_ref, bias, rank)
+    choose_rest(first, count, lax.rem(rank, 2), far_ref, mate_ref, rest)
     for fetch in fetches:
         fetch.wait()
-
-    def take(u):
-        cols = half_columns(u)
+    stores = [
+        pltpu.make_async_copy(
+            before_ref, out_hbm.at[0, :, head_columns(first - before, before)], sems.at[2]
+        )
+    ]
+    stores[0].start()
+
+    def take(cols):
         return place_rows(hot_ref[...], arrived[:, cols], local[:, cols])
 
-    core = lax.rem(rank, 2)
-    attend_halves(
-        first, count, core, kv_refs, far_ref, mate_ref, bias, rest, take, result
-    )
-    store = pltpu.make_async_copy(result, out_hbm.at[0, :, at : at + width], sems.at[3])
-    store.start()
-    early.wait()
-    store.wait()
-
-
-def attend(rank, hot, arrived, q_rows, kv_blocks, out):
-    quota, width = arrived.shape
+    attend_heads(first, count, [*kv_refs, rest], bias, take, result)
+    if last:
+        stores.append(pltpu.make_async_copy(result, out_hbm.at[0, :, cols], sems.at[3]))
+        stores[1].start()
+    for store in stores:
+        store.wait()
+
+
+def attend(rank, hot, arrived_q, q_rows, kv_blocks, out):
+    quota = hot.shape[0]
     blocks = len(kv_blocks) - 1
-    late = width // HALF_WIDTH
-    early = 2 * KEY_VALUE_HEADS - late
+    counts = [arrived.shape[1] // HEAD_SIZE for arrived in arrived_q]
+    first = QUERY_HEADS - sum(counts)
     bias = pltpu.VMEM((quota, blocks * quota), jnp.float32)
     rest = pltpu.VMEM((quota, NOTE), jnp.bfloat16)
     hints = dict(
         cost_estimate=pl.CostEstimate(flops=0, bytes_accessed=0, transcendentals=0),
         compiler_params=pltpu.CompilerParams(vmem_limit_bytes=VMEM_GRANT),
     )
+
+    def columns(count):
+        return (quota, count * HEAD_SIZE), jnp.bfloat16
+
     result = pl.pallas_call(
-        functools.partial(early_kernel, blocks, early),
+        functools.partial(early_kernel, blocks, first),
         in_specs=[SCALARS] + [WHOLE] * len(kv_blocks) + [ANYWHERE],
         out_specs=WHOLE,
-        out_shape=jax.ShapeDtypeStruct((quota, early * HALF_WIDTH), jnp.bfloat16),
-        scratch_shapes=[
-            bias,
-            rest,
-            pltpu.VMEM((quota, early * HALF_WIDTH), jnp.bfloat16),
-            pltpu.SemaphoreType.DMA,
-        ],
+        out_shape=jax.ShapeDtypeStruct(*columns(first)),
+        scratch_shapes=[bias, rest, pltpu.VMEM(*columns(first)), pltpu.SemaphoreType.DMA],
         name="attend_early",
         **hints,
     )(rank, *kv_blocks, out)
-    columns = pltpu.VMEM((quota, width), jnp.bfloat16)
-    return pl.pallas_call(
-        functools.partial(late_kernel, blocks, early, late),
-        in_specs=[SCALARS] + [WHOLE] * (len(kv_blocks) + 1) + [ANYWHERE] * 2 + [WHOLE, ANYWHERE],
-        out_specs=ANYWHERE,
-        out_shape=jax.ShapeDtypeStruct(out.shape, out.dtype),
-        input_output_aliases={len(kv_blocks) + 5: 0},
-        scratch_shapes=[bias, rest, columns, columns, columns, pltpu.SemaphoreType.DMA((4,))],
-        name="attend_late",
-        **hints,
-    )(rank, *kv_blocks, hot, arrived, q_rows, result, out)
+    before = first
+    for i, (arrived, count) in enumerate(zip(arrived_q, counts)):
+        last = i + 1 == len(counts)
+        own = columns(count)
+        handed_on = [] if last else [jax.ShapeDtypeStruct(*own)]
+        out, *result = pl.pallas_call(
+            functools.partial(late_kernel, blocks, before, first, count, last),
+            in_specs=[SCALARS]
+            + [WHOLE] * (len(kv_blocks) + 1)
+            + [ANYWHERE] * 2
+            + [WHOLE, ANYWHERE],
+            out_specs=[ANYWHERE] + [WHOLE] * len(handed_on),
+            out_shape=[jax.ShapeDtypeStruct(out.shape, out.dtype)] + handed_on,
+            input_output_aliases={len(kv_blocks) + 5: 0},
+            scratch_shapes=[
+                *([pltpu.VMEM(*own)] if last else []),
+                bias,
+                rest,
+                pltpu.VMEM(*own),
+                pltpu.VMEM(*own),
+                pltpu.SemaphoreType.DMA((4,)),
+            ],
+            name="attend_late",
+            **hints,
+        )(rank, *kv_blocks, hot, arrived, q_rows, result, out)
+        result = result[0] if result else None
+        before, first = count, first + count
+    return out
 
 
 def circular_tail(rows, later):
@@ -355,10 +371,9 @@
     q_tails = []
     first = 0
     for size in CHUNKS:
-        cols = slice(first * HALF_WIDTH, (first + size) * HALF_WIDTH)
-        q_tails.append(circular_tail(q_rows[0, :, cols], later))
+        q_tails.append(circular_tail(q_rows[0, :, head_columns(first, size)], later))
         first += size
-    q_tails = lax.optimization_barrier(q_tails)
+    q_tails[:3] = lax.optimization_barrier(q_tails[:3])
     arrived_q = [shifted(tail, "dp", 1) for tail in q_tails]
 
     shift = shift_in_known(own_count, quota)
@@ -369,14 +384,14 @@
     for back in range(1, rounds + 1):
         carried = shifted(carried, "ctx", 2)
         kv_blocks.append(carried)
-        if back <= len(CHUNKS) - 1:
+        if back <= PLACED:
             first = sum(CHUNKS[: back - 1])
             out = place_queries(hot, arrived_q[back - 1], q_rows, first, out)
             carried, out = lax.optimization_barrier((carried, out))
         if back < rounds:
             kv_blocks.append(across_cores(carried))
     kv_blocks += [across_cores(carried, (1,)), across_cores(own, (0,))]
-    return attend(rank[None], hot, arrived_q[-1], q_rows, kv_blocks, out)
+    return attend(rank[None], hot, arrived_q[PLACED:], q_rows, kv_blocks, out)
 
 
 def solution(mesh):

time: 71 us -> 74.4 us (1.048)
  starting transfers between devices: 25.3 us -> 28.3 us
  waiting for transfers between devices: 20.5 us -> 18 us
  local copies, waits for them, and re-layouts: 3.2 us -> 4.8 us
    ppermute x6 -> x7, starting transfers between devices: 16 us -> 18.2 us  [shifted(): return lax.ppermute(x, axis, [(i, i + steps) for i in range(n - steps)])]
    unnamed x10 -> x14, local copies, waits for them, and re-layouts: 2.21 us -> 3.8 us
    ppermute x3, waiting for transfers between devices: 1.51 us -> 0.01 us  [across_cores(): lax.ppermute(x, 'ctx', [(i, i ^ 1) for i in range(n) if i % 2 in sources])]
    ppermute x6 -> x7, waiting for transfers between devices: 19 us -> 18 us  [shifted(): return lax.ppermute(x, axis, [(i, i + steps) for i in range(n - steps)])]
    ppermute x3, starting transfers between devices: 9.28 us -> 10.1 us  [across_cores(): lax.ppermute(x, 'ctx', [(i, i ^ 1) for i in range(n) if i % 2 in sources])]
    select_n x3 -> x4, other arithmetic: 3.56 us -> 4.22 us  [circular_tail(): return jnp.where(later[:, None], rows[quota:], rows[:quota])]
    pallas_call x2 -> x3, Pallas kernels: 13.2 us -> 13.3 us  [the longest x2 7.76 us: attend(): pl.pallas_call(functools.partial(late_kernel, blocks, before, first, coun...]
  transfers between devices with their start and end apart: 9 -> 10, of which waited for: 4 -> 4; matrix products, arithmetic and copies ran while one was open for 5% -> 5% of each run, Pallas kernels for 15% -> 18%
where the time goes in v9:
time: 74.4 us; the launch traced here: 73 us
  starting transfers between devices  28.3 us (38%)
  waiting for transfers between devices  18 us (24%)
  Pallas kernels  16.5 us (22%)
  local copies, waits for them, and re-layouts  4.8 us (6%)
  other arithmetic  4.44 us (6%)
  between operations  1.01 us (1%)
    ppermute x7, starting transfers between devices, shifted(): return lax.ppermute(x, axis, [(i, i + steps) for i in range(n - steps)])  18.2 us
    ppermute x7, waiting for transfers between devices, shifted(): return lax.ppermute(x, axis, [(i, i + steps) for i in range(n - steps)])  18 us
    ppermute x3, starting transfers between devices, across_cores(): lax.ppermute(x, 'ctx', [(i, i ^ 1) for i in range(n) if i % 2 in sources])  10.1 us
    pallas_call x2, Pallas kernels, attend(): pl.pallas_call(functools.partial(late_kernel, blocks, before, first, coun...  7.76 us
    pallas_call x1, Pallas kernels, attend(): pl.pallas_call(functools.partial(early_kernel, blocks, first), in_specs=[...  5.59 us
    select_n x4, other arithmetic, circular_tail(): return jnp.where(later[:, None], rows[quota:], rows[:quota])  4.22 us
    unnamed x14, local copies, waits for them, and re-layouts  3.8 us
    pallas_call x2, Pallas kernels, place_queries(): pl.pallas_call(functools.partial(place_kernel, first), in_specs=in_specs,...  2.27 us
  transfers between devices with their start and end apart: 10, of which 4 were waited for; matrix products, arithmetic and copies ran while one was open for 5% of the time, Pallas kernels for 18%

profile of v9, /device:TPU:21, one launch (start us, length us, event | category | flops | bytes accessed | tf_op | source)
XLA Modules:
  0.0 73.0 jit_solution(5192691802437781645)
XLA Ops:
  0.0 0.0 copy-start.6
  0.8 0.0 copy-start
  0.8 1.5 %bitcast_select_fusion.4 = (bf16[128,1024]{1,0:T(8,128)(2,1)S(1)}, bf16[128,1024]{1,0:T(8,128)(2,1)S(1)}) fusion(bf16[1,256,1024]{2,1,0:T(8,128)(2,1)} %param.6, pred[128]{0:T(512)(128)(4,1)S(1)} %add_compare_fusion, bf16[1,256,1024]{2,1,0:T(8,128)(2,1)} %param.7), kind=kLoop, calls=%fused_computation.6 | loop fusion | flops 262144 | bytes 1572992 | tf_op jit(solution)/shard_map/jit(_where)/select_n | solution.py:349
  2.2 0.1 maximum_maximum_fusion
  2.3 3.1 %collective-permute-start = (bf16[128,2176]{1,0:T(8,128)(2,1)S(1)}, bf16[128,2176]{1,0:T(8,128)(2,1)S(1)}, u32[]{:S(2)}, u32[]{:S(2)}) collective-permute-start(bf16[128,2176]{1,0:T(8,128)(2,1)S(1)} %maximum_maximum_fusion), channel_id=1, source_target_pairs={{0,8},{8,16},{16,24},{1,9},{9,17},{17,25},{2,10},{10,18},{18,26},{... | collective-permute-start | bytes 1671176 | tf_op jit(solution)/shard_map/ppermute | solution.py:30
  5.5 0.0 copy-done.6
  5.5 1.0 %slice_bitcast_fusion = (bf16[128,1024]{1,0:T(8,128)(2,1)S(1)}, bf16[128,1024]{1,0:T(8,128)(2,1)S(1)}) fusion(bf16[1,256,1024]{2,1,0:T(8,128)(2,1)} %param.7, bf16[1,256,1024]{2,1,0:T(8,128)(2,1)S(1)} %copy-done.6), kind=kLoop, calls=%fused_computation.7 | loop fusion | bytes 1048576 | tf_op jit(solution)/shard_map/slice | solution.py:349
  6.5 0.0 copy-done
  6.5 0.0 copy-start.5
  6.5 1.1 %bitcast_select_fusion = (bf16[128,2560]{1,0:T(8,128)(2,1)}, bf16[128,2560]{1,0:T(8,128)(2,1)S(1)}) fusion(bf16[1,256,8192]{2,1,0:T(8,128)(2,1)S(1)} %copy-done, pred[128]{0:T(512)(128)(4,1)S(1)} %add_compare_fusion), kind=kLoop, calls=%fused_computation | loop fusion | flops 655360 | bytes 3932288 | tf_op jit(solution)/shard_map/jit(_where)/select_n | solution.py:349
  7.6 1.0 %bitcast_select_fusion.2 = bf16[128,2304]{1,0:T(8,128)(2,1)} fusion(bf16[1,256,8192]{2,1,0:T(8,128)(2,1)S(1)} %copy-done, pred[128]{0:T(512)(128)(4,1)S(1)} %add_compare_fusion), kind=kLoop, calls=%fused_computation.2 | loop fusion | flops 294912 | bytes 1769600 | tf_op jit(solution)/shard_map/jit(_where)/select_n | solution.py:349
  8.5 1.9 %collective-permute-start.2 = (bf16[128,2560]{1,0:T(8,128)(2,1)S(1)}, bf16[128,2560]{1,0:T(8,128)(2,1)S(1)}, u32[]{:S(2)}, u32[]{:S(2)}) collective-permute-start(bf16[128,2560]{1,0:T(8,128)(2,1)S(1)} %get-tuple-element.26), channel_id=1, source_target_pairs={{0,8},{8,16},{16,24},{1,9},{9,17},{17,25},{2,10},{10,18},{18,26},{... | collective-permute-start | bytes 1966088 | tf_op jit(solution)/shard_map/ppermute | solution.py:30
  10.5 0.1 pad_add_fusion.shift_ref
  10.6 8.1 %collective-permute-done.arrived_ref = bf16[128,2176]{1,0:T(8,128)(2,1)S(1)} collective-permute-done((bf16[128,2176]{1,0:T(8,128)(2,1)S(1)}, bf16[128,2176]{1,0:T(8,128)(2,1)S(1)}, u32[]{:S(2)}, u32[]{:S(2)}) %collective-permute-start) | collective-permute-done | bytes 557088 | tf_op jit(solution)/shard_map/ppermute | solution.py:30
  18.6 0.0 copy-done.5
  18.6 0.9 %settle_kv.1 = (bf16[128,2176]{1,0:T(8,128)(2,1)S(1)}, bf16[128,256]{1,0:T(8,128)(2,1)S(1)}) custom-call(s32[2]{0:T(128)S(1)} %pad_add_fusion.shift_ref, s32[1,128]{1,0:T(1,128)S(1)} %copy-done.5, bf16[128,2176]{1,0:T(8,128)(2,1)S(1)} %collective-permute-done.arrived_ref, bf16[128,2048]{1,0:T(8,128)(2,1)S(1)} %pad_maximum_fusion.local_ref), custom_call_target="tpu_custom_call" | custom-call | tf_op jit(solution)/shard_map/settle_kv/pallas_call | solution.py:83
  19.5 3.2 %collective-permute-start.1 = (bf16[128,2176]{1,0:T(8,128)(2,1)S(1)}, bf16[128,2176]{1,0:T(8,128)(2,1)S(1)}, u32[]{:S(2)}, u32[]{:S(2)}) collective-permute-start(bf16[128,2176]{1,0:T(8,128)(2,1)S(1)} %get-tuple-element.23.refs_0_), channel_id=1, source_target_pairs={{0,2},{1,3},{2,4},{3,5},{4,6},{5,7},{8,10},{9,11},{10,12},{11,13},... | collective-permute-start | bytes 1671176 | tf_op jit(solution)/shard_map/ppermute | solution.py:30
  22.7 2.2 %collective-permute-start.5 = (bf16[128,2560]{1,0:T(8,128)(2,1)}, bf16[128,2560]{1,0:T(8,128)(2,1)S(1)}, u32[]{:S(2)}, u32[]{:S(2)}) collective-permute-start(bf16[128,2560]{1,0:T(8,128)(2,1)} %get-tuple-element.28), channel_id=1, source_target_pairs={{0,8},{8,16},{16,24},{1,9},{9,17},{17,25},{2,10},{10,18},{18,26},{... | collective-permute-start | bytes 1966088 | tf_op jit(solution)/shard_map/ppermute | solution.py:30
  24.9 7.7 %collective-permute-done.2.arrived_ref = bf16[128,2560]{1,0:T(8,128)(2,1)S(1)} collective-permute-done((bf16[128,2560]{1,0:T(8,128)(2,1)S(1)}, bf16[128,2560]{1,0:T(8,128)(2,1)S(1)}, u32[]{:S(2)}, u32[]{:S(2)}) %collective-permute-start.2) | collective-permute-done | bytes 655392 | tf_op jit(solution)/shard_map/ppermute | solution.py:30
  32.7 0.0 copy-start.1
  32.7 2.2 %copy-done.1 = bf16[1,256,8192]{2,1,0:T(8,128)(2,1)S(1)} copy-done((bf16[1,256,8192]{2,1,0:T(8,128)(2,1)S(1)}, bf16[1,256,8192]{2,1,0:T(8,128)(2,1)}, u32[]{:S(2)}) %copy-start.1) | copy-done | bytes 4194328
  34.9 0.0 copy-start.2
  34.9 1.1 %place_queries.2.refs_0_ = bf16[1,128,8192]{2,1,0:T(8,128)(2,1)} custom-call(bf16[128,256]{1,0:T(8,128)(2,1)S(1)} %get-tuple-element.24.hot_ref.refs_6_, bf16[128,2560]{1,0:T(8,128)(2,1)S(1)} %collective-permute-done.2.arrived_ref, bf16[1,256,8192]{2,1,0:T(8,128)(2,1)S(1)} %copy-done.1), custom_call_target="tpu_custom_call" | custom-call | tf_op jit(solution)/shard_map/place_queries/pallas_call | solution.py:151
  36.0 0.0 collective-permute-done.1.refs_1_
  36.0 3.3 %collective-permute-start.4 = (bf16[128,2176]{1,0:T(8,128)(2,1)S(1)}, bf16[128,2176]{1,0:T(8,128)(2,1)S(1)}, u32[]{:S(2)}, u32[]{:S(2)}) collective-permute-start(bf16[128,2176]{1,0:T(8,128)(2,1)S(1)} %collective-permute-done.1.refs_1_), channel_id=1, source_target_pairs={{0,2},{1,3},{2,4},{3,5},{4,6},{5,7},{8,10},{9,11},{10,12},{11,13},... | collective-permute-start | bytes 1671176 | tf_op jit(solution)/shard_map/ppermute | solution.py:30
  39.4 2.2 %collective-permute-start.9 = (bf16[128,2304]{1,0:T(8,128)(2,1)}, bf16[128,2304]{1,0:T(8,128)(2,1)}, u32[]{:S(2)}, u32[]{:S(2)}) collective-permute-start(bf16[128,2304]{1,0:T(8,128)(2,1)} %bitcast_select_fusion.2), channel_id=1, source_target_pairs={{0,8},{8,16},{16,24},{1,9},{9,17},{17,25},{2,10},{10,18},{18,26},{... | collective-permute-start | bytes 1769480 | tf_op jit(solution)/shard_map/ppermute | solution.py:30
  41.6 1.3 %collective-permute-start.7 = (bf16[128,2176]{1,0:T(8,128)(2,1)S(1)}, bf16[128,2176]{1,0:T(8,128)(2,1)S(1)}, u32[]{:S(2)}, u32[]{:S(2)}) collective-permute-start(bf16[128,2176]{1,0:T(8,128)(2,1)S(1)} %get-tuple-element.23.refs_0_), channel_id=1, source_target_pairs={{0,1},{2,3},{4,5},{6,7},{8,9},{10,11},{12,13},{14,15},{16,17},{18,... | collective-permute-start | bytes 1671176 | tf_op jit(solution)/shard_map/ppermute | solution.py:35
  42.9 3.4 %collective-permute-start.3 = (bf16[128,2176]{1,0:T(8,128)(2,1)S(1)}, bf16[128,2176]{1,0:T(8,128)(2,1)S(1)}, u32[]{:S(2)}, u32[]{:S(2)}) collective-permute-start(bf16[128,2176]{1,0:T(8,128)(2,1)S(1)} %collective-permute-done.1.refs_1_), channel_id=1, source_target_pairs={{0,1},{1,0},{2,3},{3,2},{4,5},{5,4},{6,7},{7,6},{8,9},{9,8},{10,11... | collective-permute-start | bytes 1671176 | tf_op jit(solution)/shard_map/ppermute | solution.py:35
  46.3 0.5 collective-permute-done.5.arrived_ref
  46.7 0.0 copy-done.2
  46.7 1.1 %place_queries.3.refs_6_.refs_10_ = bf16[1,128,8192]{2,1,0:T(8,128)(2,1)} custom-call(bf16[128,256]{1,0:T(8,128)(2,1)S(1)} %get-tuple-element.24.hot_ref.refs_6_, bf16[128,2560]{1,0:T(8,128)(2,1)S(1)} %collective-permute-done.5.arrived_ref, bf16[1,256,8192]{2,1,0:T(8,128)(2,1)S(1)} %copy-done.2, ...), custom_call_target="tpu_custom_call", output_to_operand_aliasing={{}: (3, {})} | custom-call | tf_op jit(solution)/shard_map/place_queries/pallas_call | solution.py:151
  47.9 1.7 %collective-permute-done.4.refs_3_ = bf16[128,2176]{1,0:T(8,128)(2,1)S(1)} collective-permute-done((bf16[128,2176]{1,0:T(8,128)(2,1)S(1)}, bf16[128,2176]{1,0:T(8,128)(2,1)S(1)}, u32[]{:S(2)}, u32[]{:S(2)}) %collective-permute-start.4) | collective-permute-done | bytes 557088 | tf_op jit(solution)/shard_map/ppermute | solution.py:30
  49.6 5.4 %collective-permute-start.6 = (bf16[128,2176]{1,0:T(8,128)(2,1)S(1)}, bf16[128,2176]{1,0:T(8,128)(2,1)S(1)}, u32[]{:S(2)}, u32[]{:S(2)}) collective-permute-start(bf16[128,2176]{1,0:T(8,128)(2,1)S(1)} %collective-permute-done.4.refs_3_), channel_id=1, source_target_pairs={{1,0},{3,2},{5,4},{7,6},{9,8},{11,10},{13,12},{15,14},{17,16},{19,... | collective-permute-start | bytes 1671176 | tf_op jit(solution)/shard_map/ppermute | solution.py:35
  55.0 0.8 %bitcast_select_fusion.5 = bf16[128,768]{1,0:T(8,128)(2,1)} fusion(bf16[1,256,8192]{2,1,0:T(8,128)(2,1)S(1)} %copy-done.2, pred[128]{0:T(512)(128)(4,1)S(1)} %add_compare_fusion), kind=kLoop, calls=%fused_computation.9 | loop fusion | flops 98304 | bytes 589952 | tf_op jit(solution)/shard_map/jit(_where)/select_n | solution.py:349
  55.8 2.2 %collective-permute-start.8 = (bf16[128,768]{1,0:T(8,128)(2,1)}, bf16[128,768]{1,0:T(8,128)(2,1)}, u32[]{:S(2)}, u32[]{:S(2)}) collective-permute-start(bf16[128,768]{1,0:T(8,128)(2,1)} %bitcast_select_fusion.5), channel_id=1, source_target_pairs={{0,8},{8,16},{16,24},{1,9},{9,17},{17,25},{2,10},{10,18},{18,26},{... | collective-permute-start | bytes 589832 | tf_op jit(solution)/shard_map/ppermute | solution.py:30
  58.0 0.0 collective-permute-done.7.refs_5_
  58.0 0.0 collective-permute-done.3.refs_2_
  58.0 0.0 collective-permute-done.6.refs_4_
  58.0 0.0 copy-start.4
  58.0 1.6 %copy-done.4 = bf16[1,128,8192]{2,1,0:T(8,128)(2,1)S(1)} copy-done((bf16[1,128,8192]{2,1,0:T(8,128)(2,1)S(1)}, bf16[1,128,8192]{2,1,0:T(8,128)(2,1)}, u32[]{:S(2)}) %copy-start.4) | copy-done | bytes 2097176
  59.6 0.0 copy-start.3
  59.6 5.6 %attend_early.1.refs_9_ = bf16[128,5120]{1,0:T(8,128)(2,1)S(1)} custom-call(s32[1]{0:T(128)} %bitcast.rank_ref, bf16[128,2176]{1,0:T(8,128)(2,1)S(1)} %get-tuple-element.23.refs_0_, bf16[128,2176]{1,0:T(8,128)(2,1)S(1)} %collective-permute-done.1.refs_1_, bf16[128,2176]{1,0:T(8,128)(2,1)S(1)} %collective-permute-done.3.refs_2_, ...), custom_call_target="tpu_custom_call" | custom-call | tf_op jit(solution)/shard_map/attend_early/pallas_call | solution.py:308
  65.2 0.0 collective-permute-done.9.refs_7_
  65.2 0.0 copy-done.3
  65.2 4.7 %attend_late.2 = (bf16[1,128,8192]{2,1,0:T(8,128)(2,1)}, bf16[128,2304]{1,0:T(8,128)(2,1)S(1)}) custom-call(s32[1]{0:T(128)} %bitcast.rank_ref, bf16[128,2176]{1,0:T(8,128)(2,1)S(1)} %get-tuple-element.23.refs_0_, bf16[128,2176]{1,0:T(8,128)(2,1)S(1)} %collective-permute-done.1.refs_1_, ...), custom_call_target="tpu_custom_call", output_to_operand_aliasing={{0}: (11, {})} | custom-call | tf_op jit(solution)/shard_map/attend_late/pallas_call | solution.py:322
  70.0 0.0 collective-permute-done.8.refs_7_
  70.0 3.0 %attend_late.3 = bf16[1,128,8192]{2,1,0:T(8,128)(2,1)} custom-call(s32[1]{0:T(128)} %bitcast.rank_ref, bf16[128,2176]{1,0:T(8,128)(2,1)S(1)} %get-tuple-element.23.refs_0_, bf16[128,2176]{1,0:T(8,128)(2,1)S(1)} %collective-permute-done.1.refs_1_, bf16[128,2176]{1,0:T(8,128)(2,1)S(1)} %collective-permute-done.3.refs_2_, ...), custom_call_target="tpu_custom_call", output_to_operand_aliasing={{}: (11, {})} | custom-call | tf_op jit(solution)/shard_map/attend_late/pallas_call | solution.py:322
  (4 shorter events, 0.1 us)
Async XLA Ops:
  0.0 5.5 %copy-start.6 = (bf16[1,256,1024]{2,1,0:T(8,128)(2,1)S(1)}, bf16[1,256,1024]{2,1,0:T(8,128)(2,1)}, u32[]{:S(2)}) copy-start(bf16[1,256,1024]{2,1,0:T(8,128)(2,1)} %param.6) | copy-start | bytes 1572868
  0.8 5.8 %copy-start = (bf16[1,256,8192]{2,1,0:T(8,128)(2,1)S(1)}, bf16[1,256,8192]{2,1,0:T(8,128)(2,1)}, u32[]{:S(2)}) copy-start(bf16[1,256,8192]{2,1,0:T(8,128)(2,1)} %refs_8_.3) | copy-start | bytes 12582916
  2.3 16.3 %collective-permute-start = (bf16[128,2176]{1,0:T(8,128)(2,1)S(1)}, bf16[128,2176]{1,0:T(8,128)(2,1)S(1)}, u32[]{:S(2)}, u32[]{:S(2)}) collective-permute-start(bf16[128,2176]{1,0:T(8,128)(2,1)S(1)} %maximum_maximum_fusion), channel_id=1, source_target_pairs={{0,8},{8,16},{16,24},{1,9},{9,17},{17,25},{2,10},{10,18},{18,26},{... | collective-permute-start | bytes 1671176 | tf_op jit(solution)/shard_map/ppermute | solution.py:30
  6.5 12.1 %copy-start.5 = (s32[1,128]{1,0:T(1,128)S(1)}, s32[1,128]{1,0:T(1,128)}, u32[]{:S(2)}) copy-start(s32[1,128]{1,0:T(1,128)} %docs_ref.1) | copy-start | bytes 1540
  8.5 24.1 %collective-permute-start.2 = (bf16[128,2560]{1,0:T(8,128)(2,1)S(1)}, bf16[128,2560]{1,0:T(8,128)(2,1)S(1)}, u32[]{:S(2)}, u32[]{:S(2)}) collective-permute-start(bf16[128,2560]{1,0:T(8,128)(2,1)S(1)} %get-tuple-element.26), channel_id=1, source_target_pairs={{0,8},{8,16},{16,24},{1,9},{9,17},{17,25},{2,10},{10,18},{18,26},{... | collective-permute-start | bytes 1966088 | tf_op jit(solution)/shard_map/ppermute | solution.py:30
  19.5 16.5 %collective-permute-start.1 = (bf16[128,2176]{1,0:T(8,128)(2,1)S(1)}, bf16[128,2176]{1,0:T(8,128)(2,1)S(1)}, u32[]{:S(2)}, u32[]{:S(2)}) collective-permute-start(bf16[128,2176]{1,0:T(8,128)(2,1)S(1)} %get-tuple-element.23.refs_0_), channel_id=1, source_target_pairs={{0,2},{1,3},{2,4},{3,5},{4,6},{5,7},{8,10},{9,11},{10,12},{11,13},... | collective-permute-start | bytes 1671176 | tf_op jit(solution)/shard_map/ppermute | solution.py:30
  22.7 24.0 %collective-permute-start.5 = (bf16[128,2560]{1,0:T(8,128)(2,1)}, bf16[128,2560]{1,0:T(8,128)(2,1)S(1)}, u32[]{:S(2)}, u32[]{:S(2)}) collective-permute-start(bf16[128,2560]{1,0:T(8,128)(2,1)} %get-tuple-element.28), channel_id=1, source_target_pairs={{0,8},{8,16},{16,24},{1,9},{9,17},{17,25},{2,10},{10,18},{18,26},{... | collective-permute-start | bytes 1966088 | tf_op jit(solution)/shard_map/ppermute | solution.py:30
  32.7 2.2 %copy-start.1 = (bf16[1,256,8192]{2,1,0:T(8,128)(2,1)S(1)}, bf16[1,256,8192]{2,1,0:T(8,128)(2,1)}, u32[]{:S(2)}) copy-start(bf16[1,256,8192]{2,1,0:T(8,128)(2,1)} %refs_8_.3) | copy-start | bytes 12582916
  34.9 11.9 %copy-start.2 = (bf16[1,256,8192]{2,1,0:T(8,128)(2,1)S(1)}, bf16[1,256,8192]{2,1,0:T(8,128)(2,1)}, u32[]{:S(2)}) copy-start(bf16[1,256,8192]{2,1,0:T(8,128)(2,1)} %refs_8_.3) | copy-start | bytes 12582916
  36.0 13.6 %collective-permute-start.4 = (bf16[128,2176]{1,0:T(8,128)(2,1)S(1)}, bf16[128,2176]{1,0:T(8,128)(2,1)S(1)}, u32[]{:S(2)}, u32[]{:S(2)}) collective-permute-start(bf16[128,2176]{1,0:T(8,128)(2,1)S(1)} %collective-permute-done.1.refs_1_), channel_id=1, source_target_pairs={{0,2},{1,3},{2,4},{3,5},{4,6},{5,7},{8,10},{9,11},{10,12},{11,13},... | collective-permute-start | bytes 1671176 | tf_op jit(solution)/shard_map/ppermute | solution.py:30
  39.4 25.9 %collective-permute-start.9 = (bf16[128,2304]{1,0:T(8,128)(2,1)}, bf16[128,2304]{1,0:T(8,128)(2,1)}, u32[]{:S(2)}, u32[]{:S(2)}) collective-permute-start(bf16[128,2304]{1,0:T(8,128)(2,1)} %bitcast_select_fusion.2), channel_id=1, source_target_pairs={{0,8},{8,16},{16,24},{1,9},{9,17},{17,25},{2,10},{10,18},{18,26},{... | collective-permute-start | bytes 1769480 | tf_op jit(solution)/shard_map/ppermute | solution.py:30
  41.6 16.4 %collective-permute-start.7 = (bf16[128,2176]{1,0:T(8,128)(2,1)S(1)}, bf16[128,2176]{1,0:T(8,128)(2,1)S(1)}, u32[]{:S(2)}, u32[]{:S(2)}) collective-permute-start(bf16[128,2176]{1,0:T(8,128)(2,1)S(1)} %get-tuple-element.23.refs_0_), channel_id=1, source_target_pairs={{0,1},{2,3},{4,5},{6,7},{8,9},{10,11},{12,13},{14,15},{16,17},{18,... | collective-permute-start | bytes 1671176 | tf_op jit(solution)/shard_map/ppermute | solution.py:35
  42.9 15.1 %collective-permute-start.3 = (bf16[128,2176]{1,0:T(8,128)(2,1)S(1)}, bf16[128,2176]{1,0:T(8,128)(2,1)S(1)}, u32[]{:S(2)}, u32[]{:S(2)}) collective-permute-start(bf16[128,2176]{1,0:T(8,128)(2,1)S(1)} %collective-permute-done.1.refs_1_), channel_id=1, source_target_pairs={{0,1},{1,0},{2,3},{3,2},{4,5},{5,4},{6,7},{7,6},{8,9},{9,8},{10,11... | collective-permute-start | bytes 1671176 | tf_op jit(solution)/shard_map/ppermute | solution.py:35
  49.6 8.4 %collective-permute-start.6 = (bf16[128,2176]{1,0:T(8,128)(2,1)S(1)}, bf16[128,2176]{1,0:T(8,128)(2,1)S(1)}, u32[]{:S(2)}, u32[]{:S(2)}) collective-permute-start(bf16[128,2176]{1,0:T(8,128)(2,1)S(1)} %collective-permute-done.4.refs_3_), channel_id=1, source_target_pairs={{1,0},{3,2},{5,4},{7,6},{9,8},{11,10},{13,12},{15,14},{17,16},{19,... | collective-permute-start | bytes 1671176 | tf_op jit(solution)/shard_map/ppermute | solution.py:35
  55.8 14.2 %collective-permute-start.8 = (bf16[128,768]{1,0:T(8,128)(2,1)}, bf16[128,768]{1,0:T(8,128)(2,1)}, u32[]{:S(2)}, u32[]{:S(2)}) collective-permute-start(bf16[128,768]{1,0:T(8,128)(2,1)} %bitcast_select_fusion.5), channel_id=1, source_target_pairs={{0,8},{8,16},{16,24},{1,9},{9,17},{17,25},{2,10},{10,18},{18,26},{... | collective-permute-start | bytes 589832 | tf_op jit(solution)/shard_map/ppermute | solution.py:30
  58.0 1.6 %copy-start.4 = (bf16[1,128,8192]{2,1,0:T(8,128)(2,1)S(1)}, bf16[1,128,8192]{2,1,0:T(8,128)(2,1)}, u32[]{:S(2)}) copy-start(bf16[1,128,8192]{2,1,0:T(8,128)(2,1)} %place_queries.3.refs_6_.refs_10_) | copy-start | bytes 6291460
  59.6 5.6 %copy-start.3 = (bf16[1,256,8192]{2,1,0:T(8,128)(2,1)S(1)}, bf16[1,256,8192]{2,1,0:T(8,128)(2,1)}, u32[]{:S(2)}) copy-start(bf16[1,256,8192]{2,1,0:T(8,128)(2,1)} %refs_8_.3) | copy-start | bytes 12582916

commit v10 on v9

--- a/solution.py
+++ b/solution.py
@@ -16,9 +16,8 @@
 NOTE = 2 * KV_WIDTH
 MASKED = -1e30
 HALF = GROUP // 2
-CHUNKS = (20, 20, 18, 6)
-PLACED = 2
-VMEM_GRANT = 32 * 1024 * 1024
+CHUNKS = (20, 24, 20)
+VMEM_GRANT = 48 * 1024 * 1024
 
 WHOLE = pl.BlockSpec(memory_space=pltpu.VMEM)
 ANYWHERE = pl.BlockSpec(memory_space=pl.ANY)
@@ -119,50 +118,66 @@
     return found
 
 
-def place_kernel(start, hot_ref, arrived_ref, local_hbm, *refs):
-    out_hbm, local, placed, in_sem, out_sems = refs[-5:]
+def in_place(kernel, operands, out, more_out=(), more_specs=(), **arguments):
+    specs = arguments.pop("in_specs") + [ANYWHERE]
+    return pl.pallas_call(
+        kernel,
+        in_specs=specs,
+        out_specs=[ANYWHERE, *more_specs],
+        out_shape=[jax.ShapeDtypeStruct(out.shape, out.dtype), *more_out],
+        input_output_aliases={len(operands): 0},
+        cost_estimate=pl.CostEstimate(flops=0, bytes_accessed=0, transcendentals=0),
+        compiler_params=pltpu.CompilerParams(vmem_limit_bytes=VMEM_GRANT),
+        **arguments,
+    )(*operands, out)
+
+
+def stage_kernel(q_hbm, out_hbm, sem):
+    copy = pltpu.make_async_copy(q_hbm.at[:, 0 : out_hbm.shape[1]], out_hbm, sem)
+    copy.start()
+    copy.wait()
+
+
+def stage_local(q_rows, quota):
+    return pl.pallas_call(
+        stage_kernel,
+        in_specs=[ANYWHERE],
+        out_specs=ANYWHERE,
+        out_shape=jax.ShapeDtypeStruct((1, quota, QUERY_HEADS * HEAD_SIZE), jnp.bfloat16),
+        scratch_shapes=[pltpu.SemaphoreType.DMA],
+        compiler_params=pltpu.CompilerParams(vmem_limit_bytes=VMEM_GRANT),
+        name="stage_local",
+    )(q_rows)
+
+
+def place_kernel(first, hot_ref, arrived_ref, in_hbm, out_hbm, local, placed, in_sem, out_sem):
     quota, width = arrived_ref.shape
-    at = start * HEAD_SIZE
-    fetch = pltpu.make_async_copy(local_hbm.at[0, 0:quota, at : at + width], local, in_sem)
+    cols = head_columns(first, width // HEAD_SIZE)
+    fetch = pltpu.make_async_copy(in_hbm.at[0, :, cols], local, in_sem)
     fetch.start()
     fetch.wait()
-    stores = []
-    for u, (head, heads) in enumerate(pieces(start, width // HEAD_SIZE)):
-        cols = head_columns(head - start, heads)
-        placed[:, cols] = place_rows(hot_ref[...], arrived_ref[:, cols], local[:, cols])
-        store = pltpu.make_async_copy(
-            placed.at[:, cols], out_hbm.at[0, :, head_columns(head, heads)], out_sems.at[u]
-        )
-        store.start()
-        stores.append(store)
-    for store in stores:
-        store.wait()
-
-
-def place_queries(hot, arrived, q_rows, first, out):
-    quota, width = arrived.shape
-    in_specs = [WHOLE, WHOLE, ANYWHERE]
-    operands = [hot, arrived, q_rows]
-    aliases = {}
-    if out is not None:
-        aliases = {len(operands): 0}
-        in_specs.append(ANYWHERE)
-        operands.append(out)
-    return pl.pallas_call(
+    for head, heads in pieces(first, width // HEAD_SIZE):
+        own = head_columns(head - first, heads)
+        placed[:, own] = place_rows(hot_ref[...], arrived_ref[:, own], local[:, own])
+    store = pltpu.make_async_copy(placed, out_hbm.at[0, :, cols], out_sem)
+    store.start()
+    store.wait()
+
+
+def place_queries(hot, arrived, first, out):
+    return in_place(
         functools.partial(place_kernel, first),
-        in_specs=in_specs,
-        out_specs=ANYWHERE,
-        out_shape=jax.ShapeDtypeStruct((1, quota, QUERY_HEADS * HEAD_SIZE), jnp.bfloat16),
-        input_output_aliases=aliases,
+        [hot, arrived],
+        out,
+        in_specs=[WHOLE, WHOLE],
         scratch_shapes=[
-            pltpu.VMEM((quota, width), jnp.bfloat16),
-            pltpu.VMEM((quota, width), jnp.bfloat16),
+            pltpu.VMEM(arrived.shape, jnp.bfloat16),
+            pltpu.VMEM(arrived.shape, jnp.bfloat16),
             pltpu.SemaphoreType.DMA,
-            pltpu.SemaphoreType.DMA((len(pieces(first, width // HEAD_SIZE)),)),
+            pltpu.SemaphoreType.DMA,
         ],
-        compiler_params=pltpu.CompilerParams(vmem_limit_bytes=VMEM_GRANT),
         name="place_queries",
-    )(*operands)
+    )[0]
 
 
 def make_bias(kv_refs, far_ref, mate_ref, bias, rank):
@@ -246,102 +261,76 @@
 
 def early_kernel(blocks, count, rank_ref, *refs):
     kv_refs, far_ref, mate_ref = refs[: blocks - 1], refs[blocks - 1], refs[blocks]
-    placed_hbm, result, bias, rest, queries, in_sem = refs[blocks + 1 :]
-    fetch = pltpu.make_async_copy(placed_hbm.at[0, :, head_columns(0, count)], queries, in_sem)
+    in_hbm, _, result, local, bias, rest, queries, sems = refs[blocks + 1 :]
+    late = head_columns(count, QUERY_HEADS - count)
+    fetch = pltpu.make_async_copy(in_hbm.at[0, :, head_columns(0, count)], queries, sems.at[0])
     fetch.start()
     rank = rank_ref[0]
     make_bias(kv_refs, far_ref, mate_ref, bias, rank)
     choose_rest(0, count, lax.rem(rank, 2), far_ref, mate_ref, rest)
     fetch.wait()
+    ahead = pltpu.make_async_copy(in_hbm.at[0, :, late], local, sems.at[1])
+    ahead.start()
     attend_heads(0, count, [*kv_refs, rest], bias, lambda cols: queries[:, cols], result)
-
-
-def late_kernel(blocks, before, first, count, last, rank_ref, *refs):
+    ahead.wait()
+
+
+def late_kernel(blocks, first, rank_ref, *refs):
     kv_refs, far_ref, mate_ref = refs[: blocks - 1], refs[blocks - 1], refs[blocks]
-    hot_ref, arrived_hbm, q_hbm, before_ref, _, out_hbm = refs[blocks + 1 : blocks + 7]
-    result, bias, rest, arrived, local, sems = refs[blocks + 7 :]
-    cols = head_columns(first, count)
-    fetches = [
-        pltpu.make_async_copy(arrived_hbm, arrived, sems.at[0]),
-        pltpu.make_async_copy(q_hbm.at[0, 0 : bias.shape[0], cols], local, sems.at[1]),
-    ]
-    for fetch in fetches:
-        fetch.start()
+    hot_ref, arrived_hbm, early_ref, local_ref, _, out_hbm = refs[blocks + 1 : blocks + 7]
+    bias, rest, arrived, result, sems = refs[blocks + 7 :]
+    count = QUERY_HEADS - first
+    fetch = pltpu.make_async_copy(arrived_hbm, arrived, sems.at[0])
+    fetch.start()
     rank = rank_ref[0]
     make_bias(kv_refs, far_ref, mate_ref, bias, rank)
     choose_rest(first, count, lax.rem(rank, 2), far_ref, mate_ref, rest)
-    for fetch in fetches:
-        fetch.wait()
-    stores = [
-        pltpu.make_async_copy(
-            before_ref, out_hbm.at[0, :, head_columns(first - before, before)], sems.at[2]
-        )
-    ]
-    stores[0].start()
+    fetch.wait()
+    early = pltpu.make_async_copy(early_ref, out_hbm.at[0, :, head_columns(0, first)], sems.at[1])
+    early.start()
 
     def take(cols):
-        return place_rows(hot_ref[...], arrived[:, cols], local[:, cols])
+        return place_rows(hot_ref[...], arrived[:, cols], local_ref[:, cols])
 
     attend_heads(first, count, [*kv_refs, rest], bias, take, result)
-    if last:
-        stores.append(pltpu.make_async_copy(result, out_hbm.at[0, :, cols], sems.at[3]))
-        stores[1].start()
-    for store in stores:
-        store.wait()
-
-
-def attend(rank, hot, arrived_q, q_rows, kv_blocks, out):
-    quota = hot.shape[0]
+    store = pltpu.make_async_copy(result, out_hbm.at[0, :, head_columns(first, count)], sems.at[2])
+    store.start()
+    early.wait()
+    store.wait()
+
+
+def attend(rank, hot, arrived, kv_blocks, out):
+    quota, width = arrived.shape
     blocks = len(kv_blocks) - 1
-    counts = [arrived.shape[1] // HEAD_SIZE for arrived in arrived_q]
-    first = QUERY_HEADS - sum(counts)
+    first = QUERY_HEADS - width // HEAD_SIZE
     bias = pltpu.VMEM((quota, blocks * quota), jnp.float32)
     rest = pltpu.VMEM((quota, NOTE), jnp.bfloat16)
-    hints = dict(
-        cost_estimate=pl.CostEstimate(flops=0, bytes_accessed=0, transcendentals=0),
-        compiler_params=pltpu.CompilerParams(vmem_limit_bytes=VMEM_GRANT),
+    own = (arrived.shape, jnp.bfloat16)
+    others = ((quota, first * HEAD_SIZE), jnp.bfloat16)
+    out, result, local = in_place(
+        functools.partial(early_kernel, blocks, first),
+        [rank, *kv_blocks],
+        out,
+        more_out=[jax.ShapeDtypeStruct(*others), jax.ShapeDtypeStruct(*own)],
+        more_specs=[WHOLE, WHOLE],
+        in_specs=[SCALARS] + [WHOLE] * len(kv_blocks),
+        scratch_shapes=[bias, rest, pltpu.VMEM(*others), pltpu.SemaphoreType.DMA((2,))],
+        name="attend_early",
     )
-
-    def columns(count):
-        return (quota, count * HEAD_SIZE), jnp.bfloat16
-
-    result = pl.pallas_call(
-        functools.partial(early_kernel, blocks, first),
-        in_specs=[SCALARS] + [WHOLE] * len(kv_blocks) + [ANYWHERE],
-        out_specs=WHOLE,
-        out_shape=jax.ShapeDtypeStruct(*columns(first)),
-        scratch_shapes=[bias, rest, pltpu.VMEM(*columns(first)), pltpu.SemaphoreType.DMA],
-        name="attend_early",
-        **hints,
-    )(rank, *kv_blocks, out)
-    before = first
-    for i, (arrived, count) in enumerate(zip(arrived_q, counts)):
-        last = i + 1 == len(counts)
-        own = columns(count)
-        handed_on = [] if last else [jax.ShapeDtypeStruct(*own)]
-        out, *result = pl.pallas_call(
-            functools.partial(late_kernel, blocks, before, first, count, last),
-            in_specs=[SCALARS]
-            + [WHOLE] * (len(kv_blocks) + 1)
-            + [ANYWHERE] * 2
-            + [WHOLE, ANYWHERE],
-            out_specs=[ANYWHERE] + [WHOLE] * len(handed_on),
-            out_shape=[jax.ShapeDtypeStruct(out.shape, out.dtype)] + handed_on,
-            input_output_aliases={len(kv_blocks) + 5: 0},
-            scratch_shapes=[
-                *([pltpu.VMEM(*own)] if last else []),
-                bias,
-                rest,
-                pltpu.VMEM(*own),
-                pltpu.VMEM(*own),
-                pltpu.SemaphoreType.DMA((4,)),
-            ],
-            name="attend_late",
-            **hints,
-        )(rank, *kv_blocks, hot, arrived, q_rows, result, out)
-        result = result[0] if result else None
-        before, first = count, first + count
-    return out
+    return in_place(
+        functools.partial(late_kernel, blocks, first),
+        [rank, *kv_blocks, hot, arrived, result, local],
+        out,
+        in_specs=[SCALARS] + [WHOLE] * (len(kv_blocks) + 1) + [ANYWHERE, WHOLE, WHOLE],
+        scratch_shapes=[
+            bias,
+            rest,
+            pltpu.VMEM(*own),
+            pltpu.VMEM(*own),
+            pltpu.SemaphoreType.DMA((3,)),
+        ],
+        name="attend_late",
+    )[0]
 
 
 def circular_tail(rows, later):
@@ -373,25 +362,27 @@
     for size in CHUNKS:
         q_tails.append(circular_tail(q_rows[0, :, head_columns(first, size)], later))
         first += size
-    q_tails[:3] = lax.optimization_barrier(q_tails[:3])
+    q_tails = lax.optimization_barrier(q_tails)
     arrived_q = [shifted(tail, "dp", 1) for tail in q_tails]
 
     shift = shift_in_known(own_count, quota)
+    out = stage_local(q_rows, quota)
+    local_kv, out = lax.optimization_barrier((local_kv, out))
     own, hot = settle_kv(shift, doc_ids, arrived_kv, local_kv)
 
     kv_blocks = [own]
-    carried, out = own, None
+    carried = own
     for back in range(1, rounds + 1):
         carried = shifted(carried, "ctx", 2)
         kv_blocks.append(carried)
-        if back <= PLACED:
+        if back < len(CHUNKS):
             first = sum(CHUNKS[: back - 1])
-            out = place_queries(hot, arrived_q[back - 1], q_rows, first, out)
+            out = place_queries(hot, arrived_q[back - 1], first, out)
             carried, out = lax.optimization_barrier((carried, out))
         if back < rounds:
             kv_blocks.append(across_cores(carried))
     kv_blocks += [across_cores(carried, (1,)), across_cores(own, (0,))]
-    return attend(rank[None], hot, arrived_q[PLACED:], q_rows, kv_blocks, out)
+    return attend(rank[None], hot, arrived_q[-1], kv_blocks, out)
 
 
 def solution(mesh):

time: 74.4 us -> 71.7 us (0.964); the launches traced: 73 us -> 71.2 us
  local copies, waits for them, and re-layouts: 4.8 us -> 1.01 us
  Pallas kernels: 16.5 us -> 20 us
  starting transfers between devices: 28.3 us -> 25.2 us
  waiting for transfers between devices: 18 us -> 20.4 us
    unnamed x14 -> x6, local copies, waits for them, and re-layouts: 3.8 us -> 0.02 us
    pallas_call x5, Pallas kernels: 15.6 us -> 19.1 us  [the longest x4 17.8 us: in_place(): pl.pallas_call(kernel, in_specs=specs, out_specs=[ANYWHERE, *more_specs],...]
    ppermute x7 -> x6, starting transfers between devices: 18.2 us -> 15.9 us  [shifted(): return lax.ppermute(x, axis, [(i, i + steps) for i in range(n - steps)])]
    ppermute x3, waiting for transfers between devices: 0.01 us -> 1.51 us  [across_cores(): lax.ppermute(x, 'ctx', [(i, i ^ 1) for i in range(n) if i % 2 in sources])]
    ppermute x7 -> x6, waiting for transfers between devices: 18 us -> 18.8 us  [shifted(): return lax.ppermute(x, axis, [(i, i + steps) for i in range(n - steps)])]
    ppermute x3, starting transfers between devices: 10.1 us -> 9.28 us  [across_cores(): lax.ppermute(x, 'ctx', [(i, i ^ 1) for i in range(n) if i % 2 in sources])]
    select_n x4 -> x3, other arithmetic: 4.22 us -> 3.55 us  [circular_tail(): return jnp.where(later[:, None], rows[quota:], rows[:quota])]
  transfers between devices with their start and end apart: 10 -> 9, of which waited for: 4 -> 4; matrix products, arithmetic and copies ran while one was open for 5% -> 4% of each run, Pallas kernels for 18% -> 20%
where the time goes in v10:
time: 71.7 us; the launch traced here: 71.2 us
  starting transfers between devices  25.2 us (35%)
  waiting for transfers between devices  20.4 us (28%)
  Pallas kernels  20 us (28%)
  other arithmetic  3.77 us (5%)
  local copies, waits for them, and re-layouts  1.01 us (1%)
  between operations  0.97 us (1%)
    ppermute x6, waiting for transfers between devices, shifted(): return lax.ppermute(x, axis, [(i, i + steps) for i in range(n - steps)])  18.8 us
    pallas_call x4, Pallas kernels, in_place(): pl.pallas_call(kernel, in_specs=specs, out_specs=[ANYWHERE, *more_specs],...  17.8 us
    ppermute x6, starting transfers between devices, shifted(): return lax.ppermute(x, axis, [(i, i + steps) for i in range(n - steps)])  15.9 us
    ppermute x3, starting transfers between devices, across_cores(): lax.ppermute(x, 'ctx', [(i, i ^ 1) for i in range(n) if i % 2 in sources])  9.28 us
    select_n x3, other arithmetic, circular_tail(): return jnp.where(later[:, None], rows[quota:], rows[:quota])  3.55 us
    ppermute x3, waiting for transfers between devices, across_cores(): lax.ppermute(x, 'ctx', [(i, i ^ 1) for i in range(n) if i % 2 in sources])  1.51 us
  transfers between devices with their start and end apart: 9, of which 4 were waited for; matrix products, arithmetic and copies ran while one was open for 4% of the time, Pallas kernels for 20%

profile of v10, /device:TPU:21, one launch (start us, length us, event | category | flops | bytes accessed | tf_op | source)
XLA Modules:
  0.0 71.2 jit_solution(13124785003668018177)
XLA Ops:
  0.0 0.0 copy-start.2
  0.8 0.0 copy-start
  0.8 1.5 %bitcast_select_fusion.4 = (bf16[128,1024]{1,0:T(8,128)(2,1)S(1)}, bf16[128,1024]{1,0:T(8,128)(2,1)S(1)}) fusion(bf16[1,256,1024]{2,1,0:T(8,128)(2,1)} %param.6, pred[128]{0:T(512)(128)(4,1)S(1)} %add_compare_fusion, bf16[1,256,1024]{2,1,0:T(8,128)(2,1)} %param.7), kind=kLoop, calls=%fused_computation.6 | loop fusion | flops 262144 | bytes 1572992 | tf_op jit(solution)/shard_map/jit(_where)/select_n | solution.py:338
  2.2 0.1 maximum_maximum_fusion
  2.3 3.1 %collective-permute-start = (bf16[128,2176]{1,0:T(8,128)(2,1)S(1)}, bf16[128,2176]{1,0:T(8,128)(2,1)S(1)}, u32[]{:S(2)}, u32[]{:S(2)}) collective-permute-start(bf16[128,2176]{1,0:T(8,128)(2,1)S(1)} %maximum_maximum_fusion), channel_id=1, source_target_pairs={{0,8},{8,16},{16,24},{1,9},{9,17},{17,25},{2,10},{10,18},{18,26},{... | collective-permute-start | bytes 1671176 | tf_op jit(solution)/shard_map/ppermute | solution.py:29
  5.5 0.0 copy-done.2
  5.5 1.0 %slice_bitcast_fusion = (bf16[128,1024]{1,0:T(8,128)(2,1)S(1)}, bf16[128,1024]{1,0:T(8,128)(2,1)S(1)}) fusion(bf16[1,256,1024]{2,1,0:T(8,128)(2,1)} %param.7, bf16[1,256,1024]{2,1,0:T(8,128)(2,1)S(1)} %copy-done.2), kind=kLoop, calls=%fused_computation.7 | loop fusion | bytes 1048576 | tf_op jit(solution)/shard_map/slice | solution.py:338
  6.5 0.0 copy-done
  6.5 1.1 %bitcast_select_fusion.1 = (bf16[128,2560]{1,0:T(8,128)(2,1)}, bf16[128,2560]{1,0:T(8,128)(2,1)S(1)}) fusion(bf16[1,256,8192]{2,1,0:T(8,128)(2,1)S(1)} %copy-done, pred[128]{0:T(512)(128)(4,1)S(1)} %add_compare_fusion), kind=kLoop, calls=%fused_computation.1 | loop fusion | flops 655360 | bytes 3932288 | tf_op jit(solution)/shard_map/jit(_where)/select_n | solution.py:338
  7.6 1.0 %bitcast_select_fusion = bf16[128,3072]{1,0:T(8,128)(2,1)} fusion(bf16[1,256,8192]{2,1,0:T(8,128)(2,1)S(1)} %copy-done, pred[128]{0:T(512)(128)(4,1)S(1)} %add_compare_fusion), kind=kLoop, calls=%fused_computation | loop fusion | flops 393216 | bytes 2359424 | tf_op jit(solution)/shard_map/jit(_where)/select_n | solution.py:338
  8.6 1.9 %collective-permute-start.2 = (bf16[128,2560]{1,0:T(8,128)(2,1)S(1)}, bf16[128,2560]{1,0:T(8,128)(2,1)S(1)}, u32[]{:S(2)}, u32[]{:S(2)}) collective-permute-start(bf16[128,2560]{1,0:T(8,128)(2,1)S(1)} %get-tuple-element.30), channel_id=1, source_target_pairs={{0,8},{8,16},{16,24},{1,9},{9,17},{17,25},{2,10},{10,18},{18,26},{... | collective-permute-start | bytes 1966088 | tf_op jit(solution)/shard_map/ppermute | solution.py:29
  10.5 0.0 copy-start.1
  10.6 1.3 %stage_local.1.in_hbm = bf16[1,128,8192]{2,1,0:T(8,128)(2,1)} custom-call(bf16[1,256,8192]{2,1,0:T(8,128)(2,1)S(1)} %copy-done), custom_call_target="tpu_custom_call" | custom-call | tf_op jit(solution)/shard_map/stage_local/pallas_call | solution.py:142
  11.9 0.1 pad_add_fusion.shift_ref
  12.0 6.6 %collective-permute-done.arrived_ref = bf16[128,2176]{1,0:T(8,128)(2,1)S(1)} collective-permute-done((bf16[128,2176]{1,0:T(8,128)(2,1)S(1)}, bf16[128,2176]{1,0:T(8,128)(2,1)S(1)}, u32[]{:S(2)}, u32[]{:S(2)}) %collective-permute-start) | collective-permute-done | bytes 557088 | tf_op jit(solution)/shard_map/ppermute | solution.py:29
  18.6 0.0 copy-done.1
  18.6 0.9 %settle_kv.1 = (bf16[128,2176]{1,0:T(8,128)(2,1)S(1)}, bf16[128,256]{1,0:T(8,128)(2,1)S(1)}) custom-call(s32[2]{0:T(128)S(1)} %pad_add_fusion.shift_ref, s32[1,128]{1,0:T(1,128)S(1)} %copy-done.1, bf16[128,2176]{1,0:T(8,128)(2,1)S(1)} %collective-permute-done.arrived_ref, bf16[128,2048]{1,0:T(8,128)(2,1)S(1)} %pad_maximum_fusion.local_ref), custom_call_target="tpu_custom_call" | custom-call | tf_op jit(solution)/shard_map/settle_kv/pallas_call | solution.py:82
  19.5 3.2 %collective-permute-start.1 = (bf16[128,2176]{1,0:T(8,128)(2,1)S(1)}, bf16[128,2176]{1,0:T(8,128)(2,1)S(1)}, u32[]{:S(2)}, u32[]{:S(2)}) collective-permute-start(bf16[128,2176]{1,0:T(8,128)(2,1)S(1)} %get-tuple-element.27.refs_0_), channel_id=1, source_target_pairs={{0,2},{1,3},{2,4},{3,5},{4,6},{5,7},{8,10},{9,11},{10,12},{11,13},... | collective-permute-start | bytes 1671176 | tf_op jit(solution)/shard_map/ppermute | solution.py:29
  22.7 2.2 %collective-permute-start.5 = (bf16[128,3072]{1,0:T(8,128)(2,1)}, bf16[128,3072]{1,0:T(8,128)(2,1)S(1)}, u32[]{:S(2)}, u32[]{:S(2)}) collective-permute-start(bf16[128,3072]{1,0:T(8,128)(2,1)} %bitcast_select_fusion), channel_id=1, source_target_pairs={{0,8},{8,16},{16,24},{1,9},{9,17},{17,25},{2,10},{10,18},{18,26},{... | collective-permute-start | bytes 2359304 | tf_op jit(solution)/shard_map/ppermute | solution.py:29
  24.9 7.7 %collective-permute-done.2.arrived_ref = bf16[128,2560]{1,0:T(8,128)(2,1)S(1)} collective-permute-done((bf16[128,2560]{1,0:T(8,128)(2,1)S(1)}, bf16[128,2560]{1,0:T(8,128)(2,1)S(1)}, u32[]{:S(2)}, u32[]{:S(2)}) %collective-permute-start.2) | collective-permute-done | bytes 655392 | tf_op jit(solution)/shard_map/ppermute | solution.py:29
  32.7 2.3 %place_queries.2.in_hbm = bf16[1,128,8192]{2,1,0:T(8,128)(2,1)} custom-call(bf16[128,256]{1,0:T(8,128)(2,1)S(1)} %get-tuple-element.28.hot_ref.refs_6_, bf16[128,2560]{1,0:T(8,128)(2,1)S(1)} %collective-permute-done.2.arrived_ref, bf16[1,128,8192]{2,1,0:T(8,128)(2,1)} %stage_local.1.in_hbm), custom_call_target="tpu_custom_call", output_to_operand_aliasing={{}: (2, {})} | custom-call | tf_op jit(solution)/shard_map/place_queries/pallas_call | solution.py:123
  35.0 0.0 collective-permute-done.1.refs_1_
  35.0 3.2 %collective-permute-start.4 = (bf16[128,2176]{1,0:T(8,128)(2,1)S(1)}, bf16[128,2176]{1,0:T(8,128)(2,1)S(1)}, u32[]{:S(2)}, u32[]{:S(2)}) collective-permute-start(bf16[128,2176]{1,0:T(8,128)(2,1)S(1)} %collective-permute-done.1.refs_1_), channel_id=1, source_target_pairs={{0,2},{1,3},{2,4},{3,5},{4,6},{5,7},{8,10},{9,11},{10,12},{11,13},... | collective-permute-start | bytes 1671176 | tf_op jit(solution)/shard_map/ppermute | solution.py:29
  38.2 2.2 %collective-permute-start.8 = (bf16[128,2560]{1,0:T(8,128)(2,1)}, bf16[128,2560]{1,0:T(8,128)(2,1)}, u32[]{:S(2)}, u32[]{:S(2)}) collective-permute-start(bf16[128,2560]{1,0:T(8,128)(2,1)} %get-tuple-element.36), channel_id=1, source_target_pairs={{0,8},{8,16},{16,24},{1,9},{9,17},{17,25},{2,10},{10,18},{18,26},{... | collective-permute-start | bytes 1966088 | tf_op jit(solution)/shard_map/ppermute | solution.py:29
  40.4 1.3 %collective-permute-start.7 = (bf16[128,2176]{1,0:T(8,128)(2,1)S(1)}, bf16[128,2176]{1,0:T(8,128)(2,1)S(1)}, u32[]{:S(2)}, u32[]{:S(2)}) collective-permute-start(bf16[128,2176]{1,0:T(8,128)(2,1)S(1)} %get-tuple-element.27.refs_0_), channel_id=1, source_target_pairs={{0,1},{2,3},{4,5},{6,7},{8,9},{10,11},{12,13},{14,15},{16,17},{18,... | collective-permute-start | bytes 1671176 | tf_op jit(solution)/shard_map/ppermute | solution.py:34
  41.7 3.4 %collective-permute-start.3 = (bf16[128,2176]{1,0:T(8,128)(2,1)S(1)}, bf16[128,2176]{1,0:T(8,128)(2,1)S(1)}, u32[]{:S(2)}, u32[]{:S(2)}) collective-permute-start(bf16[128,2176]{1,0:T(8,128)(2,1)S(1)} %collective-permute-done.1.refs_1_), channel_id=1, source_target_pairs={{0,1},{1,0},{2,3},{3,2},{4,5},{5,4},{6,7},{7,6},{8,9},{9,8},{10,11... | collective-permute-start | bytes 1671176 | tf_op jit(solution)/shard_map/ppermute | solution.py:34
  45.1 4.5 %collective-permute-done.5.arrived_ref = bf16[128,3072]{1,0:T(8,128)(2,1)S(1)} collective-permute-done((bf16[128,3072]{1,0:T(8,128)(2,1)}, bf16[128,3072]{1,0:T(8,128)(2,1)S(1)}, u32[]{:S(2)}, u32[]{:S(2)}) %collective-permute-start.5) | collective-permute-done | bytes 786464 | tf_op jit(solution)/shard_map/ppermute | solution.py:29
  49.5 2.4 %place_queries.3.refs_6_ = bf16[1,128,8192]{2,1,0:T(8,128)(2,1)} custom-call(bf16[128,256]{1,0:T(8,128)(2,1)S(1)} %get-tuple-element.28.hot_ref.refs_6_, bf16[128,3072]{1,0:T(8,128)(2,1)S(1)} %collective-permute-done.5.arrived_ref, bf16[1,128,8192]{2,1,0:T(8,128)(2,1)} %place_queries.2.in_hbm), custom_call_target="tpu_custom_call", output_to_operand_aliasing={{}: (2, {})} | custom-call | tf_op jit(solution)/shard_map/place_queries/pallas_call | solution.py:123
  51.9 0.0 collective-permute-done.4.refs_3_
  51.9 4.6 %collective-permute-start.6 = (bf16[128,2176]{1,0:T(8,128)(2,1)S(1)}, bf16[128,2176]{1,0:T(8,128)(2,1)S(1)}, u32[]{:S(2)}, u32[]{:S(2)}) collective-permute-start(bf16[128,2176]{1,0:T(8,128)(2,1)S(1)} %collective-permute-done.4.refs_3_), channel_id=1, source_target_pairs={{1,0},{3,2},{5,4},{7,6},{9,8},{11,10},{13,12},{15,14},{17,16},{19,... | collective-permute-start | bytes 1671176 | tf_op jit(solution)/shard_map/ppermute | solution.py:34
  56.6 0.0 collective-permute-done.7.refs_5_
  56.6 0.0 collective-permute-done.3.refs_2_
  56.6 1.5 %collective-permute-done.6.refs_4_ = bf16[128,2176]{1,0:T(8,128)(2,1)S(1)} collective-permute-done((bf16[128,2176]{1,0:T(8,128)(2,1)S(1)}, bf16[128,2176]{1,0:T(8,128)(2,1)S(1)}, u32[]{:S(2)}, u32[]{:S(2)}) %collective-permute-start.6) | collective-permute-done | bytes 557088 | tf_op jit(solution)/shard_map/ppermute | solution.py:34
  58.1 7.7 %attend_early.1 = (bf16[1,128,8192]{2,1,0:T(8,128)(2,1)}, bf16[128,5632]{1,0:T(8,128)(2,1)S(1)}, bf16[128,2560]{1,0:T(8,128)(2,1)S(1)}) custom-call(s32[1]{0:T(128)} %bitcast.rank_ref, bf16[128,2176]{1,0:T(8,128)(2,1)S(1)} %get-tuple-element.27.refs_0_, bf16[128,2176]{1,0:T(8,128)(2,1)S(1)} %collective-permute-done.1.refs_1_, ...), custom_call_target="tpu_custom_call", output_to_operand_aliasing={{0}: (7, {})} | custom-call | tf_op jit(solution)/shard_map/attend_early/pallas_call | solution.py:123
  65.8 0.0 collective-permute-done.8.refs_7_
  65.8 5.4 %attend_late.1 = bf16[1,128,8192]{2,1,0:T(8,128)(2,1)} custom-call(s32[1]{0:T(128)} %bitcast.rank_ref, bf16[128,2176]{1,0:T(8,128)(2,1)S(1)} %get-tuple-element.27.refs_0_, bf16[128,2176]{1,0:T(8,128)(2,1)S(1)} %collective-permute-done.1.refs_1_, bf16[128,2176]{1,0:T(8,128)(2,1)S(1)} %collective-permute-done.3.refs_2_, ...), custom_call_target="tpu_custom_call", output_to_operand_aliasing={{}: (11, {})} | custom-call | tf_op jit(solution)/shard_map/attend_late/pallas_call | solution.py:123
  (4 shorter events, 0.1 us)
Async XLA Ops:
  0.0 5.5 %copy-start.2 = (bf16[1,256,1024]{2,1,0:T(8,128)(2,1)S(1)}, bf16[1,256,1024]{2,1,0:T(8,128)(2,1)}, u32[]{:S(2)}) copy-start(bf16[1,256,1024]{2,1,0:T(8,128)(2,1)} %param.6) | copy-start | bytes 1572868
  0.8 5.8 %copy-start = (bf16[1,256,8192]{2,1,0:T(8,128)(2,1)S(1)}, bf16[1,256,8192]{2,1,0:T(8,128)(2,1)}, u32[]{:S(2)}) copy-start(bf16[1,256,8192]{2,1,0:T(8,128)(2,1)} %q_hbm.1) | copy-start | bytes 12582916
  2.3 16.3 %collective-permute-start = (bf16[128,2176]{1,0:T(8,128)(2,1)S(1)}, bf16[128,2176]{1,0:T(8,128)(2,1)S(1)}, u32[]{:S(2)}, u32[]{:S(2)}) collective-permute-start(bf16[128,2176]{1,0:T(8,128)(2,1)S(1)} %maximum_maximum_fusion), channel_id=1, source_target_pairs={{0,8},{8,16},{16,24},{1,9},{9,17},{17,25},{2,10},{10,18},{18,26},{... | collective-permute-start | bytes 1671176 | tf_op jit(solution)/shard_map/ppermute | solution.py:29
  8.6 24.0 %collective-permute-start.2 = (bf16[128,2560]{1,0:T(8,128)(2,1)S(1)}, bf16[128,2560]{1,0:T(8,128)(2,1)S(1)}, u32[]{:S(2)}, u32[]{:S(2)}) collective-permute-start(bf16[128,2560]{1,0:T(8,128)(2,1)S(1)} %get-tuple-element.30), channel_id=1, source_target_pairs={{0,8},{8,16},{16,24},{1,9},{9,17},{17,25},{2,10},{10,18},{18,26},{... | collective-permute-start | bytes 1966088 | tf_op jit(solution)/shard_map/ppermute | solution.py:29
  10.5 8.1 %copy-start.1 = (s32[1,128]{1,0:T(1,128)S(1)}, s32[1,128]{1,0:T(1,128)}, u32[]{:S(2)}) copy-start(s32[1,128]{1,0:T(1,128)} %docs_ref.1) | copy-start | bytes 1540
  19.5 15.5 %collective-permute-start.1 = (bf16[128,2176]{1,0:T(8,128)(2,1)S(1)}, bf16[128,2176]{1,0:T(8,128)(2,1)S(1)}, u32[]{:S(2)}, u32[]{:S(2)}) collective-permute-start(bf16[128,2176]{1,0:T(8,128)(2,1)S(1)} %get-tuple-element.27.refs_0_), channel_id=1, source_target_pairs={{0,2},{1,3},{2,4},{3,5},{4,6},{5,7},{8,10},{9,11},{10,12},{11,13},... | collective-permute-start | bytes 1671176 | tf_op jit(solution)/shard_map/ppermute | solution.py:29
  22.7 26.8 %collective-permute-start.5 = (bf16[128,3072]{1,0:T(8,128)(2,1)}, bf16[128,3072]{1,0:T(8,128)(2,1)S(1)}, u32[]{:S(2)}, u32[]{:S(2)}) collective-permute-start(bf16[128,3072]{1,0:T(8,128)(2,1)} %bitcast_select_fusion), channel_id=1, source_target_pairs={{0,8},{8,16},{16,24},{1,9},{9,17},{17,25},{2,10},{10,18},{18,26},{... | collective-permute-start | bytes 2359304 | tf_op jit(solution)/shard_map/ppermute | solution.py:29
  35.0 17.0 %collective-permute-start.4 = (bf16[128,2176]{1,0:T(8,128)(2,1)S(1)}, bf16[128,2176]{1,0:T(8,128)(2,1)S(1)}, u32[]{:S(2)}, u32[]{:S(2)}) collective-permute-start(bf16[128,2176]{1,0:T(8,128)(2,1)S(1)} %collective-permute-done.1.refs_1_), channel_id=1, source_target_pairs={{0,2},{1,3},{2,4},{3,5},{4,6},{5,7},{8,10},{9,11},{10,12},{11,13},... | collective-permute-start | bytes 1671176 | tf_op jit(solution)/shard_map/ppermute | solution.py:29
  38.2 27.6 %collective-permute-start.8 = (bf16[128,2560]{1,0:T(8,128)(2,1)}, bf16[128,2560]{1,0:T(8,128)(2,1)}, u32[]{:S(2)}, u32[]{:S(2)}) collective-permute-start(bf16[128,2560]{1,0:T(8,128)(2,1)} %get-tuple-element.36), channel_id=1, source_target_pairs={{0,8},{8,16},{16,24},{1,9},{9,17},{17,25},{2,10},{10,18},{18,26},{... | collective-permute-start | bytes 1966088 | tf_op jit(solution)/shard_map/ppermute | solution.py:29
  40.4 16.2 %collective-permute-start.7 = (bf16[128,2176]{1,0:T(8,128)(2,1)S(1)}, bf16[128,2176]{1,0:T(8,128)(2,1)S(1)}, u32[]{:S(2)}, u32[]{:S(2)}) collective-permute-start(bf16[128,2176]{1,0:T(8,128)(2,1)S(1)} %get-tuple-element.27.refs_0_), channel_id=1, source_target_pairs={{0,1},{2,3},{4,5},{6,7},{8,9},{10,11},{12,13},{14,15},{16,17},{18,... | collective-permute-start | bytes 1671176 | tf_op jit(solution)/shard_map/ppermute | solution.py:34
  41.7 14.9 %collective-permute-start.3 = (bf16[128,2176]{1,0:T(8,128)(2,1)S(1)}, bf16[128,2176]{1,0:T(8,128)(2,1)S(1)}, u32[]{:S(2)}, u32[]{:S(2)}) collective-permute-start(bf16[128,2176]{1,0:T(8,128)(2,1)S(1)} %collective-permute-done.1.refs_1_), channel_id=1, source_target_pairs={{0,1},{1,0},{2,3},{3,2},{4,5},{5,4},{6,7},{7,6},{8,9},{9,8},{10,11... | collective-permute-start | bytes 1671176 | tf_op jit(solution)/shard_map/ppermute | solution.py:34
  51.9 6.2 %collective-permute-start.6 = (bf16[128,2176]{1,0:T(8,128)(2,1)S(1)}, bf16[128,2176]{1,0:T(8,128)(2,1)S(1)}, u32[]{:S(2)}, u32[]{:S(2)}) collective-permute-start(bf16[128,2176]{1,0:T(8,128)(2,1)S(1)} %collective-permute-done.4.refs_3_), channel_id=1, source_target_pairs={{1,0},{3,2},{5,4},{7,6},{9,8},{11,10},{13,12},{15,14},{17,16},{19,... | collective-permute-start | bytes 1671176 | tf_op jit(solution)/shard_map/ppermute | solution.py:34

commit v11 on v10

--- a/solution.py
+++ b/solution.py
@@ -16,7 +16,7 @@
 NOTE = 2 * KV_WIDTH
 MASKED = -1e30
 HALF = GROUP // 2
-CHUNKS = (20, 24, 20)
+CHUNKS = (20, 26, 18)
 VMEM_GRANT = 48 * 1024 * 1024
 
 WHOLE = pl.BlockSpec(memory_space=pltpu.VMEM)
@@ -57,6 +57,33 @@
 def place_rows(hot, arrived, local):
     both = jnp.concatenate([arrived, local], axis=0)
     return jnp.dot(hot, both, preferred_element_type=jnp.float32).astype(jnp.bfloat16)
+
+
+def pack_kernel(counts_ref, k_ref, v_ref, tail_ref, local_ref):
+    quota = tail_ref.shape[0]
+    own_count = counts_ref[0, 0]
+    row = lax.broadcasted_iota(jnp.int32, (quota, KV_WIDTH), 0)
+    later = quota + row < own_count
+    for at, ref in ((0, k_ref), (KV_WIDTH, v_ref)):
+        first = ref[0, :quota]
+        local_ref[:, at : at + KV_WIDTH] = first
+        tail_ref[:, at : at + KV_WIDTH] = jnp.where(later, ref[0, quota:], first)
+    note = jnp.full((quota, quota), own_count, jnp.int32).astype(jnp.float32)
+    tail_ref[:, NOTE:] = note.astype(jnp.bfloat16)
+
+
+def pack_kv(counts, k_rows, v_rows, quota):
+    return pl.pallas_call(
+        pack_kernel,
+        in_specs=[SCALARS, WHOLE, WHOLE],
+        out_specs=[WHOLE, WHOLE],
+        out_shape=[
+            jax.ShapeDtypeStruct((quota, NOTE + quota), jnp.bfloat16),
+            jax.ShapeDtypeStruct((quota, NOTE), jnp.bfloat16),
+        ],
+        compiler_params=pltpu.CompilerParams(vmem_limit_bytes=VMEM_GRANT),
+        name="pack_kv",
+    )(counts, k_rows, v_rows)
 
 
 def settle_kernel(shift_ref, docs_ref, arrived_ref, local_ref, out_ref, hot_ref):
@@ -118,6 +145,27 @@
     return found
 
 
+def copies(origin, target, steps, at, to, sem):
+    return [
+        pltpu.make_async_copy(
+            origin.at[:, head_columns(head - at, heads)],
+            target.at[:, head_columns(head - to, heads)],
+            sem.at[i],
+        )
+        for i, (head, heads) in enumerate(steps)
+    ]
+
+
+def start_all(started):
+    for copy in started:
+        copy.start()
+
+
+def wait_all(started):
+    for copy in started:
+        copy.wait()
+
+
 def in_place(kernel, operands, out, more_out=(), more_specs=(), **arguments):
     specs = arguments.pop("in_specs") + [ANYWHERE]
     return pl.pallas_call(
@@ -150,18 +198,17 @@
     )(q_rows)
 
 
-def place_kernel(first, hot_ref, arrived_ref, in_hbm, out_hbm, local, placed, in_sem, out_sem):
-    quota, width = arrived_ref.shape
-    cols = head_columns(first, width // HEAD_SIZE)
-    fetch = pltpu.make_async_copy(in_hbm.at[0, :, cols], local, in_sem)
-    fetch.start()
-    fetch.wait()
-    for head, heads in pieces(first, width // HEAD_SIZE):
-        own = head_columns(head - first, heads)
-        placed[:, own] = place_rows(hot_ref[...], arrived_ref[:, own], local[:, own])
-    store = pltpu.make_async_copy(placed, out_hbm.at[0, :, cols], out_sem)
-    store.start()
-    store.wait()
+def place_kernel(first, hot_ref, arrived_ref, in_hbm, out_hbm, local, placed, in_sems, out_sems):
+    steps = pieces(first, arrived_ref.shape[1] // HEAD_SIZE)
+    fetches = copies(in_hbm.at[0], local, steps, 0, first, in_sems)
+    stores = copies(placed, out_hbm.at[0], steps, first, 0, out_sems)
+    start_all(fetches)
+    for i, (head, heads) in enumerate(steps):
+        cols = head_columns(head - first, heads)
+        fetches[i].wait()
+        placed[:, cols] = place_rows(hot_ref[...], arrived_ref[:, cols], local[:, cols])
+        stores[i].start()
+    wait_all(stores)
 
 
 def place_queries(hot, arrived, first, out):
@@ -173,8 +220,8 @@
         scratch_shapes=[
             pltpu.VMEM(arrived.shape, jnp.bfloat16),
             pltpu.VMEM(arrived.shape, jnp.bfloat16),
-            pltpu.SemaphoreType.DMA,
-            pltpu.SemaphoreType.DMA,
+            pltpu.SemaphoreType.DMA((QUERY_HEADS,)),
+            pltpu.SemaphoreType.DMA((QUERY_HEADS,)),
         ],
         name="place_queries",
     )[0]
@@ -261,42 +308,42 @@
 
 def early_kernel(blocks, count, rank_ref, *refs):
     kv_refs, far_ref, mate_ref = refs[: blocks - 1], refs[blocks - 1], refs[blocks]
-    in_hbm, _, result, local, bias, rest, queries, sems = refs[blocks + 1 :]
-    late = head_columns(count, QUERY_HEADS - count)
-    fetch = pltpu.make_async_copy(in_hbm.at[0, :, head_columns(0, count)], queries, sems.at[0])
-    fetch.start()
+    in_hbm, _, result, local, bias, rest, queries, sems, late_sems = refs[blocks + 1 :]
+    fetches = copies(in_hbm.at[0], queries, pieces(0, count), 0, 0, sems)
+    ahead = copies(in_hbm.at[0], local, pieces(count, QUERY_HEADS - count), 0, count, late_sems)
+    start_all(fetches)
     rank = rank_ref[0]
     make_bias(kv_refs, far_ref, mate_ref, bias, rank)
     choose_rest(0, count, lax.rem(rank, 2), far_ref, mate_ref, rest)
-    fetch.wait()
-    ahead = pltpu.make_async_copy(in_hbm.at[0, :, late], local, sems.at[1])
-    ahead.start()
+    wait_all(fetches)
+    start_all(ahead)
     attend_heads(0, count, [*kv_refs, rest], bias, lambda cols: queries[:, cols], result)
-    ahead.wait()
+    wait_all(ahead)
 
 
 def late_kernel(blocks, first, rank_ref, *refs):
     kv_refs, far_ref, mate_ref = refs[: blocks - 1], refs[blocks - 1], refs[blocks]
     hot_ref, arrived_hbm, early_ref, local_ref, _, out_hbm = refs[blocks + 1 : blocks + 7]
-    bias, rest, arrived, result, sems = refs[blocks + 7 :]
+    bias, rest, arrived, result, early_sems, in_sems, out_sems = refs[blocks + 7 :]
     count = QUERY_HEADS - first
-    fetch = pltpu.make_async_copy(arrived_hbm, arrived, sems.at[0])
-    fetch.start()
+    steps = pieces(first, count)
+    fetches = copies(arrived_hbm, arrived, steps, first, first, in_sems)
+    early = copies(early_ref, out_hbm.at[0], pieces(0, first), 0, 0, early_sems)
+    stores = copies(result, out_hbm.at[0], steps, first, 0, out_sems)
+    start_all(fetches)
     rank = rank_ref[0]
     make_bias(kv_refs, far_ref, mate_ref, bias, rank)
     choose_rest(first, count, lax.rem(rank, 2), far_ref, mate_ref, rest)
-    fetch.wait()
-    early = pltpu.make_async_copy(early_ref, out_hbm.at[0, :, head_columns(0, first)], sems.at[1])
-    early.start()
+    wait_all(fetches)
+    start_all(early)
 
     def take(cols):
         return place_rows(hot_ref[...], arrived[:, cols], local_ref[:, cols])
 
     attend_heads(first, count, [*kv_refs, rest], bias, take, result)
-    store = pltpu.make_async_copy(result, out_hbm.at[0, :, head_columns(first, count)], sems.at[2])
-    store.start()
-    early.wait()
-    store.wait()
+    start_all(stores)
+    wait_all(early)
+    wait_all(stores)
 
 
 def attend(rank, hot, arrived, kv_blocks, out):
@@ -305,6 +352,7 @@
     first = QUERY_HEADS - width // HEAD_SIZE
     bias = pltpu.VMEM((quota, blocks * quota), jnp.float32)
     rest = pltpu.VMEM((quota, NOTE), jnp.bfloat16)
+    sems = pltpu.SemaphoreType.DMA((QUERY_HEADS,))
     own = (arrived.shape, jnp.bfloat16)
     others = ((quota, first * HEAD_SIZE), jnp.bfloat16)
     out, result, local = in_place(
@@ -314,7 +362,7 @@
         more_out=[jax.ShapeDtypeStruct(*others), jax.ShapeDtypeStruct(*own)],
         more_specs=[WHOLE, WHOLE],
         in_specs=[SCALARS] + [WHOLE] * len(kv_blocks),
-        scratch_shapes=[bias, rest, pltpu.VMEM(*others), pltpu.SemaphoreType.DMA((2,))],
+        scratch_shapes=[bias, rest, pltpu.VMEM(*others), sems, sems],
         name="attend_early",
     )
     return in_place(
@@ -327,7 +375,9 @@
             rest,
             pltpu.VMEM(*own),
             pltpu.VMEM(*own),
-            pltpu.SemaphoreType.DMA((3,)),
+            sems,
+            sems,
+            sems,
         ],
         name="attend_late",
     )[0]
@@ -345,18 +395,9 @@
     own_count = counts[0, 0]
 
     later = quota + jnp.arange(quota, dtype=jnp.int32) < own_count
-    kv_tail = jnp.concatenate(
-        [
-            circular_tail(k_rows[0], later),
-            circular_tail(value_slot_rows[0], later),
-            jnp.broadcast_to(own_count.astype(jnp.bfloat16), (quota, quota)),
-        ],
-        axis=1,
-    )
-    local_kv = jnp.concatenate([k_rows[0, :quota], value_slot_rows[0, :quota]], axis=1)
-    kv_tail, later = lax.optimization_barrier((kv_tail, later))
+    kv_tail, local_kv = pack_kv(counts, k_rows, value_slot_rows, quota)
+    arrived_kv = shifted(kv_tail, "dp", 1)
     local_kv, later = lax.optimization_barrier((local_kv, later))
-    arrived_kv = shifted(kv_tail, "dp", 1)
     q_tails = []
     first = 0
     for size in CHUNKS:
@@ -381,7 +422,7 @@
             carried, out = lax.optimization_barrier((carried, out))
         if back < rounds:
             kv_blocks.append(across_cores(carried))
-    kv_blocks += [across_cores(carried, (1,)), across_cores(own, (0,))]
+    kv_blocks += [across_cores(carried), across_cores(own, (0,))]
     return attend(rank[None], hot, arrived_q[-1], kv_blocks, out)
 
 

time: 71.7 us -> 76.4 us (1.066)
  Pallas kernels: 20 us -> 25.9 us
  starting transfers between devices: 25.2 us -> 23.3 us
  waiting for transfers between devices: 20.4 us -> 18.6 us
  other arithmetic: 3.77 us -> 5.03 us
  local copies, waits for them, and re-layouts: 1.01 us -> 2.09 us
    pallas_call x4, Pallas kernels: 17.8 us -> 23.6 us  [in_place(): pl.pallas_call(kernel, in_specs=specs, out_specs=[ANYWHERE, *more_specs],...]
    unnamed x6 -> x8, local copies, waits for them, and re-layouts: 0.02 us -> 2.09 us
    ppermute x3, starting transfers between devices: 9.28 us -> 7.39 us  [across_cores(): lax.ppermute(x, 'ctx', [(i, i ^ 1) for i in range(n) if i % 2 in sources])]
    ppermute x6, waiting for transfers between devices: 18.8 us -> 17 us  [shifted(): return lax.ppermute(x, axis, [(i, i + steps) for i in range(n - steps)])]
    select_n x3, other arithmetic: 3.55 us -> 4.95 us  [circular_tail(): return jnp.where(later[:, None], rows[quota:], rows[:quota])]
    slice x1 -> x0, local copies, waits for them, and re-layouts: 0.99 us -> none  [circular_tail(): return jnp.where(later[:, None], rows[quota:], rows[:quota])]
  transfers between devices with their start and end apart: 9 -> 9, of which waited for: 4 -> 4; matrix products, arithmetic and copies ran while one was open for 4% -> 7% of each run, Pallas kernels for 20% -> 25%
where the time goes in v11:
time: 76.4 us; the launch traced here: 75.9 us
  Pallas kernels  25.9 us (34%)
  starting transfers between devices  23.3 us (30%)
  waiting for transfers between devices  18.6 us (24%)
  other arithmetic  5.03 us (7%)
  local copies, waits for them, and re-layouts  2.09 us (3%)
  between operations  1.01 us (1%)
    pallas_call x4, Pallas kernels, in_place(): pl.pallas_call(kernel, in_specs=specs, out_specs=[ANYWHERE, *more_specs],...  23.6 us
    ppermute x6, waiting for transfers between devices, shifted(): return lax.ppermute(x, axis, [(i, i + steps) for i in range(n - steps)])  17 us
    ppermute x6, starting transfers between devices, shifted(): return lax.ppermute(x, axis, [(i, i + steps) for i in range(n - steps)])  15.9 us
    ppermute x3, starting transfers between devices, across_cores(): lax.ppermute(x, 'ctx', [(i, i ^ 1) for i in range(n) if i % 2 in sources])  7.39 us
    select_n x3, other arithmetic, circular_tail(): return jnp.where(later[:, None], rows[quota:], rows[:quota])  4.95 us
    unnamed x8, local copies, waits for them, and re-layouts  2.09 us
    ppermute x3, waiting for transfers between devices, across_cores(): lax.ppermute(x, 'ctx', [(i, i ^ 1) for i in range(n) if i % 2 in sources])  1.58 us
  transfers between devices with their start and end apart: 9, of which 4 were waited for; matrix products, arithmetic and copies ran while one was open for 7% of the time, Pallas kernels for 25%

profile of v11, /device:TPU:21, one launch (start us, length us, event | category | flops | bytes accessed | tf_op | source)
XLA Modules:
  0.0 75.9 jit_solution(7547397302418818784)
XLA Ops:
  0.7 0.0 copy-start.1
  0.7 1.0 %copy-done.1 = bf16[1,256,1024]{2,1,0:T(8,128)(2,1)S(1)} copy-done((bf16[1,256,1024]{2,1,0:T(8,128)(2,1)S(1)}, bf16[1,256,1024]{2,1,0:T(8,128)(2,1)}, u32[]{:S(2)}) %copy-start.1) | copy-done | bytes 524312
  1.7 0.0 copy-start.2
  1.7 1.0 %copy-done.2 = bf16[1,256,1024]{2,1,0:T(8,128)(2,1)S(1)} copy-done((bf16[1,256,1024]{2,1,0:T(8,128)(2,1)S(1)}, bf16[1,256,1024]{2,1,0:T(8,128)(2,1)}, u32[]{:S(2)}) %copy-start.2) | copy-done | bytes 524312
  2.7 0.1 pack_kv.1
  2.8 3.1 %collective-permute-start = (bf16[128,2176]{1,0:T(8,128)(2,1)S(1)}, bf16[128,2176]{1,0:T(8,128)(2,1)S(1)}, u32[]{:S(2)}, u32[]{:S(2)}) collective-permute-start(bf16[128,2176]{1,0:T(8,128)(2,1)S(1)} %get-tuple-element.23), channel_id=1, source_target_pairs={{0,8},{8,16},{16,24},{1,9},{9,17},{17,25},{2,10},{10,18},{18,26},{... | collective-permute-start | bytes 1671176 | tf_op jit(solution)/shard_map/ppermute | solution.py:29
  6.0 0.0 copy-start
  6.0 2.4 %bitcast_select_fusion.2 = bf16[128,2304]{1,0:T(8,128)(2,1)} fusion(bf16[1,256,8192]{2,1,0:T(8,128)(2,1)} %q_hbm.1, pred[128]{0:T(512)(128)(4,1)S(1)} %add_compare_fusion), kind=kLoop, calls=%fused_computation.2 | loop fusion | flops 294912 | bytes 1769600 | tf_op jit(solution)/shard_map/jit(_where)/select_n | solution.py:388
  8.3 2.5 %bitcast_select_fusion = bf16[128,3328]{1,0:T(8,128)(2,1)} fusion(bf16[1,256,8192]{2,1,0:T(8,128)(2,1)} %q_hbm.1, pred[128]{0:T(512)(128)(4,1)S(1)} %add_compare_fusion), kind=kLoop, calls=%fused_computation | loop fusion | flops 425984 | bytes 2556032 | tf_op jit(solution)/shard_map/jit(_where)/select_n | solution.py:388
  10.8 0.0 copy-done
  10.8 0.1 bitcast_select_fusion.1
  10.9 1.9 %collective-permute-start.2 = (bf16[128,2560]{1,0:T(8,128)(2,1)S(1)}, bf16[128,2560]{1,0:T(8,128)(2,1)S(1)}, u32[]{:S(2)}, u32[]{:S(2)}) collective-permute-start(bf16[128,2560]{1,0:T(8,128)(2,1)S(1)} %bitcast_select_fusion.1), channel_id=1, source_target_pairs={{0,8},{8,16},{16,24},{1,9},{9,17},{17,25},{2,10},{10,18},{18,26},{... | collective-permute-start | bytes 1966088 | tf_op jit(solution)/shard_map/ppermute | solution.py:29
  12.9 0.0 copy-start.3
  12.9 1.3 %stage_local.1.in_hbm = bf16[1,128,8192]{2,1,0:T(8,128)(2,1)} custom-call(bf16[1,256,8192]{2,1,0:T(8,128)(2,1)S(1)} %copy-done), custom_call_target="tpu_custom_call" | custom-call | tf_op jit(solution)/shard_map/stage_local/pallas_call | solution.py:190
  14.2 0.1 pad_add_fusion.shift_ref
  14.3 4.8 %collective-permute-done.arrived_ref = bf16[128,2176]{1,0:T(8,128)(2,1)S(1)} collective-permute-done((bf16[128,2176]{1,0:T(8,128)(2,1)S(1)}, bf16[128,2176]{1,0:T(8,128)(2,1)S(1)}, u32[]{:S(2)}, u32[]{:S(2)}) %collective-permute-start) | collective-permute-done | bytes 557088 | tf_op jit(solution)/shard_map/ppermute | solution.py:29
  19.1 0.0 copy-done.3
  19.1 0.9 %settle_kv.1 = (bf16[128,2176]{1,0:T(8,128)(2,1)S(1)}, bf16[128,256]{1,0:T(8,128)(2,1)S(1)}) custom-call(s32[2]{0:T(128)S(1)} %pad_add_fusion.shift_ref, s32[1,128]{1,0:T(1,128)S(1)} %copy-done.3, bf16[128,2176]{1,0:T(8,128)(2,1)S(1)} %collective-permute-done.arrived_ref, bf16[128,2048]{1,0:T(8,128)(2,1)S(1)} %get-tuple-element.26.local_ref), custom_call_target="tpu_custom_call" | custom-call | tf_op jit(solution)/shard_map/settle_kv/pallas_call | solution.py:109
  20.0 3.2 %collective-permute-start.1 = (bf16[128,2176]{1,0:T(8,128)(2,1)S(1)}, bf16[128,2176]{1,0:T(8,128)(2,1)S(1)}, u32[]{:S(2)}, u32[]{:S(2)}) collective-permute-start(bf16[128,2176]{1,0:T(8,128)(2,1)S(1)} %get-tuple-element.27.refs_0_), channel_id=1, source_target_pairs={{0,2},{1,3},{2,4},{3,5},{4,6},{5,7},{8,10},{9,11},{10,12},{11,13},... | collective-permute-start | bytes 1671176 | tf_op jit(solution)/shard_map/ppermute | solution.py:29
  23.2 2.2 %collective-permute-start.5 = (bf16[128,3328]{1,0:T(8,128)(2,1)}, bf16[128,3328]{1,0:T(8,128)(2,1)S(1)}, u32[]{:S(2)}, u32[]{:S(2)}) collective-permute-start(bf16[128,3328]{1,0:T(8,128)(2,1)} %bitcast_select_fusion), channel_id=1, source_target_pairs={{0,8},{8,16},{16,24},{1,9},{9,17},{17,25},{2,10},{10,18},{18,26},{... | collective-permute-start | bytes 2555912 | tf_op jit(solution)/shard_map/ppermute | solution.py:29
  25.4 7.7 %collective-permute-done.2.arrived_ref = bf16[128,2560]{1,0:T(8,128)(2,1)S(1)} collective-permute-done((bf16[128,2560]{1,0:T(8,128)(2,1)S(1)}, bf16[128,2560]{1,0:T(8,128)(2,1)S(1)}, u32[]{:S(2)}, u32[]{:S(2)}) %collective-permute-start.2) | collective-permute-done | bytes 655392 | tf_op jit(solution)/shard_map/ppermute | solution.py:29
  33.2 3.7 %place_queries.2.in_hbm = bf16[1,128,8192]{2,1,0:T(8,128)(2,1)} custom-call(bf16[128,256]{1,0:T(8,128)(2,1)S(1)} %get-tuple-element.28.hot_ref.refs_6_, bf16[128,2560]{1,0:T(8,128)(2,1)S(1)} %collective-permute-done.2.arrived_ref, bf16[1,128,8192]{2,1,0:T(8,128)(2,1)} %stage_local.1.in_hbm), custom_call_target="tpu_custom_call", output_to_operand_aliasing={{}: (2, {})} | custom-call | tf_op jit(solution)/shard_map/place_queries/pallas_call | solution.py:171
  36.8 0.0 collective-permute-done.1.refs_1_
  36.8 3.2 %collective-permute-start.4 = (bf16[128,2176]{1,0:T(8,128)(2,1)S(1)}, bf16[128,2176]{1,0:T(8,128)(2,1)S(1)}, u32[]{:S(2)}, u32[]{:S(2)}) collective-permute-start(bf16[128,2176]{1,0:T(8,128)(2,1)S(1)} %collective-permute-done.1.refs_1_), channel_id=1, source_target_pairs={{0,2},{1,3},{2,4},{3,5},{4,6},{5,7},{8,10},{9,11},{10,12},{11,13},... | collective-permute-start | bytes 1671176 | tf_op jit(solution)/shard_map/ppermute | solution.py:29
  40.0 2.2 %collective-permute-start.8 = (bf16[128,2304]{1,0:T(8,128)(2,1)}, bf16[128,2304]{1,0:T(8,128)(2,1)}, u32[]{:S(2)}, u32[]{:S(2)}) collective-permute-start(bf16[128,2304]{1,0:T(8,128)(2,1)} %bitcast_select_fusion.2), channel_id=1, source_target_pairs={{0,8},{8,16},{16,24},{1,9},{9,17},{17,25},{2,10},{10,18},{18,26},{... | collective-permute-start | bytes 1769480 | tf_op jit(solution)/shard_map/ppermute | solution.py:29
  42.3 1.3 %collective-permute-start.7 = (bf16[128,2176]{1,0:T(8,128)(2,1)S(1)}, bf16[128,2176]{1,0:T(8,128)(2,1)S(1)}, u32[]{:S(2)}, u32[]{:S(2)}) collective-permute-start(bf16[128,2176]{1,0:T(8,128)(2,1)S(1)} %get-tuple-element.27.refs_0_), channel_id=1, source_target_pairs={{0,1},{2,3},{4,5},{6,7},{8,9},{10,11},{12,13},{14,15},{16,17},{18,... | collective-permute-start | bytes 1671176 | tf_op jit(solution)/shard_map/ppermute | solution.py:34
  43.6 3.3 %collective-permute-start.3 = (bf16[128,2176]{1,0:T(8,128)(2,1)S(1)}, bf16[128,2176]{1,0:T(8,128)(2,1)S(1)}, u32[]{:S(2)}, u32[]{:S(2)}) collective-permute-start(bf16[128,2176]{1,0:T(8,128)(2,1)S(1)} %collective-permute-done.1.refs_1_), channel_id=1, source_target_pairs={{0,1},{1,0},{2,3},{3,2},{4,5},{5,4},{6,7},{7,6},{8,9},{9,8},{10,11... | collective-permute-start | bytes 1671176 | tf_op jit(solution)/shard_map/ppermute | solution.py:34
  46.9 4.5 %collective-permute-done.5.arrived_ref = bf16[128,3328]{1,0:T(8,128)(2,1)S(1)} collective-permute-done((bf16[128,3328]{1,0:T(8,128)(2,1)}, bf16[128,3328]{1,0:T(8,128)(2,1)S(1)}, u32[]{:S(2)}, u32[]{:S(2)}) %collective-permute-start.5) | collective-permute-done | bytes 852000 | tf_op jit(solution)/shard_map/ppermute | solution.py:29
  51.4 4.0 %place_queries.3.refs_6_ = bf16[1,128,8192]{2,1,0:T(8,128)(2,1)} custom-call(bf16[128,256]{1,0:T(8,128)(2,1)S(1)} %get-tuple-element.28.hot_ref.refs_6_, bf16[128,3328]{1,0:T(8,128)(2,1)S(1)} %collective-permute-done.5.arrived_ref, bf16[1,128,8192]{2,1,0:T(8,128)(2,1)} %place_queries.2.in_hbm), custom_call_target="tpu_custom_call", output_to_operand_aliasing={{}: (2, {})} | custom-call | tf_op jit(solution)/shard_map/place_queries/pallas_call | solution.py:171
  55.5 0.0 collective-permute-done.4.refs_3_
  55.5 2.8 %collective-permute-start.6 = (bf16[128,2176]{1,0:T(8,128)(2,1)S(1)}, bf16[128,2176]{1,0:T(8,128)(2,1)S(1)}, u32[]{:S(2)}, u32[]{:S(2)}) collective-permute-start(bf16[128,2176]{1,0:T(8,128)(2,1)S(1)} %collective-permute-done.4.refs_3_), channel_id=1, source_target_pairs={{0,1},{1,0},{2,3},{3,2},{4,5},{5,4},{6,7},{7,6},{8,9},{9,8},{10,11... | collective-permute-start | bytes 1671176 | tf_op jit(solution)/shard_map/ppermute | solution.py:34
  58.2 0.0 collective-permute-done.7.refs_5_
  58.2 0.0 collective-permute-done.3.refs_2_
  58.2 1.6 %collective-permute-done.6.refs_4_ = bf16[128,2176]{1,0:T(8,128)(2,1)S(1)} collective-permute-done((bf16[128,2176]{1,0:T(8,128)(2,1)S(1)}, bf16[128,2176]{1,0:T(8,128)(2,1)S(1)}, u32[]{:S(2)}, u32[]{:S(2)}) %collective-permute-start.6) | collective-permute-done | bytes 557088 | tf_op jit(solution)/shard_map/ppermute | solution.py:34
  59.8 9.1 %attend_early.1 = (bf16[1,128,8192]{2,1,0:T(8,128)(2,1)}, bf16[128,5888]{1,0:T(8,128)(2,1)S(1)}, bf16[128,2304]{1,0:T(8,128)(2,1)S(1)}) custom-call(s32[1]{0:T(128)} %bitcast.rank_ref, bf16[128,2176]{1,0:T(8,128)(2,1)S(1)} %get-tuple-element.27.refs_0_, bf16[128,2176]{1,0:T(8,128)(2,1)S(1)} %collective-permute-done.1.refs_1_, ...), custom_call_target="tpu_custom_call", output_to_operand_aliasing={{0}: (7, {})} | custom-call | tf_op jit(solution)/shard_map/attend_early/pallas_call | solution.py:171
  69.0 0.0 collective-permute-done.8.refs_7_
  69.0 6.8 %attend_late.1 = bf16[1,128,8192]{2,1,0:T(8,128)(2,1)} custom-call(s32[1]{0:T(128)} %bitcast.rank_ref, bf16[128,2176]{1,0:T(8,128)(2,1)S(1)} %get-tuple-element.27.refs_0_, bf16[128,2176]{1,0:T(8,128)(2,1)S(1)} %collective-permute-done.1.refs_1_, bf16[128,2176]{1,0:T(8,128)(2,1)S(1)} %collective-permute-done.3.refs_2_, ...), custom_call_target="tpu_custom_call", output_to_operand_aliasing={{}: (11, {})} | custom-call | tf_op jit(solution)/shard_map/attend_late/pallas_call | solution.py:171
  (1 shorter events, 0.0 us)
Async XLA Ops:
  0.7 1.0 %copy-start.1 = (bf16[1,256,1024]{2,1,0:T(8,128)(2,1)S(1)}, bf16[1,256,1024]{2,1,0:T(8,128)(2,1)}, u32[]{:S(2)}) copy-start(bf16[1,256,1024]{2,1,0:T(8,128)(2,1)} %k_ref.1) | copy-start | bytes 1572868
  1.7 1.0 %copy-start.2 = (bf16[1,256,1024]{2,1,0:T(8,128)(2,1)S(1)}, bf16[1,256,1024]{2,1,0:T(8,128)(2,1)}, u32[]{:S(2)}) copy-start(bf16[1,256,1024]{2,1,0:T(8,128)(2,1)} %v_ref.1) | copy-start | bytes 1572868
  2.8 16.3 %collective-permute-start = (bf16[128,2176]{1,0:T(8,128)(2,1)S(1)}, bf16[128,2176]{1,0:T(8,128)(2,1)S(1)}, u32[]{:S(2)}, u32[]{:S(2)}) collective-permute-start(bf16[128,2176]{1,0:T(8,128)(2,1)S(1)} %get-tuple-element.23), channel_id=1, source_target_pairs={{0,8},{8,16},{16,24},{1,9},{9,17},{17,25},{2,10},{10,18},{18,26},{... | collective-permute-start | bytes 1671176 | tf_op jit(solution)/shard_map/ppermute | solution.py:29
  6.0 4.8 %copy-start = (bf16[1,256,8192]{2,1,0:T(8,128)(2,1)S(1)}, bf16[1,256,8192]{2,1,0:T(8,128)(2,1)}, u32[]{:S(2)}) copy-start(bf16[1,256,8192]{2,1,0:T(8,128)(2,1)} %q_hbm.1) | copy-start | bytes 12582916
  10.9 22.2 %collective-permute-start.2 = (bf16[128,2560]{1,0:T(8,128)(2,1)S(1)}, bf16[128,2560]{1,0:T(8,128)(2,1)S(1)}, u32[]{:S(2)}, u32[]{:S(2)}) collective-permute-start(bf16[128,2560]{1,0:T(8,128)(2,1)S(1)} %bitcast_select_fusion.1), channel_id=1, source_target_pairs={{0,8},{8,16},{16,24},{1,9},{9,17},{17,25},{2,10},{10,18},{18,26},{... | collective-permute-start | bytes 1966088 | tf_op jit(solution)/shard_map/ppermute | solution.py:29
  12.9 6.2 %copy-start.3 = (s32[1,128]{1,0:T(1,128)S(1)}, s32[1,128]{1,0:T(1,128)}, u32[]{:S(2)}) copy-start(s32[1,128]{1,0:T(1,128)} %docs_ref.1) | copy-start | bytes 1540
  20.0 16.8 %collective-permute-start.1 = (bf16[128,2176]{1,0:T(8,128)(2,1)S(1)}, bf16[128,2176]{1,0:T(8,128)(2,1)S(1)}, u32[]{:S(2)}, u32[]{:S(2)}) collective-permute-start(bf16[128,2176]{1,0:T(8,128)(2,1)S(1)} %get-tuple-element.27.refs_0_), channel_id=1, source_target_pairs={{0,2},{1,3},{2,4},{3,5},{4,6},{5,7},{8,10},{9,11},{10,12},{11,13},... | collective-permute-start | bytes 1671176 | tf_op jit(solution)/shard_map/ppermute | solution.py:29
  23.2 28.2 %collective-permute-start.5 = (bf16[128,3328]{1,0:T(8,128)(2,1)}, bf16[128,3328]{1,0:T(8,128)(2,1)S(1)}, u32[]{:S(2)}, u32[]{:S(2)}) collective-permute-start(bf16[128,3328]{1,0:T(8,128)(2,1)} %bitcast_select_fusion), channel_id=1, source_target_pairs={{0,8},{8,16},{16,24},{1,9},{9,17},{17,25},{2,10},{10,18},{18,26},{... | collective-permute-start | bytes 2555912 | tf_op jit(solution)/shard_map/ppermute | solution.py:29
  36.8 18.6 %collective-permute-start.4 = (bf16[128,2176]{1,0:T(8,128)(2,1)S(1)}, bf16[128,2176]{1,0:T(8,128)(2,1)S(1)}, u32[]{:S(2)}, u32[]{:S(2)}) collective-permute-start(bf16[128,2176]{1,0:T(8,128)(2,1)S(1)} %collective-permute-done.1.refs_1_), channel_id=1, source_target_pairs={{0,2},{1,3},{2,4},{3,5},{4,6},{5,7},{8,10},{9,11},{10,12},{11,13},... | collective-permute-start | bytes 1671176 | tf_op jit(solution)/shard_map/ppermute | solution.py:29
  40.0 28.9 %collective-permute-start.8 = (bf16[128,2304]{1,0:T(8,128)(2,1)}, bf16[128,2304]{1,0:T(8,128)(2,1)}, u32[]{:S(2)}, u32[]{:S(2)}) collective-permute-start(bf16[128,2304]{1,0:T(8,128)(2,1)} %bitcast_select_fusion.2), channel_id=1, source_target_pairs={{0,8},{8,16},{16,24},{1,9},{9,17},{17,25},{2,10},{10,18},{18,26},{... | collective-permute-start | bytes 1769480 | tf_op jit(solution)/shard_map/ppermute | solution.py:29
  42.3 15.9 %collective-permute-start.7 = (bf16[128,2176]{1,0:T(8,128)(2,1)S(1)}, bf16[128,2176]{1,0:T(8,128)(2,1)S(1)}, u32[]{:S(2)}, u32[]{:S(2)}) collective-permute-start(bf16[128,2176]{1,0:T(8,128)(2,1)S(1)} %get-tuple-element.27.refs_0_), channel_id=1, source_target_pairs={{0,1},{2,3},{4,5},{6,7},{8,9},{10,11},{12,13},{14,15},{16,17},{18,... | collective-permute-start | bytes 1671176 | tf_op jit(solution)/shard_map/ppermute | solution.py:34
  43.6 14.6 %collective-permute-start.3 = (bf16[128,2176]{1,0:T(8,128)(2,1)S(1)}, bf16[128,2176]{1,0:T(8,128)(2,1)S(1)}, u32[]{:S(2)}, u32[]{:S(2)}) collective-permute-start(bf16[128,2176]{1,0:T(8,128)(2,1)S(1)} %collective-permute-done.1.refs_1_), channel_id=1, source_target_pairs={{0,1},{1,0},{2,3},{3,2},{4,5},{5,4},{6,7},{7,6},{8,9},{9,8},{10,11... | collective-permute-start | bytes 1671176 | tf_op jit(solution)/shard_map/ppermute | solution.py:34
  55.5 4.3 %collective-permute-start.6 = (bf16[128,2176]{1,0:T(8,128)(2,1)S(1)}, bf16[128,2176]{1,0:T(8,128)(2,1)S(1)}, u32[]{:S(2)}, u32[]{:S(2)}) collective-permute-start(bf16[128,2176]{1,0:T(8,128)(2,1)S(1)} %collective-permute-done.4.refs_3_), channel_id=1, source_target_pairs={{0,1},{1,0},{2,3},{3,2},{4,5},{5,4},{6,7},{7,6},{8,9},{9,8},{10,11... | collective-permute-start | bytes 1671176 | tf_op jit(solution)/shard_map/ppermute | solution.py:34

commit v12 on v10

--- a/solution.py
+++ b/solution.py
@@ -16,7 +16,7 @@
 NOTE = 2 * KV_WIDTH
 MASKED = -1e30
 HALF = GROUP // 2
-CHUNKS = (20, 24, 20)
+CHUNKS = (20, 26, 18)
 VMEM_GRANT = 48 * 1024 * 1024
 
 WHOLE = pl.BlockSpec(memory_space=pltpu.VMEM)
@@ -132,28 +132,11 @@
     )(*operands, out)
 
 
-def stage_kernel(q_hbm, out_hbm, sem):
-    copy = pltpu.make_async_copy(q_hbm.at[:, 0 : out_hbm.shape[1]], out_hbm, sem)
-    copy.start()
-    copy.wait()
-
-
-def stage_local(q_rows, quota):
-    return pl.pallas_call(
-        stage_kernel,
-        in_specs=[ANYWHERE],
-        out_specs=ANYWHERE,
-        out_shape=jax.ShapeDtypeStruct((1, quota, QUERY_HEADS * HEAD_SIZE), jnp.bfloat16),
-        scratch_shapes=[pltpu.SemaphoreType.DMA],
-        compiler_params=pltpu.CompilerParams(vmem_limit_bytes=VMEM_GRANT),
-        name="stage_local",
-    )(q_rows)
-
-
-def place_kernel(first, hot_ref, arrived_ref, in_hbm, out_hbm, local, placed, in_sem, out_sem):
+def place_kernel(first, hot_ref, arrived_ref, q_hbm, *refs):
+    out_hbm, local, placed, in_sem, out_sem = refs[-5:]
     quota, width = arrived_ref.shape
     cols = head_columns(first, width // HEAD_SIZE)
-    fetch = pltpu.make_async_copy(in_hbm.at[0, :, cols], local, in_sem)
+    fetch = pltpu.make_async_copy(q_hbm.at[0, 0:quota, cols], local, in_sem)
     fetch.start()
     fetch.wait()
     for head, heads in pieces(first, width // HEAD_SIZE):
@@ -164,12 +147,10 @@
     store.wait()
 
 
-def place_queries(hot, arrived, first, out):
-    return in_place(
-        functools.partial(place_kernel, first),
-        [hot, arrived],
-        out,
-        in_specs=[WHOLE, WHOLE],
+def place_queries(hot, arrived, q_rows, first, out):
+    quota = arrived.shape[0]
+    arguments = dict(
+        in_specs=[WHOLE, WHOLE, ANYWHERE],
         scratch_shapes=[
             pltpu.VMEM(arrived.shape, jnp.bfloat16),
             pltpu.VMEM(arrived.shape, jnp.bfloat16),
@@ -177,7 +158,17 @@
             pltpu.SemaphoreType.DMA,
         ],
         name="place_queries",
-    )[0]
+    )
+    kernel = functools.partial(place_kernel, first)
+    if out is not None:
+        return in_place(kernel, [hot, arrived, q_rows], out, **arguments)[0]
+    return pl.pallas_call(
+        kernel,
+        out_specs=ANYWHERE,
+        out_shape=jax.ShapeDtypeStruct((1, quota, QUERY_HEADS * HEAD_SIZE), jnp.bfloat16),
+        compiler_params=pltpu.CompilerParams(vmem_limit_bytes=VMEM_GRANT),
+        **arguments,
+    )(hot, arrived, q_rows)
 
 
 def make_bias(kv_refs, far_ref, mate_ref, bias, rank):
@@ -261,24 +252,27 @@
 
 def early_kernel(blocks, count, rank_ref, *refs):
     kv_refs, far_ref, mate_ref = refs[: blocks - 1], refs[blocks - 1], refs[blocks]
-    in_hbm, _, result, local, bias, rest, queries, sems = refs[blocks + 1 :]
-    late = head_columns(count, QUERY_HEADS - count)
-    fetch = pltpu.make_async_copy(in_hbm.at[0, :, head_columns(0, count)], queries, sems.at[0])
+    q_hbm, in_hbm, out_hbm, local, bias, rest, queries, result, sems = refs[blocks + 1 :]
+    own, others = head_columns(0, count), head_columns(count, QUERY_HEADS - count)
+    fetch = pltpu.make_async_copy(in_hbm.at[0, :, own], queries, sems.at[0])
     fetch.start()
     rank = rank_ref[0]
     make_bias(kv_refs, far_ref, mate_ref, bias, rank)
     choose_rest(0, count, lax.rem(rank, 2), far_ref, mate_ref, rest)
     fetch.wait()
-    ahead = pltpu.make_async_copy(in_hbm.at[0, :, late], local, sems.at[1])
+    attend_heads(0, count, [*kv_refs, rest], bias, lambda cols: queries[:, cols], result)
+    store = pltpu.make_async_copy(result, out_hbm.at[0, :, own], sems.at[1])
+    store.start()
+    ahead = pltpu.make_async_copy(q_hbm.at[0, 0 : bias.shape[0], others], local, sems.at[2])
     ahead.start()
-    attend_heads(0, count, [*kv_refs, rest], bias, lambda cols: queries[:, cols], result)
+    store.wait()
     ahead.wait()
 
 
 def late_kernel(blocks, first, rank_ref, *refs):
     kv_refs, far_ref, mate_ref = refs[: blocks - 1], refs[blocks - 1], refs[blocks]
-    hot_ref, arrived_hbm, early_ref, local_ref, _, out_hbm = refs[blocks + 1 : blocks + 7]
-    bias, rest, arrived, result, sems = refs[blocks + 7 :]
+    hot_ref, arrived_hbm, local_ref, _, out_hbm = refs[blocks + 1 : blocks + 6]
+    bias, rest, arrived, result, sems = refs[blocks + 6 :]
     count = QUERY_HEADS - first
     fetch = pltpu.make_async_copy(arrived_hbm, arrived, sems.at[0])
     fetch.start()
@@ -286,49 +280,40 @@
     make_bias(kv_refs, far_ref, mate_ref, bias, rank)
     choose_rest(first, count, lax.rem(rank, 2), far_ref, mate_ref, rest)
     fetch.wait()
-    early = pltpu.make_async_copy(early_ref, out_hbm.at[0, :, head_columns(0, first)], sems.at[1])
-    early.start()
 
     def take(cols):
         return place_rows(hot_ref[...], arrived[:, cols], local_ref[:, cols])
 
     attend_heads(first, count, [*kv_refs, rest], bias, take, result)
-    store = pltpu.make_async_copy(result, out_hbm.at[0, :, head_columns(first, count)], sems.at[2])
+    store = pltpu.make_async_copy(result, out_hbm.at[0, :, head_columns(first, count)], sems.at[1])
     store.start()
-    early.wait()
     store.wait()
 
 
-def attend(rank, hot, arrived, kv_blocks, out):
+def attend(rank, hot, arrived, q_rows, kv_blocks, out):
     quota, width = arrived.shape
     blocks = len(kv_blocks) - 1
     first = QUERY_HEADS - width // HEAD_SIZE
     bias = pltpu.VMEM((quota, blocks * quota), jnp.float32)
     rest = pltpu.VMEM((quota, NOTE), jnp.bfloat16)
-    own = (arrived.shape, jnp.bfloat16)
-    others = ((quota, first * HEAD_SIZE), jnp.bfloat16)
-    out, result, local = in_place(
+    own = pltpu.VMEM(arrived.shape, jnp.bfloat16)
+    others = pltpu.VMEM((quota, first * HEAD_SIZE), jnp.bfloat16)
+    out, local = in_place(
         functools.partial(early_kernel, blocks, first),
-        [rank, *kv_blocks],
+        [rank, *kv_blocks, q_rows],
         out,
-        more_out=[jax.ShapeDtypeStruct(*others), jax.ShapeDtypeStruct(*own)],
-        more_specs=[WHOLE, WHOLE],
-        in_specs=[SCALARS] + [WHOLE] * len(kv_blocks),
-        scratch_shapes=[bias, rest, pltpu.VMEM(*others), pltpu.SemaphoreType.DMA((2,))],
+        more_out=[jax.ShapeDtypeStruct(arrived.shape, jnp.bfloat16)],
+        more_specs=[WHOLE],
+        in_specs=[SCALARS] + [WHOLE] * len(kv_blocks) + [ANYWHERE],
+        scratch_shapes=[bias, rest, others, others, pltpu.SemaphoreType.DMA((3,))],
         name="attend_early",
     )
     return in_place(
         functools.partial(late_kernel, blocks, first),
-        [rank, *kv_blocks, hot, arrived, result, local],
+        [rank, *kv_blocks, hot, arrived, local],
         out,
-        in_specs=[SCALARS] + [WHOLE] * (len(kv_blocks) + 1) + [ANYWHERE, WHOLE, WHOLE],
-        scratch_shapes=[
-            bias,
-            rest,
-            pltpu.VMEM(*own),
-            pltpu.VMEM(*own),
-            pltpu.SemaphoreType.DMA((3,)),
-        ],
+        in_specs=[SCALARS] + [WHOLE] * (len(kv_blocks) + 1) + [ANYWHERE, WHOLE],
+        scratch_shapes=[bias, rest, own, own, pltpu.SemaphoreType.DMA((2,))],
         name="attend_late",
     )[0]
 
@@ -366,23 +351,21 @@
     arrived_q = [shifted(tail, "dp", 1) for tail in q_tails]
 
     shift = shift_in_known(own_count, quota)
-    out = stage_local(q_rows, quota)
-    local_kv, out = lax.optimization_barrier((local_kv, out))
     own, hot = settle_kv(shift, doc_ids, arrived_kv, local_kv)
 
     kv_blocks = [own]
-    carried = own
+    carried, out = own, None
     for back in range(1, rounds + 1):
         carried = shifted(carried, "ctx", 2)
         kv_blocks.append(carried)
         if back < len(CHUNKS):
             first = sum(CHUNKS[: back - 1])
-            out = place_queries(hot, arrived_q[back - 1], first, out)
+            out = place_queries(hot, arrived_q[back - 1], q_rows, first, out)
             carried, out = lax.optimization_barrier((carried, out))
         if back < rounds:
             kv_blocks.append(across_cores(carried))
-    kv_blocks += [across_cores(carried, (1,)), across_cores(own, (0,))]
-    return attend(rank[None], hot, arrived_q[-1], kv_blocks, out)
+    kv_blocks += [across_cores(carried), across_cores(own, (0,))]
+    return attend(rank[None], hot, arrived_q[-1], q_rows, kv_blocks, out)
 
 
 def solution(mesh):

time: 71.7 us -> 71.3 us (level)
  Pallas kernels: 20 us -> 17.5 us
  local copies, waits for them, and re-layouts: 1.01 us -> 3.2 us
  starting transfers between devices: 25.2 us -> 23.4 us
  waiting for transfers between devices: 20.4 us -> 21.8 us
    pallas_call x4 -> x3, Pallas kernels: 17.8 us -> 15.4 us  [in_place(): pl.pallas_call(kernel, in_specs=specs, out_specs=[ANYWHERE, *more_specs],...]
    unnamed x6 -> x10, local copies, waits for them, and re-layouts: 0.02 us -> 2.21 us
    ppermute x3, starting transfers between devices: 9.28 us -> 7.41 us  [across_cores(): lax.ppermute(x, 'ctx', [(i, i ^ 1) for i in range(n) if i % 2 in sources])]
    ppermute x6, waiting for transfers between devices: 18.8 us -> 20.2 us  [shifted(): return lax.ppermute(x, axis, [(i, i + steps) for i in range(n - steps)])]
    select_n x3 -> x4, other arithmetic: 3.55 us -> 3.6 us  [circular_tail(): return jnp.where(later[:, None], rows[quota:], rows[:quota])]
  transfers between devices with their start and end apart: 9 -> 9, of which waited for: 4 -> 4; matrix products, arithmetic and copies ran while one was open for 4% -> 5% of each run, Pallas kernels for 20% -> 18%
where the time goes in v12:
time: 71.3 us; the launch traced here: 70.9 us
  starting transfers between devices  23.4 us (33%)
  waiting for transfers between devices  21.8 us (31%)
  Pallas kernels  17.5 us (25%)
  other arithmetic  3.81 us (5%)
  local copies, waits for them, and re-layouts  3.2 us (4%)
  between operations  1.1 us (2%)
    ppermute x6, waiting for transfers between devices, shifted(): return lax.ppermute(x, axis, [(i, i + steps) for i in range(n - steps)])  20.2 us
    ppermute x6, starting transfers between devices, shifted(): return lax.ppermute(x, axis, [(i, i + steps) for i in range(n - steps)])  16 us
    pallas_call x3, Pallas kernels, in_place(): pl.pallas_call(kernel, in_specs=specs, out_specs=[ANYWHERE, *more_specs],...  15.4 us
    ppermute x3, starting transfers between devices, across_cores(): lax.ppermute(x, 'ctx', [(i, i ^ 1) for i in range(n) if i % 2 in sources])  7.41 us
    select_n x4, other arithmetic, circular_tail(): return jnp.where(later[:, None], rows[quota:], rows[:quota])  3.6 us
    unnamed x10, local copies, waits for them, and re-layouts  2.21 us
    ppermute x3, waiting for transfers between devices, across_cores(): lax.ppermute(x, 'ctx', [(i, i ^ 1) for i in range(n) if i % 2 in sources])  1.58 us
  transfers between devices with their start and end apart: 9, of which 4 were waited for; matrix products, arithmetic and copies ran while one was open for 5% of the time, Pallas kernels for 18%

profile of v12, /device:TPU:21, one launch (start us, length us, event | category | flops | bytes accessed | tf_op | source)
XLA Modules:
  0.0 70.9 jit_solution(16695215870708470384)
XLA Ops:
  0.0 0.0 copy-start.4
  0.8 0.0 copy-start
  0.8 1.5 %bitcast_select_fusion.4 = (bf16[128,1024]{1,0:T(8,128)(2,1)S(1)}, bf16[128,1024]{1,0:T(8,128)(2,1)S(1)}) fusion(bf16[1,256,1024]{2,1,0:T(8,128)(2,1)} %param.6, pred[128]{0:T(512)(128)(4,1)S(1)} %add_compare_fusion, bf16[1,256,1024]{2,1,0:T(8,128)(2,1)} %param.7), kind=kLoop, calls=%fused_computation.6 | loop fusion | flops 262144 | bytes 1572992 | tf_op jit(solution)/shard_map/jit(_where)/select_n | solution.py:323
  2.2 0.1 maximum_maximum_fusion
  2.3 3.1 %collective-permute-start = (bf16[128,2176]{1,0:T(8,128)(2,1)S(1)}, bf16[128,2176]{1,0:T(8,128)(2,1)S(1)}, u32[]{:S(2)}, u32[]{:S(2)}) collective-permute-start(bf16[128,2176]{1,0:T(8,128)(2,1)S(1)} %maximum_maximum_fusion), channel_id=1, source_target_pairs={{0,8},{8,16},{16,24},{1,9},{9,17},{17,25},{2,10},{10,18},{18,26},{... | collective-permute-start | bytes 1671176 | tf_op jit(solution)/shard_map/ppermute | solution.py:29
  5.5 0.0 copy-done.4
  5.5 1.0 %slice_bitcast_fusion = (bf16[128,1024]{1,0:T(8,128)(2,1)S(1)}, bf16[128,1024]{1,0:T(8,128)(2,1)S(1)}) fusion(bf16[1,256,1024]{2,1,0:T(8,128)(2,1)} %param.7, bf16[1,256,1024]{2,1,0:T(8,128)(2,1)S(1)} %copy-done.4), kind=kLoop, calls=%fused_computation.7 | loop fusion | bytes 1048576 | tf_op jit(solution)/shard_map/slice | solution.py:323
  6.5 0.0 copy-done
  6.5 1.0 %bitcast_select_fusion.2 = bf16[128,2304]{1,0:T(8,128)(2,1)} fusion(bf16[1,256,8192]{2,1,0:T(8,128)(2,1)S(1)} %copy-done, pred[128]{0:T(512)(128)(4,1)S(1)} %add_compare_fusion), kind=kLoop, calls=%fused_computation.2 | loop fusion | flops 294912 | bytes 1769600 | tf_op jit(solution)/shard_map/jit(_where)/select_n | solution.py:323
  7.5 0.0 copy-start.3
  7.5 1.0 %bitcast_select_fusion = bf16[128,3328]{1,0:T(8,128)(2,1)} fusion(bf16[1,256,8192]{2,1,0:T(8,128)(2,1)S(1)} %copy-done, pred[128]{0:T(512)(128)(4,1)S(1)} %add_compare_fusion), kind=kLoop, calls=%fused_computation | loop fusion | flops 425984 | bytes 2556032 | tf_op jit(solution)/shard_map/jit(_where)/select_n | solution.py:323
  8.5 0.1 bitcast_select_fusion.1
  8.7 1.9 %collective-permute-start.2 = (bf16[128,2560]{1,0:T(8,128)(2,1)S(1)}, bf16[128,2560]{1,0:T(8,128)(2,1)S(1)}, u32[]{:S(2)}, u32[]{:S(2)}) collective-permute-start(bf16[128,2560]{1,0:T(8,128)(2,1)S(1)} %bitcast_select_fusion.1), channel_id=1, source_target_pairs={{0,8},{8,16},{16,24},{1,9},{9,17},{17,25},{2,10},{10,18},{18,26},{... | collective-permute-start | bytes 1966088 | tf_op jit(solution)/shard_map/ppermute | solution.py:29
  10.6 0.1 pad_add_fusion.shift_ref
  10.7 7.9 %collective-permute-done.arrived_ref = bf16[128,2176]{1,0:T(8,128)(2,1)S(1)} collective-permute-done((bf16[128,2176]{1,0:T(8,128)(2,1)S(1)}, bf16[128,2176]{1,0:T(8,128)(2,1)S(1)}, u32[]{:S(2)}, u32[]{:S(2)}) %collective-permute-start) | collective-permute-done | bytes 557088 | tf_op jit(solution)/shard_map/ppermute | solution.py:29
  18.6 0.0 copy-done.3
  18.6 0.9 %settle_kv.1 = (bf16[128,2176]{1,0:T(8,128)(2,1)S(1)}, bf16[128,256]{1,0:T(8,128)(2,1)S(1)}) custom-call(s32[2]{0:T(128)S(1)} %pad_add_fusion.shift_ref, s32[1,128]{1,0:T(1,128)S(1)} %copy-done.3, bf16[128,2176]{1,0:T(8,128)(2,1)S(1)} %collective-permute-done.arrived_ref, bf16[128,2048]{1,0:T(8,128)(2,1)S(1)} %pad_maximum_fusion.local_ref), custom_call_target="tpu_custom_call" | custom-call | tf_op jit(solution)/shard_map/settle_kv/pallas_call | solution.py:82
  19.5 3.2 %collective-permute-start.1 = (bf16[128,2176]{1,0:T(8,128)(2,1)S(1)}, bf16[128,2176]{1,0:T(8,128)(2,1)S(1)}, u32[]{:S(2)}, u32[]{:S(2)}) collective-permute-start(bf16[128,2176]{1,0:T(8,128)(2,1)S(1)} %get-tuple-element.23.refs_0_), channel_id=1, source_target_pairs={{0,2},{1,3},{2,4},{3,5},{4,6},{5,7},{8,10},{9,11},{10,12},{11,13},... | collective-permute-start | bytes 1671176 | tf_op jit(solution)/shard_map/ppermute | solution.py:29
  22.7 2.2 %collective-permute-start.5 = (bf16[128,3328]{1,0:T(8,128)(2,1)}, bf16[128,3328]{1,0:T(8,128)(2,1)S(1)}, u32[]{:S(2)}, u32[]{:S(2)}) collective-permute-start(bf16[128,3328]{1,0:T(8,128)(2,1)} %bitcast_select_fusion), channel_id=1, source_target_pairs={{0,8},{8,16},{16,24},{1,9},{9,17},{17,25},{2,10},{10,18},{18,26},{... | collective-permute-start | bytes 2555912 | tf_op jit(solution)/shard_map/ppermute | solution.py:29
  24.9 7.7 %collective-permute-done.2.arrived_ref = bf16[128,2560]{1,0:T(8,128)(2,1)S(1)} collective-permute-done((bf16[128,2560]{1,0:T(8,128)(2,1)S(1)}, bf16[128,2560]{1,0:T(8,128)(2,1)S(1)}, u32[]{:S(2)}, u32[]{:S(2)}) %collective-permute-start.2) | collective-permute-done | bytes 655392 | tf_op jit(solution)/shard_map/ppermute | solution.py:29
  32.7 0.0 copy-start.1
  32.7 2.2 %copy-done.1 = bf16[1,256,8192]{2,1,0:T(8,128)(2,1)S(1)} copy-done((bf16[1,256,8192]{2,1,0:T(8,128)(2,1)S(1)}, bf16[1,256,8192]{2,1,0:T(8,128)(2,1)}, u32[]{:S(2)}) %copy-start.1) | copy-done | bytes 4194328
  34.9 0.0 copy-start.2
  34.9 1.2 %place_queries.2.refs_0_ = bf16[1,128,8192]{2,1,0:T(8,128)(2,1)} custom-call(bf16[128,256]{1,0:T(8,128)(2,1)S(1)} %get-tuple-element.24.hot_ref.refs_6_, bf16[128,2560]{1,0:T(8,128)(2,1)S(1)} %collective-permute-done.2.arrived_ref, bf16[1,256,8192]{2,1,0:T(8,128)(2,1)S(1)} %copy-done.1), custom_call_target="tpu_custom_call" | custom-call | tf_op jit(solution)/shard_map/place_queries/pallas_call | solution.py:165
  36.1 0.0 collective-permute-done.1.refs_1_
  36.1 3.3 %collective-permute-start.4 = (bf16[128,2176]{1,0:T(8,128)(2,1)S(1)}, bf16[128,2176]{1,0:T(8,128)(2,1)S(1)}, u32[]{:S(2)}, u32[]{:S(2)}) collective-permute-start(bf16[128,2176]{1,0:T(8,128)(2,1)S(1)} %collective-permute-done.1.refs_1_), channel_id=1, source_target_pairs={{0,2},{1,3},{2,4},{3,5},{4,6},{5,7},{8,10},{9,11},{10,12},{11,13},... | collective-permute-start | bytes 1671176 | tf_op jit(solution)/shard_map/ppermute | solution.py:29
  39.5 2.2 %collective-permute-start.8 = (bf16[128,2304]{1,0:T(8,128)(2,1)}, bf16[128,2304]{1,0:T(8,128)(2,1)}, u32[]{:S(2)}, u32[]{:S(2)}) collective-permute-start(bf16[128,2304]{1,0:T(8,128)(2,1)} %bitcast_select_fusion.2), channel_id=1, source_target_pairs={{0,8},{8,16},{16,24},{1,9},{9,17},{17,25},{2,10},{10,18},{18,26},{... | collective-permute-start | bytes 1769480 | tf_op jit(solution)/shard_map/ppermute | solution.py:29
  41.7 1.3 %collective-permute-start.7 = (bf16[128,2176]{1,0:T(8,128)(2,1)S(1)}, bf16[128,2176]{1,0:T(8,128)(2,1)S(1)}, u32[]{:S(2)}, u32[]{:S(2)}) collective-permute-start(bf16[128,2176]{1,0:T(8,128)(2,1)S(1)} %get-tuple-element.23.refs_0_), channel_id=1, source_target_pairs={{0,1},{2,3},{4,5},{6,7},{8,9},{10,11},{12,13},{14,15},{16,17},{18,... | collective-permute-start | bytes 1671176 | tf_op jit(solution)/shard_map/ppermute | solution.py:34
  43.0 3.4 %collective-permute-start.3 = (bf16[128,2176]{1,0:T(8,128)(2,1)S(1)}, bf16[128,2176]{1,0:T(8,128)(2,1)S(1)}, u32[]{:S(2)}, u32[]{:S(2)}) collective-permute-start(bf16[128,2176]{1,0:T(8,128)(2,1)S(1)} %collective-permute-done.1.refs_1_), channel_id=1, source_target_pairs={{0,1},{1,0},{2,3},{3,2},{4,5},{5,4},{6,7},{7,6},{8,9},{9,8},{10,11... | collective-permute-start | bytes 1671176 | tf_op jit(solution)/shard_map/ppermute | solution.py:34
  46.4 4.6 %collective-permute-done.5.arrived_ref = bf16[128,3328]{1,0:T(8,128)(2,1)S(1)} collective-permute-done((bf16[128,3328]{1,0:T(8,128)(2,1)}, bf16[128,3328]{1,0:T(8,128)(2,1)S(1)}, u32[]{:S(2)}, u32[]{:S(2)}) %collective-permute-start.5) | collective-permute-done | bytes 852000 | tf_op jit(solution)/shard_map/ppermute | solution.py:29
  50.9 0.0 copy-done.2
  50.9 1.4 %place_queries.3.refs_7_ = bf16[1,128,8192]{2,1,0:T(8,128)(2,1)} custom-call(bf16[128,256]{1,0:T(8,128)(2,1)S(1)} %get-tuple-element.24.hot_ref.refs_6_, bf16[128,3328]{1,0:T(8,128)(2,1)S(1)} %collective-permute-done.5.arrived_ref, bf16[1,256,8192]{2,1,0:T(8,128)(2,1)S(1)} %copy-done.2, ...), custom_call_target="tpu_custom_call", output_to_operand_aliasing={{}: (3, {})} | custom-call | tf_op jit(solution)/shard_map/place_queries/pallas_call | solution.py:123
  52.3 0.0 collective-permute-done.4.refs_3_
  52.3 2.8 %collective-permute-start.6 = (bf16[128,2176]{1,0:T(8,128)(2,1)S(1)}, bf16[128,2176]{1,0:T(8,128)(2,1)S(1)}, u32[]{:S(2)}, u32[]{:S(2)}) collective-permute-start(bf16[128,2176]{1,0:T(8,128)(2,1)S(1)} %collective-permute-done.4.refs_3_), channel_id=1, source_target_pairs={{0,1},{1,0},{2,3},{3,2},{4,5},{5,4},{6,7},{7,6},{8,9},{9,8},{10,11... | collective-permute-start | bytes 1671176 | tf_op jit(solution)/shard_map/ppermute | solution.py:34
  55.1 0.0 collective-permute-done.7.refs_5_
  55.1 0.0 collective-permute-done.3.refs_2_
  55.1 1.6 %collective-permute-done.6.refs_4_ = bf16[128,2176]{1,0:T(8,128)(2,1)S(1)} collective-permute-done((bf16[128,2176]{1,0:T(8,128)(2,1)S(1)}, bf16[128,2176]{1,0:T(8,128)(2,1)S(1)}, u32[]{:S(2)}, u32[]{:S(2)}) %collective-permute-start.6) | collective-permute-done | bytes 557088 | tf_op jit(solution)/shard_map/ppermute | solution.py:34
  56.7 9.0 %attend_early.1 = (bf16[1,128,8192]{2,1,0:T(8,128)(2,1)}, bf16[128,2304]{1,0:T(8,128)(2,1)S(1)}) custom-call(s32[1]{0:T(128)} %bitcast.rank_ref, bf16[128,2176]{1,0:T(8,128)(2,1)S(1)} %get-tuple-element.23.refs_0_, bf16[128,2176]{1,0:T(8,128)(2,1)S(1)} %collective-permute-done.1.refs_1_, ...), custom_call_target="tpu_custom_call", output_to_operand_aliasing={{0}: (8, {})} | custom-call | tf_op jit(solution)/shard_map/attend_early/pallas_call | solution.py:123
  65.7 0.0 collective-permute-done.8.refs_7_
  65.7 5.0 %attend_late.1 = bf16[1,128,8192]{2,1,0:T(8,128)(2,1)} custom-call(s32[1]{0:T(128)} %bitcast.rank_ref, bf16[128,2176]{1,0:T(8,128)(2,1)S(1)} %get-tuple-element.23.refs_0_, bf16[128,2176]{1,0:T(8,128)(2,1)S(1)} %collective-permute-done.1.refs_1_, bf16[128,2176]{1,0:T(8,128)(2,1)S(1)} %collective-permute-done.3.refs_2_, ...), custom_call_target="tpu_custom_call", output_to_operand_aliasing={{}: (10, {})} | custom-call | tf_op jit(solution)/shard_map/attend_late/pallas_call | solution.py:123
  (4 shorter events, 0.1 us)
Async XLA Ops:
  0.0 5.5 %copy-start.4 = (bf16[1,256,1024]{2,1,0:T(8,128)(2,1)S(1)}, bf16[1,256,1024]{2,1,0:T(8,128)(2,1)}, u32[]{:S(2)}) copy-start(bf16[1,256,1024]{2,1,0:T(8,128)(2,1)} %param.6) | copy-start | bytes 1572868
  0.8 5.8 %copy-start = (bf16[1,256,8192]{2,1,0:T(8,128)(2,1)S(1)}, bf16[1,256,8192]{2,1,0:T(8,128)(2,1)}, u32[]{:S(2)}) copy-start(bf16[1,256,8192]{2,1,0:T(8,128)(2,1)} %refs_6_.1) | copy-start | bytes 12582916
  2.3 16.3 %collective-permute-start = (bf16[128,2176]{1,0:T(8,128)(2,1)S(1)}, bf16[128,2176]{1,0:T(8,128)(2,1)S(1)}, u32[]{:S(2)}, u32[]{:S(2)}) collective-permute-start(bf16[128,2176]{1,0:T(8,128)(2,1)S(1)} %maximum_maximum_fusion), channel_id=1, source_target_pairs={{0,8},{8,16},{16,24},{1,9},{9,17},{17,25},{2,10},{10,18},{18,26},{... | collective-permute-start | bytes 1671176 | tf_op jit(solution)/shard_map/ppermute | solution.py:29
  7.5 11.1 %copy-start.3 = (s32[1,128]{1,0:T(1,128)S(1)}, s32[1,128]{1,0:T(1,128)}, u32[]{:S(2)}) copy-start(s32[1,128]{1,0:T(1,128)} %docs_ref.1) | copy-start | bytes 1540
  8.7 24.0 %collective-permute-start.2 = (bf16[128,2560]{1,0:T(8,128)(2,1)S(1)}, bf16[128,2560]{1,0:T(8,128)(2,1)S(1)}, u32[]{:S(2)}, u32[]{:S(2)}) collective-permute-start(bf16[128,2560]{1,0:T(8,128)(2,1)S(1)} %bitcast_select_fusion.1), channel_id=1, source_target_pairs={{0,8},{8,16},{16,24},{1,9},{9,17},{17,25},{2,10},{10,18},{18,26},{... | collective-permute-start | bytes 1966088 | tf_op jit(solution)/shard_map/ppermute | solution.py:29
  19.5 16.6 %collective-permute-start.1 = (bf16[128,2176]{1,0:T(8,128)(2,1)S(1)}, bf16[128,2176]{1,0:T(8,128)(2,1)S(1)}, u32[]{:S(2)}, u32[]{:S(2)}) collective-permute-start(bf16[128,2176]{1,0:T(8,128)(2,1)S(1)} %get-tuple-element.23.refs_0_), channel_id=1, source_target_pairs={{0,2},{1,3},{2,4},{3,5},{4,6},{5,7},{8,10},{9,11},{10,12},{11,13},... | collective-permute-start | bytes 1671176 | tf_op jit(solution)/shard_map/ppermute | solution.py:29
  22.7 28.2 %collective-permute-start.5 = (bf16[128,3328]{1,0:T(8,128)(2,1)}, bf16[128,3328]{1,0:T(8,128)(2,1)S(1)}, u32[]{:S(2)}, u32[]{:S(2)}) collective-permute-start(bf16[128,3328]{1,0:T(8,128)(2,1)} %bitcast_select_fusion), channel_id=1, source_target_pairs={{0,8},{8,16},{16,24},{1,9},{9,17},{17,25},{2,10},{10,18},{18,26},{... | collective-permute-start | bytes 2555912 | tf_op jit(solution)/shard_map/ppermute | solution.py:29
  32.7 2.2 %copy-start.1 = (bf16[1,256,8192]{2,1,0:T(8,128)(2,1)S(1)}, bf16[1,256,8192]{2,1,0:T(8,128)(2,1)}, u32[]{:S(2)}) copy-start(bf16[1,256,8192]{2,1,0:T(8,128)(2,1)} %refs_6_.1) | copy-start | bytes 12582916
  34.9 16.1 %copy-start.2 = (bf16[1,256,8192]{2,1,0:T(8,128)(2,1)S(1)}, bf16[1,256,8192]{2,1,0:T(8,128)(2,1)}, u32[]{:S(2)}) copy-start(bf16[1,256,8192]{2,1,0:T(8,128)(2,1)} %refs_6_.1) | copy-start | bytes 12582916
  36.1 16.2 %collective-permute-start.4 = (bf16[128,2176]{1,0:T(8,128)(2,1)S(1)}, bf16[128,2176]{1,0:T(8,128)(2,1)S(1)}, u32[]{:S(2)}, u32[]{:S(2)}) collective-permute-start(bf16[128,2176]{1,0:T(8,128)(2,1)S(1)} %collective-permute-done.1.refs_1_), channel_id=1, source_target_pairs={{0,2},{1,3},{2,4},{3,5},{4,6},{5,7},{8,10},{9,11},{10,12},{11,13},... | collective-permute-start | bytes 1671176 | tf_op jit(solution)/shard_map/ppermute | solution.py:29
  39.5 26.2 %collective-permute-start.8 = (bf16[128,2304]{1,0:T(8,128)(2,1)}, bf16[128,2304]{1,0:T(8,128)(2,1)}, u32[]{:S(2)}, u32[]{:S(2)}) collective-permute-start(bf16[128,2304]{1,0:T(8,128)(2,1)} %bitcast_select_fusion.2), channel_id=1, source_target_pairs={{0,8},{8,16},{16,24},{1,9},{9,17},{17,25},{2,10},{10,18},{18,26},{... | collective-permute-start | bytes 1769480 | tf_op jit(solution)/shard_map/ppermute | solution.py:29
  41.7 13.4 %collective-permute-start.7 = (bf16[128,2176]{1,0:T(8,128)(2,1)S(1)}, bf16[128,2176]{1,0:T(8,128)(2,1)S(1)}, u32[]{:S(2)}, u32[]{:S(2)}) collective-permute-start(bf16[128,2176]{1,0:T(8,128)(2,1)S(1)} %get-tuple-element.23.refs_0_), channel_id=1, source_target_pairs={{0,1},{2,3},{4,5},{6,7},{8,9},{10,11},{12,13},{14,15},{16,17},{18,... | collective-permute-start | bytes 1671176 | tf_op jit(solution)/shard_map/ppermute | solution.py:34
  43.0 12.1 %collective-permute-start.3 = (bf16[128,2176]{1,0:T(8,128)(2,1)S(1)}, bf16[128,2176]{1,0:T(8,128)(2,1)S(1)}, u32[]{:S(2)}, u32[]{:S(2)}) collective-permute-start(bf16[128,2176]{1,0:T(8,128)(2,1)S(1)} %collective-permute-done.1.refs_1_), channel_id=1, source_target_pairs={{0,1},{1,0},{2,3},{3,2},{4,5},{5,4},{6,7},{7,6},{8,9},{9,8},{10,11... | collective-permute-start | bytes 1671176 | tf_op jit(solution)/shard_map/ppermute | solution.py:34
  52.3 4.3 %collective-permute-start.6 = (bf16[128,2176]{1,0:T(8,128)(2,1)S(1)}, bf16[128,2176]{1,0:T(8,128)(2,1)S(1)}, u32[]{:S(2)}, u32[]{:S(2)}) collective-permute-start(bf16[128,2176]{1,0:T(8,128)(2,1)S(1)} %collective-permute-done.4.refs_3_), channel_id=1, source_target_pairs={{0,1},{1,0},{2,3},{3,2},{4,5},{5,4},{6,7},{7,6},{8,9},{9,8},{10,11... | collective-permute-start | bytes 1671176 | tf_op jit(solution)/shard_map/ppermute | solution.py:34

commit v13 on v10

--- a/solution.py
+++ b/solution.py
@@ -16,8 +16,8 @@
 NOTE = 2 * KV_WIDTH
 MASKED = -1e30
 HALF = GROUP // 2
-CHUNKS = (20, 24, 20)
-VMEM_GRANT = 48 * 1024 * 1024
+CHUNKS = (20, 26, 18)
+VMEM_GRANT = 24 * 1024 * 1024
 
 WHOLE = pl.BlockSpec(memory_space=pltpu.VMEM)
 ANYWHERE = pl.BlockSpec(memory_space=pl.ANY)
@@ -40,18 +40,16 @@
     return lax.all_to_all(spread, axis, split_axis=0, concat_axis=0)
 
 
-def shift_in_known(own_count, quota):
+def shifts_in(own_count, quota):
     n = lax.axis_size("dp")
     replica = lax.axis_index("dp")
     if n > 4:
         all_counts = everyones(own_count[None], "dp")[:, 0]
         places = jnp.arange(n, dtype=jnp.int32)
         before = jnp.sum(jnp.where(places < replica, all_counts, 0))
-        return jnp.stack([before - replica * quota, jnp.int32(0)])
-    shift = jnp.where(own_count == 0, quota, 0)
-    shift = jnp.where(replica == n - 1, quota - own_count, shift)
-    shift = jnp.where(replica == 0, 0, shift)
-    return jnp.stack([shift, (replica == 1).astype(jnp.int32)])
+        before_last = jnp.sum(jnp.where(places < replica - 1, all_counts, 0))
+        return jnp.stack([before - replica * quota, before_last - (replica - 1) * quota])
+    return jnp.stack([jnp.maximum(quota - own_count, 0), jnp.int32(0)])
 
 
 def place_rows(hot, arrived, local):
@@ -61,9 +59,7 @@
 
 def settle_kernel(shift_ref, docs_ref, arrived_ref, local_ref, out_ref, hot_ref):
     quota = out_ref.shape[0]
-    count_before = arrived_ref[:, NOTE:].astype(jnp.float32).astype(jnp.int32)
-    shift = jnp.where(shift_ref[1] == 1, count_before - quota, shift_ref[0])
-    shift_before = shift - count_before + quota
+    shift, shift_before = shift_ref[0], shift_ref[1]
     row = lax.broadcasted_iota(jnp.int32, (quota, quota), 0)
     col = lax.broadcasted_iota(jnp.int32, (quota, quota), 1)
     turned = row - shift_before
@@ -72,7 +68,7 @@
     hot_local = jnp.where(col == row - shift, 1.0, 0.0)
     hot = jnp.concatenate([hot_arrived, hot_local], axis=1).astype(jnp.bfloat16)
     hot_ref[...] = hot
-    out_ref[:, :NOTE] = place_rows(hot, arrived_ref[:, :NOTE], local_ref[...])
+    out_ref[:, :NOTE] = place_rows(hot, arrived_ref[...], local_ref[...])
     docs = jnp.broadcast_to(docs_ref[...].astype(jnp.float32), (quota, quota))
     out_ref[:, NOTE:] = docs.astype(jnp.bfloat16)
 
@@ -84,7 +80,7 @@
         in_specs=[SCALARS, WHOLE, WHOLE, WHOLE],
         out_specs=[WHOLE, WHOLE],
         out_shape=[
-            jax.ShapeDtypeStruct(arrived.shape, jnp.bfloat16),
+            jax.ShapeDtypeStruct((quota, NOTE + quota), jnp.bfloat16),
             jax.ShapeDtypeStruct((quota, 2 * quota), jnp.bfloat16),
         ],
         compiler_params=pltpu.CompilerParams(vmem_limit_bytes=VMEM_GRANT),
@@ -118,66 +114,49 @@
     return found
 
 
-def in_place(kernel, operands, out, more_out=(), more_specs=(), **arguments):
-    specs = arguments.pop("in_specs") + [ANYWHERE]
-    return pl.pallas_call(
-        kernel,
-        in_specs=specs,
-        out_specs=[ANYWHERE, *more_specs],
-        out_shape=[jax.ShapeDtypeStruct(out.shape, out.dtype), *more_out],
-        input_output_aliases={len(operands): 0},
-        cost_estimate=pl.CostEstimate(flops=0, bytes_accessed=0, transcendentals=0),
-        compiler_params=pltpu.CompilerParams(vmem_limit_bytes=VMEM_GRANT),
-        **arguments,
-    )(*operands, out)
-
-
-def stage_kernel(q_hbm, out_hbm, sem):
-    copy = pltpu.make_async_copy(q_hbm.at[:, 0 : out_hbm.shape[1]], out_hbm, sem)
-    copy.start()
-    copy.wait()
+def stage_kernel(q_hbm, *refs):
+    targets, sems = refs[:-1], refs[-1]
+    first, started = 0, []
+    for i, target in enumerate(targets):
+        quota, width = target.shape
+        copy = pltpu.make_async_copy(
+            q_hbm.at[0, 0:quota, first : first + width], target, sems.at[i]
+        )
+        copy.start()
+        started.append(copy)
+        first += width
+    for copy in started:
+        copy.wait()
 
 
 def stage_local(q_rows, quota):
     return pl.pallas_call(
         stage_kernel,
         in_specs=[ANYWHERE],
-        out_specs=ANYWHERE,
-        out_shape=jax.ShapeDtypeStruct((1, quota, QUERY_HEADS * HEAD_SIZE), jnp.bfloat16),
-        scratch_shapes=[pltpu.SemaphoreType.DMA],
+        out_specs=[WHOLE] * len(CHUNKS),
+        out_shape=[
+            jax.ShapeDtypeStruct((quota, heads * HEAD_SIZE), jnp.bfloat16) for heads in CHUNKS
+        ],
+        scratch_shapes=[pltpu.SemaphoreType.DMA((len(CHUNKS),))],
         compiler_params=pltpu.CompilerParams(vmem_limit_bytes=VMEM_GRANT),
         name="stage_local",
     )(q_rows)
 
 
-def place_kernel(first, hot_ref, arrived_ref, in_hbm, out_hbm, local, placed, in_sem, out_sem):
-    quota, width = arrived_ref.shape
-    cols = head_columns(first, width // HEAD_SIZE)
-    fetch = pltpu.make_async_copy(in_hbm.at[0, :, cols], local, in_sem)
-    fetch.start()
-    fetch.wait()
-    for head, heads in pieces(first, width // HEAD_SIZE):
-        own = head_columns(head - first, heads)
-        placed[:, own] = place_rows(hot_ref[...], arrived_ref[:, own], local[:, own])
-    store = pltpu.make_async_copy(placed, out_hbm.at[0, :, cols], out_sem)
-    store.start()
-    store.wait()
-
-
-def place_queries(hot, arrived, first, out):
-    return in_place(
-        functools.partial(place_kernel, first),
-        [hot, arrived],
-        out,
-        in_specs=[WHOLE, WHOLE],
-        scratch_shapes=[
-            pltpu.VMEM(arrived.shape, jnp.bfloat16),
-            pltpu.VMEM(arrived.shape, jnp.bfloat16),
-            pltpu.SemaphoreType.DMA,
-            pltpu.SemaphoreType.DMA,
-        ],
+def place_kernel(hot_ref, arrived_ref, local_ref, placed_ref):
+    for cols in (head_columns(*piece) for piece in pieces(0, placed_ref.shape[1] // HEAD_SIZE)):
+        placed_ref[:, cols] = place_rows(hot_ref[...], arrived_ref[:, cols], local_ref[:, cols])
+
+
+def place_queries(hot, arrived, local):
+    return pl.pallas_call(
+        place_kernel,
+        in_specs=[WHOLE, WHOLE, WHOLE],
+        out_specs=WHOLE,
+        out_shape=jax.ShapeDtypeStruct(arrived.shape, jnp.bfloat16),
+        compiler_params=pltpu.CompilerParams(vmem_limit_bytes=VMEM_GRANT),
         name="place_queries",
-    )[0]
+    )(hot, arrived, local)
 
 
 def make_bias(kv_refs, far_ref, mate_ref, bias, rank):
@@ -259,26 +238,31 @@
         scores = later
 
 
-def early_kernel(blocks, count, rank_ref, *refs):
+def early_kernel(blocks, chunks, rank_ref, *refs):
     kv_refs, far_ref, mate_ref = refs[: blocks - 1], refs[blocks - 1], refs[blocks]
-    in_hbm, _, result, local, bias, rest, queries, sems = refs[blocks + 1 :]
-    late = head_columns(count, QUERY_HEADS - count)
-    fetch = pltpu.make_async_copy(in_hbm.at[0, :, head_columns(0, count)], queries, sems.at[0])
-    fetch.start()
+    placed_refs = refs[blocks + 1 : blocks + 1 + len(chunks)]
+    result, bias, rest = refs[blocks + 1 + len(chunks) :]
+    count = sum(chunks)
     rank = rank_ref[0]
     make_bias(kv_refs, far_ref, mate_ref, bias, rank)
     choose_rest(0, count, lax.rem(rank, 2), far_ref, mate_ref, rest)
-    fetch.wait()
-    ahead = pltpu.make_async_copy(in_hbm.at[0, :, late], local, sems.at[1])
-    ahead.start()
-    attend_heads(0, count, [*kv_refs, rest], bias, lambda cols: queries[:, cols], result)
-    ahead.wait()
+
+    def take(cols):
+        found, at = [], 0
+        for ref in placed_refs:
+            start, stop = max(cols.start - at, 0), min(cols.stop - at, ref.shape[1])
+            if start < stop:
+                found.append(ref[:, start:stop])
+            at += ref.shape[1]
+        return found[0] if len(found) == 1 else jnp.concatenate(found, axis=1)
+
+    attend_heads(0, count, [*kv_refs, rest], bias, take, result)
 
 
 def late_kernel(blocks, first, rank_ref, *refs):
     kv_refs, far_ref, mate_ref = refs[: blocks - 1], refs[blocks - 1], refs[blocks]
-    hot_ref, arrived_hbm, early_ref, local_ref, _, out_hbm = refs[blocks + 1 : blocks + 7]
-    bias, rest, arrived, result, sems = refs[blocks + 7 :]
+    hot_ref, arrived_hbm, local_ref, early_ref, out_hbm = refs[blocks + 1 : blocks + 6]
+    bias, rest, arrived, result, sems = refs[blocks + 6 :]
     count = QUERY_HEADS - first
     fetch = pltpu.make_async_copy(arrived_hbm, arrived, sems.at[0])
     fetch.start()
@@ -299,38 +283,36 @@
     store.wait()
 
 
-def attend(rank, hot, arrived, kv_blocks, out):
+def attend(rank, hot, placed, arrived, local, kv_blocks):
     quota, width = arrived.shape
     blocks = len(kv_blocks) - 1
-    first = QUERY_HEADS - width // HEAD_SIZE
+    chunks = [chunk.shape[1] // HEAD_SIZE for chunk in placed]
+    first = sum(chunks)
     bias = pltpu.VMEM((quota, blocks * quota), jnp.float32)
     rest = pltpu.VMEM((quota, NOTE), jnp.bfloat16)
-    own = (arrived.shape, jnp.bfloat16)
-    others = ((quota, first * HEAD_SIZE), jnp.bfloat16)
-    out, result, local = in_place(
-        functools.partial(early_kernel, blocks, first),
-        [rank, *kv_blocks],
-        out,
-        more_out=[jax.ShapeDtypeStruct(*others), jax.ShapeDtypeStruct(*own)],
-        more_specs=[WHOLE, WHOLE],
-        in_specs=[SCALARS] + [WHOLE] * len(kv_blocks),
-        scratch_shapes=[bias, rest, pltpu.VMEM(*others), pltpu.SemaphoreType.DMA((2,))],
+    own = pltpu.VMEM(arrived.shape, jnp.bfloat16)
+    hints = dict(
+        cost_estimate=pl.CostEstimate(flops=0, bytes_accessed=0, transcendentals=0),
+        compiler_params=pltpu.CompilerParams(vmem_limit_bytes=VMEM_GRANT),
+    )
+    result = pl.pallas_call(
+        functools.partial(early_kernel, blocks, chunks),
+        in_specs=[SCALARS] + [WHOLE] * (len(kv_blocks) + len(placed)),
+        out_specs=WHOLE,
+        out_shape=jax.ShapeDtypeStruct((quota, first * HEAD_SIZE), jnp.bfloat16),
+        scratch_shapes=[bias, rest],
         name="attend_early",
-    )
-    return in_place(
+        **hints,
+    )(rank, *kv_blocks, *placed)
+    return pl.pallas_call(
         functools.partial(late_kernel, blocks, first),
-        [rank, *kv_blocks, hot, arrived, result, local],
-        out,
-        in_specs=[SCALARS] + [WHOLE] * (len(kv_blocks) + 1) + [ANYWHERE, WHOLE, WHOLE],
-        scratch_shapes=[
-            bias,
-            rest,
-            pltpu.VMEM(*own),
-            pltpu.VMEM(*own),
-            pltpu.SemaphoreType.DMA((3,)),
-        ],
+        in_specs=[SCALARS] + [WHOLE] * (len(kv_blocks) + 1) + [ANYWHERE, WHOLE, ANYWHERE],
+        out_specs=ANYWHERE,
+        out_shape=jax.ShapeDtypeStruct((1, quota, QUERY_HEADS * HEAD_SIZE), jnp.bfloat16),
+        scratch_shapes=[bias, rest, own, own, pltpu.SemaphoreType.DMA((3,))],
         name="attend_late",
-    )[0]
+        **hints,
+    )(rank, *kv_blocks, hot, arrived, local, result)
 
 
 def circular_tail(rows, later):
@@ -346,12 +328,7 @@
 
     later = quota + jnp.arange(quota, dtype=jnp.int32) < own_count
     kv_tail = jnp.concatenate(
-        [
-            circular_tail(k_rows[0], later),
-            circular_tail(value_slot_rows[0], later),
-            jnp.broadcast_to(own_count.astype(jnp.bfloat16), (quota, quota)),
-        ],
-        axis=1,
+        [circular_tail(k_rows[0], later), circular_tail(value_slot_rows[0], later)], axis=1
     )
     local_kv = jnp.concatenate([k_rows[0, :quota], value_slot_rows[0, :quota]], axis=1)
     kv_tail, later = lax.optimization_barrier((kv_tail, later))
@@ -365,24 +342,23 @@
     q_tails = lax.optimization_barrier(q_tails)
     arrived_q = [shifted(tail, "dp", 1) for tail in q_tails]
 
-    shift = shift_in_known(own_count, quota)
-    out = stage_local(q_rows, quota)
-    local_kv, out = lax.optimization_barrier((local_kv, out))
+    shift = shifts_in(own_count, quota)
+    local_q = stage_local(q_rows, quota)
+    local_kv, local_q = lax.optimization_barrier((local_kv, local_q))
     own, hot = settle_kv(shift, doc_ids, arrived_kv, local_kv)
 
-    kv_blocks = [own]
+    kv_blocks, placed = [own], []
     carried = own
     for back in range(1, rounds + 1):
         carried = shifted(carried, "ctx", 2)
         kv_blocks.append(carried)
         if back < len(CHUNKS):
-            first = sum(CHUNKS[: back - 1])
-            out = place_queries(hot, arrived_q[back - 1], first, out)
-            carried, out = lax.optimization_barrier((carried, out))
+            placed.append(place_queries(hot, arrived_q[back - 1], local_q[back - 1]))
+            carried, placed[-1] = lax.optimization_barrier((carried, placed[-1]))
         if back < rounds:
             kv_blocks.append(across_cores(carried))
-    kv_blocks += [across_cores(carried, (1,)), across_cores(own, (0,))]
-    return attend(rank[None], hot, arrived_q[-1], kv_blocks, out)
+    kv_blocks += [across_cores(carried), across_cores(own, (0,))]
+    return attend(rank[None], hot, placed, arrived_q[-1], local_q[-1], kv_blocks)
 
 
 def solution(mesh):

time: 71.7 us -> 71.5 us (level)
  starting transfers between devices: 25.2 us -> 20 us
  Pallas kernels: 20 us -> 15.7 us
  waiting for transfers between devices: 20.4 us -> 24.6 us
  local copies, waits for them, and re-layouts: 1.01 us -> 5.09 us
  other arithmetic: 3.77 us -> 4.6 us
    ppermute x3, starting transfers between devices: 9.28 us -> 4.14 us  [across_cores(): lax.ppermute(x, 'ctx', [(i, i ^ 1) for i in range(n) if i % 2 in sources])]
    pallas_call x5, Pallas kernels: 19.1 us -> 14.9 us  [the longest x1 7.57 us: attend(): pl.pallas_call(functools.partial(early_kernel, blocks, chunks), in_specs=...]
    unnamed x6 -> x16, local copies, waits for them, and re-layouts: 0.02 us -> 4.02 us
    ppermute x6, waiting for transfers between devices: 18.8 us -> 22.2 us  [shifted(): return lax.ppermute(x, axis, [(i, i + steps) for i in range(n - steps)])]
    ppermute x3, waiting for transfers between devices: 1.51 us -> 2.42 us  [across_cores(): lax.ppermute(x, 'ctx', [(i, i ^ 1) for i in range(n) if i % 2 in sources])]
    select_n x3 -> x4, other arithmetic: 3.55 us -> 4.45 us  [circular_tail(): return jnp.where(later[:, None], rows[quota:], rows[:quota])]
  transfers between devices with their start and end apart: 9 -> 9, of which waited for: 4 -> 5; matrix products, arithmetic and copies ran while one was open for 4% -> 6% of each run, Pallas kernels for 20% -> 13%
where the time goes in v13:
time: 71.5 us; the launch traced here: 71 us
  waiting for transfers between devices  24.6 us (34%)
  starting transfers between devices  20 us (28%)
  Pallas kernels  15.7 us (22%)
  local copies, waits for them, and re-layouts  5.09 us (7%)
  other arithmetic  4.6 us (6%)
  between operations  0.98 us (1%)
    ppermute x6, waiting for transfers between devices, shifted(): return lax.ppermute(x, axis, [(i, i + steps) for i in range(n - steps)])  22.2 us
    ppermute x6, starting transfers between devices, shifted(): return lax.ppermute(x, axis, [(i, i + steps) for i in range(n - steps)])  15.9 us
    pallas_call x1, Pallas kernels, attend(): pl.pallas_call(functools.partial(early_kernel, blocks, chunks), in_specs=...  7.57 us
    pallas_call x1, Pallas kernels, attend(): pl.pallas_call(functools.partial(late_kernel, blocks, first), in_specs=[S...  6.39 us
    select_n x4, other arithmetic, circular_tail(): return jnp.where(later[:, None], rows[quota:], rows[:quota])  4.45 us
    ppermute x3, starting transfers between devices, across_cores(): lax.ppermute(x, 'ctx', [(i, i ^ 1) for i in range(n) if i % 2 in sources])  4.14 us
    unnamed x16, local copies, waits for them, and re-layouts  4.02 us
    ppermute x3, waiting for transfers between devices, across_cores(): lax.ppermute(x, 'ctx', [(i, i ^ 1) for i in range(n) if i % 2 in sources])  2.42 us
  transfers between devices with their start and end apart: 9, of which 5 were waited for; matrix products, arithmetic and copies ran while one was open for 6% of the time, Pallas kernels for 13%

profile of v13, /device:TPU:21, one launch (start us, length us, event | category | flops | bytes accessed | tf_op | source)
XLA Modules:
  0.0 71.0 jit_solution(14021914963071503752)
XLA Ops:
  0.0 0.0 copy-start
  0.8 1.5 %bitcast_select_fusion.4 = (bf16[128,1024]{1,0:T(8,128)(2,1)S(1)}, bf16[128,1024]{1,0:T(8,128)(2,1)S(1)}) fusion(bf16[1,256,1024]{2,1,0:T(8,128)(2,1)} %param.6, pred[128]{0:T(512)(128)(4,1)S(1)} %add_compare_fusion, bf16[1,256,1024]{2,1,0:T(8,128)(2,1)} %param.7), kind=kLoop, calls=%fused_computation.6 | loop fusion | flops 262144 | bytes 1572992 | tf_op jit(solution)/shard_map/jit(_where)/select_n | solution.py:320
  2.3 3.1 %collective-permute-start = (bf16[128,2048]{1,0:T(8,128)(2,1)S(1)}, bf16[128,2048]{1,0:T(8,128)(2,1)S(1)}, u32[]{:S(2)}, u32[]{:S(2)}) collective-permute-start(bf16[128,2048]{1,0:T(8,128)(2,1)S(1)} %pad_maximum_fusion), channel_id=1, source_target_pairs={{0,8},{8,16},{16,24},{1,9},{9,17},{17,25},{2,10},{10,18},{18,26},{... | collective-permute-start | bytes 1572872 | tf_op jit(solution)/shard_map/ppermute | solution.py:29
  5.5 1.1 %slice_bitcast_fusion = (bf16[128,1024]{1,0:T(8,128)(2,1)S(1)}, bf16[128,1024]{1,0:T(8,128)(2,1)S(1)}) fusion(bf16[1,256,1024]{2,1,0:T(8,128)(2,1)} %param.7, bf16[1,256,1024]{2,1,0:T(8,128)(2,1)} %param.6), kind=kLoop, calls=%fused_computation.7 | loop fusion | bytes 1048576 | tf_op jit(solution)/shard_map/slice | solution.py:320
  6.6 0.0 copy-done
  6.6 1.0 %bitcast_select_fusion.2 = bf16[128,2304]{1,0:T(8,128)(2,1)} fusion(bf16[1,256,8192]{2,1,0:T(8,128)(2,1)S(1)} %copy-done, pred[128]{0:T(512)(128)(4,1)S(1)} %add_compare_fusion), kind=kLoop, calls=%fused_computation.2 | loop fusion | flops 294912 | bytes 1769600 | tf_op jit(solution)/shard_map/jit(_where)/select_n | solution.py:320
  7.6 0.0 copy-start.7
  7.6 1.1 %bitcast_select_fusion = bf16[128,3328]{1,0:T(8,128)(2,1)} fusion(bf16[1,256,8192]{2,1,0:T(8,128)(2,1)S(1)} %copy-done, pred[128]{0:T(512)(128)(4,1)S(1)} %add_compare_fusion), kind=kLoop, calls=%fused_computation | loop fusion | flops 425984 | bytes 2556032 | tf_op jit(solution)/shard_map/jit(_where)/select_n | solution.py:320
  8.6 1.0 %bitcast_select_fusion.1 = bf16[128,2560]{1,0:T(8,128)(2,1)} fusion(bf16[1,256,8192]{2,1,0:T(8,128)(2,1)S(1)} %copy-done, pred[128]{0:T(512)(128)(4,1)S(1)} %add_compare_fusion), kind=kLoop, calls=%fused_computation.1 | loop fusion | flops 327680 | bytes 1966208 | tf_op jit(solution)/shard_map/jit(_where)/select_n | solution.py:320
  9.6 1.9 %collective-permute-start.2 = (bf16[128,2560]{1,0:T(8,128)(2,1)}, bf16[128,2560]{1,0:T(8,128)(2,1)S(1)}, u32[]{:S(2)}, u32[]{:S(2)}) collective-permute-start(bf16[128,2560]{1,0:T(8,128)(2,1)} %bitcast_select_fusion.1), channel_id=1, source_target_pairs={{0,8},{8,16},{16,24},{1,9},{9,17},{17,25},{2,10},{10,18},{18,26},{... | collective-permute-start | bytes 1966088 | tf_op jit(solution)/shard_map/ppermute | solution.py:29
  11.5 0.2 stage_local.1
  11.7 0.0 copy-start.1
  11.7 0.9 %copy-done.1 = bf16[128,3328]{1,0:T(8,128)(2,1)} copy-done((bf16[128,3328]{1,0:T(8,128)(2,1)}, bf16[128,3328]{1,0:T(8,128)(2,1)S(1)}, u32[]{:S(2)}) %copy-start.1) | copy-done | bytes 851992
  12.6 0.0 copy-start.5
  12.6 0.8 %copy-done.5 = bf16[128,2304]{1,0:T(8,128)(2,1)} copy-done((bf16[128,2304]{1,0:T(8,128)(2,1)}, bf16[128,2304]{1,0:T(8,128)(2,1)S(1)}, u32[]{:S(2)}) %copy-start.5) | copy-done | bytes 589848
  13.5 0.0 copy-start.3
  13.5 0.1 pad_add_fusion.shift_ref
  13.5 4.4 %collective-permute-done.arrived_ref = bf16[128,2048]{1,0:T(8,128)(2,1)S(1)} collective-permute-done((bf16[128,2048]{1,0:T(8,128)(2,1)S(1)}, bf16[128,2048]{1,0:T(8,128)(2,1)S(1)}, u32[]{:S(2)}, u32[]{:S(2)}) %collective-permute-start) | collective-permute-done | bytes 524320 | tf_op jit(solution)/shard_map/ppermute | solution.py:29
  17.9 0.0 copy-done.7
  17.9 0.8 %settle_kv.1 = (bf16[128,2176]{1,0:T(8,128)(2,1)S(1)}, bf16[128,256]{1,0:T(8,128)(2,1)S(1)}) custom-call(s32[2]{0:T(128)S(1)} %pad_add_fusion.shift_ref, s32[1,128]{1,0:T(1,128)S(1)} %copy-done.7, bf16[128,2048]{1,0:T(8,128)(2,1)S(1)} %collective-permute-done.arrived_ref, bf16[128,2048]{1,0:T(8,128)(2,1)S(1)} %pad_maximum_fusion.1.local_ref), custom_call_target="tpu_custom_call" | custom-call | tf_op jit(solution)/shard_map/settle_kv/pallas_call | solution.py:78
  18.8 3.2 %collective-permute-start.1 = (bf16[128,2176]{1,0:T(8,128)(2,1)S(1)}, bf16[128,2176]{1,0:T(8,128)(2,1)S(1)}, u32[]{:S(2)}, u32[]{:S(2)}) collective-permute-start(bf16[128,2176]{1,0:T(8,128)(2,1)S(1)} %get-tuple-element.32.refs_0_), channel_id=1, source_target_pairs={{0,2},{1,3},{2,4},{3,5},{4,6},{5,7},{8,10},{9,11},{10,12},{11,13},... | collective-permute-start | bytes 1671176 | tf_op jit(solution)/shard_map/ppermute | solution.py:29
  22.0 2.2 %collective-permute-start.5 = (bf16[128,3328]{1,0:T(8,128)(2,1)}, bf16[128,3328]{1,0:T(8,128)(2,1)S(1)}, u32[]{:S(2)}, u32[]{:S(2)}) collective-permute-start(bf16[128,3328]{1,0:T(8,128)(2,1)} %bitcast_select_fusion), channel_id=1, source_target_pairs={{0,8},{8,16},{16,24},{1,9},{9,17},{17,25},{2,10},{10,18},{18,26},{... | collective-permute-start | bytes 2555912 | tf_op jit(solution)/shard_map/ppermute | solution.py:29
  24.2 7.7 %collective-permute-done.2.arrived_ref = bf16[128,2560]{1,0:T(8,128)(2,1)S(1)} collective-permute-done((bf16[128,2560]{1,0:T(8,128)(2,1)}, bf16[128,2560]{1,0:T(8,128)(2,1)S(1)}, u32[]{:S(2)}, u32[]{:S(2)}) %collective-permute-start.2) | collective-permute-done | bytes 655392 | tf_op jit(solution)/shard_map/ppermute | solution.py:29
  32.0 0.0 copy-done.3
  32.0 0.0 copy-start.4
  32.0 1.1 %copy-done.4 = bf16[128,2560]{1,0:T(8,128)(2,1)S(1)} copy-done((bf16[128,2560]{1,0:T(8,128)(2,1)S(1)}, bf16[128,2560]{1,0:T(8,128)(2,1)}, u32[]{:S(2)}) %copy-start.4) | copy-done | bytes 655384
  33.1 0.3 place_queries.2.refs_6_
  33.4 0.0 collective-permute-done.1.refs_1_
  33.4 3.2 %collective-permute-start.4 = (bf16[128,2176]{1,0:T(8,128)(2,1)S(1)}, bf16[128,2176]{1,0:T(8,128)(2,1)S(1)}, u32[]{:S(2)}, u32[]{:S(2)}) collective-permute-start(bf16[128,2176]{1,0:T(8,128)(2,1)S(1)} %collective-permute-done.1.refs_1_), channel_id=1, source_target_pairs={{0,2},{1,3},{2,4},{3,5},{4,6},{5,7},{8,10},{9,11},{10,12},{11,13},... | collective-permute-start | bytes 1671176 | tf_op jit(solution)/shard_map/ppermute | solution.py:29
  36.6 2.2 %collective-permute-start.8 = (bf16[128,2304]{1,0:T(8,128)(2,1)}, bf16[128,2304]{1,0:T(8,128)(2,1)}, u32[]{:S(2)}, u32[]{:S(2)}) collective-permute-start(bf16[128,2304]{1,0:T(8,128)(2,1)} %bitcast_select_fusion.2), channel_id=1, source_target_pairs={{0,8},{8,16},{16,24},{1,9},{9,17},{17,25},{2,10},{10,18},{18,26},{... | collective-permute-start | bytes 1769480 | tf_op jit(solution)/shard_map/ppermute | solution.py:29
  38.9 1.3 %collective-permute-start.7 = (bf16[128,2176]{1,0:T(8,128)(2,1)S(1)}, bf16[128,2176]{1,0:T(8,128)(2,1)}, u32[]{:S(2)}, u32[]{:S(2)}) collective-permute-start(bf16[128,2176]{1,0:T(8,128)(2,1)S(1)} %get-tuple-element.32.refs_0_), channel_id=1, source_target_pairs={{0,1},{2,3},{4,5},{6,7},{8,9},{10,11},{12,13},{14,15},{16,17},{18,... | collective-permute-start | bytes 1671176 | tf_op jit(solution)/shard_map/ppermute | solution.py:34
  40.2 10.1 %collective-permute-done.5.arrived_ref = bf16[128,3328]{1,0:T(8,128)(2,1)S(1)} collective-permute-done((bf16[128,3328]{1,0:T(8,128)(2,1)}, bf16[128,3328]{1,0:T(8,128)(2,1)S(1)}, u32[]{:S(2)}, u32[]{:S(2)}) %collective-permute-start.5) | collective-permute-done | bytes 852000 | tf_op jit(solution)/shard_map/ppermute | solution.py:29
  50.2 0.0 copy-start.2
  50.2 1.2 %copy-done.2 = bf16[128,3328]{1,0:T(8,128)(2,1)S(1)} copy-done((bf16[128,3328]{1,0:T(8,128)(2,1)S(1)}, bf16[128,3328]{1,0:T(8,128)(2,1)}, u32[]{:S(2)}) %copy-start.2) | copy-done | bytes 851992
  51.4 0.4 place_queries.3.refs_7_
  51.8 2.8 %collective-permute-start.3 = (bf16[128,2176]{1,0:T(8,128)(2,1)S(1)}, bf16[128,2176]{1,0:T(8,128)(2,1)}, u32[]{:S(2)}, u32[]{:S(2)}) collective-permute-start(bf16[128,2176]{1,0:T(8,128)(2,1)S(1)} %collective-permute-done.1.refs_1_), channel_id=1, source_target_pairs={{0,1},{1,0},{2,3},{3,2},{4,5},{5,4},{6,7},{7,6},{8,9},{9,8},{10,11... | collective-permute-start | bytes 1671176 | tf_op jit(solution)/shard_map/ppermute | solution.py:34
  54.6 0.0 collective-permute-done.4.refs_3_
  54.6 0.1 collective-permute-start.6
  54.6 0.0 copy-start.6
  54.6 0.0 collective-permute-done.7.refs_5_
  54.6 1.6 %collective-permute-done.3.refs_2_ = bf16[128,2176]{1,0:T(8,128)(2,1)} collective-permute-done((bf16[128,2176]{1,0:T(8,128)(2,1)S(1)}, bf16[128,2176]{1,0:T(8,128)(2,1)}, u32[]{:S(2)}, u32[]{:S(2)}) %collective-permute-start.3) | collective-permute-done | bytes 557088 | tf_op jit(solution)/shard_map/ppermute | solution.py:34
  56.3 0.8 %collective-permute-done.6.refs_4_ = bf16[128,2176]{1,0:T(8,128)(2,1)} collective-permute-done((bf16[128,2176]{1,0:T(8,128)(2,1)S(1)}, bf16[128,2176]{1,0:T(8,128)(2,1)}, u32[]{:S(2)}, u32[]{:S(2)}) %collective-permute-start.6) | collective-permute-done | bytes 557088 | tf_op jit(solution)/shard_map/ppermute | solution.py:34
  57.1 7.6 %attend_early.1.refs_9_ = bf16[128,5888]{1,0:T(8,128)(2,1)S(1)} custom-call(s32[1]{0:T(128)} %bitcast.rank_ref, bf16[128,2176]{1,0:T(8,128)(2,1)S(1)} %get-tuple-element.32.refs_0_, bf16[128,2176]{1,0:T(8,128)(2,1)S(1)} %collective-permute-done.1.refs_1_, bf16[128,2176]{1,0:T(8,128)(2,1)} %collective-permute-done.3.refs_2_, ...), custom_call_target="tpu_custom_call" | custom-call | tf_op jit(solution)/shard_map/attend_early/pallas_call | solution.py:298
  64.6 0.0 collective-permute-done.8.refs_7_
  64.6 0.0 copy-done.6
  64.7 6.4 %attend_late.1 = bf16[1,128,8192]{2,1,0:T(8,128)(2,1)} custom-call(s32[1]{0:T(128)} %bitcast.rank_ref, bf16[128,2176]{1,0:T(8,128)(2,1)S(1)} %get-tuple-element.32.refs_0_, bf16[128,2176]{1,0:T(8,128)(2,1)S(1)} %collective-permute-done.1.refs_1_, bf16[128,2176]{1,0:T(8,128)(2,1)} %collective-permute-done.3.refs_2_, ...), custom_call_target="tpu_custom_call" | custom-call | tf_op jit(solution)/shard_map/attend_late/pallas_call | solution.py:307
  (3 shorter events, 0.1 us)
Async XLA Ops:
  0.0 6.6 %copy-start = (bf16[1,256,8192]{2,1,0:T(8,128)(2,1)S(1)}, bf16[1,256,8192]{2,1,0:T(8,128)(2,1)}, u32[]{:S(2)}) copy-start(bf16[1,256,8192]{2,1,0:T(8,128)(2,1)} %q_hbm.1) | copy-start | bytes 12582916
  2.3 15.6 %collective-permute-start = (bf16[128,2048]{1,0:T(8,128)(2,1)S(1)}, bf16[128,2048]{1,0:T(8,128)(2,1)S(1)}, u32[]{:S(2)}, u32[]{:S(2)}) collective-permute-start(bf16[128,2048]{1,0:T(8,128)(2,1)S(1)} %pad_maximum_fusion), channel_id=1, source_target_pairs={{0,8},{8,16},{16,24},{1,9},{9,17},{17,25},{2,10},{10,18},{18,26},{... | collective-permute-start | bytes 1572872 | tf_op jit(solution)/shard_map/ppermute | solution.py:29
  7.6 10.4 %copy-start.7 = (s32[1,128]{1,0:T(1,128)S(1)}, s32[1,128]{1,0:T(1,128)}, u32[]{:S(2)}) copy-start(s32[1,128]{1,0:T(1,128)} %docs_ref.1) | copy-start | bytes 1540
  9.6 22.4 %collective-permute-start.2 = (bf16[128,2560]{1,0:T(8,128)(2,1)}, bf16[128,2560]{1,0:T(8,128)(2,1)S(1)}, u32[]{:S(2)}, u32[]{:S(2)}) collective-permute-start(bf16[128,2560]{1,0:T(8,128)(2,1)} %bitcast_select_fusion.1), channel_id=1, source_target_pairs={{0,8},{8,16},{16,24},{1,9},{9,17},{17,25},{2,10},{10,18},{18,26},{... | collective-permute-start | bytes 1966088 | tf_op jit(solution)/shard_map/ppermute | solution.py:29
  11.7 0.9 %copy-start.1 = (bf16[128,3328]{1,0:T(8,128)(2,1)}, bf16[128,3328]{1,0:T(8,128)(2,1)S(1)}, u32[]{:S(2)}) copy-start(bf16[128,3328]{1,0:T(8,128)(2,1)S(1)} %get-tuple-element.39.local_ref) | copy-start | bytes 2555908
  12.6 0.8 %copy-start.5 = (bf16[128,2304]{1,0:T(8,128)(2,1)}, bf16[128,2304]{1,0:T(8,128)(2,1)S(1)}, u32[]{:S(2)}) copy-start(bf16[128,2304]{1,0:T(8,128)(2,1)S(1)} %get-tuple-element.42.refs_8_) | copy-start | bytes 1769476
  13.5 18.5 %copy-start.3 = (bf16[128,2560]{1,0:T(8,128)(2,1)}, bf16[128,2560]{1,0:T(8,128)(2,1)S(1)}, u32[]{:S(2)}) copy-start(bf16[128,2560]{1,0:T(8,128)(2,1)S(1)} %get-tuple-element.36.local_ref) | copy-start | bytes 1966084
  18.8 14.6 %collective-permute-start.1 = (bf16[128,2176]{1,0:T(8,128)(2,1)S(1)}, bf16[128,2176]{1,0:T(8,128)(2,1)S(1)}, u32[]{:S(2)}, u32[]{:S(2)}) collective-permute-start(bf16[128,2176]{1,0:T(8,128)(2,1)S(1)} %get-tuple-element.32.refs_0_), channel_id=1, source_target_pairs={{0,2},{1,3},{2,4},{3,5},{4,6},{5,7},{8,10},{9,11},{10,12},{11,13},... | collective-permute-start | bytes 1671176 | tf_op jit(solution)/shard_map/ppermute | solution.py:29
  22.0 28.2 %collective-permute-start.5 = (bf16[128,3328]{1,0:T(8,128)(2,1)}, bf16[128,3328]{1,0:T(8,128)(2,1)S(1)}, u32[]{:S(2)}, u32[]{:S(2)}) collective-permute-start(bf16[128,3328]{1,0:T(8,128)(2,1)} %bitcast_select_fusion), channel_id=1, source_target_pairs={{0,8},{8,16},{16,24},{1,9},{9,17},{17,25},{2,10},{10,18},{18,26},{... | collective-permute-start | bytes 2555912 | tf_op jit(solution)/shard_map/ppermute | solution.py:29
  32.0 1.1 %copy-start.4 = (bf16[128,2560]{1,0:T(8,128)(2,1)S(1)}, bf16[128,2560]{1,0:T(8,128)(2,1)}, u32[]{:S(2)}) copy-start(bf16[128,2560]{1,0:T(8,128)(2,1)} %copy-done.3) | copy-start | bytes 1966084
  33.4 21.1 %collective-permute-start.4 = (bf16[128,2176]{1,0:T(8,128)(2,1)S(1)}, bf16[128,2176]{1,0:T(8,128)(2,1)S(1)}, u32[]{:S(2)}, u32[]{:S(2)}) collective-permute-start(bf16[128,2176]{1,0:T(8,128)(2,1)S(1)} %collective-permute-done.1.refs_1_), channel_id=1, source_target_pairs={{0,2},{1,3},{2,4},{3,5},{4,6},{5,7},{8,10},{9,11},{10,12},{11,13},... | collective-permute-start | bytes 1671176 | tf_op jit(solution)/shard_map/ppermute | solution.py:29
  36.6 28.0 %collective-permute-start.8 = (bf16[128,2304]{1,0:T(8,128)(2,1)}, bf16[128,2304]{1,0:T(8,128)(2,1)}, u32[]{:S(2)}, u32[]{:S(2)}) collective-permute-start(bf16[128,2304]{1,0:T(8,128)(2,1)} %bitcast_select_fusion.2), channel_id=1, source_target_pairs={{0,8},{8,16},{16,24},{1,9},{9,17},{17,25},{2,10},{10,18},{18,26},{... | collective-permute-start | bytes 1769480 | tf_op jit(solution)/shard_map/ppermute | solution.py:29
  38.9 15.8 %collective-permute-start.7 = (bf16[128,2176]{1,0:T(8,128)(2,1)S(1)}, bf16[128,2176]{1,0:T(8,128)(2,1)}, u32[]{:S(2)}, u32[]{:S(2)}) collective-permute-start(bf16[128,2176]{1,0:T(8,128)(2,1)S(1)} %get-tuple-element.32.refs_0_), channel_id=1, source_target_pairs={{0,1},{2,3},{4,5},{6,7},{8,9},{10,11},{12,13},{14,15},{16,17},{18,... | collective-permute-start | bytes 1671176 | tf_op jit(solution)/shard_map/ppermute | solution.py:34
  50.2 1.2 %copy-start.2 = (bf16[128,3328]{1,0:T(8,128)(2,1)S(1)}, bf16[128,3328]{1,0:T(8,128)(2,1)}, u32[]{:S(2)}) copy-start(bf16[128,3328]{1,0:T(8,128)(2,1)} %copy-done.1) | copy-start | bytes 2555908
  51.8 4.5 %collective-permute-start.3 = (bf16[128,2176]{1,0:T(8,128)(2,1)S(1)}, bf16[128,2176]{1,0:T(8,128)(2,1)}, u32[]{:S(2)}, u32[]{:S(2)}) collective-permute-start(bf16[128,2176]{1,0:T(8,128)(2,1)S(1)} %collective-permute-done.1.refs_1_), channel_id=1, source_target_pairs={{0,1},{1,0},{2,3},{3,2},{4,5},{5,4},{6,7},{7,6},{8,9},{9,8},{10,11... | collective-permute-start | bytes 1671176 | tf_op jit(solution)/shard_map/ppermute | solution.py:34
  54.6 2.5 %collective-permute-start.6 = (bf16[128,2176]{1,0:T(8,128)(2,1)S(1)}, bf16[128,2176]{1,0:T(8,128)(2,1)}, u32[]{:S(2)}, u32[]{:S(2)}) collective-permute-start(bf16[128,2176]{1,0:T(8,128)(2,1)S(1)} %collective-permute-done.4.refs_3_), channel_id=1, source_target_pairs={{0,1},{1,0},{2,3},{3,2},{4,5},{5,4},{6,7},{7,6},{8,9},{9,8},{10,11... | collective-permute-start | bytes 1671176 | tf_op jit(solution)/shard_map/ppermute | solution.py:34
  54.6 10.0 %copy-start.6 = (bf16[128,2304]{1,0:T(8,128)(2,1)S(1)}, bf16[128,2304]{1,0:T(8,128)(2,1)}, u32[]{:S(2)}) copy-start(bf16[128,2304]{1,0:T(8,128)(2,1)} %copy-done.5) | copy-start | bytes 1769476

commit v14 on v13

--- a/solution.py
+++ b/solution.py
@@ -17,7 +17,7 @@
 MASKED = -1e30
 HALF = GROUP // 2
 CHUNKS = (20, 26, 18)
-VMEM_GRANT = 24 * 1024 * 1024
+VMEM_GRANT = 48 * 1024 * 1024
 
 WHOLE = pl.BlockSpec(memory_space=pltpu.VMEM)
 ANYWHERE = pl.BlockSpec(memory_space=pl.ANY)
@@ -241,7 +241,7 @@
 def early_kernel(blocks, chunks, rank_ref, *refs):
     kv_refs, far_ref, mate_ref = refs[: blocks - 1], refs[blocks - 1], refs[blocks]
     placed_refs = refs[blocks + 1 : blocks + 1 + len(chunks)]
-    result, bias, rest = refs[blocks + 1 + len(chunks) :]
+    out_hbm, bias, rest, result, sem = refs[blocks + 1 + len(chunks) :]
     count = sum(chunks)
     rank = rank_ref[0]
     make_bias(kv_refs, far_ref, mate_ref, bias, rank)
@@ -257,11 +257,14 @@
         return found[0] if len(found) == 1 else jnp.concatenate(found, axis=1)
 
     attend_heads(0, count, [*kv_refs, rest], bias, take, result)
+    store = pltpu.make_async_copy(result, out_hbm.at[0, :, head_columns(0, count)], sem)
+    store.start()
+    store.wait()
 
 
 def late_kernel(blocks, first, rank_ref, *refs):
     kv_refs, far_ref, mate_ref = refs[: blocks - 1], refs[blocks - 1], refs[blocks]
-    hot_ref, arrived_hbm, local_ref, early_ref, out_hbm = refs[blocks + 1 : blocks + 6]
+    hot_ref, arrived_hbm, local_ref, _, out_hbm = refs[blocks + 1 : blocks + 6]
     bias, rest, arrived, result, sems = refs[blocks + 6 :]
     count = QUERY_HEADS - first
     fetch = pltpu.make_async_copy(arrived_hbm, arrived, sems.at[0])
@@ -270,16 +273,13 @@
     make_bias(kv_refs, far_ref, mate_ref, bias, rank)
     choose_rest(first, count, lax.rem(rank, 2), far_ref, mate_ref, rest)
     fetch.wait()
-    early = pltpu.make_async_copy(early_ref, out_hbm.at[0, :, head_columns(0, first)], sems.at[1])
-    early.start()
 
     def take(cols):
         return place_rows(hot_ref[...], arrived[:, cols], local_ref[:, cols])
 
     attend_heads(first, count, [*kv_refs, rest], bias, take, result)
-    store = pltpu.make_async_copy(result, out_hbm.at[0, :, head_columns(first, count)], sems.at[2])
+    store = pltpu.make_async_copy(result, out_hbm.at[0, :, head_columns(first, count)], sems.at[1])
     store.start()
-    early.wait()
     store.wait()
 
 
@@ -295,24 +295,32 @@
         cost_estimate=pl.CostEstimate(flops=0, bytes_accessed=0, transcendentals=0),
         compiler_params=pltpu.CompilerParams(vmem_limit_bytes=VMEM_GRANT),
     )
-    result = pl.pallas_call(
+    whole = jax.ShapeDtypeStruct((1, quota, QUERY_HEADS * HEAD_SIZE), jnp.bfloat16)
+    out = pl.pallas_call(
         functools.partial(early_kernel, blocks, chunks),
         in_specs=[SCALARS] + [WHOLE] * (len(kv_blocks) + len(placed)),
-        out_specs=WHOLE,
-        out_shape=jax.ShapeDtypeStruct((quota, first * HEAD_SIZE), jnp.bfloat16),
-        scratch_shapes=[bias, rest],
+        out_specs=ANYWHERE,
+        out_shape=whole,
+        scratch_shapes=[
+            bias,
+            rest,
+            pltpu.VMEM((quota, first * HEAD_SIZE), jnp.bfloat16),
+            pltpu.SemaphoreType.DMA,
+        ],
         name="attend_early",
         **hints,
     )(rank, *kv_blocks, *placed)
+    operands = [rank, *kv_blocks, hot, arrived, local]
     return pl.pallas_call(
         functools.partial(late_kernel, blocks, first),
         in_specs=[SCALARS] + [WHOLE] * (len(kv_blocks) + 1) + [ANYWHERE, WHOLE, ANYWHERE],
         out_specs=ANYWHERE,
-        out_shape=jax.ShapeDtypeStruct((1, quota, QUERY_HEADS * HEAD_SIZE), jnp.bfloat16),
-        scratch_shapes=[bias, rest, own, own, pltpu.SemaphoreType.DMA((3,))],
+        out_shape=whole,
+        input_output_aliases={len(operands): 0},
+        scratch_shapes=[bias, rest, own, own, pltpu.SemaphoreType.DMA((2,))],
         name="attend_late",
         **hints,
-    )(rank, *kv_blocks, hot, arrived, local, result)
+    )(*operands, out)
 
 
 def circular_tail(rows, later):

time: 71.5 us -> 72.7 us (1.017)
  Pallas kernels: 15.7 us -> 18.2 us
  waiting for transfers between devices: 24.6 us -> 23.3 us
    pallas_call x1, Pallas kernels: 0.2 us -> 1.55 us  [stage_local(): pl.pallas_call(stage_kernel, in_specs=[ANYWHERE], out_specs=[WHOLE] * len...]
    ppermute x6, waiting for transfers between devices: 22.2 us -> 20.9 us  [shifted(): return lax.ppermute(x, axis, [(i, i + steps) for i in range(n - steps)])]
    pallas_call x1, Pallas kernels: 7.57 us -> 8.73 us  [attend(): pl.pallas_call(functools.partial(early_kernel, blocks, chunks), in_specs=...]
  transfers between devices with their start and end apart: 9 -> 9, of which waited for: 5 -> 5; matrix products, arithmetic and copies ran while one was open for 6% -> 6% of each run, Pallas kernels for 13% -> 16%
where the time goes in v14:
time: 72.7 us; the launch traced here: 72.2 us
  waiting for transfers between devices  23.3 us (32%)
  starting transfers between devices  20 us (28%)
  Pallas kernels  18.2 us (25%)
  local copies, waits for them, and re-layouts  5.08 us (7%)
  other arithmetic  4.61 us (6%)
  between operations  0.98 us (1%)
    ppermute x6, waiting for transfers between devices, shifted(): return lax.ppermute(x, axis, [(i, i + steps) for i in range(n - steps)])  20.9 us
    ppermute x6, starting transfers between devices, shifted(): return lax.ppermute(x, axis, [(i, i + steps) for i in range(n - steps)])  15.9 us
    pallas_call x1, Pallas kernels, attend(): pl.pallas_call(functools.partial(early_kernel, blocks, chunks), in_specs=...  8.73 us
    pallas_call x1, Pallas kernels, attend(): pl.pallas_call(functools.partial(late_kernel, blocks, first), in_specs=[S...  6.38 us
    select_n x4, other arithmetic, circular_tail(): return jnp.where(later[:, None], rows[quota:], rows[:quota])  4.45 us
    ppermute x3, starting transfers between devices, across_cores(): lax.ppermute(x, 'ctx', [(i, i ^ 1) for i in range(n) if i % 2 in sources])  4.14 us
    unnamed x16, local copies, waits for them, and re-layouts  4.02 us
    ppermute x3, waiting for transfers between devices, across_cores(): lax.ppermute(x, 'ctx', [(i, i ^ 1) for i in range(n) if i % 2 in sources])  2.42 us
  transfers between devices with their start and end apart: 9, of which 5 were waited for; matrix products, arithmetic and copies ran while one was open for 6% of the time, Pallas kernels for 16%

profile of v14, /device:TPU:21, one launch (start us, length us, event | category | flops | bytes accessed | tf_op | source)
XLA Modules:
  0.0 72.2 jit_solution(3522069606647466410)
XLA Ops:
  0.0 0.0 copy-start.7
  0.8 1.5 %bitcast_select_fusion.4 = (bf16[128,1024]{1,0:T(8,128)(2,1)S(1)}, bf16[128,1024]{1,0:T(8,128)(2,1)S(1)}) fusion(bf16[1,256,1024]{2,1,0:T(8,128)(2,1)} %param.6, pred[128]{0:T(512)(128)(4,1)S(1)} %add_compare_fusion, bf16[1,256,1024]{2,1,0:T(8,128)(2,1)} %param.7), kind=kLoop, calls=%fused_computation.6 | loop fusion | flops 262144 | bytes 1572992 | tf_op jit(solution)/shard_map/jit(_where)/select_n | solution.py:328
  2.3 3.1 %collective-permute-start = (bf16[128,2048]{1,0:T(8,128)(2,1)S(1)}, bf16[128,2048]{1,0:T(8,128)(2,1)S(1)}, u32[]{:S(2)}, u32[]{:S(2)}) collective-permute-start(bf16[128,2048]{1,0:T(8,128)(2,1)S(1)} %pad_maximum_fusion), channel_id=1, source_target_pairs={{0,8},{8,16},{16,24},{1,9},{9,17},{17,25},{2,10},{10,18},{18,26},{... | collective-permute-start | bytes 1572872 | tf_op jit(solution)/shard_map/ppermute | solution.py:29
  5.5 1.1 %slice_bitcast_fusion = (bf16[128,1024]{1,0:T(8,128)(2,1)S(1)}, bf16[128,1024]{1,0:T(8,128)(2,1)S(1)}) fusion(bf16[1,256,1024]{2,1,0:T(8,128)(2,1)} %param.7, bf16[1,256,1024]{2,1,0:T(8,128)(2,1)} %param.6), kind=kLoop, calls=%fused_computation.7 | loop fusion | bytes 1048576 | tf_op jit(solution)/shard_map/slice | solution.py:328
  6.6 0.0 copy-done.7
  6.6 1.0 %bitcast_select_fusion.2 = bf16[128,2304]{1,0:T(8,128)(2,1)} fusion(bf16[1,256,8192]{2,1,0:T(8,128)(2,1)S(1)} %copy-done.7, pred[128]{0:T(512)(128)(4,1)S(1)} %add_compare_fusion), kind=kLoop, calls=%fused_computation.2 | loop fusion | flops 294912 | bytes 1769600 | tf_op jit(solution)/shard_map/jit(_where)/select_n | solution.py:328
  7.6 0.0 copy-start.6
  7.6 1.1 %bitcast_select_fusion = bf16[128,3328]{1,0:T(8,128)(2,1)} fusion(bf16[1,256,8192]{2,1,0:T(8,128)(2,1)S(1)} %copy-done.7, pred[128]{0:T(512)(128)(4,1)S(1)} %add_compare_fusion), kind=kLoop, calls=%fused_computation | loop fusion | flops 425984 | bytes 2556032 | tf_op jit(solution)/shard_map/jit(_where)/select_n | solution.py:328
  8.6 1.0 %bitcast_select_fusion.1 = bf16[128,2560]{1,0:T(8,128)(2,1)} fusion(bf16[1,256,8192]{2,1,0:T(8,128)(2,1)S(1)} %copy-done.7, pred[128]{0:T(512)(128)(4,1)S(1)} %add_compare_fusion), kind=kLoop, calls=%fused_computation.1 | loop fusion | flops 327680 | bytes 1966208 | tf_op jit(solution)/shard_map/jit(_where)/select_n | solution.py:328
  9.6 1.9 %collective-permute-start.2 = (bf16[128,2560]{1,0:T(8,128)(2,1)}, bf16[128,2560]{1,0:T(8,128)(2,1)S(1)}, u32[]{:S(2)}, u32[]{:S(2)}) collective-permute-start(bf16[128,2560]{1,0:T(8,128)(2,1)} %bitcast_select_fusion.1), channel_id=1, source_target_pairs={{0,8},{8,16},{16,24},{1,9},{9,17},{17,25},{2,10},{10,18},{18,26},{... | collective-permute-start | bytes 1966088 | tf_op jit(solution)/shard_map/ppermute | solution.py:29
  11.5 1.5 %stage_local.1 = (bf16[128,2560]{1,0:T(8,128)(2,1)S(1)}, bf16[128,3328]{1,0:T(8,128)(2,1)S(1)}, bf16[128,2304]{1,0:T(8,128)(2,1)S(1)}) custom-call(bf16[1,256,8192]{2,1,0:T(8,128)(2,1)} %q_hbm.1), custom_call_target="tpu_custom_call" | custom-call | tf_op jit(solution)/shard_map/stage_local/pallas_call | solution.py:133
  13.0 0.0 copy-start
  13.1 0.9 %copy-done = bf16[128,3328]{1,0:T(8,128)(2,1)} copy-done((bf16[128,3328]{1,0:T(8,128)(2,1)}, bf16[128,3328]{1,0:T(8,128)(2,1)S(1)}, u32[]{:S(2)}) %copy-start) | copy-done | bytes 851992
  14.0 0.0 copy-start.2
  14.0 0.8 %copy-done.2 = bf16[128,2560]{1,0:T(8,128)(2,1)} copy-done((bf16[128,2560]{1,0:T(8,128)(2,1)}, bf16[128,2560]{1,0:T(8,128)(2,1)S(1)}, u32[]{:S(2)}) %copy-start.2) | copy-done | bytes 655384
  14.8 0.0 copy-start.4
  14.8 0.1 pad_add_fusion.shift_ref
  14.9 3.0 %collective-permute-done.arrived_ref = bf16[128,2048]{1,0:T(8,128)(2,1)S(1)} collective-permute-done((bf16[128,2048]{1,0:T(8,128)(2,1)S(1)}, bf16[128,2048]{1,0:T(8,128)(2,1)S(1)}, u32[]{:S(2)}, u32[]{:S(2)}) %collective-permute-start) | collective-permute-done | bytes 524320 | tf_op jit(solution)/shard_map/ppermute | solution.py:29
  17.9 0.0 copy-done.6
  17.9 0.8 %settle_kv.1 = (bf16[128,2176]{1,0:T(8,128)(2,1)S(1)}, bf16[128,256]{1,0:T(8,128)(2,1)S(1)}) custom-call(s32[2]{0:T(128)S(1)} %pad_add_fusion.shift_ref, s32[1,128]{1,0:T(1,128)S(1)} %copy-done.6, bf16[128,2048]{1,0:T(8,128)(2,1)S(1)} %collective-permute-done.arrived_ref, bf16[128,2048]{1,0:T(8,128)(2,1)S(1)} %pad_maximum_fusion.1.local_ref), custom_call_target="tpu_custom_call" | custom-call | tf_op jit(solution)/shard_map/settle_kv/pallas_call | solution.py:78
  18.8 3.2 %collective-permute-start.1 = (bf16[128,2176]{1,0:T(8,128)(2,1)S(1)}, bf16[128,2176]{1,0:T(8,128)(2,1)S(1)}, u32[]{:S(2)}, u32[]{:S(2)}) collective-permute-start(bf16[128,2176]{1,0:T(8,128)(2,1)S(1)} %get-tuple-element.32.refs_0_), channel_id=1, source_target_pairs={{0,2},{1,3},{2,4},{3,5},{4,6},{5,7},{8,10},{9,11},{10,12},{11,13},... | collective-permute-start | bytes 1671176 | tf_op jit(solution)/shard_map/ppermute | solution.py:29
  22.0 2.2 %collective-permute-start.5 = (bf16[128,3328]{1,0:T(8,128)(2,1)}, bf16[128,3328]{1,0:T(8,128)(2,1)S(1)}, u32[]{:S(2)}, u32[]{:S(2)}) collective-permute-start(bf16[128,3328]{1,0:T(8,128)(2,1)} %bitcast_select_fusion), channel_id=1, source_target_pairs={{0,8},{8,16},{16,24},{1,9},{9,17},{17,25},{2,10},{10,18},{18,26},{... | collective-permute-start | bytes 2555912 | tf_op jit(solution)/shard_map/ppermute | solution.py:29
  24.2 7.7 %collective-permute-done.2.arrived_ref = bf16[128,2560]{1,0:T(8,128)(2,1)S(1)} collective-permute-done((bf16[128,2560]{1,0:T(8,128)(2,1)}, bf16[128,2560]{1,0:T(8,128)(2,1)S(1)}, u32[]{:S(2)}, u32[]{:S(2)}) %collective-permute-start.2) | collective-permute-done | bytes 655392 | tf_op jit(solution)/shard_map/ppermute | solution.py:29
  32.0 0.0 copy-done.4
  32.0 0.0 copy-start.3
  32.0 1.1 %copy-done.3 = bf16[128,2560]{1,0:T(8,128)(2,1)S(1)} copy-done((bf16[128,2560]{1,0:T(8,128)(2,1)S(1)}, bf16[128,2560]{1,0:T(8,128)(2,1)}, u32[]{:S(2)}) %copy-start.3) | copy-done | bytes 655384
  33.1 0.3 place_queries.2.refs_6_
  33.4 0.0 collective-permute-done.1.refs_1_
  33.4 3.2 %collective-permute-start.4 = (bf16[128,2176]{1,0:T(8,128)(2,1)S(1)}, bf16[128,2176]{1,0:T(8,128)(2,1)S(1)}, u32[]{:S(2)}, u32[]{:S(2)}) collective-permute-start(bf16[128,2176]{1,0:T(8,128)(2,1)S(1)} %collective-permute-done.1.refs_1_), channel_id=1, source_target_pairs={{0,2},{1,3},{2,4},{3,5},{4,6},{5,7},{8,10},{9,11},{10,12},{11,13},... | collective-permute-start | bytes 1671176 | tf_op jit(solution)/shard_map/ppermute | solution.py:29
  36.6 2.2 %collective-permute-start.8 = (bf16[128,2304]{1,0:T(8,128)(2,1)}, bf16[128,2304]{1,0:T(8,128)(2,1)}, u32[]{:S(2)}, u32[]{:S(2)}) collective-permute-start(bf16[128,2304]{1,0:T(8,128)(2,1)} %bitcast_select_fusion.2), channel_id=1, source_target_pairs={{0,8},{8,16},{16,24},{1,9},{9,17},{17,25},{2,10},{10,18},{18,26},{... | collective-permute-start | bytes 1769480 | tf_op jit(solution)/shard_map/ppermute | solution.py:29
  38.9 1.3 %collective-permute-start.7 = (bf16[128,2176]{1,0:T(8,128)(2,1)S(1)}, bf16[128,2176]{1,0:T(8,128)(2,1)}, u32[]{:S(2)}, u32[]{:S(2)}) collective-permute-start(bf16[128,2176]{1,0:T(8,128)(2,1)S(1)} %get-tuple-element.32.refs_0_), channel_id=1, source_target_pairs={{0,1},{2,3},{4,5},{6,7},{8,9},{10,11},{12,13},{14,15},{16,17},{18,... | collective-permute-start | bytes 1671176 | tf_op jit(solution)/shard_map/ppermute | solution.py:34
  40.2 10.1 %collective-permute-done.5.arrived_ref = bf16[128,3328]{1,0:T(8,128)(2,1)S(1)} collective-permute-done((bf16[128,3328]{1,0:T(8,128)(2,1)}, bf16[128,3328]{1,0:T(8,128)(2,1)S(1)}, u32[]{:S(2)}, u32[]{:S(2)}) %collective-permute-start.5) | collective-permute-done | bytes 852000 | tf_op jit(solution)/shard_map/ppermute | solution.py:29
  50.2 0.0 copy-start.1
  50.2 1.2 %copy-done.1 = bf16[128,3328]{1,0:T(8,128)(2,1)S(1)} copy-done((bf16[128,3328]{1,0:T(8,128)(2,1)S(1)}, bf16[128,3328]{1,0:T(8,128)(2,1)}, u32[]{:S(2)}) %copy-start.1) | copy-done | bytes 851992
  51.4 0.4 place_queries.3.refs_7_
  51.8 2.8 %collective-permute-start.3 = (bf16[128,2176]{1,0:T(8,128)(2,1)S(1)}, bf16[128,2176]{1,0:T(8,128)(2,1)}, u32[]{:S(2)}, u32[]{:S(2)}) collective-permute-start(bf16[128,2176]{1,0:T(8,128)(2,1)S(1)} %collective-permute-done.1.refs_1_), channel_id=1, source_target_pairs={{0,1},{1,0},{2,3},{3,2},{4,5},{5,4},{6,7},{7,6},{8,9},{9,8},{10,11... | collective-permute-start | bytes 1671176 | tf_op jit(solution)/shard_map/ppermute | solution.py:34
  54.6 0.0 collective-permute-done.4.refs_3_
  54.6 0.1 collective-permute-start.6
  54.6 0.0 copy-start.5
  54.6 0.0 collective-permute-done.7.refs_5_
  54.6 1.6 %collective-permute-done.3.refs_2_ = bf16[128,2176]{1,0:T(8,128)(2,1)} collective-permute-done((bf16[128,2176]{1,0:T(8,128)(2,1)S(1)}, bf16[128,2176]{1,0:T(8,128)(2,1)}, u32[]{:S(2)}, u32[]{:S(2)}) %collective-permute-start.3) | collective-permute-done | bytes 557088 | tf_op jit(solution)/shard_map/ppermute | solution.py:34
  56.3 0.8 %collective-permute-done.6.refs_4_ = bf16[128,2176]{1,0:T(8,128)(2,1)} collective-permute-done((bf16[128,2176]{1,0:T(8,128)(2,1)S(1)}, bf16[128,2176]{1,0:T(8,128)(2,1)}, u32[]{:S(2)}, u32[]{:S(2)}) %collective-permute-start.6) | collective-permute-done | bytes 557088 | tf_op jit(solution)/shard_map/ppermute | solution.py:34
  57.1 8.7 %attend_early.1.refs_9_ = bf16[1,128,8192]{2,1,0:T(8,128)(2,1)} custom-call(s32[1]{0:T(128)} %bitcast.rank_ref, bf16[128,2176]{1,0:T(8,128)(2,1)S(1)} %get-tuple-element.32.refs_0_, bf16[128,2176]{1,0:T(8,128)(2,1)S(1)} %collective-permute-done.1.refs_1_, bf16[128,2176]{1,0:T(8,128)(2,1)} %collective-permute-done.3.refs_2_, ...), custom_call_target="tpu_custom_call" | custom-call | tf_op jit(solution)/shard_map/attend_early/pallas_call | solution.py:299
  65.8 0.0 collective-permute-done.8.refs_7_
  65.8 0.0 copy-done.5
  65.8 6.4 %attend_late.1 = bf16[1,128,8192]{2,1,0:T(8,128)(2,1)} custom-call(s32[1]{0:T(128)} %bitcast.rank_ref, bf16[128,2176]{1,0:T(8,128)(2,1)S(1)} %get-tuple-element.32.refs_0_, bf16[128,2176]{1,0:T(8,128)(2,1)S(1)} %collective-permute-done.1.refs_1_, bf16[128,2176]{1,0:T(8,128)(2,1)} %collective-permute-done.3.refs_2_, ...), custom_call_target="tpu_custom_call", output_to_operand_aliasing={{}: (10, {})} | custom-call | tf_op jit(solution)/shard_map/attend_late/pallas_call | solution.py:314
  (3 shorter events, 0.1 us)
Async XLA Ops:
  0.0 6.6 %copy-start.7 = (bf16[1,256,8192]{2,1,0:T(8,128)(2,1)S(1)}, bf16[1,256,8192]{2,1,0:T(8,128)(2,1)}, u32[]{:S(2)}) copy-start(bf16[1,256,8192]{2,1,0:T(8,128)(2,1)} %q_hbm.1) | copy-start | bytes 12582916
  2.3 15.6 %collective-permute-start = (bf16[128,2048]{1,0:T(8,128)(2,1)S(1)}, bf16[128,2048]{1,0:T(8,128)(2,1)S(1)}, u32[]{:S(2)}, u32[]{:S(2)}) collective-permute-start(bf16[128,2048]{1,0:T(8,128)(2,1)S(1)} %pad_maximum_fusion), channel_id=1, source_target_pairs={{0,8},{8,16},{16,24},{1,9},{9,17},{17,25},{2,10},{10,18},{18,26},{... | collective-permute-start | bytes 1572872 | tf_op jit(solution)/shard_map/ppermute | solution.py:29
  7.6 10.4 %copy-start.6 = (s32[1,128]{1,0:T(1,128)S(1)}, s32[1,128]{1,0:T(1,128)}, u32[]{:S(2)}) copy-start(s32[1,128]{1,0:T(1,128)} %docs_ref.1) | copy-start | bytes 1540
  9.6 22.4 %collective-permute-start.2 = (bf16[128,2560]{1,0:T(8,128)(2,1)}, bf16[128,2560]{1,0:T(8,128)(2,1)S(1)}, u32[]{:S(2)}, u32[]{:S(2)}) collective-permute-start(bf16[128,2560]{1,0:T(8,128)(2,1)} %bitcast_select_fusion.1), channel_id=1, source_target_pairs={{0,8},{8,16},{16,24},{1,9},{9,17},{17,25},{2,10},{10,18},{18,26},{... | collective-permute-start | bytes 1966088 | tf_op jit(solution)/shard_map/ppermute | solution.py:29
  13.0 0.9 %copy-start = (bf16[128,3328]{1,0:T(8,128)(2,1)}, bf16[128,3328]{1,0:T(8,128)(2,1)S(1)}, u32[]{:S(2)}) copy-start(bf16[128,3328]{1,0:T(8,128)(2,1)S(1)} %get-tuple-element.39.local_ref) | copy-start | bytes 2555908
  14.0 0.8 %copy-start.2 = (bf16[128,2560]{1,0:T(8,128)(2,1)}, bf16[128,2560]{1,0:T(8,128)(2,1)S(1)}, u32[]{:S(2)}) copy-start(bf16[128,2560]{1,0:T(8,128)(2,1)S(1)} %get-tuple-element.36.local_ref) | copy-start | bytes 1966084
  14.8 17.2 %copy-start.4 = (bf16[128,2304]{1,0:T(8,128)(2,1)}, bf16[128,2304]{1,0:T(8,128)(2,1)S(1)}, u32[]{:S(2)}) copy-start(bf16[128,2304]{1,0:T(8,128)(2,1)S(1)} %get-tuple-element.42.refs_8_) | copy-start | bytes 1769476
  18.8 14.6 %collective-permute-start.1 = (bf16[128,2176]{1,0:T(8,128)(2,1)S(1)}, bf16[128,2176]{1,0:T(8,128)(2,1)S(1)}, u32[]{:S(2)}, u32[]{:S(2)}) collective-permute-start(bf16[128,2176]{1,0:T(8,128)(2,1)S(1)} %get-tuple-element.32.refs_0_), channel_id=1, source_target_pairs={{0,2},{1,3},{2,4},{3,5},{4,6},{5,7},{8,10},{9,11},{10,12},{11,13},... | collective-permute-start | bytes 1671176 | tf_op jit(solution)/shard_map/ppermute | solution.py:29
  22.0 28.2 %collective-permute-start.5 = (bf16[128,3328]{1,0:T(8,128)(2,1)}, bf16[128,3328]{1,0:T(8,128)(2,1)S(1)}, u32[]{:S(2)}, u32[]{:S(2)}) collective-permute-start(bf16[128,3328]{1,0:T(8,128)(2,1)} %bitcast_select_fusion), channel_id=1, source_target_pairs={{0,8},{8,16},{16,24},{1,9},{9,17},{17,25},{2,10},{10,18},{18,26},{... | collective-permute-start | bytes 2555912 | tf_op jit(solution)/shard_map/ppermute | solution.py:29
  32.0 1.1 %copy-start.3 = (bf16[128,2560]{1,0:T(8,128)(2,1)S(1)}, bf16[128,2560]{1,0:T(8,128)(2,1)}, u32[]{:S(2)}) copy-start(bf16[128,2560]{1,0:T(8,128)(2,1)} %copy-done.2) | copy-start | bytes 1966084
  33.4 21.1 %collective-permute-start.4 = (bf16[128,2176]{1,0:T(8,128)(2,1)S(1)}, bf16[128,2176]{1,0:T(8,128)(2,1)S(1)}, u32[]{:S(2)}, u32[]{:S(2)}) collective-permute-start(bf16[128,2176]{1,0:T(8,128)(2,1)S(1)} %collective-permute-done.1.refs_1_), channel_id=1, source_target_pairs={{0,2},{1,3},{2,4},{3,5},{4,6},{5,7},{8,10},{9,11},{10,12},{11,13},... | collective-permute-start | bytes 1671176 | tf_op jit(solution)/shard_map/ppermute | solution.py:29
  36.6 29.2 %collective-permute-start.8 = (bf16[128,2304]{1,0:T(8,128)(2,1)}, bf16[128,2304]{1,0:T(8,128)(2,1)}, u32[]{:S(2)}, u32[]{:S(2)}) collective-permute-start(bf16[128,2304]{1,0:T(8,128)(2,1)} %bitcast_select_fusion.2), channel_id=1, source_target_pairs={{0,8},{8,16},{16,24},{1,9},{9,17},{17,25},{2,10},{10,18},{18,26},{... | collective-permute-start | bytes 1769480 | tf_op jit(solution)/shard_map/ppermute | solution.py:29
  38.9 15.8 %collective-permute-start.7 = (bf16[128,2176]{1,0:T(8,128)(2,1)S(1)}, bf16[128,2176]{1,0:T(8,128)(2,1)}, u32[]{:S(2)}, u32[]{:S(2)}) collective-permute-start(bf16[128,2176]{1,0:T(8,128)(2,1)S(1)} %get-tuple-element.32.refs_0_), channel_id=1, source_target_pairs={{0,1},{2,3},{4,5},{6,7},{8,9},{10,11},{12,13},{14,15},{16,17},{18,... | collective-permute-start | bytes 1671176 | tf_op jit(solution)/shard_map/ppermute | solution.py:34
  50.2 1.2 %copy-start.1 = (bf16[128,3328]{1,0:T(8,128)(2,1)S(1)}, bf16[128,3328]{1,0:T(8,128)(2,1)}, u32[]{:S(2)}) copy-start(bf16[128,3328]{1,0:T(8,128)(2,1)} %copy-done) | copy-start | bytes 2555908
  51.8 4.5 %collective-permute-start.3 = (bf16[128,2176]{1,0:T(8,128)(2,1)S(1)}, bf16[128,2176]{1,0:T(8,128)(2,1)}, u32[]{:S(2)}, u32[]{:S(2)}) collective-permute-start(bf16[128,2176]{1,0:T(8,128)(2,1)S(1)} %collective-permute-done.1.refs_1_), channel_id=1, source_target_pairs={{0,1},{1,0},{2,3},{3,2},{4,5},{5,4},{6,7},{7,6},{8,9},{9,8},{10,11... | collective-permute-start | bytes 1671176 | tf_op jit(solution)/shard_map/ppermute | solution.py:34
  54.6 2.5 %collective-permute-start.6 = (bf16[128,2176]{1,0:T(8,128)(2,1)S(1)}, bf16[128,2176]{1,0:T(8,128)(2,1)}, u32[]{:S(2)}, u32[]{:S(2)}) collective-permute-start(bf16[128,2176]{1,0:T(8,128)(2,1)S(1)} %collective-permute-done.4.refs_3_), channel_id=1, source_target_pairs={{0,1},{1,0},{2,3},{3,2},{4,5},{5,4},{6,7},{7,6},{8,9},{9,8},{10,11... | collective-permute-start | bytes 1671176 | tf_op jit(solution)/shard_map/ppermute | solution.py:34
  54.6 11.2 %copy-start.5 = (bf16[128,2304]{1,0:T(8,128)(2,1)S(1)}, bf16[128,2304]{1,0:T(8,128)(2,1)}, u32[]{:S(2)}) copy-start(bf16[128,2304]{1,0:T(8,128)(2,1)} %copy-done.4) | copy-start | bytes 1769476

commit v15 on v12

--- a/solution.py
+++ b/solution.py
@@ -16,7 +16,7 @@
 NOTE = 2 * KV_WIDTH
 MASKED = -1e30
 HALF = GROUP // 2
-CHUNKS = (20, 26, 18)
+CHUNKS = (20, 24, 20)
 VMEM_GRANT = 48 * 1024 * 1024
 
 WHOLE = pl.BlockSpec(memory_space=pltpu.VMEM)
@@ -40,18 +40,16 @@
     return lax.all_to_all(spread, axis, split_axis=0, concat_axis=0)
 
 
-def shift_in_known(own_count, quota):
+def shifts_in(own_count, quota):
     n = lax.axis_size("dp")
     replica = lax.axis_index("dp")
     if n > 4:
         all_counts = everyones(own_count[None], "dp")[:, 0]
         places = jnp.arange(n, dtype=jnp.int32)
         before = jnp.sum(jnp.where(places < replica, all_counts, 0))
-        return jnp.stack([before - replica * quota, jnp.int32(0)])
-    shift = jnp.where(own_count == 0, quota, 0)
-    shift = jnp.where(replica == n - 1, quota - own_count, shift)
-    shift = jnp.where(replica == 0, 0, shift)
-    return jnp.stack([shift, (replica == 1).astype(jnp.int32)])
+        before_last = jnp.sum(jnp.where(places < replica - 1, all_counts, 0))
+        return jnp.stack([before - replica * quota, before_last - (replica - 1) * quota])
+    return jnp.stack([jnp.maximum(quota - own_count, 0), jnp.int32(0)])
 
 
 def place_rows(hot, arrived, local):
@@ -61,9 +59,7 @@
 
 def settle_kernel(shift_ref, docs_ref, arrived_ref, local_ref, out_ref, hot_ref):
     quota = out_ref.shape[0]
-    count_before = arrived_ref[:, NOTE:].astype(jnp.float32).astype(jnp.int32)
-    shift = jnp.where(shift_ref[1] == 1, count_before - quota, shift_ref[0])
-    shift_before = shift - count_before + quota
+    shift, shift_before = shift_ref[0], shift_ref[1]
     row = lax.broadcasted_iota(jnp.int32, (quota, quota), 0)
     col = lax.broadcasted_iota(jnp.int32, (quota, quota), 1)
     turned = row - shift_before
@@ -72,7 +68,7 @@
     hot_local = jnp.where(col == row - shift, 1.0, 0.0)
     hot = jnp.concatenate([hot_arrived, hot_local], axis=1).astype(jnp.bfloat16)
     hot_ref[...] = hot
-    out_ref[:, :NOTE] = place_rows(hot, arrived_ref[:, :NOTE], local_ref[...])
+    out_ref[:, :NOTE] = place_rows(hot, arrived_ref[...], local_ref[...])
     docs = jnp.broadcast_to(docs_ref[...].astype(jnp.float32), (quota, quota))
     out_ref[:, NOTE:] = docs.astype(jnp.bfloat16)
 
@@ -84,7 +80,7 @@
         in_specs=[SCALARS, WHOLE, WHOLE, WHOLE],
         out_specs=[WHOLE, WHOLE],
         out_shape=[
-            jax.ShapeDtypeStruct(arrived.shape, jnp.bfloat16),
+            jax.ShapeDtypeStruct((quota, NOTE + quota), jnp.bfloat16),
             jax.ShapeDtypeStruct((quota, 2 * quota), jnp.bfloat16),
         ],
         compiler_params=pltpu.CompilerParams(vmem_limit_bytes=VMEM_GRANT),
@@ -331,12 +327,7 @@
 
     later = quota + jnp.arange(quota, dtype=jnp.int32) < own_count
     kv_tail = jnp.concatenate(
-        [
-            circular_tail(k_rows[0], later),
-            circular_tail(value_slot_rows[0], later),
-            jnp.broadcast_to(own_count.astype(jnp.bfloat16), (quota, quota)),
-        ],
-        axis=1,
+        [circular_tail(k_rows[0], later), circular_tail(value_slot_rows[0], later)], axis=1
     )
     local_kv = jnp.concatenate([k_rows[0, :quota], value_slot_rows[0, :quota]], axis=1)
     kv_tail, later = lax.optimization_barrier((kv_tail, later))
@@ -350,7 +341,7 @@
     q_tails = lax.optimization_barrier(q_tails)
     arrived_q = [shifted(tail, "dp", 1) for tail in q_tails]
 
-    shift = shift_in_known(own_count, quota)
+    shift = shifts_in(own_count, quota)
     own, hot = settle_kv(shift, doc_ids, arrived_kv, local_kv)
 
     kv_blocks = [own]

time: 71.3 us -> 69.7 us (0.978)
  waiting for transfers between devices: 21.8 us -> 19.8 us
    ppermute x6, waiting for transfers between devices: 20.2 us -> 18.2 us  [shifted(): return lax.ppermute(x, axis, [(i, i + steps) for i in range(n - steps)])]
    select_n x4 -> x3, other arithmetic: 3.6 us -> 3.57 us  [circular_tail(): return jnp.where(later[:, None], rows[quota:], rows[:quota])]
where the time goes in v15:
time: 69.7 us; the launch traced here: 68.7 us
  starting transfers between devices  23.6 us (34%)
  waiting for transfers between devices  19.8 us (28%)
  Pallas kernels  17.5 us (25%)
  other arithmetic  3.72 us (5%)
  local copies, waits for them, and re-layouts  3.19 us (5%)
  between operations  0.89 us (1%)
    ppermute x6, waiting for transfers between devices, shifted(): return lax.ppermute(x, axis, [(i, i + steps) for i in range(n - steps)])  18.2 us
    ppermute x6, starting transfers between devices, shifted(): return lax.ppermute(x, axis, [(i, i + steps) for i in range(n - steps)])  16.1 us
    pallas_call x3, Pallas kernels, in_place(): pl.pallas_call(kernel, in_specs=specs, out_specs=[ANYWHERE, *more_specs],...  15.4 us
    ppermute x3, starting transfers between devices, across_cores(): lax.ppermute(x, 'ctx', [(i, i ^ 1) for i in range(n) if i % 2 in sources])  7.4 us
    select_n x3, other arithmetic, circular_tail(): return jnp.where(later[:, None], rows[quota:], rows[:quota])  3.57 us
    unnamed x10, local copies, waits for them, and re-layouts  2.21 us
    ppermute x3, waiting for transfers between devices, across_cores(): lax.ppermute(x, 'ctx', [(i, i ^ 1) for i in range(n) if i % 2 in sources])  1.58 us
  transfers between devices with their start and end apart: 9, of which 4 were waited for; matrix products, arithmetic and copies ran while one was open for 5% of the time, Pallas kernels for 18%

profile of v15, /device:TPU:21, one launch (start us, length us, event | category | flops | bytes accessed | tf_op | source)
XLA Modules:
  0.0 68.7 jit_solution(3905419429343977753)
XLA Ops:
  0.0 0.0 copy-start.4
  0.7 0.0 copy-start
  0.7 1.5 %bitcast_select_fusion.4 = (bf16[128,1024]{1,0:T(8,128)(2,1)S(1)}, bf16[128,1024]{1,0:T(8,128)(2,1)S(1)}) fusion(bf16[1,256,1024]{2,1,0:T(8,128)(2,1)} %param.6, pred[128]{0:T(512)(128)(4,1)S(1)} %add_compare_fusion, bf16[1,256,1024]{2,1,0:T(8,128)(2,1)} %param.7), kind=kLoop, calls=%fused_computation.6 | loop fusion | flops 262144 | bytes 1572992 | tf_op jit(solution)/shard_map/jit(_where)/select_n | solution.py:319
  2.2 3.3 %collective-permute-start = (bf16[128,2048]{1,0:T(8,128)(2,1)S(1)}, bf16[128,2048]{1,0:T(8,128)(2,1)S(1)}, u32[]{:S(2)}, u32[]{:S(2)}) collective-permute-start(bf16[128,2048]{1,0:T(8,128)(2,1)S(1)} %pad_maximum_fusion), channel_id=1, source_target_pairs={{0,8},{8,16},{16,24},{1,9},{9,17},{17,25},{2,10},{10,18},{18,26},{... | collective-permute-start | bytes 1572872 | tf_op jit(solution)/shard_map/ppermute | solution.py:29
  5.5 0.0 copy-done.4
  5.5 1.0 %slice_bitcast_fusion = (bf16[128,1024]{1,0:T(8,128)(2,1)S(1)}, bf16[128,1024]{1,0:T(8,128)(2,1)S(1)}) fusion(bf16[1,256,1024]{2,1,0:T(8,128)(2,1)} %param.7, bf16[1,256,1024]{2,1,0:T(8,128)(2,1)S(1)} %copy-done.4), kind=kLoop, calls=%fused_computation.7 | loop fusion | bytes 1048576 | tf_op jit(solution)/shard_map/slice | solution.py:319
  6.5 0.0 copy-done
  6.6 1.1 %bitcast_select_fusion.1 = (bf16[128,2560]{1,0:T(8,128)(2,1)}, bf16[128,2560]{1,0:T(8,128)(2,1)S(1)}) fusion(bf16[1,256,8192]{2,1,0:T(8,128)(2,1)S(1)} %copy-done, pred[128]{0:T(512)(128)(4,1)S(1)} %add_compare_fusion), kind=kLoop, calls=%fused_computation.1 | loop fusion | flops 655360 | bytes 3932288 | tf_op jit(solution)/shard_map/jit(_where)/select_n | solution.py:319
  7.6 0.0 copy-start.3
  7.6 1.0 %bitcast_select_fusion = bf16[128,3072]{1,0:T(8,128)(2,1)} fusion(bf16[1,256,8192]{2,1,0:T(8,128)(2,1)S(1)} %copy-done, pred[128]{0:T(512)(128)(4,1)S(1)} %add_compare_fusion), kind=kLoop, calls=%fused_computation | loop fusion | flops 393216 | bytes 2359424 | tf_op jit(solution)/shard_map/jit(_where)/select_n | solution.py:319
  8.7 1.9 %collective-permute-start.2 = (bf16[128,2560]{1,0:T(8,128)(2,1)S(1)}, bf16[128,2560]{1,0:T(8,128)(2,1)S(1)}, u32[]{:S(2)}, u32[]{:S(2)}) collective-permute-start(bf16[128,2560]{1,0:T(8,128)(2,1)S(1)} %get-tuple-element.26), channel_id=1, source_target_pairs={{0,8},{8,16},{16,24},{1,9},{9,17},{17,25},{2,10},{10,18},{18,26},{... | collective-permute-start | bytes 1966088 | tf_op jit(solution)/shard_map/ppermute | solution.py:29
  10.6 0.1 pad_add_fusion.shift_ref
  10.7 7.3 %collective-permute-done.arrived_ref = bf16[128,2048]{1,0:T(8,128)(2,1)S(1)} collective-permute-done((bf16[128,2048]{1,0:T(8,128)(2,1)S(1)}, bf16[128,2048]{1,0:T(8,128)(2,1)S(1)}, u32[]{:S(2)}, u32[]{:S(2)}) %collective-permute-start) | collective-permute-done | bytes 524320 | tf_op jit(solution)/shard_map/ppermute | solution.py:29
  18.0 0.0 copy-done.3
  18.0 0.8 %settle_kv.1 = (bf16[128,2176]{1,0:T(8,128)(2,1)S(1)}, bf16[128,256]{1,0:T(8,128)(2,1)S(1)}) custom-call(s32[2]{0:T(128)S(1)} %pad_add_fusion.shift_ref, s32[1,128]{1,0:T(1,128)S(1)} %copy-done.3, bf16[128,2048]{1,0:T(8,128)(2,1)S(1)} %collective-permute-done.arrived_ref, bf16[128,2048]{1,0:T(8,128)(2,1)S(1)} %pad_maximum_fusion.1.local_ref), custom_call_target="tpu_custom_call" | custom-call | tf_op jit(solution)/shard_map/settle_kv/pallas_call | solution.py:78
  18.8 3.2 %collective-permute-start.1 = (bf16[128,2176]{1,0:T(8,128)(2,1)S(1)}, bf16[128,2176]{1,0:T(8,128)(2,1)S(1)}, u32[]{:S(2)}, u32[]{:S(2)}) collective-permute-start(bf16[128,2176]{1,0:T(8,128)(2,1)S(1)} %get-tuple-element.23.refs_0_), channel_id=1, source_target_pairs={{0,2},{1,3},{2,4},{3,5},{4,6},{5,7},{8,10},{9,11},{10,12},{11,13},... | collective-permute-start | bytes 1671176 | tf_op jit(solution)/shard_map/ppermute | solution.py:29
  22.0 2.2 %collective-permute-start.5 = (bf16[128,3072]{1,0:T(8,128)(2,1)}, bf16[128,3072]{1,0:T(8,128)(2,1)S(1)}, u32[]{:S(2)}, u32[]{:S(2)}) collective-permute-start(bf16[128,3072]{1,0:T(8,128)(2,1)} %bitcast_select_fusion), channel_id=1, source_target_pairs={{0,8},{8,16},{16,24},{1,9},{9,17},{17,25},{2,10},{10,18},{18,26},{... | collective-permute-start | bytes 2359304 | tf_op jit(solution)/shard_map/ppermute | solution.py:29
  24.3 7.7 %collective-permute-done.2.arrived_ref = bf16[128,2560]{1,0:T(8,128)(2,1)S(1)} collective-permute-done((bf16[128,2560]{1,0:T(8,128)(2,1)S(1)}, bf16[128,2560]{1,0:T(8,128)(2,1)S(1)}, u32[]{:S(2)}, u32[]{:S(2)}) %collective-permute-start.2) | collective-permute-done | bytes 655392 | tf_op jit(solution)/shard_map/ppermute | solution.py:29
  32.0 0.0 copy-start.1
  32.0 2.2 %copy-done.1 = bf16[1,256,8192]{2,1,0:T(8,128)(2,1)S(1)} copy-done((bf16[1,256,8192]{2,1,0:T(8,128)(2,1)S(1)}, bf16[1,256,8192]{2,1,0:T(8,128)(2,1)}, u32[]{:S(2)}) %copy-start.1) | copy-done | bytes 4194328
  34.2 0.0 copy-start.2
  34.2 1.2 %place_queries.2.refs_0_ = bf16[1,128,8192]{2,1,0:T(8,128)(2,1)} custom-call(bf16[128,256]{1,0:T(8,128)(2,1)S(1)} %get-tuple-element.24.hot_ref.refs_6_, bf16[128,2560]{1,0:T(8,128)(2,1)S(1)} %collective-permute-done.2.arrived_ref, bf16[1,256,8192]{2,1,0:T(8,128)(2,1)S(1)} %copy-done.1), custom_call_target="tpu_custom_call" | custom-call | tf_op jit(solution)/shard_map/place_queries/pallas_call | solution.py:161
  35.5 0.0 collective-permute-done.1.refs_1_
  35.5 3.3 %collective-permute-start.4 = (bf16[128,2176]{1,0:T(8,128)(2,1)S(1)}, bf16[128,2176]{1,0:T(8,128)(2,1)S(1)}, u32[]{:S(2)}, u32[]{:S(2)}) collective-permute-start(bf16[128,2176]{1,0:T(8,128)(2,1)S(1)} %collective-permute-done.1.refs_1_), channel_id=1, source_target_pairs={{0,2},{1,3},{2,4},{3,5},{4,6},{5,7},{8,10},{9,11},{10,12},{11,13},... | collective-permute-start | bytes 1671176 | tf_op jit(solution)/shard_map/ppermute | solution.py:29
  38.8 2.2 %collective-permute-start.8 = (bf16[128,2560]{1,0:T(8,128)(2,1)}, bf16[128,2560]{1,0:T(8,128)(2,1)}, u32[]{:S(2)}, u32[]{:S(2)}) collective-permute-start(bf16[128,2560]{1,0:T(8,128)(2,1)} %get-tuple-element.31), channel_id=1, source_target_pairs={{0,8},{8,16},{16,24},{1,9},{9,17},{17,25},{2,10},{10,18},{18,26},{... | collective-permute-start | bytes 1966088 | tf_op jit(solution)/shard_map/ppermute | solution.py:29
  41.0 1.3 %collective-permute-start.7 = (bf16[128,2176]{1,0:T(8,128)(2,1)S(1)}, bf16[128,2176]{1,0:T(8,128)(2,1)S(1)}, u32[]{:S(2)}, u32[]{:S(2)}) collective-permute-start(bf16[128,2176]{1,0:T(8,128)(2,1)S(1)} %get-tuple-element.23.refs_0_), channel_id=1, source_target_pairs={{0,1},{2,3},{4,5},{6,7},{8,9},{10,11},{12,13},{14,15},{16,17},{18,... | collective-permute-start | bytes 1671176 | tf_op jit(solution)/shard_map/ppermute | solution.py:34
  42.3 3.4 %collective-permute-start.3 = (bf16[128,2176]{1,0:T(8,128)(2,1)S(1)}, bf16[128,2176]{1,0:T(8,128)(2,1)S(1)}, u32[]{:S(2)}, u32[]{:S(2)}) collective-permute-start(bf16[128,2176]{1,0:T(8,128)(2,1)S(1)} %collective-permute-done.1.refs_1_), channel_id=1, source_target_pairs={{0,1},{1,0},{2,3},{3,2},{4,5},{5,4},{6,7},{7,6},{8,9},{9,8},{10,11... | collective-permute-start | bytes 1671176 | tf_op jit(solution)/shard_map/ppermute | solution.py:34
  45.7 3.2 %collective-permute-done.5.arrived_ref = bf16[128,3072]{1,0:T(8,128)(2,1)S(1)} collective-permute-done((bf16[128,3072]{1,0:T(8,128)(2,1)}, bf16[128,3072]{1,0:T(8,128)(2,1)S(1)}, u32[]{:S(2)}, u32[]{:S(2)}) %collective-permute-start.5) | collective-permute-done | bytes 786464 | tf_op jit(solution)/shard_map/ppermute | solution.py:29
  48.9 0.0 copy-done.2
  48.9 1.3 %place_queries.3.refs_7_ = bf16[1,128,8192]{2,1,0:T(8,128)(2,1)} custom-call(bf16[128,256]{1,0:T(8,128)(2,1)S(1)} %get-tuple-element.24.hot_ref.refs_6_, bf16[128,3072]{1,0:T(8,128)(2,1)S(1)} %collective-permute-done.5.arrived_ref, bf16[1,256,8192]{2,1,0:T(8,128)(2,1)S(1)} %copy-done.2, ...), custom_call_target="tpu_custom_call", output_to_operand_aliasing={{}: (3, {})} | custom-call | tf_op jit(solution)/shard_map/place_queries/pallas_call | solution.py:119
  50.2 0.0 collective-permute-done.4.refs_3_
  50.2 2.8 %collective-permute-start.6 = (bf16[128,2176]{1,0:T(8,128)(2,1)S(1)}, bf16[128,2176]{1,0:T(8,128)(2,1)S(1)}, u32[]{:S(2)}, u32[]{:S(2)}) collective-permute-start(bf16[128,2176]{1,0:T(8,128)(2,1)S(1)} %collective-permute-done.4.refs_3_), channel_id=1, source_target_pairs={{0,1},{1,0},{2,3},{3,2},{4,5},{5,4},{6,7},{7,6},{8,9},{9,8},{10,11... | collective-permute-start | bytes 1671176 | tf_op jit(solution)/shard_map/ppermute | solution.py:34
  53.0 0.0 collective-permute-done.7.refs_5_
  53.0 0.0 collective-permute-done.3.refs_2_
  53.0 1.6 %collective-permute-done.6.refs_4_ = bf16[128,2176]{1,0:T(8,128)(2,1)S(1)} collective-permute-done((bf16[128,2176]{1,0:T(8,128)(2,1)S(1)}, bf16[128,2176]{1,0:T(8,128)(2,1)S(1)}, u32[]{:S(2)}, u32[]{:S(2)}) %collective-permute-start.6) | collective-permute-done | bytes 557088 | tf_op jit(solution)/shard_map/ppermute | solution.py:34
  54.6 8.7 %attend_early.1 = (bf16[1,128,8192]{2,1,0:T(8,128)(2,1)}, bf16[128,2560]{1,0:T(8,128)(2,1)S(1)}) custom-call(s32[1]{0:T(128)} %bitcast.rank_ref, bf16[128,2176]{1,0:T(8,128)(2,1)S(1)} %get-tuple-element.23.refs_0_, bf16[128,2176]{1,0:T(8,128)(2,1)S(1)} %collective-permute-done.1.refs_1_, ...), custom_call_target="tpu_custom_call", output_to_operand_aliasing={{0}: (8, {})} | custom-call | tf_op jit(solution)/shard_map/attend_early/pallas_call | solution.py:119
  63.3 0.0 collective-permute-done.8.refs_7_
  63.3 5.4 %attend_late.1 = bf16[1,128,8192]{2,1,0:T(8,128)(2,1)} custom-call(s32[1]{0:T(128)} %bitcast.rank_ref, bf16[128,2176]{1,0:T(8,128)(2,1)S(1)} %get-tuple-element.23.refs_0_, bf16[128,2176]{1,0:T(8,128)(2,1)S(1)} %collective-permute-done.1.refs_1_, bf16[128,2176]{1,0:T(8,128)(2,1)S(1)} %collective-permute-done.3.refs_2_, ...), custom_call_target="tpu_custom_call", output_to_operand_aliasing={{}: (10, {})} | custom-call | tf_op jit(solution)/shard_map/attend_late/pallas_call | solution.py:119
  (3 shorter events, 0.1 us)
Async XLA Ops:
  0.0 5.5 %copy-start.4 = (bf16[1,256,1024]{2,1,0:T(8,128)(2,1)S(1)}, bf16[1,256,1024]{2,1,0:T(8,128)(2,1)}, u32[]{:S(2)}) copy-start(bf16[1,256,1024]{2,1,0:T(8,128)(2,1)} %param.6) | copy-start | bytes 1572868
  0.7 5.8 %copy-start = (bf16[1,256,8192]{2,1,0:T(8,128)(2,1)S(1)}, bf16[1,256,8192]{2,1,0:T(8,128)(2,1)}, u32[]{:S(2)}) copy-start(bf16[1,256,8192]{2,1,0:T(8,128)(2,1)} %refs_6_.1) | copy-start | bytes 12582916
  2.2 15.7 %collective-permute-start = (bf16[128,2048]{1,0:T(8,128)(2,1)S(1)}, bf16[128,2048]{1,0:T(8,128)(2,1)S(1)}, u32[]{:S(2)}, u32[]{:S(2)}) collective-permute-start(bf16[128,2048]{1,0:T(8,128)(2,1)S(1)} %pad_maximum_fusion), channel_id=1, source_target_pairs={{0,8},{8,16},{16,24},{1,9},{9,17},{17,25},{2,10},{10,18},{18,26},{... | collective-permute-start | bytes 1572872 | tf_op jit(solution)/shard_map/ppermute | solution.py:29
  7.6 10.3 %copy-start.3 = (s32[1,128]{1,0:T(1,128)S(1)}, s32[1,128]{1,0:T(1,128)}, u32[]{:S(2)}) copy-start(s32[1,128]{1,0:T(1,128)} %docs_ref.1) | copy-start | bytes 1540
  8.7 23.3 %collective-permute-start.2 = (bf16[128,2560]{1,0:T(8,128)(2,1)S(1)}, bf16[128,2560]{1,0:T(8,128)(2,1)S(1)}, u32[]{:S(2)}, u32[]{:S(2)}) collective-permute-start(bf16[128,2560]{1,0:T(8,128)(2,1)S(1)} %get-tuple-element.26), channel_id=1, source_target_pairs={{0,8},{8,16},{16,24},{1,9},{9,17},{17,25},{2,10},{10,18},{18,26},{... | collective-permute-start | bytes 1966088 | tf_op jit(solution)/shard_map/ppermute | solution.py:29
  18.8 16.6 %collective-permute-start.1 = (bf16[128,2176]{1,0:T(8,128)(2,1)S(1)}, bf16[128,2176]{1,0:T(8,128)(2,1)S(1)}, u32[]{:S(2)}, u32[]{:S(2)}) collective-permute-start(bf16[128,2176]{1,0:T(8,128)(2,1)S(1)} %get-tuple-element.23.refs_0_), channel_id=1, source_target_pairs={{0,2},{1,3},{2,4},{3,5},{4,6},{5,7},{8,10},{9,11},{10,12},{11,13},... | collective-permute-start | bytes 1671176 | tf_op jit(solution)/shard_map/ppermute | solution.py:29
  22.0 26.8 %collective-permute-start.5 = (bf16[128,3072]{1,0:T(8,128)(2,1)}, bf16[128,3072]{1,0:T(8,128)(2,1)S(1)}, u32[]{:S(2)}, u32[]{:S(2)}) collective-permute-start(bf16[128,3072]{1,0:T(8,128)(2,1)} %bitcast_select_fusion), channel_id=1, source_target_pairs={{0,8},{8,16},{16,24},{1,9},{9,17},{17,25},{2,10},{10,18},{18,26},{... | collective-permute-start | bytes 2359304 | tf_op jit(solution)/shard_map/ppermute | solution.py:29
  32.0 2.2 %copy-start.1 = (bf16[1,256,8192]{2,1,0:T(8,128)(2,1)S(1)}, bf16[1,256,8192]{2,1,0:T(8,128)(2,1)}, u32[]{:S(2)}) copy-start(bf16[1,256,8192]{2,1,0:T(8,128)(2,1)} %refs_6_.1) | copy-start | bytes 12582916
  34.2 14.7 %copy-start.2 = (bf16[1,256,8192]{2,1,0:T(8,128)(2,1)S(1)}, bf16[1,256,8192]{2,1,0:T(8,128)(2,1)}, u32[]{:S(2)}) copy-start(bf16[1,256,8192]{2,1,0:T(8,128)(2,1)} %refs_6_.1) | copy-start | bytes 12582916
  35.5 14.7 %collective-permute-start.4 = (bf16[128,2176]{1,0:T(8,128)(2,1)S(1)}, bf16[128,2176]{1,0:T(8,128)(2,1)S(1)}, u32[]{:S(2)}, u32[]{:S(2)}) collective-permute-start(bf16[128,2176]{1,0:T(8,128)(2,1)S(1)} %collective-permute-done.1.refs_1_), channel_id=1, source_target_pairs={{0,2},{1,3},{2,4},{3,5},{4,6},{5,7},{8,10},{9,11},{10,12},{11,13},... | collective-permute-start | bytes 1671176 | tf_op jit(solution)/shard_map/ppermute | solution.py:29
  38.8 24.5 %collective-permute-start.8 = (bf16[128,2560]{1,0:T(8,128)(2,1)}, bf16[128,2560]{1,0:T(8,128)(2,1)}, u32[]{:S(2)}, u32[]{:S(2)}) collective-permute-start(bf16[128,2560]{1,0:T(8,128)(2,1)} %get-tuple-element.31), channel_id=1, source_target_pairs={{0,8},{8,16},{16,24},{1,9},{9,17},{17,25},{2,10},{10,18},{18,26},{... | collective-permute-start | bytes 1966088 | tf_op jit(solution)/shard_map/ppermute | solution.py:29
  41.0 11.9 %collective-permute-start.7 = (bf16[128,2176]{1,0:T(8,128)(2,1)S(1)}, bf16[128,2176]{1,0:T(8,128)(2,1)S(1)}, u32[]{:S(2)}, u32[]{:S(2)}) collective-permute-start(bf16[128,2176]{1,0:T(8,128)(2,1)S(1)} %get-tuple-element.23.refs_0_), channel_id=1, source_target_pairs={{0,1},{2,3},{4,5},{6,7},{8,9},{10,11},{12,13},{14,15},{16,17},{18,... | collective-permute-start | bytes 1671176 | tf_op jit(solution)/shard_map/ppermute | solution.py:34
  42.3 10.6 %collective-permute-start.3 = (bf16[128,2176]{1,0:T(8,128)(2,1)S(1)}, bf16[128,2176]{1,0:T(8,128)(2,1)S(1)}, u32[]{:S(2)}, u32[]{:S(2)}) collective-permute-start(bf16[128,2176]{1,0:T(8,128)(2,1)S(1)} %collective-permute-done.1.refs_1_), channel_id=1, source_target_pairs={{0,1},{1,0},{2,3},{3,2},{4,5},{5,4},{6,7},{7,6},{8,9},{9,8},{10,11... | collective-permute-start | bytes 1671176 | tf_op jit(solution)/shard_map/ppermute | solution.py:34
  50.2 4.3 %collective-permute-start.6 = (bf16[128,2176]{1,0:T(8,128)(2,1)S(1)}, bf16[128,2176]{1,0:T(8,128)(2,1)S(1)}, u32[]{:S(2)}, u32[]{:S(2)}) collective-permute-start(bf16[128,2176]{1,0:T(8,128)(2,1)S(1)} %collective-permute-done.4.refs_3_), channel_id=1, source_target_pairs={{0,1},{1,0},{2,3},{3,2},{4,5},{5,4},{6,7},{7,6},{8,9},{9,8},{10,11... | collective-permute-start | bytes 1671176 | tf_op jit(solution)/shard_map/ppermute | solution.py:34

commit v16 on v15

--- a/solution.py
+++ b/solution.py
@@ -16,7 +16,7 @@
 NOTE = 2 * KV_WIDTH
 MASKED = -1e30
 HALF = GROUP // 2
-CHUNKS = (20, 24, 20)
+CHUNKS = (20, 26, 18)
 VMEM_GRANT = 48 * 1024 * 1024
 
 WHOLE = pl.BlockSpec(memory_space=pltpu.VMEM)
@@ -203,7 +203,7 @@
         rest[:, values] = mate_ref[:, values]
 
 
-def attend_heads(first, count, kv_refs, bias, take, result):
+def attend_heads(first, steps, kv_refs, bias, take, result):
     quota = bias.shape[0]
     unit = math.log2(math.e) / math.sqrt(HEAD_SIZE)
 
@@ -233,8 +233,7 @@
         for h in range(heads):
             result[:, head_columns(head - first + h)] = mixed[h * quota : (h + 1) * quota]
 
-    steps = pieces(first, count)
-    keys, values = key_head(first // GROUP)
+    keys, values = key_head(steps[0][0] // GROUP)
     scores = scored(*steps[0], keys)
     for i, (head, heads) in enumerate(steps):
         own_values, later = values, None
@@ -256,7 +255,7 @@
     make_bias(kv_refs, far_ref, mate_ref, bias, rank)
     choose_rest(0, count, lax.rem(rank, 2), far_ref, mate_ref, rest)
     fetch.wait()
-    attend_heads(0, count, [*kv_refs, rest], bias, lambda cols: queries[:, cols], result)
+    attend_heads(0, pieces(0, count), [*kv_refs, rest], bias, lambda cols: queries[:, cols], result)
     store = pltpu.make_async_copy(result, out_hbm.at[0, :, own], sems.at[1])
     store.start()
     ahead = pltpu.make_async_copy(q_hbm.at[0, 0 : bias.shape[0], others], local, sems.at[2])
@@ -280,7 +279,8 @@
     def take(cols):
         return place_rows(hot_ref[...], arrived[:, cols], local_ref[:, cols])
 
-    attend_heads(first, count, [*kv_refs, rest], bias, take, result)
+    steps = sorted(pieces(first, count), key=lambda piece: -piece[1])
+    attend_heads(first, steps, [*kv_refs, rest], bias, take, result)
     store = pltpu.make_async_copy(result, out_hbm.at[0, :, head_columns(first, count)], sems.at[1])
     store.start()
     store.wait()
@@ -350,9 +350,13 @@
         carried = shifted(carried, "ctx", 2)
         kv_blocks.append(carried)
         if back < len(CHUNKS):
-            first = sum(CHUNKS[: back - 1])
-            out = place_queries(hot, arrived_q[back - 1], q_rows, first, out)
-            carried, out = lax.optimization_barrier((carried, out))
+            first, arrived = sum(CHUNKS[: back - 1]), arrived_q[back - 1]
+            if back < rounds:
+                out = place_queries(hot, arrived, q_rows, first, out)
+                carried, out = lax.optimization_barrier((carried, out))
+            else:
+                carried, arrived = lax.optimization_barrier((carried, arrived))
+                out = place_queries(hot, arrived, q_rows, first, out)
         if back < rounds:
             kv_blocks.append(across_cores(carried))
     kv_blocks += [across_cores(carried), across_cores(own, (0,))]

time: 69.7 us -> 72.9 us (1.046)
  local copies, waits for them, and re-layouts: 3.19 us -> 7.52 us
    unnamed x10 -> x12, local copies, waits for them, and re-layouts: 2.21 us -> 6.45 us
    ppermute x3, waiting for transfers between devices: 1.58 us -> 0.01 us  [across_cores(): lax.ppermute(x, 'ctx', [(i, i ^ 1) for i in range(n) if i % 2 in sources])]
    ppermute x6, waiting for transfers between devices: 18.2 us -> 19.6 us  [shifted(): return lax.ppermute(x, axis, [(i, i + steps) for i in range(n - steps)])]
    select_n x3 -> x4, other arithmetic: 3.57 us -> 3.65 us  [circular_tail(): return jnp.where(later[:, None], rows[quota:], rows[:quota])]
  transfers between devices with their start and end apart: 9 -> 9, of which waited for: 4 -> 3; matrix products, arithmetic and copies ran while one was open for 5% -> 5% of each run, Pallas kernels for 18% -> 17%
where the time goes in v16:
time: 72.9 us; the launch traced here: 72.4 us
  starting transfers between devices  23.2 us (32%)
  waiting for transfers between devices  19.6 us (27%)
  Pallas kernels  17.3 us (24%)
  local copies, waits for them, and re-layouts  7.52 us (10%)
  other arithmetic  3.8 us (5%)
  between operations  1 us (1%)
    ppermute x6, waiting for transfers between devices, shifted(): return lax.ppermute(x, axis, [(i, i + steps) for i in range(n - steps)])  19.6 us
    ppermute x6, starting transfers between devices, shifted(): return lax.ppermute(x, axis, [(i, i + steps) for i in range(n - steps)])  15.9 us
    pallas_call x3, Pallas kernels, in_place(): pl.pallas_call(kernel, in_specs=specs, out_specs=[ANYWHERE, *more_specs],...  15.2 us
    ppermute x3, starting transfers between devices, across_cores(): lax.ppermute(x, 'ctx', [(i, i ^ 1) for i in range(n) if i % 2 in sources])  7.34 us
    unnamed x12, local copies, waits for them, and re-layouts  6.45 us
    select_n x4, other arithmetic, circular_tail(): return jnp.where(later[:, None], rows[quota:], rows[:quota])  3.65 us
  transfers between devices with their start and end apart: 9, of which 3 were waited for; matrix products, arithmetic and copies ran while one was open for 5% of the time, Pallas kernels for 17%

profile of v16, /device:TPU:21, one launch (start us, length us, event | category | flops | bytes accessed | tf_op | source)
XLA Modules:
  0.0 72.4 jit_solution(636767078834258476)
XLA Ops:
  0.0 0.0 copy-start
  0.8 1.5 %bitcast_select_fusion.4 = (bf16[128,1024]{1,0:T(8,128)(2,1)S(1)}, bf16[128,1024]{1,0:T(8,128)(2,1)S(1)}) fusion(bf16[1,256,1024]{2,1,0:T(8,128)(2,1)} %param.6, pred[128]{0:T(512)(128)(4,1)S(1)} %add_compare_fusion, bf16[1,256,1024]{2,1,0:T(8,128)(2,1)} %param.7), kind=kLoop, calls=%fused_computation.6 | loop fusion | flops 262144 | bytes 1572992 | tf_op jit(solution)/shard_map/jit(_where)/select_n | solution.py:319
  2.3 0.0 copy-start.5
  2.4 3.1 %collective-permute-start = (bf16[128,2048]{1,0:T(8,128)(2,1)S(1)}, bf16[128,2048]{1,0:T(8,128)(2,1)S(1)}, u32[]{:S(2)}, u32[]{:S(2)}) collective-permute-start(bf16[128,2048]{1,0:T(8,128)(2,1)S(1)} %pad_maximum_fusion), channel_id=1, source_target_pairs={{0,8},{8,16},{16,24},{1,9},{9,17},{17,25},{2,10},{10,18},{18,26},{... | collective-permute-start | bytes 1572872 | tf_op jit(solution)/shard_map/ppermute | solution.py:29
  5.5 1.1 %slice_bitcast_fusion = (bf16[128,1024]{1,0:T(8,128)(2,1)S(1)}, bf16[128,1024]{1,0:T(8,128)(2,1)S(1)}) fusion(bf16[1,256,1024]{2,1,0:T(8,128)(2,1)} %param.7, bf16[1,256,1024]{2,1,0:T(8,128)(2,1)} %param.6), kind=kLoop, calls=%fused_computation.7 | loop fusion | bytes 1048576 | tf_op jit(solution)/shard_map/slice | solution.py:319
  6.6 0.0 copy-done
  6.6 1.0 %bitcast_select_fusion.2 = bf16[128,2304]{1,0:T(8,128)(2,1)} fusion(bf16[1,256,8192]{2,1,0:T(8,128)(2,1)S(1)} %copy-done, pred[128]{0:T(512)(128)(4,1)S(1)} %add_compare_fusion), kind=kLoop, calls=%fused_computation.2 | loop fusion | flops 294912 | bytes 1769600 | tf_op jit(solution)/shard_map/jit(_where)/select_n | solution.py:319
  7.6 1.1 %bitcast_select_fusion = bf16[128,3328]{1,0:T(8,128)(2,1)} fusion(bf16[1,256,8192]{2,1,0:T(8,128)(2,1)S(1)} %copy-done, pred[128]{0:T(512)(128)(4,1)S(1)} %add_compare_fusion), kind=kLoop, calls=%fused_computation | loop fusion | flops 425984 | bytes 2556032 | tf_op jit(solution)/shard_map/jit(_where)/select_n | solution.py:319
  8.7 0.1 bitcast_select_fusion.1
  8.8 1.9 %collective-permute-start.2 = (bf16[128,2560]{1,0:T(8,128)(2,1)S(1)}, bf16[128,2560]{1,0:T(8,128)(2,1)S(1)}, u32[]{:S(2)}, u32[]{:S(2)}) collective-permute-start(bf16[128,2560]{1,0:T(8,128)(2,1)S(1)} %bitcast_select_fusion.1), channel_id=1, source_target_pairs={{0,8},{8,16},{16,24},{1,9},{9,17},{17,25},{2,10},{10,18},{18,26},{... | collective-permute-start | bytes 1966088 | tf_op jit(solution)/shard_map/ppermute | solution.py:29
  10.7 0.1 pad_add_fusion.shift_ref
  10.8 7.1 %collective-permute-done.arrived_ref = bf16[128,2048]{1,0:T(8,128)(2,1)S(1)} collective-permute-done((bf16[128,2048]{1,0:T(8,128)(2,1)S(1)}, bf16[128,2048]{1,0:T(8,128)(2,1)S(1)}, u32[]{:S(2)}, u32[]{:S(2)}) %collective-permute-start) | collective-permute-done | bytes 524320 | tf_op jit(solution)/shard_map/ppermute | solution.py:29
  17.9 0.0 copy-done.5
  17.9 0.8 %settle_kv.1 = (bf16[128,2176]{1,0:T(8,128)(2,1)S(1)}, bf16[128,256]{1,0:T(8,128)(2,1)S(1)}) custom-call(s32[2]{0:T(128)S(1)} %pad_add_fusion.shift_ref, s32[1,128]{1,0:T(1,128)S(1)} %copy-done.5, bf16[128,2048]{1,0:T(8,128)(2,1)S(1)} %collective-permute-done.arrived_ref, bf16[128,2048]{1,0:T(8,128)(2,1)S(1)} %pad_maximum_fusion.1.local_ref), custom_call_target="tpu_custom_call" | custom-call | tf_op jit(solution)/shard_map/settle_kv/pallas_call | solution.py:78
  18.8 3.2 %collective-permute-start.1 = (bf16[128,2176]{1,0:T(8,128)(2,1)S(1)}, bf16[128,2176]{1,0:T(8,128)(2,1)S(1)}, u32[]{:S(2)}, u32[]{:S(2)}) collective-permute-start(bf16[128,2176]{1,0:T(8,128)(2,1)S(1)} %get-tuple-element.23.refs_0_), channel_id=1, source_target_pairs={{0,2},{1,3},{2,4},{3,5},{4,6},{5,7},{8,10},{9,11},{10,12},{11,13},... | collective-permute-start | bytes 1671176 | tf_op jit(solution)/shard_map/ppermute | solution.py:29
  22.0 2.2 %collective-permute-start.5 = (bf16[128,3328]{1,0:T(8,128)(2,1)}, bf16[128,3328]{1,0:T(8,128)(2,1)S(1)}, u32[]{:S(2)}, u32[]{:S(2)}) collective-permute-start(bf16[128,3328]{1,0:T(8,128)(2,1)} %bitcast_select_fusion), channel_id=1, source_target_pairs={{0,8},{8,16},{16,24},{1,9},{9,17},{17,25},{2,10},{10,18},{18,26},{... | collective-permute-start | bytes 2555912 | tf_op jit(solution)/shard_map/ppermute | solution.py:29
  24.2 7.7 %collective-permute-done.2.arrived_ref = bf16[128,2560]{1,0:T(8,128)(2,1)S(1)} collective-permute-done((bf16[128,2560]{1,0:T(8,128)(2,1)S(1)}, bf16[128,2560]{1,0:T(8,128)(2,1)S(1)}, u32[]{:S(2)}, u32[]{:S(2)}) %collective-permute-start.2) | collective-permute-done | bytes 655392 | tf_op jit(solution)/shard_map/ppermute | solution.py:29
  32.0 0.0 copy-start.1
  32.0 2.2 %copy-done.1 = bf16[1,256,8192]{2,1,0:T(8,128)(2,1)S(1)} copy-done((bf16[1,256,8192]{2,1,0:T(8,128)(2,1)S(1)}, bf16[1,256,8192]{2,1,0:T(8,128)(2,1)}, u32[]{:S(2)}) %copy-start.1) | copy-done | bytes 4194328
  34.2 1.2 %place_queries.2.refs_0_ = bf16[1,128,8192]{2,1,0:T(8,128)(2,1)} custom-call(bf16[128,256]{1,0:T(8,128)(2,1)S(1)} %get-tuple-element.24.hot_ref.refs_6_, bf16[128,2560]{1,0:T(8,128)(2,1)S(1)} %collective-permute-done.2.arrived_ref, bf16[1,256,8192]{2,1,0:T(8,128)(2,1)S(1)} %copy-done.1), custom_call_target="tpu_custom_call" | custom-call | tf_op jit(solution)/shard_map/place_queries/pallas_call | solution.py:161
  35.4 0.0 collective-permute-done.1.refs_1_
  35.4 3.2 %collective-permute-start.4 = (bf16[128,2176]{1,0:T(8,128)(2,1)S(1)}, bf16[128,2176]{1,0:T(8,128)(2,1)S(1)}, u32[]{:S(2)}, u32[]{:S(2)}) collective-permute-start(bf16[128,2176]{1,0:T(8,128)(2,1)S(1)} %collective-permute-done.1.refs_1_), channel_id=1, source_target_pairs={{0,2},{1,3},{2,4},{3,5},{4,6},{5,7},{8,10},{9,11},{10,12},{11,13},... | collective-permute-start | bytes 1671176 | tf_op jit(solution)/shard_map/ppermute | solution.py:29
  38.7 2.2 %collective-permute-start.8 = (bf16[128,2304]{1,0:T(8,128)(2,1)}, bf16[128,2304]{1,0:T(8,128)(2,1)}, u32[]{:S(2)}, u32[]{:S(2)}) collective-permute-start(bf16[128,2304]{1,0:T(8,128)(2,1)} %bitcast_select_fusion.2), channel_id=1, source_target_pairs={{0,8},{8,16},{16,24},{1,9},{9,17},{17,25},{2,10},{10,18},{18,26},{... | collective-permute-start | bytes 1769480 | tf_op jit(solution)/shard_map/ppermute | solution.py:29
  40.9 1.3 %collective-permute-start.7 = (bf16[128,2176]{1,0:T(8,128)(2,1)S(1)}, bf16[128,2176]{1,0:T(8,128)(2,1)S(1)}, u32[]{:S(2)}, u32[]{:S(2)}) collective-permute-start(bf16[128,2176]{1,0:T(8,128)(2,1)S(1)} %get-tuple-element.23.refs_0_), channel_id=1, source_target_pairs={{0,1},{2,3},{4,5},{6,7},{8,9},{10,11},{12,13},{14,15},{16,17},{18,... | collective-permute-start | bytes 1671176 | tf_op jit(solution)/shard_map/ppermute | solution.py:34
  42.2 3.4 %collective-permute-start.3 = (bf16[128,2176]{1,0:T(8,128)(2,1)S(1)}, bf16[128,2176]{1,0:T(8,128)(2,1)S(1)}, u32[]{:S(2)}, u32[]{:S(2)}) collective-permute-start(bf16[128,2176]{1,0:T(8,128)(2,1)S(1)} %collective-permute-done.1.refs_1_), channel_id=1, source_target_pairs={{0,1},{1,0},{2,3},{3,2},{4,5},{5,4},{6,7},{7,6},{8,9},{9,8},{10,11... | collective-permute-start | bytes 1671176 | tf_op jit(solution)/shard_map/ppermute | solution.py:34
  45.5 4.7 %collective-permute-done.5.arrived_ref = bf16[128,3328]{1,0:T(8,128)(2,1)S(1)} collective-permute-done((bf16[128,3328]{1,0:T(8,128)(2,1)}, bf16[128,3328]{1,0:T(8,128)(2,1)S(1)}, u32[]{:S(2)}, u32[]{:S(2)}) %collective-permute-start.5) | collective-permute-done | bytes 852000 | tf_op jit(solution)/shard_map/ppermute | solution.py:29
  50.2 0.0 copy-start.3
  50.2 0.9 %copy-done.3 = bf16[128,3328]{1,0:T(8,128)(2,1)} copy-done((bf16[128,3328]{1,0:T(8,128)(2,1)}, bf16[128,3328]{1,0:T(8,128)(2,1)S(1)}, u32[]{:S(2)}) %copy-start.3) | copy-done | bytes 851992
  51.2 0.0 collective-permute-done.4.refs_3_
  51.2 2.7 %collective-permute-start.6 = (bf16[128,2176]{1,0:T(8,128)(2,1)S(1)}, bf16[128,2176]{1,0:T(8,128)(2,1)S(1)}, u32[]{:S(2)}, u32[]{:S(2)}) collective-permute-start(bf16[128,2176]{1,0:T(8,128)(2,1)S(1)} %collective-permute-done.4.refs_3_), channel_id=1, source_target_pairs={{0,1},{1,0},{2,3},{3,2},{4,5},{5,4},{6,7},{7,6},{8,9},{9,8},{10,11... | collective-permute-start | bytes 1671176 | tf_op jit(solution)/shard_map/ppermute | solution.py:34
  53.9 0.0 copy-start.2
  53.9 2.2 %copy-done.2 = bf16[1,256,8192]{2,1,0:T(8,128)(2,1)S(1)} copy-done((bf16[1,256,8192]{2,1,0:T(8,128)(2,1)S(1)}, bf16[1,256,8192]{2,1,0:T(8,128)(2,1)}, u32[]{:S(2)}) %copy-start.2) | copy-done | bytes 4194328
  56.0 0.0 copy-start.4
  56.0 1.2 %copy-done.4 = bf16[128,3328]{1,0:T(8,128)(2,1)S(1)} copy-done((bf16[128,3328]{1,0:T(8,128)(2,1)S(1)}, bf16[128,3328]{1,0:T(8,128)(2,1)}, u32[]{:S(2)}) %copy-start.4) | copy-done | bytes 851992
  57.2 1.4 %place_queries.3.refs_7_ = bf16[1,128,8192]{2,1,0:T(8,128)(2,1)} custom-call(bf16[128,256]{1,0:T(8,128)(2,1)S(1)} %get-tuple-element.24.hot_ref.refs_6_, bf16[128,3328]{1,0:T(8,128)(2,1)S(1)} %copy-done.4, bf16[1,256,8192]{2,1,0:T(8,128)(2,1)S(1)} %copy-done.2, bf16[1,128,8192]{2,1,0:T(8,128)(2,1)} %place_queries.2.refs_0_), custom_call_target="tpu_custom_call", output_to_operand_aliasing={{}: (3, {})} | custom-call | tf_op jit(solution)/shard_map/place_queries/pallas_call | solution.py:119
  58.6 0.0 collective-permute-done.7.refs_5_
  58.6 0.0 collective-permute-done.3.refs_2_
  58.6 0.0 collective-permute-done.6.refs_4_
  58.6 9.0 %attend_early.1 = (bf16[1,128,8192]{2,1,0:T(8,128)(2,1)}, bf16[128,2304]{1,0:T(8,128)(2,1)S(1)}) custom-call(s32[1]{0:T(128)} %bitcast.rank_ref, bf16[128,2176]{1,0:T(8,128)(2,1)S(1)} %get-tuple-element.23.refs_0_, bf16[128,2176]{1,0:T(8,128)(2,1)S(1)} %collective-permute-done.1.refs_1_, ...), custom_call_target="tpu_custom_call", output_to_operand_aliasing={{0}: (8, {})} | custom-call | tf_op jit(solution)/shard_map/attend_early/pallas_call | solution.py:119
  67.6 0.0 collective-permute-done.8.refs_7_
  67.6 4.8 %attend_late.1 = bf16[1,128,8192]{2,1,0:T(8,128)(2,1)} custom-call(s32[1]{0:T(128)} %bitcast.rank_ref, bf16[128,2176]{1,0:T(8,128)(2,1)S(1)} %get-tuple-element.23.refs_0_, bf16[128,2176]{1,0:T(8,128)(2,1)S(1)} %collective-permute-done.1.refs_1_, bf16[128,2176]{1,0:T(8,128)(2,1)S(1)} %collective-permute-done.3.refs_2_, ...), custom_call_target="tpu_custom_call", output_to_operand_aliasing={{}: (10, {})} | custom-call | tf_op jit(solution)/shard_map/attend_late/pallas_call | solution.py:119
  (3 shorter events, 0.1 us)
Async XLA Ops:
  0.0 6.6 %copy-start = (bf16[1,256,8192]{2,1,0:T(8,128)(2,1)S(1)}, bf16[1,256,8192]{2,1,0:T(8,128)(2,1)}, u32[]{:S(2)}) copy-start(bf16[1,256,8192]{2,1,0:T(8,128)(2,1)} %refs_6_.1) | copy-start | bytes 12582916
  2.3 15.6 %copy-start.5 = (s32[1,128]{1,0:T(1,128)S(1)}, s32[1,128]{1,0:T(1,128)}, u32[]{:S(2)}) copy-start(s32[1,128]{1,0:T(1,128)} %docs_ref.1) | copy-start | bytes 1540
  2.4 15.6 %collective-permute-start = (bf16[128,2048]{1,0:T(8,128)(2,1)S(1)}, bf16[128,2048]{1,0:T(8,128)(2,1)S(1)}, u32[]{:S(2)}, u32[]{:S(2)}) collective-permute-start(bf16[128,2048]{1,0:T(8,128)(2,1)S(1)} %pad_maximum_fusion), channel_id=1, source_target_pairs={{0,8},{8,16},{16,24},{1,9},{9,17},{17,25},{2,10},{10,18},{18,26},{... | collective-permute-start | bytes 1572872 | tf_op jit(solution)/shard_map/ppermute | solution.py:29
  8.8 23.2 %collective-permute-start.2 = (bf16[128,2560]{1,0:T(8,128)(2,1)S(1)}, bf16[128,2560]{1,0:T(8,128)(2,1)S(1)}, u32[]{:S(2)}, u32[]{:S(2)}) collective-permute-start(bf16[128,2560]{1,0:T(8,128)(2,1)S(1)} %bitcast_select_fusion.1), channel_id=1, source_target_pairs={{0,8},{8,16},{16,24},{1,9},{9,17},{17,25},{2,10},{10,18},{18,26},{... | collective-permute-start | bytes 1966088 | tf_op jit(solution)/shard_map/ppermute | solution.py:29
  18.8 16.6 %collective-permute-start.1 = (bf16[128,2176]{1,0:T(8,128)(2,1)S(1)}, bf16[128,2176]{1,0:T(8,128)(2,1)S(1)}, u32[]{:S(2)}, u32[]{:S(2)}) collective-permute-start(bf16[128,2176]{1,0:T(8,128)(2,1)S(1)} %get-tuple-element.23.refs_0_), channel_id=1, source_target_pairs={{0,2},{1,3},{2,4},{3,5},{4,6},{5,7},{8,10},{9,11},{10,12},{11,13},... | collective-permute-start | bytes 1671176 | tf_op jit(solution)/shard_map/ppermute | solution.py:29
  22.0 28.2 %collective-permute-start.5 = (bf16[128,3328]{1,0:T(8,128)(2,1)}, bf16[128,3328]{1,0:T(8,128)(2,1)S(1)}, u32[]{:S(2)}, u32[]{:S(2)}) collective-permute-start(bf16[128,3328]{1,0:T(8,128)(2,1)} %bitcast_select_fusion), channel_id=1, source_target_pairs={{0,8},{8,16},{16,24},{1,9},{9,17},{17,25},{2,10},{10,18},{18,26},{... | collective-permute-start | bytes 2555912 | tf_op jit(solution)/shard_map/ppermute | solution.py:29
  32.0 2.2 %copy-start.1 = (bf16[1,256,8192]{2,1,0:T(8,128)(2,1)S(1)}, bf16[1,256,8192]{2,1,0:T(8,128)(2,1)}, u32[]{:S(2)}) copy-start(bf16[1,256,8192]{2,1,0:T(8,128)(2,1)} %refs_6_.1) | copy-start | bytes 12582916
  35.4 15.7 %collective-permute-start.4 = (bf16[128,2176]{1,0:T(8,128)(2,1)S(1)}, bf16[128,2176]{1,0:T(8,128)(2,1)S(1)}, u32[]{:S(2)}, u32[]{:S(2)}) collective-permute-start(bf16[128,2176]{1,0:T(8,128)(2,1)S(1)} %collective-permute-done.1.refs_1_), channel_id=1, source_target_pairs={{0,2},{1,3},{2,4},{3,5},{4,6},{5,7},{8,10},{9,11},{10,12},{11,13},... | collective-permute-start | bytes 1671176 | tf_op jit(solution)/shard_map/ppermute | solution.py:29
  38.7 29.0 %collective-permute-start.8 = (bf16[128,2304]{1,0:T(8,128)(2,1)}, bf16[128,2304]{1,0:T(8,128)(2,1)}, u32[]{:S(2)}, u32[]{:S(2)}) collective-permute-start(bf16[128,2304]{1,0:T(8,128)(2,1)} %bitcast_select_fusion.2), channel_id=1, source_target_pairs={{0,8},{8,16},{16,24},{1,9},{9,17},{17,25},{2,10},{10,18},{18,26},{... | collective-permute-start | bytes 1769480 | tf_op jit(solution)/shard_map/ppermute | solution.py:29
  40.9 17.7 %collective-permute-start.7 = (bf16[128,2176]{1,0:T(8,128)(2,1)S(1)}, bf16[128,2176]{1,0:T(8,128)(2,1)S(1)}, u32[]{:S(2)}, u32[]{:S(2)}) collective-permute-start(bf16[128,2176]{1,0:T(8,128)(2,1)S(1)} %get-tuple-element.23.refs_0_), channel_id=1, source_target_pairs={{0,1},{2,3},{4,5},{6,7},{8,9},{10,11},{12,13},{14,15},{16,17},{18,... | collective-permute-start | bytes 1671176 | tf_op jit(solution)/shard_map/ppermute | solution.py:34
  42.2 16.4 %collective-permute-start.3 = (bf16[128,2176]{1,0:T(8,128)(2,1)S(1)}, bf16[128,2176]{1,0:T(8,128)(2,1)S(1)}, u32[]{:S(2)}, u32[]{:S(2)}) collective-permute-start(bf16[128,2176]{1,0:T(8,128)(2,1)S(1)} %collective-permute-done.1.refs_1_), channel_id=1, source_target_pairs={{0,1},{1,0},{2,3},{3,2},{4,5},{5,4},{6,7},{7,6},{8,9},{9,8},{10,11... | collective-permute-start | bytes 1671176 | tf_op jit(solution)/shard_map/ppermute | solution.py:34
  50.2 0.9 %copy-start.3 = (bf16[128,3328]{1,0:T(8,128)(2,1)}, bf16[128,3328]{1,0:T(8,128)(2,1)S(1)}, u32[]{:S(2)}) copy-start(bf16[128,3328]{1,0:T(8,128)(2,1)S(1)} %collective-permute-done.5.arrived_ref) | copy-start | bytes 2555908
  51.2 7.5 %collective-permute-start.6 = (bf16[128,2176]{1,0:T(8,128)(2,1)S(1)}, bf16[128,2176]{1,0:T(8,128)(2,1)S(1)}, u32[]{:S(2)}, u32[]{:S(2)}) collective-permute-start(bf16[128,2176]{1,0:T(8,128)(2,1)S(1)} %collective-permute-done.4.refs_3_), channel_id=1, source_target_pairs={{0,1},{1,0},{2,3},{3,2},{4,5},{5,4},{6,7},{7,6},{8,9},{9,8},{10,11... | collective-permute-start | bytes 1671176 | tf_op jit(solution)/shard_map/ppermute | solution.py:34
  53.9 2.2 %copy-start.2 = (bf16[1,256,8192]{2,1,0:T(8,128)(2,1)S(1)}, bf16[1,256,8192]{2,1,0:T(8,128)(2,1)}, u32[]{:S(2)}) copy-start(bf16[1,256,8192]{2,1,0:T(8,128)(2,1)} %refs_6_.1) | copy-start | bytes 12582916
  56.0 1.2 %copy-start.4 = (bf16[128,3328]{1,0:T(8,128)(2,1)S(1)}, bf16[128,3328]{1,0:T(8,128)(2,1)}, u32[]{:S(2)}) copy-start(bf16[128,3328]{1,0:T(8,128)(2,1)} %copy-done.3) | copy-start | bytes 2555908

commit v17 on v16

--- a/solution.py
+++ b/solution.py
@@ -167,6 +167,30 @@
     )(hot, arrived, q_rows)
 
 
+def place_soon_kernel(first, hot_ref, arrived_ref, q_hbm, placed_ref, local, sem):
+    quota, width = arrived_ref.shape
+    fetch = pltpu.make_async_copy(
+        q_hbm.at[0, 0:quota, head_columns(first, width // HEAD_SIZE)], local, sem
+    )
+    fetch.start()
+    fetch.wait()
+    for head, heads in pieces(first, width // HEAD_SIZE):
+        own = head_columns(head - first, heads)
+        placed_ref[:, own] = place_rows(hot_ref[...], arrived_ref[:, own], local[:, own])
+
+
+def place_soon(hot, arrived, q_rows, first):
+    return pl.pallas_call(
+        functools.partial(place_soon_kernel, first),
+        in_specs=[WHOLE, WHOLE, ANYWHERE],
+        out_specs=WHOLE,
+        out_shape=jax.ShapeDtypeStruct(arrived.shape, jnp.bfloat16),
+        scratch_shapes=[pltpu.VMEM(arrived.shape, jnp.bfloat16), pltpu.SemaphoreType.DMA],
+        compiler_params=pltpu.CompilerParams(vmem_limit_bytes=VMEM_GRANT),
+        name="place_soon",
+    )(hot, arrived, q_rows)
+
+
 def make_bias(kv_refs, far_ref, mate_ref, bias, rank):
     quota = bias.shape[0]
     core = lax.rem(rank, 2)
@@ -245,17 +269,29 @@
         scores = later
 
 
-def early_kernel(blocks, count, rank_ref, *refs):
+def early_kernel(blocks, ahead_count, rank_ref, *refs):
     kv_refs, far_ref, mate_ref = refs[: blocks - 1], refs[blocks - 1], refs[blocks]
-    q_hbm, in_hbm, out_hbm, local, bias, rest, queries, result, sems = refs[blocks + 1 :]
+    placed_ref, q_hbm, in_hbm, out_hbm, local = refs[blocks + 1 : blocks + 6]
+    bias, rest, queries, result, sems = refs[blocks + 6 :]
+    count = ahead_count + placed_ref.shape[1] // HEAD_SIZE
     own, others = head_columns(0, count), head_columns(count, QUERY_HEADS - count)
-    fetch = pltpu.make_async_copy(in_hbm.at[0, :, own], queries, sems.at[0])
+    fetch = pltpu.make_async_copy(in_hbm.at[0, :, head_columns(0, ahead_count)], queries, sems.at[0])
     fetch.start()
     rank = rank_ref[0]
     make_bias(kv_refs, far_ref, mate_ref, bias, rank)
     choose_rest(0, count, lax.rem(rank, 2), far_ref, mate_ref, rest)
     fetch.wait()
-    attend_heads(0, pieces(0, count), [*kv_refs, rest], bias, lambda cols: queries[:, cols], result)
+    edge = queries.shape[1]
+
+    def take(cols):
+        if cols.stop <= edge:
+            return queries[:, cols]
+        if cols.start >= edge:
+            return placed_ref[:, cols.start - edge : cols.stop - edge]
+        halves = queries[:, cols.start : edge], placed_ref[:, 0 : cols.stop - edge]
+        return jnp.concatenate(halves, axis=1)
+
+    attend_heads(0, pieces(0, count), [*kv_refs, rest], bias, take, result)
     store = pltpu.make_async_copy(result, out_hbm.at[0, :, own], sems.at[1])
     store.start()
     ahead = pltpu.make_async_copy(q_hbm.at[0, 0 : bias.shape[0], others], local, sems.at[2])
@@ -286,7 +322,7 @@
     store.wait()
 
 
-def attend(rank, hot, arrived, q_rows, kv_blocks, out):
+def attend(rank, hot, placed, arrived, q_rows, kv_blocks, out):
     quota, width = arrived.shape
     blocks = len(kv_blocks) - 1
     first = QUERY_HEADS - width // HEAD_SIZE
@@ -294,14 +330,15 @@
     rest = pltpu.VMEM((quota, NOTE), jnp.bfloat16)
     own = pltpu.VMEM(arrived.shape, jnp.bfloat16)
     others = pltpu.VMEM((quota, first * HEAD_SIZE), jnp.bfloat16)
+    ahead = pltpu.VMEM((quota, first * HEAD_SIZE - placed.shape[1]), jnp.bfloat16)
     out, local = in_place(
-        functools.partial(early_kernel, blocks, first),
-        [rank, *kv_blocks, q_rows],
+        functools.partial(early_kernel, blocks, first - placed.shape[1] // HEAD_SIZE),
+        [rank, *kv_blocks, placed, q_rows],
         out,
         more_out=[jax.ShapeDtypeStruct(arrived.shape, jnp.bfloat16)],
         more_specs=[WHOLE],
-        in_specs=[SCALARS] + [WHOLE] * len(kv_blocks) + [ANYWHERE],
-        scratch_shapes=[bias, rest, others, others, pltpu.SemaphoreType.DMA((3,))],
+        in_specs=[SCALARS] + [WHOLE] * (len(kv_blocks) + 1) + [ANYWHERE],
+        scratch_shapes=[bias, rest, ahead, others, pltpu.SemaphoreType.DMA((3,))],
         name="attend_early",
     )
     return in_place(
@@ -344,23 +381,27 @@
     shift = shifts_in(own_count, quota)
     own, hot = settle_kv(shift, doc_ids, arrived_kv, local_kv)
 
-    kv_blocks = [own]
+    swapped = [across_cores(own, (0,))]
+    same_core = []
     carried, out = own, None
     for back in range(1, rounds + 1):
         carried = shifted(carried, "ctx", 2)
-        kv_blocks.append(carried)
+        same_core.append(carried)
         if back < len(CHUNKS):
             first, arrived = sum(CHUNKS[: back - 1]), arrived_q[back - 1]
-            if back < rounds:
+            if back < min(rounds, len(CHUNKS) - 1):
                 out = place_queries(hot, arrived, q_rows, first, out)
                 carried, out = lax.optimization_barrier((carried, out))
             else:
-                carried, arrived = lax.optimization_barrier((carried, arrived))
-                out = place_queries(hot, arrived, q_rows, first, out)
-        if back < rounds:
-            kv_blocks.append(across_cores(carried))
-    kv_blocks += [across_cores(carried), across_cores(own, (0,))]
-    return attend(rank[None], hot, arrived_q[-1], q_rows, kv_blocks, out)
+                placed = place_soon(hot, arrived, q_rows, first)
+                carried, placed = lax.optimization_barrier((carried, placed))
+        swapped.append(across_cores(carried))
+    mate, *others = swapped
+    kv_blocks = [own]
+    for same, other in zip(same_core, others):
+        kv_blocks += [same, other]
+    kv_blocks.append(mate)
+    return attend(rank[None], hot, placed, arrived_q[-1], q_rows, kv_blocks, out)
 
 
 def solution(mesh):

time: 72.9 us -> 72.4 us (level)
  waiting for transfers between devices: 19.6 us -> 25.4 us
  local copies, waits for them, and re-layouts: 7.52 us -> 3.27 us
  starting transfers between devices: 23.2 us -> 20.2 us
  Pallas kernels: 17.3 us -> 18.5 us
    unnamed x12 -> x8, local copies, waits for them, and re-layouts: 6.45 us -> 2.2 us
    ppermute x6, waiting for transfers between devices: 19.6 us -> 22.9 us  [shifted(): return lax.ppermute(x, axis, [(i, i + steps) for i in range(n - steps)])]
    ppermute x3, starting transfers between devices: 7.34 us -> 4.14 us  [across_cores(): lax.ppermute(x, 'ctx', [(i, i ^ 1) for i in range(n) if i % 2 in sources])]
    ppermute x3, waiting for transfers between devices: 0.01 us -> 2.42 us  [across_cores(): lax.ppermute(x, 'ctx', [(i, i ^ 1) for i in range(n) if i % 2 in sources])]
    pallas_call x3 -> x2, Pallas kernels: 15.2 us -> 15.9 us  [in_place(): pl.pallas_call(kernel, in_specs=specs, out_specs=[ANYWHERE, *more_specs],...]
  transfers between devices with their start and end apart: 9 -> 9, of which waited for: 3 -> 5; matrix products, arithmetic and copies ran while one was open for 5% -> 5% of each run, Pallas kernels for 17% -> 17%
where the time goes in v17:
time: 72.4 us; the launch traced here: 71.9 us
  waiting for transfers between devices  25.4 us (35%)
  starting transfers between devices  20.2 us (28%)
  Pallas kernels  18.5 us (26%)
  other arithmetic  3.69 us (5%)
  local copies, waits for them, and re-layouts  3.27 us (5%)
  between operations  0.98 us (1%)
    ppermute x6, waiting for transfers between devices, shifted(): return lax.ppermute(x, axis, [(i, i + steps) for i in range(n - steps)])  22.9 us
    ppermute x6, starting transfers between devices, shifted(): return lax.ppermute(x, axis, [(i, i + steps) for i in range(n - steps)])  16 us
    pallas_call x2, Pallas kernels, in_place(): pl.pallas_call(kernel, in_specs=specs, out_specs=[ANYWHERE, *more_specs],...  15.9 us
    ppermute x3, starting transfers between devices, across_cores(): lax.ppermute(x, 'ctx', [(i, i ^ 1) for i in range(n) if i % 2 in sources])  4.14 us
    select_n x4, other arithmetic, circular_tail(): return jnp.where(later[:, None], rows[quota:], rows[:quota])  3.54 us
    ppermute x3, waiting for transfers between devices, across_cores(): lax.ppermute(x, 'ctx', [(i, i ^ 1) for i in range(n) if i % 2 in sources])  2.42 us
    unnamed x8, local copies, waits for them, and re-layouts  2.2 us
  transfers between devices with their start and end apart: 9, of which 5 were waited for; matrix products, arithmetic and copies ran while one was open for 5% of the time, Pallas kernels for 17%

profile of v17, /device:TPU:21, one launch (start us, length us, event | category | flops | bytes accessed | tf_op | source)
XLA Modules:
  0.0 71.9 jit_solution(839353579725541154)
XLA Ops:
  0.0 0.0 copy-start
  0.8 1.5 %bitcast_select_fusion.4 = (bf16[128,1024]{1,0:T(8,128)(2,1)S(1)}, bf16[128,1024]{1,0:T(8,128)(2,1)S(1)}) fusion(bf16[1,256,1024]{2,1,0:T(8,128)(2,1)} %param.6, pred[128]{0:T(512)(128)(4,1)S(1)} %add_compare_fusion, bf16[1,256,1024]{2,1,0:T(8,128)(2,1)} %param.7), kind=kLoop, calls=%fused_computation.6 | loop fusion | flops 262144 | bytes 1572992 | tf_op jit(solution)/shard_map/jit(_where)/select_n | solution.py:356
  2.3 0.0 copy-start.3
  2.4 3.1 %collective-permute-start = (bf16[128,2048]{1,0:T(8,128)(2,1)S(1)}, bf16[128,2048]{1,0:T(8,128)(2,1)S(1)}, u32[]{:S(2)}, u32[]{:S(2)}) collective-permute-start(bf16[128,2048]{1,0:T(8,128)(2,1)S(1)} %pad_maximum_fusion), channel_id=1, source_target_pairs={{0,8},{8,16},{16,24},{1,9},{9,17},{17,25},{2,10},{10,18},{18,26},{... | collective-permute-start | bytes 1572872 | tf_op jit(solution)/shard_map/ppermute | solution.py:29
  5.5 1.1 %slice_bitcast_fusion = (bf16[128,1024]{1,0:T(8,128)(2,1)S(1)}, bf16[128,1024]{1,0:T(8,128)(2,1)S(1)}) fusion(bf16[1,256,1024]{2,1,0:T(8,128)(2,1)} %param.7, bf16[1,256,1024]{2,1,0:T(8,128)(2,1)} %param.6), kind=kLoop, calls=%fused_computation.7 | loop fusion | bytes 1048576 | tf_op jit(solution)/shard_map/slice | solution.py:356
  6.6 0.0 copy-done
  6.6 0.9 %bitcast_select_fusion.2 = bf16[128,2304]{1,0:T(8,128)(2,1)} fusion(bf16[1,256,8192]{2,1,0:T(8,128)(2,1)S(1)} %copy-done, pred[128]{0:T(512)(128)(4,1)S(1)} %add_compare_fusion), kind=kLoop, calls=%fused_computation.2 | loop fusion | flops 294912 | bytes 1769600 | tf_op jit(solution)/shard_map/jit(_where)/select_n | solution.py:356
  7.6 0.1 bitcast_select_fusion
  7.7 1.0 %bitcast_select_fusion.1 = bf16[128,2560]{1,0:T(8,128)(2,1)} fusion(bf16[1,256,8192]{2,1,0:T(8,128)(2,1)S(1)} %copy-done, pred[128]{0:T(512)(128)(4,1)S(1)} %add_compare_fusion), kind=kLoop, calls=%fused_computation.1 | loop fusion | flops 327680 | bytes 1966208 | tf_op jit(solution)/shard_map/jit(_where)/select_n | solution.py:356
  8.7 1.9 %collective-permute-start.2 = (bf16[128,2560]{1,0:T(8,128)(2,1)}, bf16[128,2560]{1,0:T(8,128)(2,1)S(1)}, u32[]{:S(2)}, u32[]{:S(2)}) collective-permute-start(bf16[128,2560]{1,0:T(8,128)(2,1)} %bitcast_select_fusion.1), channel_id=1, source_target_pairs={{0,8},{8,16},{16,24},{1,9},{9,17},{17,25},{2,10},{10,18},{18,26},{... | collective-permute-start | bytes 1966088 | tf_op jit(solution)/shard_map/ppermute | solution.py:29
  10.6 0.1 pad_add_fusion.shift_ref
  10.7 7.3 %collective-permute-done.arrived_ref = bf16[128,2048]{1,0:T(8,128)(2,1)S(1)} collective-permute-done((bf16[128,2048]{1,0:T(8,128)(2,1)S(1)}, bf16[128,2048]{1,0:T(8,128)(2,1)S(1)}, u32[]{:S(2)}, u32[]{:S(2)}) %collective-permute-start) | collective-permute-done | bytes 524320 | tf_op jit(solution)/shard_map/ppermute | solution.py:29
  17.9 0.0 copy-done.3
  17.9 0.8 %settle_kv.1 = (bf16[128,2176]{1,0:T(8,128)(2,1)S(1)}, bf16[128,256]{1,0:T(8,128)(2,1)S(1)}) custom-call(s32[2]{0:T(128)S(1)} %pad_add_fusion.shift_ref, s32[1,128]{1,0:T(1,128)S(1)} %copy-done.3, bf16[128,2048]{1,0:T(8,128)(2,1)S(1)} %collective-permute-done.arrived_ref, bf16[128,2048]{1,0:T(8,128)(2,1)S(1)} %pad_maximum_fusion.1.local_ref), custom_call_target="tpu_custom_call" | custom-call | tf_op jit(solution)/shard_map/settle_kv/pallas_call | solution.py:78
  18.8 3.2 %collective-permute-start.1 = (bf16[128,2176]{1,0:T(8,128)(2,1)S(1)}, bf16[128,2176]{1,0:T(8,128)(2,1)S(1)}, u32[]{:S(2)}, u32[]{:S(2)}) collective-permute-start(bf16[128,2176]{1,0:T(8,128)(2,1)S(1)} %get-tuple-element.23.refs_0_), channel_id=1, source_target_pairs={{0,2},{1,3},{2,4},{3,5},{4,6},{5,7},{8,10},{9,11},{10,12},{11,13},... | collective-permute-start | bytes 1671176 | tf_op jit(solution)/shard_map/ppermute | solution.py:29
  22.0 2.2 %collective-permute-start.5 = (bf16[128,3328]{1,0:T(8,128)(2,1)S(1)}, bf16[128,3328]{1,0:T(8,128)(2,1)S(1)}, u32[]{:S(2)}, u32[]{:S(2)}) collective-permute-start(bf16[128,3328]{1,0:T(8,128)(2,1)S(1)} %bitcast_select_fusion), channel_id=1, source_target_pairs={{0,8},{8,16},{16,24},{1,9},{9,17},{17,25},{2,10},{10,18},{18,26},{... | collective-permute-start | bytes 2555912 | tf_op jit(solution)/shard_map/ppermute | solution.py:29
  24.2 7.7 %collective-permute-done.2.arrived_ref = bf16[128,2560]{1,0:T(8,128)(2,1)S(1)} collective-permute-done((bf16[128,2560]{1,0:T(8,128)(2,1)}, bf16[128,2560]{1,0:T(8,128)(2,1)S(1)}, u32[]{:S(2)}, u32[]{:S(2)}) %collective-permute-start.2) | collective-permute-done | bytes 655392 | tf_op jit(solution)/shard_map/ppermute | solution.py:29
  32.0 0.0 copy-start.1
  32.0 2.2 %copy-done.1 = bf16[1,256,8192]{2,1,0:T(8,128)(2,1)S(1)} copy-done((bf16[1,256,8192]{2,1,0:T(8,128)(2,1)S(1)}, bf16[1,256,8192]{2,1,0:T(8,128)(2,1)}, u32[]{:S(2)}) %copy-start.1) | copy-done | bytes 4194328
  34.2 0.0 copy-start.2
  34.2 1.2 %place_queries.1.refs_8_ = bf16[1,128,8192]{2,1,0:T(8,128)(2,1)} custom-call(bf16[128,256]{1,0:T(8,128)(2,1)S(1)} %get-tuple-element.24.hot_ref.refs_6_, bf16[128,2560]{1,0:T(8,128)(2,1)S(1)} %collective-permute-done.2.arrived_ref, bf16[1,256,8192]{2,1,0:T(8,128)(2,1)S(1)} %copy-done.1), custom_call_target="tpu_custom_call" | custom-call | tf_op jit(solution)/shard_map/place_queries/pallas_call | solution.py:161
  35.4 0.0 collective-permute-done.1.refs_1_
  35.4 3.3 %collective-permute-start.4 = (bf16[128,2176]{1,0:T(8,128)(2,1)S(1)}, bf16[128,2176]{1,0:T(8,128)(2,1)S(1)}, u32[]{:S(2)}, u32[]{:S(2)}) collective-permute-start(bf16[128,2176]{1,0:T(8,128)(2,1)S(1)} %collective-permute-done.1.refs_1_), channel_id=1, source_target_pairs={{0,2},{1,3},{2,4},{3,5},{4,6},{5,7},{8,10},{9,11},{10,12},{11,13},... | collective-permute-start | bytes 1671176 | tf_op jit(solution)/shard_map/ppermute | solution.py:29
  38.8 2.2 %collective-permute-start.8 = (bf16[128,2304]{1,0:T(8,128)(2,1)}, bf16[128,2304]{1,0:T(8,128)(2,1)}, u32[]{:S(2)}, u32[]{:S(2)}) collective-permute-start(bf16[128,2304]{1,0:T(8,128)(2,1)} %bitcast_select_fusion.2), channel_id=1, source_target_pairs={{0,8},{8,16},{16,24},{1,9},{9,17},{17,25},{2,10},{10,18},{18,26},{... | collective-permute-start | bytes 1769480 | tf_op jit(solution)/shard_map/ppermute | solution.py:29
  41.0 1.3 %collective-permute-start.7 = (bf16[128,2176]{1,0:T(8,128)(2,1)S(1)}, bf16[128,2176]{1,0:T(8,128)(2,1)S(1)}, u32[]{:S(2)}, u32[]{:S(2)}) collective-permute-start(bf16[128,2176]{1,0:T(8,128)(2,1)S(1)} %get-tuple-element.23.refs_0_), channel_id=1, source_target_pairs={{0,1},{2,3},{4,5},{6,7},{8,9},{10,11},{12,13},{14,15},{16,17},{18,... | collective-permute-start | bytes 1671176 | tf_op jit(solution)/shard_map/ppermute | solution.py:34
  42.3 7.9 %collective-permute-done.5.arrived_ref = bf16[128,3328]{1,0:T(8,128)(2,1)S(1)} collective-permute-done((bf16[128,3328]{1,0:T(8,128)(2,1)S(1)}, bf16[128,3328]{1,0:T(8,128)(2,1)S(1)}, u32[]{:S(2)}, u32[]{:S(2)}) %collective-permute-start.5) | collective-permute-done | bytes 852000 | tf_op jit(solution)/shard_map/ppermute | solution.py:29
  50.2 0.0 copy-done.2
  50.2 0.5 place_soon.1.refs_6_
  50.7 2.8 %collective-permute-start.3 = (bf16[128,2176]{1,0:T(8,128)(2,1)S(1)}, bf16[128,2176]{1,0:T(8,128)(2,1)}, u32[]{:S(2)}, u32[]{:S(2)}) collective-permute-start(bf16[128,2176]{1,0:T(8,128)(2,1)S(1)} %collective-permute-done.1.refs_1_), channel_id=1, source_target_pairs={{0,1},{1,0},{2,3},{3,2},{4,5},{5,4},{6,7},{7,6},{8,9},{9,8},{10,11... | collective-permute-start | bytes 1671176 | tf_op jit(solution)/shard_map/ppermute | solution.py:34
  53.5 0.0 collective-permute-done.4.refs_3_
  53.5 0.1 collective-permute-start.6
  53.6 0.0 collective-permute-done.7.refs_5_
  53.6 1.6 %collective-permute-done.3.refs_2_ = bf16[128,2176]{1,0:T(8,128)(2,1)} collective-permute-done((bf16[128,2176]{1,0:T(8,128)(2,1)S(1)}, bf16[128,2176]{1,0:T(8,128)(2,1)}, u32[]{:S(2)}, u32[]{:S(2)}) %collective-permute-start.3) | collective-permute-done | bytes 557088 | tf_op jit(solution)/shard_map/ppermute | solution.py:34
  55.2 0.8 %collective-permute-done.6.refs_4_ = bf16[128,2176]{1,0:T(8,128)(2,1)} collective-permute-done((bf16[128,2176]{1,0:T(8,128)(2,1)S(1)}, bf16[128,2176]{1,0:T(8,128)(2,1)}, u32[]{:S(2)}, u32[]{:S(2)}) %collective-permute-start.6) | collective-permute-done | bytes 557088 | tf_op jit(solution)/shard_map/ppermute | solution.py:34
  56.0 9.9 %attend_early.1 = (bf16[1,128,8192]{2,1,0:T(8,128)(2,1)}, bf16[128,2304]{1,0:T(8,128)(2,1)S(1)}) custom-call(s32[1]{0:T(128)} %bitcast.rank_ref, bf16[128,2176]{1,0:T(8,128)(2,1)S(1)} %get-tuple-element.23.refs_0_, bf16[128,2176]{1,0:T(8,128)(2,1)S(1)} %collective-permute-done.1.refs_1_, ...), custom_call_target="tpu_custom_call", output_to_operand_aliasing={{0}: (9, {})} | custom-call | tf_op jit(solution)/shard_map/attend_early/pallas_call | solution.py:119
  65.9 0.0 collective-permute-done.8.refs_7_
  65.9 6.0 %attend_late.1 = bf16[1,128,8192]{2,1,0:T(8,128)(2,1)} custom-call(s32[1]{0:T(128)} %bitcast.rank_ref, bf16[128,2176]{1,0:T(8,128)(2,1)S(1)} %get-tuple-element.23.refs_0_, bf16[128,2176]{1,0:T(8,128)(2,1)S(1)} %collective-permute-done.1.refs_1_, bf16[128,2176]{1,0:T(8,128)(2,1)} %collective-permute-done.3.refs_2_, ...), custom_call_target="tpu_custom_call", output_to_operand_aliasing={{}: (10, {})} | custom-call | tf_op jit(solution)/shard_map/attend_late/pallas_call | solution.py:119
  (3 shorter events, 0.1 us)
Async XLA Ops:
  0.0 6.6 %copy-start = (bf16[1,256,8192]{2,1,0:T(8,128)(2,1)S(1)}, bf16[1,256,8192]{2,1,0:T(8,128)(2,1)}, u32[]{:S(2)}) copy-start(bf16[1,256,8192]{2,1,0:T(8,128)(2,1)} %refs_7_.1) | copy-start | bytes 12582916
  2.3 15.6 %copy-start.3 = (s32[1,128]{1,0:T(1,128)S(1)}, s32[1,128]{1,0:T(1,128)}, u32[]{:S(2)}) copy-start(s32[1,128]{1,0:T(1,128)} %docs_ref.1) | copy-start | bytes 1540
  2.4 15.6 %collective-permute-start = (bf16[128,2048]{1,0:T(8,128)(2,1)S(1)}, bf16[128,2048]{1,0:T(8,128)(2,1)S(1)}, u32[]{:S(2)}, u32[]{:S(2)}) collective-permute-start(bf16[128,2048]{1,0:T(8,128)(2,1)S(1)} %pad_maximum_fusion), channel_id=1, source_target_pairs={{0,8},{8,16},{16,24},{1,9},{9,17},{17,25},{2,10},{10,18},{18,26},{... | collective-permute-start | bytes 1572872 | tf_op jit(solution)/shard_map/ppermute | solution.py:29
  8.7 23.3 %collective-permute-start.2 = (bf16[128,2560]{1,0:T(8,128)(2,1)}, bf16[128,2560]{1,0:T(8,128)(2,1)S(1)}, u32[]{:S(2)}, u32[]{:S(2)}) collective-permute-start(bf16[128,2560]{1,0:T(8,128)(2,1)} %bitcast_select_fusion.1), channel_id=1, source_target_pairs={{0,8},{8,16},{16,24},{1,9},{9,17},{17,25},{2,10},{10,18},{18,26},{... | collective-permute-start | bytes 1966088 | tf_op jit(solution)/shard_map/ppermute | solution.py:29
  18.8 16.6 %collective-permute-start.1 = (bf16[128,2176]{1,0:T(8,128)(2,1)S(1)}, bf16[128,2176]{1,0:T(8,128)(2,1)S(1)}, u32[]{:S(2)}, u32[]{:S(2)}) collective-permute-start(bf16[128,2176]{1,0:T(8,128)(2,1)S(1)} %get-tuple-element.23.refs_0_), channel_id=1, source_target_pairs={{0,2},{1,3},{2,4},{3,5},{4,6},{5,7},{8,10},{9,11},{10,12},{11,13},... | collective-permute-start | bytes 1671176 | tf_op jit(solution)/shard_map/ppermute | solution.py:29
  22.0 28.2 %collective-permute-start.5 = (bf16[128,3328]{1,0:T(8,128)(2,1)S(1)}, bf16[128,3328]{1,0:T(8,128)(2,1)S(1)}, u32[]{:S(2)}, u32[]{:S(2)}) collective-permute-start(bf16[128,3328]{1,0:T(8,128)(2,1)S(1)} %bitcast_select_fusion), channel_id=1, source_target_pairs={{0,8},{8,16},{16,24},{1,9},{9,17},{17,25},{2,10},{10,18},{18,26},{... | collective-permute-start | bytes 2555912 | tf_op jit(solution)/shard_map/ppermute | solution.py:29
  32.0 2.2 %copy-start.1 = (bf16[1,256,8192]{2,1,0:T(8,128)(2,1)S(1)}, bf16[1,256,8192]{2,1,0:T(8,128)(2,1)}, u32[]{:S(2)}) copy-start(bf16[1,256,8192]{2,1,0:T(8,128)(2,1)} %refs_7_.1) | copy-start | bytes 12582916
  34.2 16.1 %copy-start.2 = (bf16[1,256,8192]{2,1,0:T(8,128)(2,1)S(1)}, bf16[1,256,8192]{2,1,0:T(8,128)(2,1)}, u32[]{:S(2)}) copy-start(bf16[1,256,8192]{2,1,0:T(8,128)(2,1)} %refs_7_.1) | copy-start | bytes 12582916
  35.4 18.1 %collective-permute-start.4 = (bf16[128,2176]{1,0:T(8,128)(2,1)S(1)}, bf16[128,2176]{1,0:T(8,128)(2,1)S(1)}, u32[]{:S(2)}, u32[]{:S(2)}) collective-permute-start(bf16[128,2176]{1,0:T(8,128)(2,1)S(1)} %collective-permute-done.1.refs_1_), channel_id=1, source_target_pairs={{0,2},{1,3},{2,4},{3,5},{4,6},{5,7},{8,10},{9,11},{10,12},{11,13},... | collective-permute-start | bytes 1671176 | tf_op jit(solution)/shard_map/ppermute | solution.py:29
  38.8 27.1 %collective-permute-start.8 = (bf16[128,2304]{1,0:T(8,128)(2,1)}, bf16[128,2304]{1,0:T(8,128)(2,1)}, u32[]{:S(2)}, u32[]{:S(2)}) collective-permute-start(bf16[128,2304]{1,0:T(8,128)(2,1)} %bitcast_select_fusion.2), channel_id=1, source_target_pairs={{0,8},{8,16},{16,24},{1,9},{9,17},{17,25},{2,10},{10,18},{18,26},{... | collective-permute-start | bytes 1769480 | tf_op jit(solution)/shard_map/ppermute | solution.py:29
  41.0 12.6 %collective-permute-start.7 = (bf16[128,2176]{1,0:T(8,128)(2,1)S(1)}, bf16[128,2176]{1,0:T(8,128)(2,1)S(1)}, u32[]{:S(2)}, u32[]{:S(2)}) collective-permute-start(bf16[128,2176]{1,0:T(8,128)(2,1)S(1)} %get-tuple-element.23.refs_0_), channel_id=1, source_target_pairs={{0,1},{2,3},{4,5},{6,7},{8,9},{10,11},{12,13},{14,15},{16,17},{18,... | collective-permute-start | bytes 1671176 | tf_op jit(solution)/shard_map/ppermute | solution.py:34
  50.7 4.5 %collective-permute-start.3 = (bf16[128,2176]{1,0:T(8,128)(2,1)S(1)}, bf16[128,2176]{1,0:T(8,128)(2,1)}, u32[]{:S(2)}, u32[]{:S(2)}) collective-permute-start(bf16[128,2176]{1,0:T(8,128)(2,1)S(1)} %collective-permute-done.1.refs_1_), channel_id=1, source_target_pairs={{0,1},{1,0},{2,3},{3,2},{4,5},{5,4},{6,7},{7,6},{8,9},{9,8},{10,11... | collective-permute-start | bytes 1671176 | tf_op jit(solution)/shard_map/ppermute | solution.py:34
  53.5 2.5 %collective-permute-start.6 = (bf16[128,2176]{1,0:T(8,128)(2,1)S(1)}, bf16[128,2176]{1,0:T(8,128)(2,1)}, u32[]{:S(2)}, u32[]{:S(2)}) collective-permute-start(bf16[128,2176]{1,0:T(8,128)(2,1)S(1)} %collective-permute-done.4.refs_3_), channel_id=1, source_target_pairs={{0,1},{1,0},{2,3},{3,2},{4,5},{5,4},{6,7},{7,6},{8,9},{9,8},{10,11... | collective-permute-start | bytes 1671176 | tf_op jit(solution)/shard_map/ppermute | solution.py:34

commit v18 on v17

--- a/solution.py
+++ b/solution.py
@@ -394,7 +394,7 @@
                 carried, out = lax.optimization_barrier((carried, out))
             else:
                 placed = place_soon(hot, arrived, q_rows, first)
-                carried, placed = lax.optimization_barrier((carried, placed))
+                carried, placed, swapped = lax.optimization_barrier((carried, placed, swapped))
         swapped.append(across_cores(carried))
     mate, *others = swapped
     kv_blocks = [own]

time: 72.4 us -> 73.6 us (1.017)
    ppermute x6, waiting for transfers between devices: 22.9 us -> 23.8 us  [shifted(): return lax.ppermute(x, axis, [(i, i + steps) for i in range(n - steps)])]
    ppermute x3, starting transfers between devices: 4.14 us -> 5.01 us  [across_cores(): lax.ppermute(x, 'ctx', [(i, i ^ 1) for i in range(n) if i % 2 in sources])]
  transfers between devices with their start and end apart: 9 -> 9, of which waited for: 5 -> 5; matrix products, arithmetic and copies ran while one was open for 5% -> 4% of each run, Pallas kernels for 17% -> 17%
where the time goes in v18:
time: 73.6 us; the launch traced here: 73.1 us
  waiting for transfers between devices  25.8 us (35%)
  starting transfers between devices  20.9 us (28%)
  Pallas kernels  18.5 us (25%)
  other arithmetic  3.69 us (5%)
  local copies, waits for them, and re-layouts  3.27 us (4%)
  between operations  0.99 us (1%)
    ppermute x6, waiting for transfers between devices, shifted(): return lax.ppermute(x, axis, [(i, i + steps) for i in range(n - steps)])  23.8 us
    pallas_call x2, Pallas kernels, in_place(): pl.pallas_call(kernel, in_specs=specs, out_specs=[ANYWHERE, *more_specs],...  15.9 us
    ppermute x6, starting transfers between devices, shifted(): return lax.ppermute(x, axis, [(i, i + steps) for i in range(n - steps)])  15.9 us
    ppermute x3, starting transfers between devices, across_cores(): lax.ppermute(x, 'ctx', [(i, i ^ 1) for i in range(n) if i % 2 in sources])  5.01 us
    select_n x4, other arithmetic, circular_tail(): return jnp.where(later[:, None], rows[quota:], rows[:quota])  3.54 us
    unnamed x8, local copies, waits for them, and re-layouts  2.2 us
    ppermute x3, waiting for transfers between devices, across_cores(): lax.ppermute(x, 'ctx', [(i, i ^ 1) for i in range(n) if i % 2 in sources])  1.93 us
  transfers between devices with their start and end apart: 9, of which 5 were waited for; matrix products, arithmetic and copies ran while one was open for 4% of the time, Pallas kernels for 17%

profile of v18, /device:TPU:21, one launch (start us, length us, event | category | flops | bytes accessed | tf_op | source)
XLA Modules:
  0.0 73.1 jit_solution(4288670323159047558)
XLA Ops:
  0.0 0.0 copy-start
  0.8 1.5 %bitcast_select_fusion.4 = (bf16[128,1024]{1,0:T(8,128)(2,1)S(1)}, bf16[128,1024]{1,0:T(8,128)(2,1)S(1)}) fusion(bf16[1,256,1024]{2,1,0:T(8,128)(2,1)} %param.6, pred[128]{0:T(512)(128)(4,1)S(1)} %add_compare_fusion, bf16[1,256,1024]{2,1,0:T(8,128)(2,1)} %param.7), kind=kLoop, calls=%fused_computation.6 | loop fusion | flops 262144 | bytes 1572992 | tf_op jit(solution)/shard_map/jit(_where)/select_n | solution.py:356
  2.3 0.0 copy-start.3
  2.4 3.1 %collective-permute-start = (bf16[128,2048]{1,0:T(8,128)(2,1)S(1)}, bf16[128,2048]{1,0:T(8,128)(2,1)S(1)}, u32[]{:S(2)}, u32[]{:S(2)}) collective-permute-start(bf16[128,2048]{1,0:T(8,128)(2,1)S(1)} %pad_maximum_fusion), channel_id=1, source_target_pairs={{0,8},{8,16},{16,24},{1,9},{9,17},{17,25},{2,10},{10,18},{18,26},{... | collective-permute-start | bytes 1572872 | tf_op jit(solution)/shard_map/ppermute | solution.py:29
  5.5 1.1 %slice_bitcast_fusion = (bf16[128,1024]{1,0:T(8,128)(2,1)S(1)}, bf16[128,1024]{1,0:T(8,128)(2,1)S(1)}) fusion(bf16[1,256,1024]{2,1,0:T(8,128)(2,1)} %param.7, bf16[1,256,1024]{2,1,0:T(8,128)(2,1)} %param.6), kind=kLoop, calls=%fused_computation.7 | loop fusion | bytes 1048576 | tf_op jit(solution)/shard_map/slice | solution.py:356
  6.6 0.0 copy-done
  6.6 0.9 %bitcast_select_fusion.2 = bf16[128,2304]{1,0:T(8,128)(2,1)} fusion(bf16[1,256,8192]{2,1,0:T(8,128)(2,1)S(1)} %copy-done, pred[128]{0:T(512)(128)(4,1)S(1)} %add_compare_fusion), kind=kLoop, calls=%fused_computation.2 | loop fusion | flops 294912 | bytes 1769600 | tf_op jit(solution)/shard_map/jit(_where)/select_n | solution.py:356
  7.6 0.1 bitcast_select_fusion
  7.7 1.0 %bitcast_select_fusion.1 = bf16[128,2560]{1,0:T(8,128)(2,1)} fusion(bf16[1,256,8192]{2,1,0:T(8,128)(2,1)S(1)} %copy-done, pred[128]{0:T(512)(128)(4,1)S(1)} %add_compare_fusion), kind=kLoop, calls=%fused_computation.1 | loop fusion | flops 327680 | bytes 1966208 | tf_op jit(solution)/shard_map/jit(_where)/select_n | solution.py:356
  8.7 1.9 %collective-permute-start.2 = (bf16[128,2560]{1,0:T(8,128)(2,1)}, bf16[128,2560]{1,0:T(8,128)(2,1)S(1)}, u32[]{:S(2)}, u32[]{:S(2)}) collective-permute-start(bf16[128,2560]{1,0:T(8,128)(2,1)} %bitcast_select_fusion.1), channel_id=1, source_target_pairs={{0,8},{8,16},{16,24},{1,9},{9,17},{17,25},{2,10},{10,18},{18,26},{... | collective-permute-start | bytes 1966088 | tf_op jit(solution)/shard_map/ppermute | solution.py:29
  10.6 0.1 pad_add_fusion.shift_ref
  10.7 7.3 %collective-permute-done.arrived_ref = bf16[128,2048]{1,0:T(8,128)(2,1)S(1)} collective-permute-done((bf16[128,2048]{1,0:T(8,128)(2,1)S(1)}, bf16[128,2048]{1,0:T(8,128)(2,1)S(1)}, u32[]{:S(2)}, u32[]{:S(2)}) %collective-permute-start) | collective-permute-done | bytes 524320 | tf_op jit(solution)/shard_map/ppermute | solution.py:29
  17.9 0.0 copy-done.3
  17.9 0.9 %settle_kv.1 = (bf16[128,2176]{1,0:T(8,128)(2,1)S(1)}, bf16[128,256]{1,0:T(8,128)(2,1)S(1)}) custom-call(s32[2]{0:T(128)S(1)} %pad_add_fusion.shift_ref, s32[1,128]{1,0:T(1,128)S(1)} %copy-done.3, bf16[128,2048]{1,0:T(8,128)(2,1)S(1)} %collective-permute-done.arrived_ref, bf16[128,2048]{1,0:T(8,128)(2,1)S(1)} %pad_maximum_fusion.1.local_ref), custom_call_target="tpu_custom_call" | custom-call | tf_op jit(solution)/shard_map/settle_kv/pallas_call | solution.py:78
  18.8 3.2 %collective-permute-start.1 = (bf16[128,2176]{1,0:T(8,128)(2,1)S(1)}, bf16[128,2176]{1,0:T(8,128)(2,1)S(1)}, u32[]{:S(2)}, u32[]{:S(2)}) collective-permute-start(bf16[128,2176]{1,0:T(8,128)(2,1)S(1)} %get-tuple-element.25.refs_0_), channel_id=1, source_target_pairs={{0,2},{1,3},{2,4},{3,5},{4,6},{5,7},{8,10},{9,11},{10,12},{11,13},... | collective-permute-start | bytes 1671176 | tf_op jit(solution)/shard_map/ppermute | solution.py:29
  22.0 2.2 %collective-permute-start.4 = (bf16[128,3328]{1,0:T(8,128)(2,1)S(1)}, bf16[128,3328]{1,0:T(8,128)(2,1)S(1)}, u32[]{:S(2)}, u32[]{:S(2)}) collective-permute-start(bf16[128,3328]{1,0:T(8,128)(2,1)S(1)} %bitcast_select_fusion), channel_id=1, source_target_pairs={{0,8},{8,16},{16,24},{1,9},{9,17},{17,25},{2,10},{10,18},{18,26},{... | collective-permute-start | bytes 2555912 | tf_op jit(solution)/shard_map/ppermute | solution.py:29
  24.2 1.3 %collective-permute-start.5 = (bf16[128,2176]{1,0:T(8,128)(2,1)S(1)}, bf16[128,2176]{1,0:T(8,128)(2,1)S(1)}, u32[]{:S(2)}, u32[]{:S(2)}) collective-permute-start(bf16[128,2176]{1,0:T(8,128)(2,1)S(1)} %get-tuple-element.25.refs_0_), channel_id=1, source_target_pairs={{0,1},{2,3},{4,5},{6,7},{8,9},{10,11},{12,13},{14,15},{16,17},{18,... | collective-permute-start | bytes 1671176 | tf_op jit(solution)/shard_map/ppermute | solution.py:34
  25.5 6.4 %collective-permute-done.2.arrived_ref = bf16[128,2560]{1,0:T(8,128)(2,1)S(1)} collective-permute-done((bf16[128,2560]{1,0:T(8,128)(2,1)}, bf16[128,2560]{1,0:T(8,128)(2,1)S(1)}, u32[]{:S(2)}, u32[]{:S(2)}) %collective-permute-start.2) | collective-permute-done | bytes 655392 | tf_op jit(solution)/shard_map/ppermute | solution.py:29
  32.0 0.0 copy-start.1
  32.0 2.2 %copy-done.1 = bf16[1,256,8192]{2,1,0:T(8,128)(2,1)S(1)} copy-done((bf16[1,256,8192]{2,1,0:T(8,128)(2,1)S(1)}, bf16[1,256,8192]{2,1,0:T(8,128)(2,1)}, u32[]{:S(2)}) %copy-start.1) | copy-done | bytes 4194328
  34.2 0.0 copy-start.2
  34.2 1.2 %place_queries.1.refs_8_ = bf16[1,128,8192]{2,1,0:T(8,128)(2,1)} custom-call(bf16[128,256]{1,0:T(8,128)(2,1)S(1)} %get-tuple-element.26.hot_ref.refs_6_, bf16[128,2560]{1,0:T(8,128)(2,1)S(1)} %collective-permute-done.2.arrived_ref, bf16[1,256,8192]{2,1,0:T(8,128)(2,1)S(1)} %copy-done.1), custom_call_target="tpu_custom_call" | custom-call | tf_op jit(solution)/shard_map/place_queries/pallas_call | solution.py:161
  35.4 0.0 collective-permute-done.1.refs_1_
  35.4 2.8 %collective-permute-start.6 = (bf16[128,2176]{1,0:T(8,128)(2,1)S(1)}, bf16[128,2176]{1,0:T(8,128)(2,1)S(1)}, u32[]{:S(2)}, u32[]{:S(2)}) collective-permute-start(bf16[128,2176]{1,0:T(8,128)(2,1)S(1)} %collective-permute-done.1.refs_1_), channel_id=1, source_target_pairs={{0,1},{1,0},{2,3},{3,2},{4,5},{5,4},{6,7},{7,6},{8,9},{9,8},{10,11... | collective-permute-start | bytes 1671176 | tf_op jit(solution)/shard_map/ppermute | solution.py:34
  38.2 3.2 %collective-permute-start.3 = (bf16[128,2176]{1,0:T(8,128)(2,1)S(1)}, bf16[128,2176]{1,0:T(8,128)(2,1)}, u32[]{:S(2)}, u32[]{:S(2)}) collective-permute-start(bf16[128,2176]{1,0:T(8,128)(2,1)S(1)} %collective-permute-done.1.refs_1_), channel_id=1, source_target_pairs={{0,2},{1,3},{2,4},{3,5},{4,6},{5,7},{8,10},{9,11},{10,12},{11,13},... | collective-permute-start | bytes 1671176 | tf_op jit(solution)/shard_map/ppermute | solution.py:29
  41.4 2.2 %collective-permute-start.8 = (bf16[128,2304]{1,0:T(8,128)(2,1)}, bf16[128,2304]{1,0:T(8,128)(2,1)}, u32[]{:S(2)}, u32[]{:S(2)}) collective-permute-start(bf16[128,2304]{1,0:T(8,128)(2,1)} %bitcast_select_fusion.2), channel_id=1, source_target_pairs={{0,8},{8,16},{16,24},{1,9},{9,17},{17,25},{2,10},{10,18},{18,26},{... | collective-permute-start | bytes 1769480 | tf_op jit(solution)/shard_map/ppermute | solution.py:29
  43.6 6.6 %collective-permute-done.4.arrived_ref = bf16[128,3328]{1,0:T(8,128)(2,1)S(1)} collective-permute-done((bf16[128,3328]{1,0:T(8,128)(2,1)S(1)}, bf16[128,3328]{1,0:T(8,128)(2,1)S(1)}, u32[]{:S(2)}, u32[]{:S(2)}) %collective-permute-start.4) | collective-permute-done | bytes 852000 | tf_op jit(solution)/shard_map/ppermute | solution.py:29
  50.2 0.0 copy-done.2
  50.2 0.5 place_soon.1.refs_6_
  50.7 0.0 collective-permute-done.5.refs_5_
  50.8 0.0 collective-permute-done.6.refs_2_
  50.8 3.5 %collective-permute-done.3.refs_3_ = bf16[128,2176]{1,0:T(8,128)(2,1)} collective-permute-done((bf16[128,2176]{1,0:T(8,128)(2,1)S(1)}, bf16[128,2176]{1,0:T(8,128)(2,1)}, u32[]{:S(2)}, u32[]{:S(2)}) %collective-permute-start.3) | collective-permute-done | bytes 557088 | tf_op jit(solution)/shard_map/ppermute | solution.py:29
  54.3 1.0 %collective-permute-start.7 = (bf16[128,2176]{1,0:T(8,128)(2,1)}, bf16[128,2176]{1,0:T(8,128)(2,1)}, u32[]{:S(2)}, u32[]{:S(2)}) collective-permute-start(bf16[128,2176]{1,0:T(8,128)(2,1)} %collective-permute-done.3.refs_3_), channel_id=1, source_target_pairs={{0,1},{1,0},{2,3},{3,2},{4,5},{5,4},{6,7},{7,6},{8,9},{9,8},{10,11... | collective-permute-start | bytes 1671176 | tf_op jit(solution)/shard_map/ppermute | solution.py:34
  55.2 1.9 %collective-permute-done.7.refs_4_ = bf16[128,2176]{1,0:T(8,128)(2,1)} collective-permute-done((bf16[128,2176]{1,0:T(8,128)(2,1)}, bf16[128,2176]{1,0:T(8,128)(2,1)}, u32[]{:S(2)}, u32[]{:S(2)}) %collective-permute-start.7) | collective-permute-done | bytes 557088 | tf_op jit(solution)/shard_map/ppermute | solution.py:34
  57.2 9.9 %attend_early.1 = (bf16[1,128,8192]{2,1,0:T(8,128)(2,1)}, bf16[128,2304]{1,0:T(8,128)(2,1)S(1)}) custom-call(s32[1]{0:T(128)} %bitcast.rank_ref, bf16[128,2176]{1,0:T(8,128)(2,1)S(1)} %get-tuple-element.25.refs_0_, bf16[128,2176]{1,0:T(8,128)(2,1)S(1)} %collective-permute-done.1.refs_1_, ...), custom_call_target="tpu_custom_call", output_to_operand_aliasing={{0}: (9, {})} | custom-call | tf_op jit(solution)/shard_map/attend_early/pallas_call | solution.py:119
  67.1 0.0 collective-permute-done.8.refs_7_
  67.1 6.0 %attend_late.1 = bf16[1,128,8192]{2,1,0:T(8,128)(2,1)} custom-call(s32[1]{0:T(128)} %bitcast.rank_ref, bf16[128,2176]{1,0:T(8,128)(2,1)S(1)} %get-tuple-element.25.refs_0_, bf16[128,2176]{1,0:T(8,128)(2,1)S(1)} %collective-permute-done.1.refs_1_, bf16[128,2176]{1,0:T(8,128)(2,1)S(1)} %collective-permute-done.6.refs_2_, ...), custom_call_target="tpu_custom_call", output_to_operand_aliasing={{}: (10, {})} | custom-call | tf_op jit(solution)/shard_map/attend_late/pallas_call | solution.py:119
  (3 shorter events, 0.1 us)
Async XLA Ops:
  0.0 6.6 %copy-start = (bf16[1,256,8192]{2,1,0:T(8,128)(2,1)S(1)}, bf16[1,256,8192]{2,1,0:T(8,128)(2,1)}, u32[]{:S(2)}) copy-start(bf16[1,256,8192]{2,1,0:T(8,128)(2,1)} %refs_7_.1) | copy-start | bytes 12582916
  2.3 15.6 %copy-start.3 = (s32[1,128]{1,0:T(1,128)S(1)}, s32[1,128]{1,0:T(1,128)}, u32[]{:S(2)}) copy-start(s32[1,128]{1,0:T(1,128)} %docs_ref.1) | copy-start | bytes 1540
  2.4 15.6 %collective-permute-start = (bf16[128,2048]{1,0:T(8,128)(2,1)S(1)}, bf16[128,2048]{1,0:T(8,128)(2,1)S(1)}, u32[]{:S(2)}, u32[]{:S(2)}) collective-permute-start(bf16[128,2048]{1,0:T(8,128)(2,1)S(1)} %pad_maximum_fusion), channel_id=1, source_target_pairs={{0,8},{8,16},{16,24},{1,9},{9,17},{17,25},{2,10},{10,18},{18,26},{... | collective-permute-start | bytes 1572872 | tf_op jit(solution)/shard_map/ppermute | solution.py:29
  8.7 23.3 %collective-permute-start.2 = (bf16[128,2560]{1,0:T(8,128)(2,1)}, bf16[128,2560]{1,0:T(8,128)(2,1)S(1)}, u32[]{:S(2)}, u32[]{:S(2)}) collective-permute-start(bf16[128,2560]{1,0:T(8,128)(2,1)} %bitcast_select_fusion.1), channel_id=1, source_target_pairs={{0,8},{8,16},{16,24},{1,9},{9,17},{17,25},{2,10},{10,18},{18,26},{... | collective-permute-start | bytes 1966088 | tf_op jit(solution)/shard_map/ppermute | solution.py:29
  18.8 16.6 %collective-permute-start.1 = (bf16[128,2176]{1,0:T(8,128)(2,1)S(1)}, bf16[128,2176]{1,0:T(8,128)(2,1)S(1)}, u32[]{:S(2)}, u32[]{:S(2)}) collective-permute-start(bf16[128,2176]{1,0:T(8,128)(2,1)S(1)} %get-tuple-element.25.refs_0_), channel_id=1, source_target_pairs={{0,2},{1,3},{2,4},{3,5},{4,6},{5,7},{8,10},{9,11},{10,12},{11,13},... | collective-permute-start | bytes 1671176 | tf_op jit(solution)/shard_map/ppermute | solution.py:29
  22.0 28.2 %collective-permute-start.4 = (bf16[128,3328]{1,0:T(8,128)(2,1)S(1)}, bf16[128,3328]{1,0:T(8,128)(2,1)S(1)}, u32[]{:S(2)}, u32[]{:S(2)}) collective-permute-start(bf16[128,3328]{1,0:T(8,128)(2,1)S(1)} %bitcast_select_fusion), channel_id=1, source_target_pairs={{0,8},{8,16},{16,24},{1,9},{9,17},{17,25},{2,10},{10,18},{18,26},{... | collective-permute-start | bytes 2555912 | tf_op jit(solution)/shard_map/ppermute | solution.py:29
  24.2 26.5 %collective-permute-start.5 = (bf16[128,2176]{1,0:T(8,128)(2,1)S(1)}, bf16[128,2176]{1,0:T(8,128)(2,1)S(1)}, u32[]{:S(2)}, u32[]{:S(2)}) collective-permute-start(bf16[128,2176]{1,0:T(8,128)(2,1)S(1)} %get-tuple-element.25.refs_0_), channel_id=1, source_target_pairs={{0,1},{2,3},{4,5},{6,7},{8,9},{10,11},{12,13},{14,15},{16,17},{18,... | collective-permute-start | bytes 1671176 | tf_op jit(solution)/shard_map/ppermute | solution.py:34
  32.0 2.2 %copy-start.1 = (bf16[1,256,8192]{2,1,0:T(8,128)(2,1)S(1)}, bf16[1,256,8192]{2,1,0:T(8,128)(2,1)}, u32[]{:S(2)}) copy-start(bf16[1,256,8192]{2,1,0:T(8,128)(2,1)} %refs_7_.1) | copy-start | bytes 12582916
  34.2 16.1 %copy-start.2 = (bf16[1,256,8192]{2,1,0:T(8,128)(2,1)S(1)}, bf16[1,256,8192]{2,1,0:T(8,128)(2,1)}, u32[]{:S(2)}) copy-start(bf16[1,256,8192]{2,1,0:T(8,128)(2,1)} %refs_7_.1) | copy-start | bytes 12582916
  35.4 15.3 %collective-permute-start.6 = (bf16[128,2176]{1,0:T(8,128)(2,1)S(1)}, bf16[128,2176]{1,0:T(8,128)(2,1)S(1)}, u32[]{:S(2)}, u32[]{:S(2)}) collective-permute-start(bf16[128,2176]{1,0:T(8,128)(2,1)S(1)} %collective-permute-done.1.refs_1_), channel_id=1, source_target_pairs={{0,1},{1,0},{2,3},{3,2},{4,5},{5,4},{6,7},{7,6},{8,9},{9,8},{10,11... | collective-permute-start | bytes 1671176 | tf_op jit(solution)/shard_map/ppermute | solution.py:34
  38.2 16.1 %collective-permute-start.3 = (bf16[128,2176]{1,0:T(8,128)(2,1)S(1)}, bf16[128,2176]{1,0:T(8,128)(2,1)}, u32[]{:S(2)}, u32[]{:S(2)}) collective-permute-start(bf16[128,2176]{1,0:T(8,128)(2,1)S(1)} %collective-permute-done.1.refs_1_), channel_id=1, source_target_pairs={{0,2},{1,3},{2,4},{3,5},{4,6},{5,7},{8,10},{9,11},{10,12},{11,13},... | collective-permute-start | bytes 1671176 | tf_op jit(solution)/shard_map/ppermute | solution.py:29
  41.4 25.7 %collective-permute-start.8 = (bf16[128,2304]{1,0:T(8,128)(2,1)}, bf16[128,2304]{1,0:T(8,128)(2,1)}, u32[]{:S(2)}, u32[]{:S(2)}) collective-permute-start(bf16[128,2304]{1,0:T(8,128)(2,1)} %bitcast_select_fusion.2), channel_id=1, source_target_pairs={{0,8},{8,16},{16,24},{1,9},{9,17},{17,25},{2,10},{10,18},{18,26},{... | collective-permute-start | bytes 1769480 | tf_op jit(solution)/shard_map/ppermute | solution.py:29
  54.3 2.9 %collective-permute-start.7 = (bf16[128,2176]{1,0:T(8,128)(2,1)}, bf16[128,2176]{1,0:T(8,128)(2,1)}, u32[]{:S(2)}, u32[]{:S(2)}) collective-permute-start(bf16[128,2176]{1,0:T(8,128)(2,1)} %collective-permute-done.3.refs_3_), channel_id=1, source_target_pairs={{0,1},{1,0},{2,3},{3,2},{4,5},{5,4},{6,7},{7,6},{8,9},{9,8},{10,11... | collective-permute-start | bytes 1671176 | tf_op jit(solution)/shard_map/ppermute | solution.py:34

commit v19 on v15

--- a/solution.py
+++ b/solution.py
@@ -203,7 +203,7 @@
         rest[:, values] = mate_ref[:, values]
 
 
-def attend_heads(first, count, kv_refs, bias, take, result):
+def attend_heads(first, steps, kv_refs, bias, take, result):
     quota = bias.shape[0]
     unit = math.log2(math.e) / math.sqrt(HEAD_SIZE)
 
@@ -233,8 +233,7 @@
         for h in range(heads):
             result[:, head_columns(head - first + h)] = mixed[h * quota : (h + 1) * quota]
 
-    steps = pieces(first, count)
-    keys, values = key_head(first // GROUP)
+    keys, values = key_head(steps[0][0] // GROUP)
     scores = scored(*steps[0], keys)
     for i, (head, heads) in enumerate(steps):
         own_values, later = values, None
@@ -256,7 +255,7 @@
     make_bias(kv_refs, far_ref, mate_ref, bias, rank)
     choose_rest(0, count, lax.rem(rank, 2), far_ref, mate_ref, rest)
     fetch.wait()
-    attend_heads(0, count, [*kv_refs, rest], bias, lambda cols: queries[:, cols], result)
+    attend_heads(0, pieces(0, count), [*kv_refs, rest], bias, lambda cols: queries[:, cols], result)
     store = pltpu.make_async_copy(result, out_hbm.at[0, :, own], sems.at[1])
     store.start()
     ahead = pltpu.make_async_copy(q_hbm.at[0, 0 : bias.shape[0], others], local, sems.at[2])
@@ -280,7 +279,13 @@
     def take(cols):
         return place_rows(hot_ref[...], arrived[:, cols], local_ref[:, cols])
 
-    attend_heads(first, count, [*kv_refs, rest], bias, take, result)
+    steps = sorted(pieces(first, count), key=lambda piece: -piece[1])
+    head, heads = steps.pop()
+    if heads == HALF:
+        steps += [(head, heads // 2), (head + heads // 2, heads // 2)]
+    else:
+        steps.append((head, heads))
+    attend_heads(first, steps, [*kv_refs, rest], bias, take, result)
     store = pltpu.make_async_copy(result, out_hbm.at[0, :, head_columns(first, count)], sems.at[1])
     store.start()
     store.wait()
@@ -319,6 +324,12 @@
     return jnp.where(later[:, None], rows[quota:], rows[:quota])
 
 
+def sent(rows, later):
+    if lax.axis_size("dp") > 4:
+        return circular_tail(rows, later)
+    return rows[later.shape[0] :]
+
+
 def body(q_rows, k_rows, value_slot_rows, counts, doc_ids):
     quota = doc_ids.shape[1]
     rounds = lax.axis_size("ctx") // 4
@@ -326,17 +337,16 @@
     own_count = counts[0, 0]
 
     later = quota + jnp.arange(quota, dtype=jnp.int32) < own_count
-    kv_tail = jnp.concatenate(
-        [circular_tail(k_rows[0], later), circular_tail(value_slot_rows[0], later)], axis=1
-    )
-    local_kv = jnp.concatenate([k_rows[0, :quota], value_slot_rows[0, :quota]], axis=1)
-    kv_tail, later = lax.optimization_barrier((kv_tail, later))
-    local_kv, later = lax.optimization_barrier((local_kv, later))
+    k_local, v_local = k_rows[0], value_slot_rows[0]
+    kv_tail = jnp.concatenate([sent(k_local, later), sent(v_local, later)], axis=1)
     arrived_kv = shifted(kv_tail, "dp", 1)
+    zero = (kv_tail[:1, :1] + kv_tail[:1, -1:]) * 0
+    local_kv = jnp.concatenate([k_local[:quota] + zero, v_local[:quota] + zero], axis=1)
+    local_kv, zero = lax.optimization_barrier((local_kv, zero))
     q_tails = []
     first = 0
     for size in CHUNKS:
-        q_tails.append(circular_tail(q_rows[0, :, head_columns(first, size)], later))
+        q_tails.append(sent(q_rows[0, :, head_columns(first, size)], later) + zero)
         first += size
     q_tails = lax.optimization_barrier(q_tails)
     arrived_q = [shifted(tail, "dp", 1) for tail in q_tails]

time: 69.7 us -> 68.5 us (0.983)
  between operations: 0.89 us -> 2.11 us
  local copies, waits for them, and re-layouts: 3.19 us -> 2.35 us
    select_n x3 -> x0, other arithmetic: 3.57 us -> none  [circular_tail(): return jnp.where(later[:, None], rows[quota:], rows[:quota])]
    add x0 -> x4, other arithmetic: none -> 2.93 us  [the longest x2 0.99 us: body(): q_tails.append(sent(q_rows[0, :, head_columns(first, size)], later) + zero)]
    unnamed x10 -> x4, local copies, waits for them, and re-layouts: 2.21 us -> 0.01 us
    slice x1 -> x3, local copies, waits for them, and re-layouts: 0.99 us -> 2.34 us  [the longest x1 1.21 us: sent(): return rows[later.shape[0]:]]
  transfers between devices with their start and end apart: 9 -> 9, of which waited for: 4 -> 4; matrix products, arithmetic and copies ran while one was open for 5% -> 6% of each run, Pallas kernels for 18% -> 18%
where the time goes in v19:
time: 68.5 us; the launch traced here: 67.5 us
  starting transfers between devices  23.4 us (34%)
  waiting for transfers between devices  19.2 us (28%)
  Pallas kernels  17.3 us (25%)
  other arithmetic  3.08 us (4%)
  local copies, waits for them, and re-layouts  2.35 us (3%)
  between operations  2.11 us (3%)
    ppermute x6, waiting for transfers between devices, shifted(): return lax.ppermute(x, axis, [(i, i + steps) for i in range(n - steps)])  17.6 us
    ppermute x6, starting transfers between devices, shifted(): return lax.ppermute(x, axis, [(i, i + steps) for i in range(n - steps)])  16 us
    pallas_call x3, Pallas kernels, in_place(): pl.pallas_call(kernel, in_specs=specs, out_specs=[ANYWHERE, *more_specs],...  15.2 us
    ppermute x3, starting transfers between devices, across_cores(): lax.ppermute(x, 'ctx', [(i, i ^ 1) for i in range(n) if i % 2 in sources])  7.41 us
    ppermute x3, waiting for transfers between devices, across_cores(): lax.ppermute(x, 'ctx', [(i, i ^ 1) for i in range(n) if i % 2 in sources])  1.58 us
  transfers between devices with their start and end apart: 9, of which 4 were waited for; matrix products, arithmetic and copies ran while one was open for 6% of the time, Pallas kernels for 18%

profile of v19, /device:TPU:21, one launch (start us, length us, event | category | flops | bytes accessed | tf_op | source)
XLA Modules:
  0.0 67.5 jit_solution(18044688434079626737)
XLA Ops:
  0.0 0.0 copy-start
  0.0 1.2 %slice_bitcast_fusion = (bf16[128,1024]{1,0:T(8,128)(2,1)S(1)}, bf16[128,1024]{1,0:T(8,128)(2,1)S(1)}) fusion(bf16[1,256,1024]{2,1,0:T(8,128)(2,1)} %param.7, bf16[1,256,1024]{2,1,0:T(8,128)(2,1)} %param.6), kind=kLoop, calls=%fused_computation.7 | loop fusion | bytes 1048576 | tf_op jit(solution)/shard_map/slice | solution.py:330
  1.3 3.3 %collective-permute-start = (bf16[128,2048]{1,0:T(8,128)(2,1)S(1)}, bf16[128,2048]{1,0:T(8,128)(2,1)S(1)}, u32[]{:S(2)}, u32[]{:S(2)}) collective-permute-start(bf16[128,2048]{1,0:T(8,128)(2,1)S(1)} %pad_maximum_fusion), channel_id=1, source_target_pairs={{0,8},{8,16},{16,24},{1,9},{9,17},{17,25},{2,10},{10,18},{18,26},{... | collective-permute-start | bytes 1572872 | tf_op jit(solution)/shard_map/ppermute | solution.py:29
  4.5 0.5 slice.55
  5.0 0.6 slice.56
  6.9 1.0 %add_bitcast_fusion.3 = bf16[128,1024]{1,0:T(8,128)(2,1)S(1)} fusion(bf16[1,256,1024]{2,1,0:T(8,128)(2,1)} %param.7, bf16[]{:T(256)} %bitcast.4), kind=kLoop, calls=%fused_computation.5 | loop fusion | flops 131072 | bytes 524290 | tf_op jit(solution)/shard_map/add | solution.py:344
  7.9 1.0 %add_bitcast_fusion.4 = bf16[128,1024]{1,0:T(8,128)(2,1)S(1)} fusion(bf16[1,256,1024]{2,1,0:T(8,128)(2,1)} %param.6, bf16[]{:T(256)} %bitcast.4), kind=kLoop, calls=%fused_computation.6 | loop fusion | flops 131072 | bytes 524290 | tf_op jit(solution)/shard_map/add | solution.py:344
  8.9 0.0 copy-done
  9.0 0.0 copy-start.1
  9.0 0.9 %add_bitcast_fusion.1 = (bf16[128,2560]{1,0:T(8,128)(2,1)}, bf16[128,2560]{1,0:T(8,128)(2,1)S(1)}) fusion(bf16[1,256,8192]{2,1,0:T(8,128)(2,1)S(1)} %copy-done, bf16[]{:T(256)} %bitcast.7), kind=kLoop, calls=%fused_computation.1 | loop fusion | flops 655360 | bytes 2621442 | tf_op jit(solution)/shard_map/add | solution.py:349
  9.9 0.1 add_bitcast_fusion
  10.0 1.9 %collective-permute-start.2 = (bf16[128,2560]{1,0:T(8,128)(2,1)S(1)}, bf16[128,2560]{1,0:T(8,128)(2,1)S(1)}, u32[]{:S(2)}, u32[]{:S(2)}) collective-permute-start(bf16[128,2560]{1,0:T(8,128)(2,1)S(1)} %get-tuple-element.22), channel_id=1, source_target_pairs={{0,8},{8,16},{16,24},{1,9},{9,17},{17,25},{2,10},{10,18},{18,26},{... | collective-permute-start | bytes 1966088 | tf_op jit(solution)/shard_map/ppermute | solution.py:29
  12.5 0.1 pad_add_fusion.shift_ref
  12.6 4.4 %collective-permute-done.arrived_ref = bf16[128,2048]{1,0:T(8,128)(2,1)S(1)} collective-permute-done((bf16[128,2048]{1,0:T(8,128)(2,1)S(1)}, bf16[128,2048]{1,0:T(8,128)(2,1)S(1)}, u32[]{:S(2)}, u32[]{:S(2)}) %collective-permute-start) | collective-permute-done | bytes 524320 | tf_op jit(solution)/shard_map/ppermute | solution.py:29
  17.0 0.0 copy-done.1
  17.0 0.9 %settle_kv.1 = (bf16[128,2176]{1,0:T(8,128)(2,1)S(1)}, bf16[128,256]{1,0:T(8,128)(2,1)S(1)}) custom-call(s32[2]{0:T(128)S(1)} %pad_add_fusion.shift_ref, s32[1,128]{1,0:T(1,128)S(1)} %copy-done.1, bf16[128,2048]{1,0:T(8,128)(2,1)S(1)} %collective-permute-done.arrived_ref, bf16[128,2048]{1,0:T(8,128)(2,1)S(1)} %pad_maximum_fusion.1.local_ref), custom_call_target="tpu_custom_call" | custom-call | tf_op jit(solution)/shard_map/settle_kv/pallas_call | solution.py:78
  17.8 3.2 %collective-permute-start.1 = (bf16[128,2176]{1,0:T(8,128)(2,1)S(1)}, bf16[128,2176]{1,0:T(8,128)(2,1)S(1)}, u32[]{:S(2)}, u32[]{:S(2)}) collective-permute-start(bf16[128,2176]{1,0:T(8,128)(2,1)S(1)} %get-tuple-element.19.refs_0_), channel_id=1, source_target_pairs={{0,2},{1,3},{2,4},{3,5},{4,6},{5,7},{8,10},{9,11},{10,12},{11,13},... | collective-permute-start | bytes 1671176 | tf_op jit(solution)/shard_map/ppermute | solution.py:29
  21.0 2.2 %collective-permute-start.5 = (bf16[128,3072]{1,0:T(8,128)(2,1)S(1)}, bf16[128,3072]{1,0:T(8,128)(2,1)S(1)}, u32[]{:S(2)}, u32[]{:S(2)}) collective-permute-start(bf16[128,3072]{1,0:T(8,128)(2,1)S(1)} %add_bitcast_fusion), channel_id=1, source_target_pairs={{0,8},{8,16},{16,24},{1,9},{9,17},{17,25},{2,10},{10,18},{18,26},{... | collective-permute-start | bytes 2359304 | tf_op jit(solution)/shard_map/ppermute | solution.py:29
  23.3 7.7 %collective-permute-done.2.arrived_ref = bf16[128,2560]{1,0:T(8,128)(2,1)S(1)} collective-permute-done((bf16[128,2560]{1,0:T(8,128)(2,1)S(1)}, bf16[128,2560]{1,0:T(8,128)(2,1)S(1)}, u32[]{:S(2)}, u32[]{:S(2)}) %collective-permute-start.2) | collective-permute-done | bytes 655392 | tf_op jit(solution)/shard_map/ppermute | solution.py:29
  31.0 1.3 %place_queries.2.refs_0_ = bf16[1,128,8192]{2,1,0:T(8,128)(2,1)} custom-call(bf16[128,256]{1,0:T(8,128)(2,1)S(1)} %get-tuple-element.20.hot_ref.refs_6_, bf16[128,2560]{1,0:T(8,128)(2,1)S(1)} %collective-permute-done.2.arrived_ref, bf16[1,256,8192]{2,1,0:T(8,128)(2,1)S(1)} %copy-done), custom_call_target="tpu_custom_call" | custom-call | tf_op jit(solution)/shard_map/place_queries/pallas_call | solution.py:161
  32.3 0.0 collective-permute-done.1.refs_1_
  32.3 3.2 %collective-permute-start.4 = (bf16[128,2176]{1,0:T(8,128)(2,1)S(1)}, bf16[128,2176]{1,0:T(8,128)(2,1)S(1)}, u32[]{:S(2)}, u32[]{:S(2)}) collective-permute-start(bf16[128,2176]{1,0:T(8,128)(2,1)S(1)} %collective-permute-done.1.refs_1_), channel_id=1, source_target_pairs={{0,2},{1,3},{2,4},{3,5},{4,6},{5,7},{8,10},{9,11},{10,12},{11,13},... | collective-permute-start | bytes 1671176 | tf_op jit(solution)/shard_map/ppermute | solution.py:29
  35.5 2.2 %collective-permute-start.8 = (bf16[128,2560]{1,0:T(8,128)(2,1)}, bf16[128,2560]{1,0:T(8,128)(2,1)}, u32[]{:S(2)}, u32[]{:S(2)}) collective-permute-start(bf16[128,2560]{1,0:T(8,128)(2,1)} %get-tuple-element.27), channel_id=1, source_target_pairs={{0,8},{8,16},{16,24},{1,9},{9,17},{17,25},{2,10},{10,18},{18,26},{... | collective-permute-start | bytes 1966088 | tf_op jit(solution)/shard_map/ppermute | solution.py:29
  37.7 1.3 %collective-permute-start.7 = (bf16[128,2176]{1,0:T(8,128)(2,1)S(1)}, bf16[128,2176]{1,0:T(8,128)(2,1)S(1)}, u32[]{:S(2)}, u32[]{:S(2)}) collective-permute-start(bf16[128,2176]{1,0:T(8,128)(2,1)S(1)} %get-tuple-element.19.refs_0_), channel_id=1, source_target_pairs={{0,1},{2,3},{4,5},{6,7},{8,9},{10,11},{12,13},{14,15},{16,17},{18,... | collective-permute-start | bytes 1671176 | tf_op jit(solution)/shard_map/ppermute | solution.py:34
  39.0 3.4 %collective-permute-start.3 = (bf16[128,2176]{1,0:T(8,128)(2,1)S(1)}, bf16[128,2176]{1,0:T(8,128)(2,1)S(1)}, u32[]{:S(2)}, u32[]{:S(2)}) collective-permute-start(bf16[128,2176]{1,0:T(8,128)(2,1)S(1)} %collective-permute-done.1.refs_1_), channel_id=1, source_target_pairs={{0,1},{1,0},{2,3},{3,2},{4,5},{5,4},{6,7},{7,6},{8,9},{9,8},{10,11... | collective-permute-start | bytes 1671176 | tf_op jit(solution)/shard_map/ppermute | solution.py:34
  42.4 5.5 %collective-permute-done.5.arrived_ref = bf16[128,3072]{1,0:T(8,128)(2,1)S(1)} collective-permute-done((bf16[128,3072]{1,0:T(8,128)(2,1)S(1)}, bf16[128,3072]{1,0:T(8,128)(2,1)S(1)}, u32[]{:S(2)}, u32[]{:S(2)}) %collective-permute-start.5) | collective-permute-done | bytes 786464 | tf_op jit(solution)/shard_map/ppermute | solution.py:29
  47.9 1.3 %place_queries.3.refs_7_ = bf16[1,128,8192]{2,1,0:T(8,128)(2,1)} custom-call(bf16[128,256]{1,0:T(8,128)(2,1)S(1)} %get-tuple-element.20.hot_ref.refs_6_, bf16[128,3072]{1,0:T(8,128)(2,1)S(1)} %collective-permute-done.5.arrived_ref, bf16[1,256,8192]{2,1,0:T(8,128)(2,1)S(1)} %copy-done, ...), custom_call_target="tpu_custom_call", output_to_operand_aliasing={{}: (3, {})} | custom-call | tf_op jit(solution)/shard_map/place_queries/pallas_call | solution.py:119
  49.2 0.0 collective-permute-done.4.refs_3_
  49.2 2.8 %collective-permute-start.6 = (bf16[128,2176]{1,0:T(8,128)(2,1)S(1)}, bf16[128,2176]{1,0:T(8,128)(2,1)S(1)}, u32[]{:S(2)}, u32[]{:S(2)}) collective-permute-start(bf16[128,2176]{1,0:T(8,128)(2,1)S(1)} %collective-permute-done.4.refs_3_), channel_id=1, source_target_pairs={{0,1},{1,0},{2,3},{3,2},{4,5},{5,4},{6,7},{7,6},{8,9},{9,8},{10,11... | collective-permute-start | bytes 1671176 | tf_op jit(solution)/shard_map/ppermute | solution.py:34
  52.0 0.0 collective-permute-done.7.refs_5_
  52.0 0.0 collective-permute-done.3.refs_2_
  52.0 1.6 %collective-permute-done.6.refs_4_ = bf16[128,2176]{1,0:T(8,128)(2,1)S(1)} collective-permute-done((bf16[128,2176]{1,0:T(8,128)(2,1)S(1)}, bf16[128,2176]{1,0:T(8,128)(2,1)S(1)}, u32[]{:S(2)}, u32[]{:S(2)}) %collective-permute-start.6) | collective-permute-done | bytes 557088 | tf_op jit(solution)/shard_map/ppermute | solution.py:34
  53.6 8.7 %attend_early.1 = (bf16[1,128,8192]{2,1,0:T(8,128)(2,1)}, bf16[128,2560]{1,0:T(8,128)(2,1)S(1)}) custom-call(s32[1]{0:T(128)} %bitcast.rank_ref, bf16[128,2176]{1,0:T(8,128)(2,1)S(1)} %get-tuple-element.19.refs_0_, bf16[128,2176]{1,0:T(8,128)(2,1)S(1)} %collective-permute-done.1.refs_1_, ...), custom_call_target="tpu_custom_call", output_to_operand_aliasing={{0}: (8, {})} | custom-call | tf_op jit(solution)/shard_map/attend_early/pallas_call | solution.py:119
  62.3 0.0 collective-permute-done.8.refs_7_
  62.3 5.2 %attend_late.1 = bf16[1,128,8192]{2,1,0:T(8,128)(2,1)} custom-call(s32[1]{0:T(128)} %bitcast.rank_ref, bf16[128,2176]{1,0:T(8,128)(2,1)S(1)} %get-tuple-element.19.refs_0_, bf16[128,2176]{1,0:T(8,128)(2,1)S(1)} %collective-permute-done.1.refs_1_, bf16[128,2176]{1,0:T(8,128)(2,1)S(1)} %collective-permute-done.3.refs_2_, ...), custom_call_target="tpu_custom_call", output_to_operand_aliasing={{}: (10, {})} | custom-call | tf_op jit(solution)/shard_map/attend_late/pallas_call | solution.py:119
  (2 shorter events, 0.1 us)
Async XLA Ops:
  0.0 8.9 %copy-start = (bf16[1,256,8192]{2,1,0:T(8,128)(2,1)S(1)}, bf16[1,256,8192]{2,1,0:T(8,128)(2,1)}, u32[]{:S(2)}) copy-start(bf16[1,256,8192]{2,1,0:T(8,128)(2,1)} %refs_6_.1) | copy-start | bytes 12582916
  1.3 15.7 %collective-permute-start = (bf16[128,2048]{1,0:T(8,128)(2,1)S(1)}, bf16[128,2048]{1,0:T(8,128)(2,1)S(1)}, u32[]{:S(2)}, u32[]{:S(2)}) collective-permute-start(bf16[128,2048]{1,0:T(8,128)(2,1)S(1)} %pad_maximum_fusion), channel_id=1, source_target_pairs={{0,8},{8,16},{16,24},{1,9},{9,17},{17,25},{2,10},{10,18},{18,26},{... | collective-permute-start | bytes 1572872 | tf_op jit(solution)/shard_map/ppermute | solution.py:29
  9.0 8.0 %copy-start.1 = (s32[1,128]{1,0:T(1,128)S(1)}, s32[1,128]{1,0:T(1,128)}, u32[]{:S(2)}) copy-start(s32[1,128]{1,0:T(1,128)} %docs_ref.1) | copy-start | bytes 1540
  10.0 21.1 %collective-permute-start.2 = (bf16[128,2560]{1,0:T(8,128)(2,1)S(1)}, bf16[128,2560]{1,0:T(8,128)(2,1)S(1)}, u32[]{:S(2)}, u32[]{:S(2)}) collective-permute-start(bf16[128,2560]{1,0:T(8,128)(2,1)S(1)} %get-tuple-element.22), channel_id=1, source_target_pairs={{0,8},{8,16},{16,24},{1,9},{9,17},{17,25},{2,10},{10,18},{18,26},{... | collective-permute-start | bytes 1966088 | tf_op jit(solution)/shard_map/ppermute | solution.py:29
  17.8 14.4 %collective-permute-start.1 = (bf16[128,2176]{1,0:T(8,128)(2,1)S(1)}, bf16[128,2176]{1,0:T(8,128)(2,1)S(1)}, u32[]{:S(2)}, u32[]{:S(2)}) collective-permute-start(bf16[128,2176]{1,0:T(8,128)(2,1)S(1)} %get-tuple-element.19.refs_0_), channel_id=1, source_target_pairs={{0,2},{1,3},{2,4},{3,5},{4,6},{5,7},{8,10},{9,11},{10,12},{11,13},... | collective-permute-start | bytes 1671176 | tf_op jit(solution)/shard_map/ppermute | solution.py:29
  21.0 26.8 %collective-permute-start.5 = (bf16[128,3072]{1,0:T(8,128)(2,1)S(1)}, bf16[128,3072]{1,0:T(8,128)(2,1)S(1)}, u32[]{:S(2)}, u32[]{:S(2)}) collective-permute-start(bf16[128,3072]{1,0:T(8,128)(2,1)S(1)} %add_bitcast_fusion), channel_id=1, source_target_pairs={{0,8},{8,16},{16,24},{1,9},{9,17},{17,25},{2,10},{10,18},{18,26},{... | collective-permute-start | bytes 2359304 | tf_op jit(solution)/shard_map/ppermute | solution.py:29
  32.3 16.9 %collective-permute-start.4 = (bf16[128,2176]{1,0:T(8,128)(2,1)S(1)}, bf16[128,2176]{1,0:T(8,128)(2,1)S(1)}, u32[]{:S(2)}, u32[]{:S(2)}) collective-permute-start(bf16[128,2176]{1,0:T(8,128)(2,1)S(1)} %collective-permute-done.1.refs_1_), channel_id=1, source_target_pairs={{0,2},{1,3},{2,4},{3,5},{4,6},{5,7},{8,10},{9,11},{10,12},{11,13},... | collective-permute-start | bytes 1671176 | tf_op jit(solution)/shard_map/ppermute | solution.py:29
  35.5 26.8 %collective-permute-start.8 = (bf16[128,2560]{1,0:T(8,128)(2,1)}, bf16[128,2560]{1,0:T(8,128)(2,1)}, u32[]{:S(2)}, u32[]{:S(2)}) collective-permute-start(bf16[128,2560]{1,0:T(8,128)(2,1)} %get-tuple-element.27), channel_id=1, source_target_pairs={{0,8},{8,16},{16,24},{1,9},{9,17},{17,25},{2,10},{10,18},{18,26},{... | collective-permute-start | bytes 1966088 | tf_op jit(solution)/shard_map/ppermute | solution.py:29
  37.7 14.3 %collective-permute-start.7 = (bf16[128,2176]{1,0:T(8,128)(2,1)S(1)}, bf16[128,2176]{1,0:T(8,128)(2,1)S(1)}, u32[]{:S(2)}, u32[]{:S(2)}) collective-permute-start(bf16[128,2176]{1,0:T(8,128)(2,1)S(1)} %get-tuple-element.19.refs_0_), channel_id=1, source_target_pairs={{0,1},{2,3},{4,5},{6,7},{8,9},{10,11},{12,13},{14,15},{16,17},{18,... | collective-permute-start | bytes 1671176 | tf_op jit(solution)/shard_map/ppermute | solution.py:34
  39.0 13.0 %collective-permute-start.3 = (bf16[128,2176]{1,0:T(8,128)(2,1)S(1)}, bf16[128,2176]{1,0:T(8,128)(2,1)S(1)}, u32[]{:S(2)}, u32[]{:S(2)}) collective-permute-start(bf16[128,2176]{1,0:T(8,128)(2,1)S(1)} %collective-permute-done.1.refs_1_), channel_id=1, source_target_pairs={{0,1},{1,0},{2,3},{3,2},{4,5},{5,4},{6,7},{7,6},{8,9},{9,8},{10,11... | collective-permute-start | bytes 1671176 | tf_op jit(solution)/shard_map/ppermute | solution.py:34
  49.2 4.3 %collective-permute-start.6 = (bf16[128,2176]{1,0:T(8,128)(2,1)S(1)}, bf16[128,2176]{1,0:T(8,128)(2,1)S(1)}, u32[]{:S(2)}, u32[]{:S(2)}) collective-permute-start(bf16[128,2176]{1,0:T(8,128)(2,1)S(1)} %collective-permute-done.4.refs_3_), channel_id=1, source_target_pairs={{0,1},{1,0},{2,3},{3,2},{4,5},{5,4},{6,7},{7,6},{8,9},{9,8},{10,11... | collective-permute-start | bytes 1671176 | tf_op jit(solution)/shard_map/ppermute | solution.py:34

commit v20 on v19

--- a/solution.py
+++ b/solution.py
@@ -16,7 +16,7 @@
 NOTE = 2 * KV_WIDTH
 MASKED = -1e30
 HALF = GROUP // 2
-CHUNKS = (20, 24, 20)
+CHUNKS = (20, 26, 18)
 VMEM_GRANT = 48 * 1024 * 1024
 
 WHOLE = pl.BlockSpec(memory_space=pltpu.VMEM)
@@ -203,7 +203,7 @@
         rest[:, values] = mate_ref[:, values]
 
 
-def attend_heads(first, steps, kv_refs, bias, take, result):
+def attend_heads(first, steps, kv_refs, bias, take, result, after_first, before_last):
     quota = bias.shape[0]
     unit = math.log2(math.e) / math.sqrt(HEAD_SIZE)
 
@@ -235,12 +235,15 @@
 
     keys, values = key_head(steps[0][0] // GROUP)
     scores = scored(*steps[0], keys)
+    after_first()
     for i, (head, heads) in enumerate(steps):
         own_values, later = values, None
         if i + 1 < len(steps):
             if steps[i + 1][0] // GROUP != head // GROUP:
                 keys, values = key_head(steps[i + 1][0] // GROUP)
             later = scored(*steps[i + 1], keys)
+        if i + 1 == len(steps):
+            before_last()
         finished(head, heads, scores, own_values)
         scores = later
 
@@ -248,19 +251,41 @@
 def early_kernel(blocks, count, rank_ref, *refs):
     kv_refs, far_ref, mate_ref = refs[: blocks - 1], refs[blocks - 1], refs[blocks]
     q_hbm, in_hbm, out_hbm, local, bias, rest, queries, result, sems = refs[blocks + 1 :]
-    own, others = head_columns(0, count), head_columns(count, QUERY_HEADS - count)
-    fetch = pltpu.make_async_copy(in_hbm.at[0, :, own], queries, sems.at[0])
+    steps = pieces(0, count)
+    edge, end = steps[0][1], steps[-1][0]
+
+    def fetching(cols, sem):
+        return pltpu.make_async_copy(in_hbm.at[0, :, cols], queries.at[:, cols], sem)
+
+    def storing(cols, sem):
+        return pltpu.make_async_copy(result.at[:, cols], out_hbm.at[0, :, cols], sem)
+
+    fetch = fetching(head_columns(0, edge), sems.at[0])
+    fetch_rest = fetching(head_columns(edge, count - edge), sems.at[1])
+    store = storing(head_columns(0, end), sems.at[2])
+    store_last = storing(head_columns(end, count - end), sems.at[3])
+    others = head_columns(count, QUERY_HEADS - count)
+    ahead = pltpu.make_async_copy(q_hbm.at[0, 0 : bias.shape[0], others], local, sems.at[4])
     fetch.start()
+    fetch_rest.start()
     rank = rank_ref[0]
     make_bias(kv_refs, far_ref, mate_ref, bias, rank)
     choose_rest(0, count, lax.rem(rank, 2), far_ref, mate_ref, rest)
     fetch.wait()
-    attend_heads(0, pieces(0, count), [*kv_refs, rest], bias, lambda cols: queries[:, cols], result)
-    store = pltpu.make_async_copy(result, out_hbm.at[0, :, own], sems.at[1])
-    store.start()
-    ahead = pltpu.make_async_copy(q_hbm.at[0, 0 : bias.shape[0], others], local, sems.at[2])
+    attend_heads(
+        0,
+        steps,
+        [*kv_refs, rest],
+        bias,
+        lambda cols: queries[:, cols],
+        result,
+        fetch_rest.wait,
+        store.start,
+    )
+    store_last.start()
     ahead.start()
     store.wait()
+    store_last.wait()
     ahead.wait()
 
 
@@ -269,8 +294,24 @@
     hot_ref, arrived_hbm, local_ref, _, out_hbm = refs[blocks + 1 : blocks + 6]
     bias, rest, arrived, result, sems = refs[blocks + 6 :]
     count = QUERY_HEADS - first
-    fetch = pltpu.make_async_copy(arrived_hbm, arrived, sems.at[0])
+    steps = pieces(first, count)[::-1]
+    edge, end = steps[0][0], sum(steps[-1])
+
+    def fetching(cols, sem):
+        return pltpu.make_async_copy(arrived_hbm.at[:, cols], arrived.at[:, cols], sem)
+
+    def storing(at, heads, sem):
+        own = head_columns(at - first, heads)
+        return pltpu.make_async_copy(
+            result.at[:, own], out_hbm.at[0, :, head_columns(at, heads)], sem
+        )
+
+    fetch = fetching(head_columns(edge - first, QUERY_HEADS - edge), sems.at[0])
+    fetch_rest = fetching(head_columns(0, edge - first), sems.at[1])
+    store = storing(end, QUERY_HEADS - end, sems.at[2])
+    store_last = storing(first, end - first, sems.at[3])
     fetch.start()
+    fetch_rest.start()
     rank = rank_ref[0]
     make_bias(kv_refs, far_ref, mate_ref, bias, rank)
     choose_rest(first, count, lax.rem(rank, 2), far_ref, mate_ref, rest)
@@ -279,16 +320,12 @@
     def take(cols):
         return place_rows(hot_ref[...], arrived[:, cols], local_ref[:, cols])
 
-    steps = sorted(pieces(first, count), key=lambda piece: -piece[1])
-    head, heads = steps.pop()
-    if heads == HALF:
-        steps += [(head, heads // 2), (head + heads // 2, heads // 2)]
-    else:
-        steps.append((head, heads))
-    attend_heads(first, steps, [*kv_refs, rest], bias, take, result)
-    store = pltpu.make_async_copy(result, out_hbm.at[0, :, head_columns(first, count)], sems.at[1])
-    store.start()
+    attend_heads(
+        first, steps, [*kv_refs, rest], bias, take, result, fetch_rest.wait, store.start
+    )
+    store_last.start()
     store.wait()
+    store_last.wait()
 
 
 def attend(rank, hot, arrived, q_rows, kv_blocks, out):
@@ -306,7 +343,7 @@
         more_out=[jax.ShapeDtypeStruct(arrived.shape, jnp.bfloat16)],
         more_specs=[WHOLE],
         in_specs=[SCALARS] + [WHOLE] * len(kv_blocks) + [ANYWHERE],
-        scratch_shapes=[bias, rest, others, others, pltpu.SemaphoreType.DMA((3,))],
+        scratch_shapes=[bias, rest, others, others, pltpu.SemaphoreType.DMA((5,))],
         name="attend_early",
     )
     return in_place(
@@ -314,7 +351,7 @@
         [rank, *kv_blocks, hot, arrived, local],
         out,
         in_specs=[SCALARS] + [WHOLE] * (len(kv_blocks) + 1) + [ANYWHERE, WHOLE],
-        scratch_shapes=[bias, rest, own, own, pltpu.SemaphoreType.DMA((2,))],
+        scratch_shapes=[bias, rest, own, own, pltpu.SemaphoreType.DMA((4,))],
         name="attend_late",
     )[0]
 

time: 68.5 us -> 68.8 us (level)
  waiting for transfers between devices: 19.2 us -> 20.7 us
    ppermute x6, waiting for transfers between devices: 17.6 us -> 19.1 us  [shifted(): return lax.ppermute(x, axis, [(i, i + steps) for i in range(n - steps)])]
where the time goes in v20:
time: 68.8 us; the launch traced here: 68.4 us
  starting transfers between devices  23.4 us (34%)
  waiting for transfers between devices  20.7 us (30%)
  Pallas kernels  16.9 us (25%)
  other arithmetic  3.06 us (4%)
  local copies, waits for them, and re-layouts  2.32 us (3%)
  between operations  2.04 us (3%)
    ppermute x6, waiting for transfers between devices, shifted(): return lax.ppermute(x, axis, [(i, i + steps) for i in range(n - steps)])  19.1 us
    ppermute x6, starting transfers between devices, shifted(): return lax.ppermute(x, axis, [(i, i + steps) for i in range(n - steps)])  16 us
    pallas_call x3, Pallas kernels, in_place(): pl.pallas_call(kernel, in_specs=specs, out_specs=[ANYWHERE, *more_specs],...  14.8 us
    ppermute x3, starting transfers between devices, across_cores(): lax.ppermute(x, 'ctx', [(i, i ^ 1) for i in range(n) if i % 2 in sources])  7.4 us
    ppermute x3, waiting for transfers between devices, across_cores(): lax.ppermute(x, 'ctx', [(i, i ^ 1) for i in range(n) if i % 2 in sources])  1.58 us
  transfers between devices with their start and end apart: 9, of which 4 were waited for; matrix products, arithmetic and copies ran while one was open for 6% of the time, Pallas kernels for 18%

profile of v20, /device:TPU:21, one launch (start us, length us, event | category | flops | bytes accessed | tf_op | source)
XLA Modules:
  0.0 68.4 jit_solution(1380518974518051972)
XLA Ops:
  0.0 0.0 copy-start
  0.0 0.0 copy-start.1
  0.0 1.2 %slice_bitcast_fusion = (bf16[128,1024]{1,0:T(8,128)(2,1)S(1)}, bf16[128,1024]{1,0:T(8,128)(2,1)S(1)}) fusion(bf16[1,256,1024]{2,1,0:T(8,128)(2,1)} %param.7, bf16[1,256,1024]{2,1,0:T(8,128)(2,1)} %param.6), kind=kLoop, calls=%fused_computation.7 | loop fusion | bytes 1048576 | tf_op jit(solution)/shard_map/slice | solution.py:367
  1.3 3.3 %collective-permute-start = (bf16[128,2048]{1,0:T(8,128)(2,1)S(1)}, bf16[128,2048]{1,0:T(8,128)(2,1)S(1)}, u32[]{:S(2)}, u32[]{:S(2)}) collective-permute-start(bf16[128,2048]{1,0:T(8,128)(2,1)S(1)} %pad_maximum_fusion), channel_id=1, source_target_pairs={{0,8},{8,16},{16,24},{1,9},{9,17},{17,25},{2,10},{10,18},{18,26},{... | collective-permute-start | bytes 1572872 | tf_op jit(solution)/shard_map/ppermute | solution.py:29
  4.5 0.5 slice.55
  5.0 0.6 slice.56
  6.9 1.0 %add_bitcast_fusion.3 = bf16[128,1024]{1,0:T(8,128)(2,1)S(1)} fusion(bf16[1,256,1024]{2,1,0:T(8,128)(2,1)} %param.7, bf16[]{:T(256)} %bitcast.4), kind=kLoop, calls=%fused_computation.5 | loop fusion | flops 131072 | bytes 524290 | tf_op jit(solution)/shard_map/add | solution.py:381
  7.8 1.0 %add_bitcast_fusion.4 = bf16[128,1024]{1,0:T(8,128)(2,1)S(1)} fusion(bf16[1,256,1024]{2,1,0:T(8,128)(2,1)} %param.6, bf16[]{:T(256)} %bitcast.4), kind=kLoop, calls=%fused_computation.6 | loop fusion | flops 131072 | bytes 524290 | tf_op jit(solution)/shard_map/add | solution.py:381
  8.8 0.0 copy-done
  8.9 0.9 %add_bitcast_fusion.2 = bf16[128,2304]{1,0:T(8,128)(2,1)} fusion(bf16[1,256,8192]{2,1,0:T(8,128)(2,1)S(1)} %copy-done, bf16[]{:T(256)} %bitcast.7), kind=kLoop, calls=%fused_computation.2 | loop fusion | flops 294912 | bytes 1179650 | tf_op jit(solution)/shard_map/add | solution.py:386
  9.7 0.1 add_bitcast_fusion
  9.8 1.9 %collective-permute-start.2 = (bf16[128,2560]{1,0:T(8,128)(2,1)S(1)}, bf16[128,2560]{1,0:T(8,128)(2,1)S(1)}, u32[]{:S(2)}, u32[]{:S(2)}) collective-permute-start(bf16[128,2560]{1,0:T(8,128)(2,1)S(1)} %add_bitcast_fusion.1), channel_id=1, source_target_pairs={{0,8},{8,16},{16,24},{1,9},{9,17},{17,25},{2,10},{10,18},{18,26},{... | collective-permute-start | bytes 1966088 | tf_op jit(solution)/shard_map/ppermute | solution.py:29
  12.4 0.1 pad_add_fusion.shift_ref
  12.5 4.5 %collective-permute-done.arrived_ref = bf16[128,2048]{1,0:T(8,128)(2,1)S(1)} collective-permute-done((bf16[128,2048]{1,0:T(8,128)(2,1)S(1)}, bf16[128,2048]{1,0:T(8,128)(2,1)S(1)}, u32[]{:S(2)}, u32[]{:S(2)}) %collective-permute-start) | collective-permute-done | bytes 524320 | tf_op jit(solution)/shard_map/ppermute | solution.py:29
  17.0 0.0 copy-done.1
  17.0 0.8 %settle_kv.1 = (bf16[128,2176]{1,0:T(8,128)(2,1)S(1)}, bf16[128,256]{1,0:T(8,128)(2,1)S(1)}) custom-call(s32[2]{0:T(128)S(1)} %pad_add_fusion.shift_ref, s32[1,128]{1,0:T(1,128)S(1)} %copy-done.1, bf16[128,2048]{1,0:T(8,128)(2,1)S(1)} %collective-permute-done.arrived_ref, bf16[128,2048]{1,0:T(8,128)(2,1)S(1)} %pad_maximum_fusion.1.local_ref), custom_call_target="tpu_custom_call" | custom-call | tf_op jit(solution)/shard_map/settle_kv/pallas_call | solution.py:78
  17.8 3.2 %collective-permute-start.1 = (bf16[128,2176]{1,0:T(8,128)(2,1)S(1)}, bf16[128,2176]{1,0:T(8,128)(2,1)S(1)}, u32[]{:S(2)}, u32[]{:S(2)}) collective-permute-start(bf16[128,2176]{1,0:T(8,128)(2,1)S(1)} %get-tuple-element.19.refs_0_), channel_id=1, source_target_pairs={{0,2},{1,3},{2,4},{3,5},{4,6},{5,7},{8,10},{9,11},{10,12},{11,13},... | collective-permute-start | bytes 1671176 | tf_op jit(solution)/shard_map/ppermute | solution.py:29
  21.1 2.2 %collective-permute-start.5 = (bf16[128,3328]{1,0:T(8,128)(2,1)S(1)}, bf16[128,3328]{1,0:T(8,128)(2,1)S(1)}, u32[]{:S(2)}, u32[]{:S(2)}) collective-permute-start(bf16[128,3328]{1,0:T(8,128)(2,1)S(1)} %add_bitcast_fusion), channel_id=1, source_target_pairs={{0,8},{8,16},{16,24},{1,9},{9,17},{17,25},{2,10},{10,18},{18,26},{... | collective-permute-start | bytes 2555912 | tf_op jit(solution)/shard_map/ppermute | solution.py:29
  23.3 7.7 %collective-permute-done.2.arrived_ref = bf16[128,2560]{1,0:T(8,128)(2,1)S(1)} collective-permute-done((bf16[128,2560]{1,0:T(8,128)(2,1)S(1)}, bf16[128,2560]{1,0:T(8,128)(2,1)S(1)}, u32[]{:S(2)}, u32[]{:S(2)}) %collective-permute-start.2) | collective-permute-done | bytes 655392 | tf_op jit(solution)/shard_map/ppermute | solution.py:29
  31.0 1.3 %place_queries.2.refs_0_ = bf16[1,128,8192]{2,1,0:T(8,128)(2,1)} custom-call(bf16[128,256]{1,0:T(8,128)(2,1)S(1)} %get-tuple-element.20.hot_ref.refs_6_, bf16[128,2560]{1,0:T(8,128)(2,1)S(1)} %collective-permute-done.2.arrived_ref, bf16[1,256,8192]{2,1,0:T(8,128)(2,1)S(1)} %copy-done), custom_call_target="tpu_custom_call" | custom-call | tf_op jit(solution)/shard_map/place_queries/pallas_call | solution.py:161
  32.3 0.0 collective-permute-done.1.refs_1_
  32.3 3.2 %collective-permute-start.4 = (bf16[128,2176]{1,0:T(8,128)(2,1)S(1)}, bf16[128,2176]{1,0:T(8,128)(2,1)S(1)}, u32[]{:S(2)}, u32[]{:S(2)}) collective-permute-start(bf16[128,2176]{1,0:T(8,128)(2,1)S(1)} %collective-permute-done.1.refs_1_), channel_id=1, source_target_pairs={{0,2},{1,3},{2,4},{3,5},{4,6},{5,7},{8,10},{9,11},{10,12},{11,13},... | collective-permute-start | bytes 1671176 | tf_op jit(solution)/shard_map/ppermute | solution.py:29
  35.5 2.2 %collective-permute-start.8 = (bf16[128,2304]{1,0:T(8,128)(2,1)}, bf16[128,2304]{1,0:T(8,128)(2,1)}, u32[]{:S(2)}, u32[]{:S(2)}) collective-permute-start(bf16[128,2304]{1,0:T(8,128)(2,1)} %add_bitcast_fusion.2), channel_id=1, source_target_pairs={{0,8},{8,16},{16,24},{1,9},{9,17},{17,25},{2,10},{10,18},{18,26},{... | collective-permute-start | bytes 1769480 | tf_op jit(solution)/shard_map/ppermute | solution.py:29
  37.7 1.3 %collective-permute-start.7 = (bf16[128,2176]{1,0:T(8,128)(2,1)S(1)}, bf16[128,2176]{1,0:T(8,128)(2,1)S(1)}, u32[]{:S(2)}, u32[]{:S(2)}) collective-permute-start(bf16[128,2176]{1,0:T(8,128)(2,1)S(1)} %get-tuple-element.19.refs_0_), channel_id=1, source_target_pairs={{0,1},{2,3},{4,5},{6,7},{8,9},{10,11},{12,13},{14,15},{16,17},{18,... | collective-permute-start | bytes 1671176 | tf_op jit(solution)/shard_map/ppermute | solution.py:34
  39.0 3.4 %collective-permute-start.3 = (bf16[128,2176]{1,0:T(8,128)(2,1)S(1)}, bf16[128,2176]{1,0:T(8,128)(2,1)S(1)}, u32[]{:S(2)}, u32[]{:S(2)}) collective-permute-start(bf16[128,2176]{1,0:T(8,128)(2,1)S(1)} %collective-permute-done.1.refs_1_), channel_id=1, source_target_pairs={{0,1},{1,0},{2,3},{3,2},{4,5},{5,4},{6,7},{7,6},{8,9},{9,8},{10,11... | collective-permute-start | bytes 1671176 | tf_op jit(solution)/shard_map/ppermute | solution.py:34
  42.4 6.9 %collective-permute-done.5.arrived_ref = bf16[128,3328]{1,0:T(8,128)(2,1)S(1)} collective-permute-done((bf16[128,3328]{1,0:T(8,128)(2,1)S(1)}, bf16[128,3328]{1,0:T(8,128)(2,1)S(1)}, u32[]{:S(2)}, u32[]{:S(2)}) %collective-permute-start.5) | collective-permute-done | bytes 852000 | tf_op jit(solution)/shard_map/ppermute | solution.py:29
  49.3 1.4 %place_queries.3.refs_7_ = bf16[1,128,8192]{2,1,0:T(8,128)(2,1)} custom-call(bf16[128,256]{1,0:T(8,128)(2,1)S(1)} %get-tuple-element.20.hot_ref.refs_6_, bf16[128,3328]{1,0:T(8,128)(2,1)S(1)} %collective-permute-done.5.arrived_ref, bf16[1,256,8192]{2,1,0:T(8,128)(2,1)S(1)} %copy-done, ...), custom_call_target="tpu_custom_call", output_to_operand_aliasing={{}: (3, {})} | custom-call | tf_op jit(solution)/shard_map/place_queries/pallas_call | solution.py:119
  50.7 0.0 collective-permute-done.4.refs_3_
  50.7 2.8 %collective-permute-start.6 = (bf16[128,2176]{1,0:T(8,128)(2,1)S(1)}, bf16[128,2176]{1,0:T(8,128)(2,1)S(1)}, u32[]{:S(2)}, u32[]{:S(2)}) collective-permute-start(bf16[128,2176]{1,0:T(8,128)(2,1)S(1)} %collective-permute-done.4.refs_3_), channel_id=1, source_target_pairs={{0,1},{1,0},{2,3},{3,2},{4,5},{5,4},{6,7},{7,6},{8,9},{9,8},{10,11... | collective-permute-start | bytes 1671176 | tf_op jit(solution)/shard_map/ppermute | solution.py:34
  53.5 0.0 collective-permute-done.7.refs_5_
  53.5 0.0 collective-permute-done.3.refs_2_
  53.5 1.6 %collective-permute-done.6.refs_4_ = bf16[128,2176]{1,0:T(8,128)(2,1)S(1)} collective-permute-done((bf16[128,2176]{1,0:T(8,128)(2,1)S(1)}, bf16[128,2176]{1,0:T(8,128)(2,1)S(1)}, u32[]{:S(2)}, u32[]{:S(2)}) %collective-permute-start.6) | collective-permute-done | bytes 557088 | tf_op jit(solution)/shard_map/ppermute | solution.py:34
  55.0 8.6 %attend_early.1 = (bf16[1,128,8192]{2,1,0:T(8,128)(2,1)}, bf16[128,2304]{1,0:T(8,128)(2,1)S(1)}) custom-call(s32[1]{0:T(128)} %bitcast.rank_ref, bf16[128,2176]{1,0:T(8,128)(2,1)S(1)} %get-tuple-element.19.refs_0_, bf16[128,2176]{1,0:T(8,128)(2,1)S(1)} %collective-permute-done.1.refs_1_, ...), custom_call_target="tpu_custom_call", output_to_operand_aliasing={{0}: (8, {})} | custom-call | tf_op jit(solution)/shard_map/attend_early/pallas_call | solution.py:119
  63.6 0.0 collective-permute-done.8.refs_7_
  63.6 4.8 %attend_late.1 = bf16[1,128,8192]{2,1,0:T(8,128)(2,1)} custom-call(s32[1]{0:T(128)} %bitcast.rank_ref, bf16[128,2176]{1,0:T(8,128)(2,1)S(1)} %get-tuple-element.19.refs_0_, bf16[128,2176]{1,0:T(8,128)(2,1)S(1)} %collective-permute-done.1.refs_1_, bf16[128,2176]{1,0:T(8,128)(2,1)S(1)} %collective-permute-done.3.refs_2_, ...), custom_call_target="tpu_custom_call", output_to_operand_aliasing={{}: (10, {})} | custom-call | tf_op jit(solution)/shard_map/attend_late/pallas_call | solution.py:119
  (3 shorter events, 0.1 us)
Async XLA Ops:
  0.0 8.8 %copy-start = (bf16[1,256,8192]{2,1,0:T(8,128)(2,1)S(1)}, bf16[1,256,8192]{2,1,0:T(8,128)(2,1)}, u32[]{:S(2)}) copy-start(bf16[1,256,8192]{2,1,0:T(8,128)(2,1)} %refs_6_.1) | copy-start | bytes 12582916
  0.0 17.0 %copy-start.1 = (s32[1,128]{1,0:T(1,128)S(1)}, s32[1,128]{1,0:T(1,128)}, u32[]{:S(2)}) copy-start(s32[1,128]{1,0:T(1,128)} %docs_ref.1) | copy-start | bytes 1540
  1.3 15.7 %collective-permute-start = (bf16[128,2048]{1,0:T(8,128)(2,1)S(1)}, bf16[128,2048]{1,0:T(8,128)(2,1)S(1)}, u32[]{:S(2)}, u32[]{:S(2)}) collective-permute-start(bf16[128,2048]{1,0:T(8,128)(2,1)S(1)} %pad_maximum_fusion), channel_id=1, source_target_pairs={{0,8},{8,16},{16,24},{1,9},{9,17},{17,25},{2,10},{10,18},{18,26},{... | collective-permute-start | bytes 1572872 | tf_op jit(solution)/shard_map/ppermute | solution.py:29
  9.8 21.2 %collective-permute-start.2 = (bf16[128,2560]{1,0:T(8,128)(2,1)S(1)}, bf16[128,2560]{1,0:T(8,128)(2,1)S(1)}, u32[]{:S(2)}, u32[]{:S(2)}) collective-permute-start(bf16[128,2560]{1,0:T(8,128)(2,1)S(1)} %add_bitcast_fusion.1), channel_id=1, source_target_pairs={{0,8},{8,16},{16,24},{1,9},{9,17},{17,25},{2,10},{10,18},{18,26},{... | collective-permute-start | bytes 1966088 | tf_op jit(solution)/shard_map/ppermute | solution.py:29
  17.8 14.5 %collective-permute-start.1 = (bf16[128,2176]{1,0:T(8,128)(2,1)S(1)}, bf16[128,2176]{1,0:T(8,128)(2,1)S(1)}, u32[]{:S(2)}, u32[]{:S(2)}) collective-permute-start(bf16[128,2176]{1,0:T(8,128)(2,1)S(1)} %get-tuple-element.19.refs_0_), channel_id=1, source_target_pairs={{0,2},{1,3},{2,4},{3,5},{4,6},{5,7},{8,10},{9,11},{10,12},{11,13},... | collective-permute-start | bytes 1671176 | tf_op jit(solution)/shard_map/ppermute | solution.py:29
  21.1 28.2 %collective-permute-start.5 = (bf16[128,3328]{1,0:T(8,128)(2,1)S(1)}, bf16[128,3328]{1,0:T(8,128)(2,1)S(1)}, u32[]{:S(2)}, u32[]{:S(2)}) collective-permute-start(bf16[128,3328]{1,0:T(8,128)(2,1)S(1)} %add_bitcast_fusion), channel_id=1, source_target_pairs={{0,8},{8,16},{16,24},{1,9},{9,17},{17,25},{2,10},{10,18},{18,26},{... | collective-permute-start | bytes 2555912 | tf_op jit(solution)/shard_map/ppermute | solution.py:29
  32.3 18.4 %collective-permute-start.4 = (bf16[128,2176]{1,0:T(8,128)(2,1)S(1)}, bf16[128,2176]{1,0:T(8,128)(2,1)S(1)}, u32[]{:S(2)}, u32[]{:S(2)}) collective-permute-start(bf16[128,2176]{1,0:T(8,128)(2,1)S(1)} %collective-permute-done.1.refs_1_), channel_id=1, source_target_pairs={{0,2},{1,3},{2,4},{3,5},{4,6},{5,7},{8,10},{9,11},{10,12},{11,13},... | collective-permute-start | bytes 1671176 | tf_op jit(solution)/shard_map/ppermute | solution.py:29
  35.5 28.1 %collective-permute-start.8 = (bf16[128,2304]{1,0:T(8,128)(2,1)}, bf16[128,2304]{1,0:T(8,128)(2,1)}, u32[]{:S(2)}, u32[]{:S(2)}) collective-permute-start(bf16[128,2304]{1,0:T(8,128)(2,1)} %add_bitcast_fusion.2), channel_id=1, source_target_pairs={{0,8},{8,16},{16,24},{1,9},{9,17},{17,25},{2,10},{10,18},{18,26},{... | collective-permute-start | bytes 1769480 | tf_op jit(solution)/shard_map/ppermute | solution.py:29
  37.7 15.7 %collective-permute-start.7 = (bf16[128,2176]{1,0:T(8,128)(2,1)S(1)}, bf16[128,2176]{1,0:T(8,128)(2,1)S(1)}, u32[]{:S(2)}, u32[]{:S(2)}) collective-permute-start(bf16[128,2176]{1,0:T(8,128)(2,1)S(1)} %get-tuple-element.19.refs_0_), channel_id=1, source_target_pairs={{0,1},{2,3},{4,5},{6,7},{8,9},{10,11},{12,13},{14,15},{16,17},{18,... | collective-permute-start | bytes 1671176 | tf_op jit(solution)/shard_map/ppermute | solution.py:34
  39.0 14.4 %collective-permute-start.3 = (bf16[128,2176]{1,0:T(8,128)(2,1)S(1)}, bf16[128,2176]{1,0:T(8,128)(2,1)S(1)}, u32[]{:S(2)}, u32[]{:S(2)}) collective-permute-start(bf16[128,2176]{1,0:T(8,128)(2,1)S(1)} %collective-permute-done.1.refs_1_), channel_id=1, source_target_pairs={{0,1},{1,0},{2,3},{3,2},{4,5},{5,4},{6,7},{7,6},{8,9},{9,8},{10,11... | collective-permute-start | bytes 1671176 | tf_op jit(solution)/shard_map/ppermute | solution.py:34
  50.7 4.3 %collective-permute-start.6 = (bf16[128,2176]{1,0:T(8,128)(2,1)S(1)}, bf16[128,2176]{1,0:T(8,128)(2,1)S(1)}, u32[]{:S(2)}, u32[]{:S(2)}) collective-permute-start(bf16[128,2176]{1,0:T(8,128)(2,1)S(1)} %collective-permute-done.4.refs_3_), channel_id=1, source_target_pairs={{0,1},{1,0},{2,3},{3,2},{4,5},{5,4},{6,7},{7,6},{8,9},{9,8},{10,11... | collective-permute-start | bytes 1671176 | tf_op jit(solution)/shard_map/ppermute | solution.py:34

commit v21 on v20

--- a/solution.py
+++ b/solution.py
@@ -16,7 +16,7 @@
 NOTE = 2 * KV_WIDTH
 MASKED = -1e30
 HALF = GROUP // 2
-CHUNKS = (20, 26, 18)
+CHUNKS = (20, 25, 19)
 VMEM_GRANT = 48 * 1024 * 1024
 
 WHOLE = pl.BlockSpec(memory_space=pltpu.VMEM)
@@ -272,6 +272,11 @@
     make_bias(kv_refs, far_ref, mate_ref, bias, rank)
     choose_rest(0, count, lax.rem(rank, 2), far_ref, mate_ref, rest)
     fetch.wait()
+
+    def after_first():
+        fetch_rest.wait()
+        ahead.start()
+
     attend_heads(
         0,
         steps,
@@ -279,11 +284,10 @@
         bias,
         lambda cols: queries[:, cols],
         result,
-        fetch_rest.wait,
+        after_first,
         store.start,
     )
     store_last.start()
-    ahead.start()
     store.wait()
     store_last.wait()
     ahead.wait()

time: 68.8 us -> 68.3 us (level); the launches traced: 68.4 us -> 67.2 us
  waiting for transfers between devices: 20.7 us -> 20 us
    ppermute x6, waiting for transfers between devices: 19.1 us -> 18.4 us  [shifted(): return lax.ppermute(x, axis, [(i, i + steps) for i in range(n - steps)])]
  transfers between devices with their start and end apart: 9 -> 9, of which waited for: 4 -> 4; matrix products, arithmetic and copies ran while one was open for 6% -> 6% of each run, Pallas kernels for 18% -> 17%
where the time goes in v21:
time: 68.3 us; the launch traced here: 67.2 us
  starting transfers between devices  23.4 us (34%)
  waiting for transfers between devices  20 us (29%)
  Pallas kernels  16.3 us (24%)
  other arithmetic  3.11 us (5%)
  local copies, waits for them, and re-layouts  2.32 us (3%)
  between operations  2.04 us (3%)
    ppermute x6, waiting for transfers between devices, shifted(): return lax.ppermute(x, axis, [(i, i + steps) for i in range(n - steps)])  18.4 us
    ppermute x6, starting transfers between devices, shifted(): return lax.ppermute(x, axis, [(i, i + steps) for i in range(n - steps)])  16 us
    pallas_call x3, Pallas kernels, in_place(): pl.pallas_call(kernel, in_specs=specs, out_specs=[ANYWHERE, *more_specs],...  14.2 us
    ppermute x3, starting transfers between devices, across_cores(): lax.ppermute(x, 'ctx', [(i, i ^ 1) for i in range(n) if i % 2 in sources])  7.4 us
    ppermute x3, waiting for transfers between devices, across_cores(): lax.ppermute(x, 'ctx', [(i, i ^ 1) for i in range(n) if i % 2 in sources])  1.58 us
  transfers between devices with their start and end apart: 9, of which 4 were waited for; matrix products, arithmetic and copies ran while one was open for 6% of the time, Pallas kernels for 17%

profile of v21, /device:TPU:21, one launch (start us, length us, event | category | flops | bytes accessed | tf_op | source)
XLA Modules:
  0.0 67.2 jit_solution(17731162386394872693)
XLA Ops:
  0.0 0.0 copy-start
  0.0 0.0 copy-start.1
  0.0 1.2 %slice_bitcast_fusion = (bf16[128,1024]{1,0:T(8,128)(2,1)S(1)}, bf16[128,1024]{1,0:T(8,128)(2,1)S(1)}) fusion(bf16[1,256,1024]{2,1,0:T(8,128)(2,1)} %param.7, bf16[1,256,1024]{2,1,0:T(8,128)(2,1)} %param.6), kind=kLoop, calls=%fused_computation.7 | loop fusion | bytes 1048576 | tf_op jit(solution)/shard_map/slice | solution.py:371
  1.3 3.3 %collective-permute-start = (bf16[128,2048]{1,0:T(8,128)(2,1)S(1)}, bf16[128,2048]{1,0:T(8,128)(2,1)S(1)}, u32[]{:S(2)}, u32[]{:S(2)}) collective-permute-start(bf16[128,2048]{1,0:T(8,128)(2,1)S(1)} %pad_maximum_fusion), channel_id=1, source_target_pairs={{0,8},{8,16},{16,24},{1,9},{9,17},{17,25},{2,10},{10,18},{18,26},{... | collective-permute-start | bytes 1572872 | tf_op jit(solution)/shard_map/ppermute | solution.py:29
  4.5 0.5 slice.55
  5.0 0.6 slice.56
  6.9 1.0 %add_bitcast_fusion.3 = bf16[128,1024]{1,0:T(8,128)(2,1)S(1)} fusion(bf16[1,256,1024]{2,1,0:T(8,128)(2,1)} %param.7, bf16[]{:T(256)} %bitcast.4), kind=kLoop, calls=%fused_computation.5 | loop fusion | flops 131072 | bytes 524290 | tf_op jit(solution)/shard_map/add | solution.py:385
  7.8 1.0 %add_bitcast_fusion.4 = bf16[128,1024]{1,0:T(8,128)(2,1)S(1)} fusion(bf16[1,256,1024]{2,1,0:T(8,128)(2,1)} %param.6, bf16[]{:T(256)} %bitcast.4), kind=kLoop, calls=%fused_computation.6 | loop fusion | flops 131072 | bytes 524290 | tf_op jit(solution)/shard_map/add | solution.py:385
  8.8 0.0 copy-done
  8.9 0.9 %add_bitcast_fusion.2 = bf16[128,2432]{1,0:T(8,128)(2,1)} fusion(bf16[1,256,8192]{2,1,0:T(8,128)(2,1)S(1)} %copy-done, bf16[]{:T(256)} %bitcast.7), kind=kLoop, calls=%fused_computation.2 | loop fusion | flops 311296 | bytes 1245186 | tf_op jit(solution)/shard_map/add | solution.py:390
  9.8 0.1 add_bitcast_fusion
  9.9 1.9 %collective-permute-start.2 = (bf16[128,2560]{1,0:T(8,128)(2,1)S(1)}, bf16[128,2560]{1,0:T(8,128)(2,1)S(1)}, u32[]{:S(2)}, u32[]{:S(2)}) collective-permute-start(bf16[128,2560]{1,0:T(8,128)(2,1)S(1)} %add_bitcast_fusion.1), channel_id=1, source_target_pairs={{0,8},{8,16},{16,24},{1,9},{9,17},{17,25},{2,10},{10,18},{18,26},{... | collective-permute-start | bytes 1966088 | tf_op jit(solution)/shard_map/ppermute | solution.py:29
  12.5 0.1 pad_add_fusion.shift_ref
  12.5 4.4 %collective-permute-done.arrived_ref = bf16[128,2048]{1,0:T(8,128)(2,1)S(1)} collective-permute-done((bf16[128,2048]{1,0:T(8,128)(2,1)S(1)}, bf16[128,2048]{1,0:T(8,128)(2,1)S(1)}, u32[]{:S(2)}, u32[]{:S(2)}) %collective-permute-start) | collective-permute-done | bytes 524320 | tf_op jit(solution)/shard_map/ppermute | solution.py:29
  17.0 0.0 copy-done.1
  17.0 0.8 %settle_kv.1 = (bf16[128,2176]{1,0:T(8,128)(2,1)S(1)}, bf16[128,256]{1,0:T(8,128)(2,1)S(1)}) custom-call(s32[2]{0:T(128)S(1)} %pad_add_fusion.shift_ref, s32[1,128]{1,0:T(1,128)S(1)} %copy-done.1, bf16[128,2048]{1,0:T(8,128)(2,1)S(1)} %collective-permute-done.arrived_ref, bf16[128,2048]{1,0:T(8,128)(2,1)S(1)} %pad_maximum_fusion.1.local_ref), custom_call_target="tpu_custom_call" | custom-call | tf_op jit(solution)/shard_map/settle_kv/pallas_call | solution.py:78
  17.8 3.2 %collective-permute-start.1 = (bf16[128,2176]{1,0:T(8,128)(2,1)S(1)}, bf16[128,2176]{1,0:T(8,128)(2,1)S(1)}, u32[]{:S(2)}, u32[]{:S(2)}) collective-permute-start(bf16[128,2176]{1,0:T(8,128)(2,1)S(1)} %get-tuple-element.19.refs_0_), channel_id=1, source_target_pairs={{0,2},{1,3},{2,4},{3,5},{4,6},{5,7},{8,10},{9,11},{10,12},{11,13},... | collective-permute-start | bytes 1671176 | tf_op jit(solution)/shard_map/ppermute | solution.py:29
  21.1 2.2 %collective-permute-start.5 = (bf16[128,3200]{1,0:T(8,128)(2,1)S(1)}, bf16[128,3200]{1,0:T(8,128)(2,1)S(1)}, u32[]{:S(2)}, u32[]{:S(2)}) collective-permute-start(bf16[128,3200]{1,0:T(8,128)(2,1)S(1)} %add_bitcast_fusion), channel_id=1, source_target_pairs={{0,8},{8,16},{16,24},{1,9},{9,17},{17,25},{2,10},{10,18},{18,26},{... | collective-permute-start | bytes 2457608 | tf_op jit(solution)/shard_map/ppermute | solution.py:29
  23.3 7.7 %collective-permute-done.2.arrived_ref = bf16[128,2560]{1,0:T(8,128)(2,1)S(1)} collective-permute-done((bf16[128,2560]{1,0:T(8,128)(2,1)S(1)}, bf16[128,2560]{1,0:T(8,128)(2,1)S(1)}, u32[]{:S(2)}, u32[]{:S(2)}) %collective-permute-start.2) | collective-permute-done | bytes 655392 | tf_op jit(solution)/shard_map/ppermute | solution.py:29
  31.0 1.3 %place_queries.2.refs_0_ = bf16[1,128,8192]{2,1,0:T(8,128)(2,1)} custom-call(bf16[128,256]{1,0:T(8,128)(2,1)S(1)} %get-tuple-element.20.hot_ref.refs_6_, bf16[128,2560]{1,0:T(8,128)(2,1)S(1)} %collective-permute-done.2.arrived_ref, bf16[1,256,8192]{2,1,0:T(8,128)(2,1)S(1)} %copy-done), custom_call_target="tpu_custom_call" | custom-call | tf_op jit(solution)/shard_map/place_queries/pallas_call | solution.py:161
  32.3 0.0 collective-permute-done.1.refs_1_
  32.3 3.2 %collective-permute-start.4 = (bf16[128,2176]{1,0:T(8,128)(2,1)S(1)}, bf16[128,2176]{1,0:T(8,128)(2,1)S(1)}, u32[]{:S(2)}, u32[]{:S(2)}) collective-permute-start(bf16[128,2176]{1,0:T(8,128)(2,1)S(1)} %collective-permute-done.1.refs_1_), channel_id=1, source_target_pairs={{0,2},{1,3},{2,4},{3,5},{4,6},{5,7},{8,10},{9,11},{10,12},{11,13},... | collective-permute-start | bytes 1671176 | tf_op jit(solution)/shard_map/ppermute | solution.py:29
  35.5 2.2 %collective-permute-start.8 = (bf16[128,2432]{1,0:T(8,128)(2,1)}, bf16[128,2432]{1,0:T(8,128)(2,1)}, u32[]{:S(2)}, u32[]{:S(2)}) collective-permute-start(bf16[128,2432]{1,0:T(8,128)(2,1)} %add_bitcast_fusion.2), channel_id=1, source_target_pairs={{0,8},{8,16},{16,24},{1,9},{9,17},{17,25},{2,10},{10,18},{18,26},{... | collective-permute-start | bytes 1867784 | tf_op jit(solution)/shard_map/ppermute | solution.py:29
  37.7 1.3 %collective-permute-start.7 = (bf16[128,2176]{1,0:T(8,128)(2,1)S(1)}, bf16[128,2176]{1,0:T(8,128)(2,1)S(1)}, u32[]{:S(2)}, u32[]{:S(2)}) collective-permute-start(bf16[128,2176]{1,0:T(8,128)(2,1)S(1)} %get-tuple-element.19.refs_0_), channel_id=1, source_target_pairs={{0,1},{2,3},{4,5},{6,7},{8,9},{10,11},{12,13},{14,15},{16,17},{18,... | collective-permute-start | bytes 1671176 | tf_op jit(solution)/shard_map/ppermute | solution.py:34
  39.0 3.4 %collective-permute-start.3 = (bf16[128,2176]{1,0:T(8,128)(2,1)S(1)}, bf16[128,2176]{1,0:T(8,128)(2,1)S(1)}, u32[]{:S(2)}, u32[]{:S(2)}) collective-permute-start(bf16[128,2176]{1,0:T(8,128)(2,1)S(1)} %collective-permute-done.1.refs_1_), channel_id=1, source_target_pairs={{0,1},{1,0},{2,3},{3,2},{4,5},{5,4},{6,7},{7,6},{8,9},{9,8},{10,11... | collective-permute-start | bytes 1671176 | tf_op jit(solution)/shard_map/ppermute | solution.py:34
  42.4 6.2 %collective-permute-done.5.arrived_ref = bf16[128,3200]{1,0:T(8,128)(2,1)S(1)} collective-permute-done((bf16[128,3200]{1,0:T(8,128)(2,1)S(1)}, bf16[128,3200]{1,0:T(8,128)(2,1)S(1)}, u32[]{:S(2)}, u32[]{:S(2)}) %collective-permute-start.5) | collective-permute-done | bytes 819232 | tf_op jit(solution)/shard_map/ppermute | solution.py:29
  48.6 1.4 %place_queries.3.refs_7_ = bf16[1,128,8192]{2,1,0:T(8,128)(2,1)} custom-call(bf16[128,256]{1,0:T(8,128)(2,1)S(1)} %get-tuple-element.20.hot_ref.refs_6_, bf16[128,3200]{1,0:T(8,128)(2,1)S(1)} %collective-permute-done.5.arrived_ref, bf16[1,256,8192]{2,1,0:T(8,128)(2,1)S(1)} %copy-done, ...), custom_call_target="tpu_custom_call", output_to_operand_aliasing={{}: (3, {})} | custom-call | tf_op jit(solution)/shard_map/place_queries/pallas_call | solution.py:119
  50.0 0.0 collective-permute-done.4.refs_3_
  50.0 2.8 %collective-permute-start.6 = (bf16[128,2176]{1,0:T(8,128)(2,1)S(1)}, bf16[128,2176]{1,0:T(8,128)(2,1)S(1)}, u32[]{:S(2)}, u32[]{:S(2)}) collective-permute-start(bf16[128,2176]{1,0:T(8,128)(2,1)S(1)} %collective-permute-done.4.refs_3_), channel_id=1, source_target_pairs={{0,1},{1,0},{2,3},{3,2},{4,5},{5,4},{6,7},{7,6},{8,9},{9,8},{10,11... | collective-permute-start | bytes 1671176 | tf_op jit(solution)/shard_map/ppermute | solution.py:34
  52.7 0.0 collective-permute-done.7.refs_5_
  52.7 0.0 collective-permute-done.3.refs_2_
  52.7 1.6 %collective-permute-done.6.refs_4_ = bf16[128,2176]{1,0:T(8,128)(2,1)S(1)} collective-permute-done((bf16[128,2176]{1,0:T(8,128)(2,1)S(1)}, bf16[128,2176]{1,0:T(8,128)(2,1)S(1)}, u32[]{:S(2)}, u32[]{:S(2)}) %collective-permute-start.6) | collective-permute-done | bytes 557088 | tf_op jit(solution)/shard_map/ppermute | solution.py:34
  54.3 7.9 %attend_early.1 = (bf16[1,128,8192]{2,1,0:T(8,128)(2,1)}, bf16[128,2432]{1,0:T(8,128)(2,1)S(1)}) custom-call(s32[1]{0:T(128)} %bitcast.rank_ref, bf16[128,2176]{1,0:T(8,128)(2,1)S(1)} %get-tuple-element.19.refs_0_, bf16[128,2176]{1,0:T(8,128)(2,1)S(1)} %collective-permute-done.1.refs_1_, ...), custom_call_target="tpu_custom_call", output_to_operand_aliasing={{0}: (8, {})} | custom-call | tf_op jit(solution)/shard_map/attend_early/pallas_call | solution.py:119
  62.2 0.0 collective-permute-done.8.refs_7_
  62.2 5.0 %attend_late.1 = bf16[1,128,8192]{2,1,0:T(8,128)(2,1)} custom-call(s32[1]{0:T(128)} %bitcast.rank_ref, bf16[128,2176]{1,0:T(8,128)(2,1)S(1)} %get-tuple-element.19.refs_0_, bf16[128,2176]{1,0:T(8,128)(2,1)S(1)} %collective-permute-done.1.refs_1_, bf16[128,2176]{1,0:T(8,128)(2,1)S(1)} %collective-permute-done.3.refs_2_, ...), custom_call_target="tpu_custom_call", output_to_operand_aliasing={{}: (10, {})} | custom-call | tf_op jit(solution)/shard_map/attend_late/pallas_call | solution.py:119
  (3 shorter events, 0.1 us)
Async XLA Ops:
  0.0 8.8 %copy-start = (bf16[1,256,8192]{2,1,0:T(8,128)(2,1)S(1)}, bf16[1,256,8192]{2,1,0:T(8,128)(2,1)}, u32[]{:S(2)}) copy-start(bf16[1,256,8192]{2,1,0:T(8,128)(2,1)} %refs_6_.1) | copy-start | bytes 12582916
  0.0 17.0 %copy-start.1 = (s32[1,128]{1,0:T(1,128)S(1)}, s32[1,128]{1,0:T(1,128)}, u32[]{:S(2)}) copy-start(s32[1,128]{1,0:T(1,128)} %docs_ref.1) | copy-start | bytes 1540
  1.3 15.7 %collective-permute-start = (bf16[128,2048]{1,0:T(8,128)(2,1)S(1)}, bf16[128,2048]{1,0:T(8,128)(2,1)S(1)}, u32[]{:S(2)}, u32[]{:S(2)}) collective-permute-start(bf16[128,2048]{1,0:T(8,128)(2,1)S(1)} %pad_maximum_fusion), channel_id=1, source_target_pairs={{0,8},{8,16},{16,24},{1,9},{9,17},{17,25},{2,10},{10,18},{18,26},{... | collective-permute-start | bytes 1572872 | tf_op jit(solution)/shard_map/ppermute | solution.py:29
  9.9 21.1 %collective-permute-start.2 = (bf16[128,2560]{1,0:T(8,128)(2,1)S(1)}, bf16[128,2560]{1,0:T(8,128)(2,1)S(1)}, u32[]{:S(2)}, u32[]{:S(2)}) collective-permute-start(bf16[128,2560]{1,0:T(8,128)(2,1)S(1)} %add_bitcast_fusion.1), channel_id=1, source_target_pairs={{0,8},{8,16},{16,24},{1,9},{9,17},{17,25},{2,10},{10,18},{18,26},{... | collective-permute-start | bytes 1966088 | tf_op jit(solution)/shard_map/ppermute | solution.py:29
  17.8 14.5 %collective-permute-start.1 = (bf16[128,2176]{1,0:T(8,128)(2,1)S(1)}, bf16[128,2176]{1,0:T(8,128)(2,1)S(1)}, u32[]{:S(2)}, u32[]{:S(2)}) collective-permute-start(bf16[128,2176]{1,0:T(8,128)(2,1)S(1)} %get-tuple-element.19.refs_0_), channel_id=1, source_target_pairs={{0,2},{1,3},{2,4},{3,5},{4,6},{5,7},{8,10},{9,11},{10,12},{11,13},... | collective-permute-start | bytes 1671176 | tf_op jit(solution)/shard_map/ppermute | solution.py:29
  21.1 27.5 %collective-permute-start.5 = (bf16[128,3200]{1,0:T(8,128)(2,1)S(1)}, bf16[128,3200]{1,0:T(8,128)(2,1)S(1)}, u32[]{:S(2)}, u32[]{:S(2)}) collective-permute-start(bf16[128,3200]{1,0:T(8,128)(2,1)S(1)} %add_bitcast_fusion), channel_id=1, source_target_pairs={{0,8},{8,16},{16,24},{1,9},{9,17},{17,25},{2,10},{10,18},{18,26},{... | collective-permute-start | bytes 2457608 | tf_op jit(solution)/shard_map/ppermute | solution.py:29
  32.3 17.7 %collective-permute-start.4 = (bf16[128,2176]{1,0:T(8,128)(2,1)S(1)}, bf16[128,2176]{1,0:T(8,128)(2,1)S(1)}, u32[]{:S(2)}, u32[]{:S(2)}) collective-permute-start(bf16[128,2176]{1,0:T(8,128)(2,1)S(1)} %collective-permute-done.1.refs_1_), channel_id=1, source_target_pairs={{0,2},{1,3},{2,4},{3,5},{4,6},{5,7},{8,10},{9,11},{10,12},{11,13},... | collective-permute-start | bytes 1671176 | tf_op jit(solution)/shard_map/ppermute | solution.py:29
  35.5 26.7 %collective-permute-start.8 = (bf16[128,2432]{1,0:T(8,128)(2,1)}, bf16[128,2432]{1,0:T(8,128)(2,1)}, u32[]{:S(2)}, u32[]{:S(2)}) collective-permute-start(bf16[128,2432]{1,0:T(8,128)(2,1)} %add_bitcast_fusion.2), channel_id=1, source_target_pairs={{0,8},{8,16},{16,24},{1,9},{9,17},{17,25},{2,10},{10,18},{18,26},{... | collective-permute-start | bytes 1867784 | tf_op jit(solution)/shard_map/ppermute | solution.py:29
  37.7 15.0 %collective-permute-start.7 = (bf16[128,2176]{1,0:T(8,128)(2,1)S(1)}, bf16[128,2176]{1,0:T(8,128)(2,1)S(1)}, u32[]{:S(2)}, u32[]{:S(2)}) collective-permute-start(bf16[128,2176]{1,0:T(8,128)(2,1)S(1)} %get-tuple-element.19.refs_0_), channel_id=1, source_target_pairs={{0,1},{2,3},{4,5},{6,7},{8,9},{10,11},{12,13},{14,15},{16,17},{18,... | collective-permute-start | bytes 1671176 | tf_op jit(solution)/shard_map/ppermute | solution.py:34
  39.0 13.7 %collective-permute-start.3 = (bf16[128,2176]{1,0:T(8,128)(2,1)S(1)}, bf16[128,2176]{1,0:T(8,128)(2,1)S(1)}, u32[]{:S(2)}, u32[]{:S(2)}) collective-permute-start(bf16[128,2176]{1,0:T(8,128)(2,1)S(1)} %collective-permute-done.1.refs_1_), channel_id=1, source_target_pairs={{0,1},{1,0},{2,3},{3,2},{4,5},{5,4},{6,7},{7,6},{8,9},{9,8},{10,11... | collective-permute-start | bytes 1671176 | tf_op jit(solution)/shard_map/ppermute | solution.py:34
  50.0 4.3 %collective-permute-start.6 = (bf16[128,2176]{1,0:T(8,128)(2,1)S(1)}, bf16[128,2176]{1,0:T(8,128)(2,1)S(1)}, u32[]{:S(2)}, u32[]{:S(2)}) collective-permute-start(bf16[128,2176]{1,0:T(8,128)(2,1)S(1)} %collective-permute-done.4.refs_3_), channel_id=1, source_target_pairs={{0,1},{1,0},{2,3},{3,2},{4,5},{5,4},{6,7},{7,6},{8,9},{9,8},{10,11... | collective-permute-start | bytes 1671176 | tf_op jit(solution)/shard_map/ppermute | solution.py:34

commit v22 on v21

--- a/solution.py
+++ b/solution.py
@@ -16,7 +16,7 @@
 NOTE = 2 * KV_WIDTH
 MASKED = -1e30
 HALF = GROUP // 2
-CHUNKS = (20, 25, 19)
+CHUNKS = (24, 22, 18)
 VMEM_GRANT = 48 * 1024 * 1024
 
 WHOLE = pl.BlockSpec(memory_space=pltpu.VMEM)

time: 68.3 us -> 68.3 us (level); the launches traced: 67.2 us -> 68 us
  no operation moved by 1% of the time
where the time goes in v22:
time: 68.3 us; the launch traced here: 68 us
  starting transfers between devices  23.4 us (34%)
  waiting for transfers between devices  20.6 us (30%)
  Pallas kernels  16.5 us (24%)
  other arithmetic  3.06 us (4%)
  local copies, waits for them, and re-layouts  2.32 us (3%)
  between operations  2.04 us (3%)
    ppermute x6, waiting for transfers between devices, shifted(): return lax.ppermute(x, axis, [(i, i + steps) for i in range(n - steps)])  19 us
    ppermute x6, starting transfers between devices, shifted(): return lax.ppermute(x, axis, [(i, i + steps) for i in range(n - steps)])  16 us
    pallas_call x3, Pallas kernels, in_place(): pl.pallas_call(kernel, in_specs=specs, out_specs=[ANYWHERE, *more_specs],...  14.3 us
    ppermute x3, starting transfers between devices, across_cores(): lax.ppermute(x, 'ctx', [(i, i ^ 1) for i in range(n) if i % 2 in sources])  7.41 us
    ppermute x3, waiting for transfers between devices, across_cores(): lax.ppermute(x, 'ctx', [(i, i ^ 1) for i in range(n) if i % 2 in sources])  1.58 us
  transfers between devices with their start and end apart: 9, of which 4 were waited for; matrix products, arithmetic and copies ran while one was open for 6% of the time, Pallas kernels for 17%

profile of v22, /device:TPU:21, one launch (start us, length us, event | category | flops | bytes accessed | tf_op | source)
XLA Modules:
  0.0 68.0 jit_solution(8993095105358539392)
XLA Ops:
  0.0 0.0 copy-start
  0.0 0.0 copy-start.1
  0.0 1.2 %slice_bitcast_fusion = (bf16[128,1024]{1,0:T(8,128)(2,1)S(1)}, bf16[128,1024]{1,0:T(8,128)(2,1)S(1)}) fusion(bf16[1,256,1024]{2,1,0:T(8,128)(2,1)} %param.7, bf16[1,256,1024]{2,1,0:T(8,128)(2,1)} %param.6), kind=kLoop, calls=%fused_computation.7 | loop fusion | bytes 1048576 | tf_op jit(solution)/shard_map/slice | solution.py:371
  1.3 3.3 %collective-permute-start = (bf16[128,2048]{1,0:T(8,128)(2,1)S(1)}, bf16[128,2048]{1,0:T(8,128)(2,1)S(1)}, u32[]{:S(2)}, u32[]{:S(2)}) collective-permute-start(bf16[128,2048]{1,0:T(8,128)(2,1)S(1)} %pad_maximum_fusion), channel_id=1, source_target_pairs={{0,8},{8,16},{16,24},{1,9},{9,17},{17,25},{2,10},{10,18},{18,26},{... | collective-permute-start | bytes 1572872 | tf_op jit(solution)/shard_map/ppermute | solution.py:29
  4.5 0.5 slice.55
  5.0 0.6 slice.56
  6.9 1.0 %add_bitcast_fusion.3 = bf16[128,1024]{1,0:T(8,128)(2,1)S(1)} fusion(bf16[1,256,1024]{2,1,0:T(8,128)(2,1)} %param.7, bf16[]{:T(256)} %bitcast.4), kind=kLoop, calls=%fused_computation.5 | loop fusion | flops 131072 | bytes 524290 | tf_op jit(solution)/shard_map/add | solution.py:385
  7.8 1.0 %add_bitcast_fusion.4 = bf16[128,1024]{1,0:T(8,128)(2,1)S(1)} fusion(bf16[1,256,1024]{2,1,0:T(8,128)(2,1)} %param.6, bf16[]{:T(256)} %bitcast.4), kind=kLoop, calls=%fused_computation.6 | loop fusion | flops 131072 | bytes 524290 | tf_op jit(solution)/shard_map/add | solution.py:385
  8.8 0.0 copy-done
  8.9 0.9 %add_bitcast_fusion.2 = bf16[128,2304]{1,0:T(8,128)(2,1)} fusion(bf16[1,256,8192]{2,1,0:T(8,128)(2,1)S(1)} %copy-done, bf16[]{:T(256)} %bitcast.7), kind=kLoop, calls=%fused_computation.2 | loop fusion | flops 294912 | bytes 1179650 | tf_op jit(solution)/shard_map/add | solution.py:390
  9.7 0.1 add_bitcast_fusion.1
  9.8 0.1 add_bitcast_fusion
  9.8 1.9 %collective-permute-start.2 = (bf16[128,3072]{1,0:T(8,128)(2,1)S(1)}, bf16[128,3072]{1,0:T(8,128)(2,1)S(1)}, u32[]{:S(2)}, u32[]{:S(2)}) collective-permute-start(bf16[128,3072]{1,0:T(8,128)(2,1)S(1)} %add_bitcast_fusion), channel_id=1, source_target_pairs={{0,8},{8,16},{16,24},{1,9},{9,17},{17,25},{2,10},{10,18},{18,26},{... | collective-permute-start | bytes 2359304 | tf_op jit(solution)/shard_map/ppermute | solution.py:29
  12.4 0.1 pad_add_fusion.shift_ref
  12.5 4.5 %collective-permute-done.arrived_ref = bf16[128,2048]{1,0:T(8,128)(2,1)S(1)} collective-permute-done((bf16[128,2048]{1,0:T(8,128)(2,1)S(1)}, bf16[128,2048]{1,0:T(8,128)(2,1)S(1)}, u32[]{:S(2)}, u32[]{:S(2)}) %collective-permute-start) | collective-permute-done | bytes 524320 | tf_op jit(solution)/shard_map/ppermute | solution.py:29
  17.0 0.0 copy-done.1
  17.0 0.8 %settle_kv.1 = (bf16[128,2176]{1,0:T(8,128)(2,1)S(1)}, bf16[128,256]{1,0:T(8,128)(2,1)S(1)}) custom-call(s32[2]{0:T(128)S(1)} %pad_add_fusion.shift_ref, s32[1,128]{1,0:T(1,128)S(1)} %copy-done.1, bf16[128,2048]{1,0:T(8,128)(2,1)S(1)} %collective-permute-done.arrived_ref, bf16[128,2048]{1,0:T(8,128)(2,1)S(1)} %pad_maximum_fusion.1.local_ref), custom_call_target="tpu_custom_call" | custom-call | tf_op jit(solution)/shard_map/settle_kv/pallas_call | solution.py:78
  17.8 3.2 %collective-permute-start.1 = (bf16[128,2176]{1,0:T(8,128)(2,1)S(1)}, bf16[128,2176]{1,0:T(8,128)(2,1)S(1)}, u32[]{:S(2)}, u32[]{:S(2)}) collective-permute-start(bf16[128,2176]{1,0:T(8,128)(2,1)S(1)} %get-tuple-element.19.refs_0_), channel_id=1, source_target_pairs={{0,2},{1,3},{2,4},{3,5},{4,6},{5,7},{8,10},{9,11},{10,12},{11,13},... | collective-permute-start | bytes 1671176 | tf_op jit(solution)/shard_map/ppermute | solution.py:29
  21.1 2.2 %collective-permute-start.5 = (bf16[128,2816]{1,0:T(8,128)(2,1)S(1)}, bf16[128,2816]{1,0:T(8,128)(2,1)S(1)}, u32[]{:S(2)}, u32[]{:S(2)}) collective-permute-start(bf16[128,2816]{1,0:T(8,128)(2,1)S(1)} %add_bitcast_fusion.1), channel_id=1, source_target_pairs={{0,8},{8,16},{16,24},{1,9},{9,17},{17,25},{2,10},{10,18},{18,26},{... | collective-permute-start | bytes 2162696 | tf_op jit(solution)/shard_map/ppermute | solution.py:29
  23.3 10.6 %collective-permute-done.2.arrived_ref = bf16[128,3072]{1,0:T(8,128)(2,1)S(1)} collective-permute-done((bf16[128,3072]{1,0:T(8,128)(2,1)S(1)}, bf16[128,3072]{1,0:T(8,128)(2,1)S(1)}, u32[]{:S(2)}, u32[]{:S(2)}) %collective-permute-start.2) | collective-permute-done | bytes 786464 | tf_op jit(solution)/shard_map/ppermute | solution.py:29
  33.8 1.4 %place_queries.2.refs_0_ = bf16[1,128,8192]{2,1,0:T(8,128)(2,1)} custom-call(bf16[128,256]{1,0:T(8,128)(2,1)S(1)} %get-tuple-element.20.hot_ref.refs_6_, bf16[128,3072]{1,0:T(8,128)(2,1)S(1)} %collective-permute-done.2.arrived_ref, bf16[1,256,8192]{2,1,0:T(8,128)(2,1)S(1)} %copy-done), custom_call_target="tpu_custom_call" | custom-call | tf_op jit(solution)/shard_map/place_queries/pallas_call | solution.py:161
  35.2 0.0 collective-permute-done.1.refs_1_
  35.2 3.2 %collective-permute-start.4 = (bf16[128,2176]{1,0:T(8,128)(2,1)S(1)}, bf16[128,2176]{1,0:T(8,128)(2,1)S(1)}, u32[]{:S(2)}, u32[]{:S(2)}) collective-permute-start(bf16[128,2176]{1,0:T(8,128)(2,1)S(1)} %collective-permute-done.1.refs_1_), channel_id=1, source_target_pairs={{0,2},{1,3},{2,4},{3,5},{4,6},{5,7},{8,10},{9,11},{10,12},{11,13},... | collective-permute-start | bytes 1671176 | tf_op jit(solution)/shard_map/ppermute | solution.py:29
  38.4 2.2 %collective-permute-start.8 = (bf16[128,2304]{1,0:T(8,128)(2,1)}, bf16[128,2304]{1,0:T(8,128)(2,1)}, u32[]{:S(2)}, u32[]{:S(2)}) collective-permute-start(bf16[128,2304]{1,0:T(8,128)(2,1)} %add_bitcast_fusion.2), channel_id=1, source_target_pairs={{0,8},{8,16},{16,24},{1,9},{9,17},{17,25},{2,10},{10,18},{18,26},{... | collective-permute-start | bytes 1769480 | tf_op jit(solution)/shard_map/ppermute | solution.py:29
  40.6 1.3 %collective-permute-start.7 = (bf16[128,2176]{1,0:T(8,128)(2,1)S(1)}, bf16[128,2176]{1,0:T(8,128)(2,1)S(1)}, u32[]{:S(2)}, u32[]{:S(2)}) collective-permute-start(bf16[128,2176]{1,0:T(8,128)(2,1)S(1)} %get-tuple-element.19.refs_0_), channel_id=1, source_target_pairs={{0,1},{2,3},{4,5},{6,7},{8,9},{10,11},{12,13},{14,15},{16,17},{18,... | collective-permute-start | bytes 1671176 | tf_op jit(solution)/shard_map/ppermute | solution.py:34
  41.9 3.4 %collective-permute-start.3 = (bf16[128,2176]{1,0:T(8,128)(2,1)S(1)}, bf16[128,2176]{1,0:T(8,128)(2,1)S(1)}, u32[]{:S(2)}, u32[]{:S(2)}) collective-permute-start(bf16[128,2176]{1,0:T(8,128)(2,1)S(1)} %collective-permute-done.1.refs_1_), channel_id=1, source_target_pairs={{0,1},{1,0},{2,3},{3,2},{4,5},{5,4},{6,7},{7,6},{8,9},{9,8},{10,11... | collective-permute-start | bytes 1671176 | tf_op jit(solution)/shard_map/ppermute | solution.py:34
  45.3 4.0 %collective-permute-done.5.arrived_ref = bf16[128,2816]{1,0:T(8,128)(2,1)S(1)} collective-permute-done((bf16[128,2816]{1,0:T(8,128)(2,1)S(1)}, bf16[128,2816]{1,0:T(8,128)(2,1)S(1)}, u32[]{:S(2)}, u32[]{:S(2)}) %collective-permute-start.5) | collective-permute-done | bytes 720928 | tf_op jit(solution)/shard_map/ppermute | solution.py:29
  49.3 1.3 %place_queries.3.refs_7_ = bf16[1,128,8192]{2,1,0:T(8,128)(2,1)} custom-call(bf16[128,256]{1,0:T(8,128)(2,1)S(1)} %get-tuple-element.20.hot_ref.refs_6_, bf16[128,2816]{1,0:T(8,128)(2,1)S(1)} %collective-permute-done.5.arrived_ref, bf16[1,256,8192]{2,1,0:T(8,128)(2,1)S(1)} %copy-done, ...), custom_call_target="tpu_custom_call", output_to_operand_aliasing={{}: (3, {})} | custom-call | tf_op jit(solution)/shard_map/place_queries/pallas_call | solution.py:119
  50.6 0.0 collective-permute-done.4.refs_3_
  50.6 2.8 %collective-permute-start.6 = (bf16[128,2176]{1,0:T(8,128)(2,1)S(1)}, bf16[128,2176]{1,0:T(8,128)(2,1)S(1)}, u32[]{:S(2)}, u32[]{:S(2)}) collective-permute-start(bf16[128,2176]{1,0:T(8,128)(2,1)S(1)} %collective-permute-done.4.refs_3_), channel_id=1, source_target_pairs={{0,1},{1,0},{2,3},{3,2},{4,5},{5,4},{6,7},{7,6},{8,9},{9,8},{10,11... | collective-permute-start | bytes 1671176 | tf_op jit(solution)/shard_map/ppermute | solution.py:34
  53.4 0.0 collective-permute-done.7.refs_5_
  53.4 0.0 collective-permute-done.3.refs_2_
  53.4 1.6 %collective-permute-done.6.refs_4_ = bf16[128,2176]{1,0:T(8,128)(2,1)S(1)} collective-permute-done((bf16[128,2176]{1,0:T(8,128)(2,1)S(1)}, bf16[128,2176]{1,0:T(8,128)(2,1)S(1)}, u32[]{:S(2)}, u32[]{:S(2)}) %collective-permute-start.6) | collective-permute-done | bytes 557088 | tf_op jit(solution)/shard_map/ppermute | solution.py:34
  55.0 8.2 %attend_early.1 = (bf16[1,128,8192]{2,1,0:T(8,128)(2,1)}, bf16[128,2304]{1,0:T(8,128)(2,1)S(1)}) custom-call(s32[1]{0:T(128)} %bitcast.rank_ref, bf16[128,2176]{1,0:T(8,128)(2,1)S(1)} %get-tuple-element.19.refs_0_, bf16[128,2176]{1,0:T(8,128)(2,1)S(1)} %collective-permute-done.1.refs_1_, ...), custom_call_target="tpu_custom_call", output_to_operand_aliasing={{0}: (8, {})} | custom-call | tf_op jit(solution)/shard_map/attend_early/pallas_call | solution.py:119
  63.2 0.0 collective-permute-done.8.refs_7_
  63.2 4.8 %attend_late.1 = bf16[1,128,8192]{2,1,0:T(8,128)(2,1)} custom-call(s32[1]{0:T(128)} %bitcast.rank_ref, bf16[128,2176]{1,0:T(8,128)(2,1)S(1)} %get-tuple-element.19.refs_0_, bf16[128,2176]{1,0:T(8,128)(2,1)S(1)} %collective-permute-done.1.refs_1_, bf16[128,2176]{1,0:T(8,128)(2,1)S(1)} %collective-permute-done.3.refs_2_, ...), custom_call_target="tpu_custom_call", output_to_operand_aliasing={{}: (10, {})} | custom-call | tf_op jit(solution)/shard_map/attend_late/pallas_call | solution.py:119
  (2 shorter events, 0.1 us)
Async XLA Ops:
  0.0 8.8 %copy-start = (bf16[1,256,8192]{2,1,0:T(8,128)(2,1)S(1)}, bf16[1,256,8192]{2,1,0:T(8,128)(2,1)}, u32[]{:S(2)}) copy-start(bf16[1,256,8192]{2,1,0:T(8,128)(2,1)} %refs_6_.1) | copy-start | bytes 12582916
  0.0 17.0 %copy-start.1 = (s32[1,128]{1,0:T(1,128)S(1)}, s32[1,128]{1,0:T(1,128)}, u32[]{:S(2)}) copy-start(s32[1,128]{1,0:T(1,128)} %docs_ref.1) | copy-start | bytes 1540
  1.3 15.7 %collective-permute-start = (bf16[128,2048]{1,0:T(8,128)(2,1)S(1)}, bf16[128,2048]{1,0:T(8,128)(2,1)S(1)}, u32[]{:S(2)}, u32[]{:S(2)}) collective-permute-start(bf16[128,2048]{1,0:T(8,128)(2,1)S(1)} %pad_maximum_fusion), channel_id=1, source_target_pairs={{0,8},{8,16},{16,24},{1,9},{9,17},{17,25},{2,10},{10,18},{18,26},{... | collective-permute-start | bytes 1572872 | tf_op jit(solution)/shard_map/ppermute | solution.py:29
  9.8 24.0 %collective-permute-start.2 = (bf16[128,3072]{1,0:T(8,128)(2,1)S(1)}, bf16[128,3072]{1,0:T(8,128)(2,1)S(1)}, u32[]{:S(2)}, u32[]{:S(2)}) collective-permute-start(bf16[128,3072]{1,0:T(8,128)(2,1)S(1)} %add_bitcast_fusion), channel_id=1, source_target_pairs={{0,8},{8,16},{16,24},{1,9},{9,17},{17,25},{2,10},{10,18},{18,26},{... | collective-permute-start | bytes 2359304 | tf_op jit(solution)/shard_map/ppermute | solution.py:29
  17.8 17.4 %collective-permute-start.1 = (bf16[128,2176]{1,0:T(8,128)(2,1)S(1)}, bf16[128,2176]{1,0:T(8,128)(2,1)S(1)}, u32[]{:S(2)}, u32[]{:S(2)}) collective-permute-start(bf16[128,2176]{1,0:T(8,128)(2,1)S(1)} %get-tuple-element.19.refs_0_), channel_id=1, source_target_pairs={{0,2},{1,3},{2,4},{3,5},{4,6},{5,7},{8,10},{9,11},{10,12},{11,13},... | collective-permute-start | bytes 1671176 | tf_op jit(solution)/shard_map/ppermute | solution.py:29
  21.1 28.2 %collective-permute-start.5 = (bf16[128,2816]{1,0:T(8,128)(2,1)S(1)}, bf16[128,2816]{1,0:T(8,128)(2,1)S(1)}, u32[]{:S(2)}, u32[]{:S(2)}) collective-permute-start(bf16[128,2816]{1,0:T(8,128)(2,1)S(1)} %add_bitcast_fusion.1), channel_id=1, source_target_pairs={{0,8},{8,16},{16,24},{1,9},{9,17},{17,25},{2,10},{10,18},{18,26},{... | collective-permute-start | bytes 2162696 | tf_op jit(solution)/shard_map/ppermute | solution.py:29
  35.2 15.4 %collective-permute-start.4 = (bf16[128,2176]{1,0:T(8,128)(2,1)S(1)}, bf16[128,2176]{1,0:T(8,128)(2,1)S(1)}, u32[]{:S(2)}, u32[]{:S(2)}) collective-permute-start(bf16[128,2176]{1,0:T(8,128)(2,1)S(1)} %collective-permute-done.1.refs_1_), channel_id=1, source_target_pairs={{0,2},{1,3},{2,4},{3,5},{4,6},{5,7},{8,10},{9,11},{10,12},{11,13},... | collective-permute-start | bytes 1671176 | tf_op jit(solution)/shard_map/ppermute | solution.py:29
  38.4 24.8 %collective-permute-start.8 = (bf16[128,2304]{1,0:T(8,128)(2,1)}, bf16[128,2304]{1,0:T(8,128)(2,1)}, u32[]{:S(2)}, u32[]{:S(2)}) collective-permute-start(bf16[128,2304]{1,0:T(8,128)(2,1)} %add_bitcast_fusion.2), channel_id=1, source_target_pairs={{0,8},{8,16},{16,24},{1,9},{9,17},{17,25},{2,10},{10,18},{18,26},{... | collective-permute-start | bytes 1769480 | tf_op jit(solution)/shard_map/ppermute | solution.py:29
  40.6 12.7 %collective-permute-start.7 = (bf16[128,2176]{1,0:T(8,128)(2,1)S(1)}, bf16[128,2176]{1,0:T(8,128)(2,1)S(1)}, u32[]{:S(2)}, u32[]{:S(2)}) collective-permute-start(bf16[128,2176]{1,0:T(8,128)(2,1)S(1)} %get-tuple-element.19.refs_0_), channel_id=1, source_target_pairs={{0,1},{2,3},{4,5},{6,7},{8,9},{10,11},{12,13},{14,15},{16,17},{18,... | collective-permute-start | bytes 1671176 | tf_op jit(solution)/shard_map/ppermute | solution.py:34
  41.9 11.4 %collective-permute-start.3 = (bf16[128,2176]{1,0:T(8,128)(2,1)S(1)}, bf16[128,2176]{1,0:T(8,128)(2,1)S(1)}, u32[]{:S(2)}, u32[]{:S(2)}) collective-permute-start(bf16[128,2176]{1,0:T(8,128)(2,1)S(1)} %collective-permute-done.1.refs_1_), channel_id=1, source_target_pairs={{0,1},{1,0},{2,3},{3,2},{4,5},{5,4},{6,7},{7,6},{8,9},{9,8},{10,11... | collective-permute-start | bytes 1671176 | tf_op jit(solution)/shard_map/ppermute | solution.py:34
  50.6 4.3 %collective-permute-start.6 = (bf16[128,2176]{1,0:T(8,128)(2,1)S(1)}, bf16[128,2176]{1,0:T(8,128)(2,1)S(1)}, u32[]{:S(2)}, u32[]{:S(2)}) collective-permute-start(bf16[128,2176]{1,0:T(8,128)(2,1)S(1)} %collective-permute-done.4.refs_3_), channel_id=1, source_target_pairs={{0,1},{1,0},{2,3},{3,2},{4,5},{5,4},{6,7},{7,6},{8,9},{9,8},{10,11... | collective-permute-start | bytes 1671176 | tf_op jit(solution)/shard_map/ppermute | solution.py:34

commit v23 on v21

--- a/solution.py
+++ b/solution.py
@@ -17,7 +17,7 @@
 MASKED = -1e30
 HALF = GROUP // 2
 CHUNKS = (20, 25, 19)
-VMEM_GRANT = 48 * 1024 * 1024
+VMEM_GRANT = 30 * 1024 * 1024
 
 WHOLE = pl.BlockSpec(memory_space=pltpu.VMEM)
 ANYWHERE = pl.BlockSpec(memory_space=pl.ANY)

time: 68.3 us -> 69.8 us (1.022); the launches traced: 67.2 us -> 69.4 us
  local copies, waits for them, and re-layouts: 2.32 us -> 4.54 us
    unnamed x4 -> x6, local copies, waits for them, and re-layouts: 0.01 us -> 2.19 us
  transfers between devices with their start and end apart: 9 -> 9, of which waited for: 4 -> 4; matrix products, arithmetic and copies ran while one was open for 6% -> 6% of each run, Pallas kernels for 17% -> 16%
where the time goes in v23:
time: 69.8 us; the launch traced here: 69.4 us
  starting transfers between devices  23.4 us (34%)
  waiting for transfers between devices  19.9 us (29%)
  Pallas kernels  16.4 us (23%)
  local copies, waits for them, and re-layouts  4.54 us (7%)
  other arithmetic  3.1 us (4%)
  between operations  2.11 us (3%)
    ppermute x6, waiting for transfers between devices, shifted(): return lax.ppermute(x, axis, [(i, i + steps) for i in range(n - steps)])  18.3 us
    ppermute x6, starting transfers between devices, shifted(): return lax.ppermute(x, axis, [(i, i + steps) for i in range(n - steps)])  16 us
    pallas_call x3, Pallas kernels, in_place(): pl.pallas_call(kernel, in_specs=specs, out_specs=[ANYWHERE, *more_specs],...  14.3 us
    ppermute x3, starting transfers between devices, across_cores(): lax.ppermute(x, 'ctx', [(i, i ^ 1) for i in range(n) if i % 2 in sources])  7.4 us
    unnamed x6, local copies, waits for them, and re-layouts  2.19 us
    ppermute x3, waiting for transfers between devices, across_cores(): lax.ppermute(x, 'ctx', [(i, i ^ 1) for i in range(n) if i % 2 in sources])  1.58 us
  transfers between devices with their start and end apart: 9, of which 4 were waited for; matrix products, arithmetic and copies ran while one was open for 6% of the time, Pallas kernels for 16%

profile of v23, /device:TPU:21, one launch (start us, length us, event | category | flops | bytes accessed | tf_op | source)
XLA Modules:
  0.0 69.4 jit_solution(6085697058670753259)
XLA Ops:
  0.0 0.0 copy-start
  0.0 0.0 copy-start.2
  0.0 1.2 %slice_bitcast_fusion = (bf16[128,1024]{1,0:T(8,128)(2,1)S(1)}, bf16[128,1024]{1,0:T(8,128)(2,1)S(1)}) fusion(bf16[1,256,1024]{2,1,0:T(8,128)(2,1)} %param.7, bf16[1,256,1024]{2,1,0:T(8,128)(2,1)} %param.6), kind=kLoop, calls=%fused_computation.7 | loop fusion | bytes 1048576 | tf_op jit(solution)/shard_map/slice | solution.py:371
  1.3 3.3 %collective-permute-start = (bf16[128,2048]{1,0:T(8,128)(2,1)S(1)}, bf16[128,2048]{1,0:T(8,128)(2,1)S(1)}, u32[]{:S(2)}, u32[]{:S(2)}) collective-permute-start(bf16[128,2048]{1,0:T(8,128)(2,1)S(1)} %pad_maximum_fusion), channel_id=1, source_target_pairs={{0,8},{8,16},{16,24},{1,9},{9,17},{17,25},{2,10},{10,18},{18,26},{... | collective-permute-start | bytes 1572872 | tf_op jit(solution)/shard_map/ppermute | solution.py:29
  4.5 0.5 slice.55
  5.0 0.6 slice.56
  7.0 1.0 %add_bitcast_fusion.3 = bf16[128,1024]{1,0:T(8,128)(2,1)S(1)} fusion(bf16[1,256,1024]{2,1,0:T(8,128)(2,1)} %param.7, bf16[]{:T(256)} %bitcast.4), kind=kLoop, calls=%fused_computation.5 | loop fusion | flops 131072 | bytes 524290 | tf_op jit(solution)/shard_map/add | solution.py:385
  7.9 1.0 %add_bitcast_fusion.4 = bf16[128,1024]{1,0:T(8,128)(2,1)S(1)} fusion(bf16[1,256,1024]{2,1,0:T(8,128)(2,1)} %param.6, bf16[]{:T(256)} %bitcast.4), kind=kLoop, calls=%fused_computation.6 | loop fusion | flops 131072 | bytes 524290 | tf_op jit(solution)/shard_map/add | solution.py:385
  8.9 0.0 copy-done
  9.0 0.9 %add_bitcast_fusion.2 = bf16[128,2432]{1,0:T(8,128)(2,1)} fusion(bf16[1,256,8192]{2,1,0:T(8,128)(2,1)S(1)} %copy-done, bf16[]{:T(256)} %bitcast.7), kind=kLoop, calls=%fused_computation.2 | loop fusion | flops 311296 | bytes 1245186 | tf_op jit(solution)/shard_map/add | solution.py:390
  9.8 0.1 add_bitcast_fusion
  10.0 1.9 %collective-permute-start.2 = (bf16[128,2560]{1,0:T(8,128)(2,1)S(1)}, bf16[128,2560]{1,0:T(8,128)(2,1)S(1)}, u32[]{:S(2)}, u32[]{:S(2)}) collective-permute-start(bf16[128,2560]{1,0:T(8,128)(2,1)S(1)} %add_bitcast_fusion.1), channel_id=1, source_target_pairs={{0,8},{8,16},{16,24},{1,9},{9,17},{17,25},{2,10},{10,18},{18,26},{... | collective-permute-start | bytes 1966088 | tf_op jit(solution)/shard_map/ppermute | solution.py:29
  12.6 0.1 pad_add_fusion.shift_ref
  12.6 4.3 %collective-permute-done.arrived_ref = bf16[128,2048]{1,0:T(8,128)(2,1)S(1)} collective-permute-done((bf16[128,2048]{1,0:T(8,128)(2,1)S(1)}, bf16[128,2048]{1,0:T(8,128)(2,1)S(1)}, u32[]{:S(2)}, u32[]{:S(2)}) %collective-permute-start) | collective-permute-done | bytes 524320 | tf_op jit(solution)/shard_map/ppermute | solution.py:29
  17.0 0.0 copy-done.2
  17.0 0.8 %settle_kv.1 = (bf16[128,2176]{1,0:T(8,128)(2,1)S(1)}, bf16[128,256]{1,0:T(8,128)(2,1)S(1)}) custom-call(s32[2]{0:T(128)S(1)} %pad_add_fusion.shift_ref, s32[1,128]{1,0:T(1,128)S(1)} %copy-done.2, bf16[128,2048]{1,0:T(8,128)(2,1)S(1)} %collective-permute-done.arrived_ref, bf16[128,2048]{1,0:T(8,128)(2,1)S(1)} %pad_maximum_fusion.1.local_ref), custom_call_target="tpu_custom_call" | custom-call | tf_op jit(solution)/shard_map/settle_kv/pallas_call | solution.py:78
  17.8 3.2 %collective-permute-start.1 = (bf16[128,2176]{1,0:T(8,128)(2,1)S(1)}, bf16[128,2176]{1,0:T(8,128)(2,1)S(1)}, u32[]{:S(2)}, u32[]{:S(2)}) collective-permute-start(bf16[128,2176]{1,0:T(8,128)(2,1)S(1)} %get-tuple-element.19.refs_0_), channel_id=1, source_target_pairs={{0,2},{1,3},{2,4},{3,5},{4,6},{5,7},{8,10},{9,11},{10,12},{11,13},... | collective-permute-start | bytes 1671176 | tf_op jit(solution)/shard_map/ppermute | solution.py:29
  21.1 2.2 %collective-permute-start.5 = (bf16[128,3200]{1,0:T(8,128)(2,1)S(1)}, bf16[128,3200]{1,0:T(8,128)(2,1)S(1)}, u32[]{:S(2)}, u32[]{:S(2)}) collective-permute-start(bf16[128,3200]{1,0:T(8,128)(2,1)S(1)} %add_bitcast_fusion), channel_id=1, source_target_pairs={{0,8},{8,16},{16,24},{1,9},{9,17},{17,25},{2,10},{10,18},{18,26},{... | collective-permute-start | bytes 2457608 | tf_op jit(solution)/shard_map/ppermute | solution.py:29
  23.3 7.7 %collective-permute-done.2.arrived_ref = bf16[128,2560]{1,0:T(8,128)(2,1)S(1)} collective-permute-done((bf16[128,2560]{1,0:T(8,128)(2,1)S(1)}, bf16[128,2560]{1,0:T(8,128)(2,1)S(1)}, u32[]{:S(2)}, u32[]{:S(2)}) %collective-permute-start.2) | collective-permute-done | bytes 655392 | tf_op jit(solution)/shard_map/ppermute | solution.py:29
  31.0 1.3 %place_queries.2.refs_0_ = bf16[1,128,8192]{2,1,0:T(8,128)(2,1)} custom-call(bf16[128,256]{1,0:T(8,128)(2,1)S(1)} %get-tuple-element.20.hot_ref.refs_6_, bf16[128,2560]{1,0:T(8,128)(2,1)S(1)} %collective-permute-done.2.arrived_ref, bf16[1,256,8192]{2,1,0:T(8,128)(2,1)S(1)} %copy-done), custom_call_target="tpu_custom_call" | custom-call | tf_op jit(solution)/shard_map/place_queries/pallas_call | solution.py:161
  32.3 0.0 collective-permute-done.1.refs_1_
  32.3 3.2 %collective-permute-start.4 = (bf16[128,2176]{1,0:T(8,128)(2,1)S(1)}, bf16[128,2176]{1,0:T(8,128)(2,1)S(1)}, u32[]{:S(2)}, u32[]{:S(2)}) collective-permute-start(bf16[128,2176]{1,0:T(8,128)(2,1)S(1)} %collective-permute-done.1.refs_1_), channel_id=1, source_target_pairs={{0,2},{1,3},{2,4},{3,5},{4,6},{5,7},{8,10},{9,11},{10,12},{11,13},... | collective-permute-start | bytes 1671176 | tf_op jit(solution)/shard_map/ppermute | solution.py:29
  35.5 2.2 %collective-permute-start.8 = (bf16[128,2432]{1,0:T(8,128)(2,1)}, bf16[128,2432]{1,0:T(8,128)(2,1)}, u32[]{:S(2)}, u32[]{:S(2)}) collective-permute-start(bf16[128,2432]{1,0:T(8,128)(2,1)} %add_bitcast_fusion.2), channel_id=1, source_target_pairs={{0,8},{8,16},{16,24},{1,9},{9,17},{17,25},{2,10},{10,18},{18,26},{... | collective-permute-start | bytes 1867784 | tf_op jit(solution)/shard_map/ppermute | solution.py:29
  37.7 1.3 %collective-permute-start.7 = (bf16[128,2176]{1,0:T(8,128)(2,1)S(1)}, bf16[128,2176]{1,0:T(8,128)(2,1)S(1)}, u32[]{:S(2)}, u32[]{:S(2)}) collective-permute-start(bf16[128,2176]{1,0:T(8,128)(2,1)S(1)} %get-tuple-element.19.refs_0_), channel_id=1, source_target_pairs={{0,1},{2,3},{4,5},{6,7},{8,9},{10,11},{12,13},{14,15},{16,17},{18,... | collective-permute-start | bytes 1671176 | tf_op jit(solution)/shard_map/ppermute | solution.py:34
  39.0 3.4 %collective-permute-start.3 = (bf16[128,2176]{1,0:T(8,128)(2,1)S(1)}, bf16[128,2176]{1,0:T(8,128)(2,1)S(1)}, u32[]{:S(2)}, u32[]{:S(2)}) collective-permute-start(bf16[128,2176]{1,0:T(8,128)(2,1)S(1)} %collective-permute-done.1.refs_1_), channel_id=1, source_target_pairs={{0,1},{1,0},{2,3},{3,2},{4,5},{5,4},{6,7},{7,6},{8,9},{9,8},{10,11... | collective-permute-start | bytes 1671176 | tf_op jit(solution)/shard_map/ppermute | solution.py:34
  42.4 6.2 %collective-permute-done.5.arrived_ref = bf16[128,3200]{1,0:T(8,128)(2,1)S(1)} collective-permute-done((bf16[128,3200]{1,0:T(8,128)(2,1)S(1)}, bf16[128,3200]{1,0:T(8,128)(2,1)S(1)}, u32[]{:S(2)}, u32[]{:S(2)}) %collective-permute-start.5) | collective-permute-done | bytes 819232 | tf_op jit(solution)/shard_map/ppermute | solution.py:29
  48.6 1.4 %place_queries.3.refs_7_ = bf16[1,128,8192]{2,1,0:T(8,128)(2,1)} custom-call(bf16[128,256]{1,0:T(8,128)(2,1)S(1)} %get-tuple-element.20.hot_ref.refs_6_, bf16[128,3200]{1,0:T(8,128)(2,1)S(1)} %collective-permute-done.5.arrived_ref, bf16[1,256,8192]{2,1,0:T(8,128)(2,1)S(1)} %copy-done, ...), custom_call_target="tpu_custom_call", output_to_operand_aliasing={{}: (3, {})} | custom-call | tf_op jit(solution)/shard_map/place_queries/pallas_call | solution.py:119
  50.0 0.0 collective-permute-done.4.refs_3_
  50.0 2.8 %collective-permute-start.6 = (bf16[128,2176]{1,0:T(8,128)(2,1)S(1)}, bf16[128,2176]{1,0:T(8,128)(2,1)S(1)}, u32[]{:S(2)}, u32[]{:S(2)}) collective-permute-start(bf16[128,2176]{1,0:T(8,128)(2,1)S(1)} %collective-permute-done.4.refs_3_), channel_id=1, source_target_pairs={{0,1},{1,0},{2,3},{3,2},{4,5},{5,4},{6,7},{7,6},{8,9},{9,8},{10,11... | collective-permute-start | bytes 1671176 | tf_op jit(solution)/shard_map/ppermute | solution.py:34
  52.7 0.0 collective-permute-done.7.refs_5_
  52.7 0.0 collective-permute-done.3.refs_2_
  52.7 1.6 %collective-permute-done.6.refs_4_ = bf16[128,2176]{1,0:T(8,128)(2,1)S(1)} collective-permute-done((bf16[128,2176]{1,0:T(8,128)(2,1)S(1)}, bf16[128,2176]{1,0:T(8,128)(2,1)S(1)}, u32[]{:S(2)}, u32[]{:S(2)}) %collective-permute-start.6) | collective-permute-done | bytes 557088 | tf_op jit(solution)/shard_map/ppermute | solution.py:34
  54.3 0.0 copy-start.1
  54.3 2.2 %copy-done.1 = bf16[1,256,8192]{2,1,0:T(8,128)(2,1)S(1)} copy-done((bf16[1,256,8192]{2,1,0:T(8,128)(2,1)S(1)}, bf16[1,256,8192]{2,1,0:T(8,128)(2,1)}, u32[]{:S(2)}) %copy-start.1) | copy-done | bytes 4194328
  56.5 7.9 %attend_early.1 = (bf16[1,128,8192]{2,1,0:T(8,128)(2,1)}, bf16[128,2432]{1,0:T(8,128)(2,1)S(1)}) custom-call(s32[1]{0:T(128)} %bitcast.rank_ref, bf16[128,2176]{1,0:T(8,128)(2,1)S(1)} %get-tuple-element.19.refs_0_, bf16[128,2176]{1,0:T(8,128)(2,1)S(1)} %collective-permute-done.1.refs_1_, ...), custom_call_target="tpu_custom_call", output_to_operand_aliasing={{0}: (8, {})} | custom-call | tf_op jit(solution)/shard_map/attend_early/pallas_call | solution.py:119
  64.4 0.0 collective-permute-done.8.refs_7_
  64.4 5.0 %attend_late.1 = bf16[1,128,8192]{2,1,0:T(8,128)(2,1)} custom-call(s32[1]{0:T(128)} %bitcast.rank_ref, bf16[128,2176]{1,0:T(8,128)(2,1)S(1)} %get-tuple-element.19.refs_0_, bf16[128,2176]{1,0:T(8,128)(2,1)S(1)} %collective-permute-done.1.refs_1_, bf16[128,2176]{1,0:T(8,128)(2,1)S(1)} %collective-permute-done.3.refs_2_, ...), custom_call_target="tpu_custom_call", output_to_operand_aliasing={{}: (10, {})} | custom-call | tf_op jit(solution)/shard_map/attend_late/pallas_call | solution.py:119
  (3 shorter events, 0.1 us)
Async XLA Ops:
  0.0 8.9 %copy-start = (bf16[1,256,8192]{2,1,0:T(8,128)(2,1)S(1)}, bf16[1,256,8192]{2,1,0:T(8,128)(2,1)}, u32[]{:S(2)}) copy-start(bf16[1,256,8192]{2,1,0:T(8,128)(2,1)} %refs_6_.1) | copy-start | bytes 12582916
  0.0 17.0 %copy-start.2 = (s32[1,128]{1,0:T(1,128)S(1)}, s32[1,128]{1,0:T(1,128)}, u32[]{:S(2)}) copy-start(s32[1,128]{1,0:T(1,128)} %docs_ref.1) | copy-start | bytes 1540
  1.3 15.7 %collective-permute-start = (bf16[128,2048]{1,0:T(8,128)(2,1)S(1)}, bf16[128,2048]{1,0:T(8,128)(2,1)S(1)}, u32[]{:S(2)}, u32[]{:S(2)}) collective-permute-start(bf16[128,2048]{1,0:T(8,128)(2,1)S(1)} %pad_maximum_fusion), channel_id=1, source_target_pairs={{0,8},{8,16},{16,24},{1,9},{9,17},{17,25},{2,10},{10,18},{18,26},{... | collective-permute-start | bytes 1572872 | tf_op jit(solution)/shard_map/ppermute | solution.py:29
  10.0 21.0 %collective-permute-start.2 = (bf16[128,2560]{1,0:T(8,128)(2,1)S(1)}, bf16[128,2560]{1,0:T(8,128)(2,1)S(1)}, u32[]{:S(2)}, u32[]{:S(2)}) collective-permute-start(bf16[128,2560]{1,0:T(8,128)(2,1)S(1)} %add_bitcast_fusion.1), channel_id=1, source_target_pairs={{0,8},{8,16},{16,24},{1,9},{9,17},{17,25},{2,10},{10,18},{18,26},{... | collective-permute-start | bytes 1966088 | tf_op jit(solution)/shard_map/ppermute | solution.py:29
  17.8 14.5 %collective-permute-start.1 = (bf16[128,2176]{1,0:T(8,128)(2,1)S(1)}, bf16[128,2176]{1,0:T(8,128)(2,1)S(1)}, u32[]{:S(2)}, u32[]{:S(2)}) collective-permute-start(bf16[128,2176]{1,0:T(8,128)(2,1)S(1)} %get-tuple-element.19.refs_0_), channel_id=1, source_target_pairs={{0,2},{1,3},{2,4},{3,5},{4,6},{5,7},{8,10},{9,11},{10,12},{11,13},... | collective-permute-start | bytes 1671176 | tf_op jit(solution)/shard_map/ppermute | solution.py:29
  21.1 27.5 %collective-permute-start.5 = (bf16[128,3200]{1,0:T(8,128)(2,1)S(1)}, bf16[128,3200]{1,0:T(8,128)(2,1)S(1)}, u32[]{:S(2)}, u32[]{:S(2)}) collective-permute-start(bf16[128,3200]{1,0:T(8,128)(2,1)S(1)} %add_bitcast_fusion), channel_id=1, source_target_pairs={{0,8},{8,16},{16,24},{1,9},{9,17},{17,25},{2,10},{10,18},{18,26},{... | collective-permute-start | bytes 2457608 | tf_op jit(solution)/shard_map/ppermute | solution.py:29
  32.3 17.7 %collective-permute-start.4 = (bf16[128,2176]{1,0:T(8,128)(2,1)S(1)}, bf16[128,2176]{1,0:T(8,128)(2,1)S(1)}, u32[]{:S(2)}, u32[]{:S(2)}) collective-permute-start(bf16[128,2176]{1,0:T(8,128)(2,1)S(1)} %collective-permute-done.1.refs_1_), channel_id=1, source_target_pairs={{0,2},{1,3},{2,4},{3,5},{4,6},{5,7},{8,10},{9,11},{10,12},{11,13},... | collective-permute-start | bytes 1671176 | tf_op jit(solution)/shard_map/ppermute | solution.py:29
  35.5 28.9 %collective-permute-start.8 = (bf16[128,2432]{1,0:T(8,128)(2,1)}, bf16[128,2432]{1,0:T(8,128)(2,1)}, u32[]{:S(2)}, u32[]{:S(2)}) collective-permute-start(bf16[128,2432]{1,0:T(8,128)(2,1)} %add_bitcast_fusion.2), channel_id=1, source_target_pairs={{0,8},{8,16},{16,24},{1,9},{9,17},{17,25},{2,10},{10,18},{18,26},{... | collective-permute-start | bytes 1867784 | tf_op jit(solution)/shard_map/ppermute | solution.py:29
  37.7 15.0 %collective-permute-start.7 = (bf16[128,2176]{1,0:T(8,128)(2,1)S(1)}, bf16[128,2176]{1,0:T(8,128)(2,1)S(1)}, u32[]{:S(2)}, u32[]{:S(2)}) collective-permute-start(bf16[128,2176]{1,0:T(8,128)(2,1)S(1)} %get-tuple-element.19.refs_0_), channel_id=1, source_target_pairs={{0,1},{2,3},{4,5},{6,7},{8,9},{10,11},{12,13},{14,15},{16,17},{18,... | collective-permute-start | bytes 1671176 | tf_op jit(solution)/shard_map/ppermute | solution.py:34
  39.0 13.7 %collective-permute-start.3 = (bf16[128,2176]{1,0:T(8,128)(2,1)S(1)}, bf16[128,2176]{1,0:T(8,128)(2,1)S(1)}, u32[]{:S(2)}, u32[]{:S(2)}) collective-permute-start(bf16[128,2176]{1,0:T(8,128)(2,1)S(1)} %collective-permute-done.1.refs_1_), channel_id=1, source_target_pairs={{0,1},{1,0},{2,3},{3,2},{4,5},{5,4},{6,7},{7,6},{8,9},{9,8},{10,11... | collective-permute-start | bytes 1671176 | tf_op jit(solution)/shard_map/ppermute | solution.py:34
  50.0 4.3 %collective-permute-start.6 = (bf16[128,2176]{1,0:T(8,128)(2,1)S(1)}, bf16[128,2176]{1,0:T(8,128)(2,1)S(1)}, u32[]{:S(2)}, u32[]{:S(2)}) collective-permute-start(bf16[128,2176]{1,0:T(8,128)(2,1)S(1)} %collective-permute-done.4.refs_3_), channel_id=1, source_target_pairs={{0,1},{1,0},{2,3},{3,2},{4,5},{5,4},{6,7},{7,6},{8,9},{9,8},{10,11... | collective-permute-start | bytes 1671176 | tf_op jit(solution)/shard_map/ppermute | solution.py:34
  54.3 2.2 %copy-start.1 = (bf16[1,256,8192]{2,1,0:T(8,128)(2,1)S(1)}, bf16[1,256,8192]{2,1,0:T(8,128)(2,1)}, u32[]{:S(2)}) copy-start(bf16[1,256,8192]{2,1,0:T(8,128)(2,1)} %refs_6_.1) | copy-start | bytes 12582916

commit v24 on v22

--- a/solution.py
+++ b/solution.py
@@ -16,7 +16,7 @@
 NOTE = 2 * KV_WIDTH
 MASKED = -1e30
 HALF = GROUP // 2
-CHUNKS = (24, 22, 18)
+CHUNKS = (20, 26, 18)
 VMEM_GRANT = 48 * 1024 * 1024
 
 WHOLE = pl.BlockSpec(memory_space=pltpu.VMEM)

time: 68.3 us -> 68.4 us (level)
  no operation moved by 1% of the time
where the time goes in v24:
time: 68.4 us; the launch traced here: 68 us
  starting transfers between devices  23.4 us (34%)
  waiting for transfers between devices  20.7 us (30%)
  Pallas kernels  16.5 us (24%)
  other arithmetic  3.06 us (4%)
  local copies, waits for them, and re-layouts  2.32 us (3%)
  between operations  2.04 us (3%)
    ppermute x6, waiting for transfers between devices, shifted(): return lax.ppermute(x, axis, [(i, i + steps) for i in range(n - steps)])  19.1 us
    ppermute x6, starting transfers between devices, shifted(): return lax.ppermute(x, axis, [(i, i + steps) for i in range(n - steps)])  16 us
    pallas_call x3, Pallas kernels, in_place(): pl.pallas_call(kernel, in_specs=specs, out_specs=[ANYWHERE, *more_specs],...  14.4 us
    ppermute x3, starting transfers between devices, across_cores(): lax.ppermute(x, 'ctx', [(i, i ^ 1) for i in range(n) if i % 2 in sources])  7.4 us
    ppermute x3, waiting for transfers between devices, across_cores(): lax.ppermute(x, 'ctx', [(i, i ^ 1) for i in range(n) if i % 2 in sources])  1.58 us
  transfers between devices with their start and end apart: 9, of which 4 were waited for; matrix products, arithmetic and copies ran while one was open for 6% of the time, Pallas kernels for 17%

profile of v24, /device:TPU:21, one launch (start us, length us, event | category | flops | bytes accessed | tf_op | source)
XLA Modules:
  0.0 68.0 jit_solution(4673942917422252226)
XLA Ops:
  0.0 0.0 copy-start
  0.0 0.0 copy-start.1
  0.0 1.2 %slice_bitcast_fusion = (bf16[128,1024]{1,0:T(8,128)(2,1)S(1)}, bf16[128,1024]{1,0:T(8,128)(2,1)S(1)}) fusion(bf16[1,256,1024]{2,1,0:T(8,128)(2,1)} %param.7, bf16[1,256,1024]{2,1,0:T(8,128)(2,1)} %param.6), kind=kLoop, calls=%fused_computation.7 | loop fusion | bytes 1048576 | tf_op jit(solution)/shard_map/slice | solution.py:371
  1.3 3.3 %collective-permute-start = (bf16[128,2048]{1,0:T(8,128)(2,1)S(1)}, bf16[128,2048]{1,0:T(8,128)(2,1)S(1)}, u32[]{:S(2)}, u32[]{:S(2)}) collective-permute-start(bf16[128,2048]{1,0:T(8,128)(2,1)S(1)} %pad_maximum_fusion), channel_id=1, source_target_pairs={{0,8},{8,16},{16,24},{1,9},{9,17},{17,25},{2,10},{10,18},{18,26},{... | collective-permute-start | bytes 1572872 | tf_op jit(solution)/shard_map/ppermute | solution.py:29
  4.5 0.5 slice.55
  5.0 0.6 slice.56
  6.9 1.0 %add_bitcast_fusion.3 = bf16[128,1024]{1,0:T(8,128)(2,1)S(1)} fusion(bf16[1,256,1024]{2,1,0:T(8,128)(2,1)} %param.7, bf16[]{:T(256)} %bitcast.4), kind=kLoop, calls=%fused_computation.5 | loop fusion | flops 131072 | bytes 524290 | tf_op jit(solution)/shard_map/add | solution.py:385
  7.8 1.0 %add_bitcast_fusion.4 = bf16[128,1024]{1,0:T(8,128)(2,1)S(1)} fusion(bf16[1,256,1024]{2,1,0:T(8,128)(2,1)} %param.6, bf16[]{:T(256)} %bitcast.4), kind=kLoop, calls=%fused_computation.6 | loop fusion | flops 131072 | bytes 524290 | tf_op jit(solution)/shard_map/add | solution.py:385
  8.8 0.0 copy-done
  8.9 0.9 %add_bitcast_fusion.2 = bf16[128,2304]{1,0:T(8,128)(2,1)} fusion(bf16[1,256,8192]{2,1,0:T(8,128)(2,1)S(1)} %copy-done, bf16[]{:T(256)} %bitcast.7), kind=kLoop, calls=%fused_computation.2 | loop fusion | flops 294912 | bytes 1179650 | tf_op jit(solution)/shard_map/add | solution.py:390
  9.7 0.1 add_bitcast_fusion
  9.8 1.9 %collective-permute-start.2 = (bf16[128,2560]{1,0:T(8,128)(2,1)S(1)}, bf16[128,2560]{1,0:T(8,128)(2,1)S(1)}, u32[]{:S(2)}, u32[]{:S(2)}) collective-permute-start(bf16[128,2560]{1,0:T(8,128)(2,1)S(1)} %add_bitcast_fusion.1), channel_id=1, source_target_pairs={{0,8},{8,16},{16,24},{1,9},{9,17},{17,25},{2,10},{10,18},{18,26},{... | collective-permute-start | bytes 1966088 | tf_op jit(solution)/shard_map/ppermute | solution.py:29
  12.4 0.1 pad_add_fusion.shift_ref
  12.5 4.5 %collective-permute-done.arrived_ref = bf16[128,2048]{1,0:T(8,128)(2,1)S(1)} collective-permute-done((bf16[128,2048]{1,0:T(8,128)(2,1)S(1)}, bf16[128,2048]{1,0:T(8,128)(2,1)S(1)}, u32[]{:S(2)}, u32[]{:S(2)}) %collective-permute-start) | collective-permute-done | bytes 524320 | tf_op jit(solution)/shard_map/ppermute | solution.py:29
  17.0 0.0 copy-done.1
  17.0 0.8 %settle_kv.1 = (bf16[128,2176]{1,0:T(8,128)(2,1)S(1)}, bf16[128,256]{1,0:T(8,128)(2,1)S(1)}) custom-call(s32[2]{0:T(128)S(1)} %pad_add_fusion.shift_ref, s32[1,128]{1,0:T(1,128)S(1)} %copy-done.1, bf16[128,2048]{1,0:T(8,128)(2,1)S(1)} %collective-permute-done.arrived_ref, bf16[128,2048]{1,0:T(8,128)(2,1)S(1)} %pad_maximum_fusion.1.local_ref), custom_call_target="tpu_custom_call" | custom-call | tf_op jit(solution)/shard_map/settle_kv/pallas_call | solution.py:78
  17.8 3.2 %collective-permute-start.1 = (bf16[128,2176]{1,0:T(8,128)(2,1)S(1)}, bf16[128,2176]{1,0:T(8,128)(2,1)S(1)}, u32[]{:S(2)}, u32[]{:S(2)}) collective-permute-start(bf16[128,2176]{1,0:T(8,128)(2,1)S(1)} %get-tuple-element.19.refs_0_), channel_id=1, source_target_pairs={{0,2},{1,3},{2,4},{3,5},{4,6},{5,7},{8,10},{9,11},{10,12},{11,13},... | collective-permute-start | bytes 1671176 | tf_op jit(solution)/shard_map/ppermute | solution.py:29
  21.1 2.2 %collective-permute-start.5 = (bf16[128,3328]{1,0:T(8,128)(2,1)S(1)}, bf16[128,3328]{1,0:T(8,128)(2,1)S(1)}, u32[]{:S(2)}, u32[]{:S(2)}) collective-permute-start(bf16[128,3328]{1,0:T(8,128)(2,1)S(1)} %add_bitcast_fusion), channel_id=1, source_target_pairs={{0,8},{8,16},{16,24},{1,9},{9,17},{17,25},{2,10},{10,18},{18,26},{... | collective-permute-start | bytes 2555912 | tf_op jit(solution)/shard_map/ppermute | solution.py:29
  23.3 7.7 %collective-permute-done.2.arrived_ref = bf16[128,2560]{1,0:T(8,128)(2,1)S(1)} collective-permute-done((bf16[128,2560]{1,0:T(8,128)(2,1)S(1)}, bf16[128,2560]{1,0:T(8,128)(2,1)S(1)}, u32[]{:S(2)}, u32[]{:S(2)}) %collective-permute-start.2) | collective-permute-done | bytes 655392 | tf_op jit(solution)/shard_map/ppermute | solution.py:29
  31.0 1.3 %place_queries.2.refs_0_ = bf16[1,128,8192]{2,1,0:T(8,128)(2,1)} custom-call(bf16[128,256]{1,0:T(8,128)(2,1)S(1)} %get-tuple-element.20.hot_ref.refs_6_, bf16[128,2560]{1,0:T(8,128)(2,1)S(1)} %collective-permute-done.2.arrived_ref, bf16[1,256,8192]{2,1,0:T(8,128)(2,1)S(1)} %copy-done), custom_call_target="tpu_custom_call" | custom-call | tf_op jit(solution)/shard_map/place_queries/pallas_call | solution.py:161
  32.3 0.0 collective-permute-done.1.refs_1_
  32.3 3.2 %collective-permute-start.4 = (bf16[128,2176]{1,0:T(8,128)(2,1)S(1)}, bf16[128,2176]{1,0:T(8,128)(2,1)S(1)}, u32[]{:S(2)}, u32[]{:S(2)}) collective-permute-start(bf16[128,2176]{1,0:T(8,128)(2,1)S(1)} %collective-permute-done.1.refs_1_), channel_id=1, source_target_pairs={{0,2},{1,3},{2,4},{3,5},{4,6},{5,7},{8,10},{9,11},{10,12},{11,13},... | collective-permute-start | bytes 1671176 | tf_op jit(solution)/shard_map/ppermute | solution.py:29
  35.5 2.2 %collective-permute-start.8 = (bf16[128,2304]{1,0:T(8,128)(2,1)}, bf16[128,2304]{1,0:T(8,128)(2,1)}, u32[]{:S(2)}, u32[]{:S(2)}) collective-permute-start(bf16[128,2304]{1,0:T(8,128)(2,1)} %add_bitcast_fusion.2), channel_id=1, source_target_pairs={{0,8},{8,16},{16,24},{1,9},{9,17},{17,25},{2,10},{10,18},{18,26},{... | collective-permute-start | bytes 1769480 | tf_op jit(solution)/shard_map/ppermute | solution.py:29
  37.7 1.3 %collective-permute-start.7 = (bf16[128,2176]{1,0:T(8,128)(2,1)S(1)}, bf16[128,2176]{1,0:T(8,128)(2,1)S(1)}, u32[]{:S(2)}, u32[]{:S(2)}) collective-permute-start(bf16[128,2176]{1,0:T(8,128)(2,1)S(1)} %get-tuple-element.19.refs_0_), channel_id=1, source_target_pairs={{0,1},{2,3},{4,5},{6,7},{8,9},{10,11},{12,13},{14,15},{16,17},{18,... | collective-permute-start | bytes 1671176 | tf_op jit(solution)/shard_map/ppermute | solution.py:34
  39.0 3.4 %collective-permute-start.3 = (bf16[128,2176]{1,0:T(8,128)(2,1)S(1)}, bf16[128,2176]{1,0:T(8,128)(2,1)S(1)}, u32[]{:S(2)}, u32[]{:S(2)}) collective-permute-start(bf16[128,2176]{1,0:T(8,128)(2,1)S(1)} %collective-permute-done.1.refs_1_), channel_id=1, source_target_pairs={{0,1},{1,0},{2,3},{3,2},{4,5},{5,4},{6,7},{7,6},{8,9},{9,8},{10,11... | collective-permute-start | bytes 1671176 | tf_op jit(solution)/shard_map/ppermute | solution.py:34
  42.4 6.9 %collective-permute-done.5.arrived_ref = bf16[128,3328]{1,0:T(8,128)(2,1)S(1)} collective-permute-done((bf16[128,3328]{1,0:T(8,128)(2,1)S(1)}, bf16[128,3328]{1,0:T(8,128)(2,1)S(1)}, u32[]{:S(2)}, u32[]{:S(2)}) %collective-permute-start.5) | collective-permute-done | bytes 852000 | tf_op jit(solution)/shard_map/ppermute | solution.py:29
  49.3 1.4 %place_queries.3.refs_7_ = bf16[1,128,8192]{2,1,0:T(8,128)(2,1)} custom-call(bf16[128,256]{1,0:T(8,128)(2,1)S(1)} %get-tuple-element.20.hot_ref.refs_6_, bf16[128,3328]{1,0:T(8,128)(2,1)S(1)} %collective-permute-done.5.arrived_ref, bf16[1,256,8192]{2,1,0:T(8,128)(2,1)S(1)} %copy-done, ...), custom_call_target="tpu_custom_call", output_to_operand_aliasing={{}: (3, {})} | custom-call | tf_op jit(solution)/shard_map/place_queries/pallas_call | solution.py:119
  50.7 0.0 collective-permute-done.4.refs_3_
  50.7 2.8 %collective-permute-start.6 = (bf16[128,2176]{1,0:T(8,128)(2,1)S(1)}, bf16[128,2176]{1,0:T(8,128)(2,1)S(1)}, u32[]{:S(2)}, u32[]{:S(2)}) collective-permute-start(bf16[128,2176]{1,0:T(8,128)(2,1)S(1)} %collective-permute-done.4.refs_3_), channel_id=1, source_target_pairs={{0,1},{1,0},{2,3},{3,2},{4,5},{5,4},{6,7},{7,6},{8,9},{9,8},{10,11... | collective-permute-start | bytes 1671176 | tf_op jit(solution)/shard_map/ppermute | solution.py:34
  53.5 0.0 collective-permute-done.7.refs_5_
  53.5 0.0 collective-permute-done.3.refs_2_
  53.5 1.6 %collective-permute-done.6.refs_4_ = bf16[128,2176]{1,0:T(8,128)(2,1)S(1)} collective-permute-done((bf16[128,2176]{1,0:T(8,128)(2,1)S(1)}, bf16[128,2176]{1,0:T(8,128)(2,1)S(1)}, u32[]{:S(2)}, u32[]{:S(2)}) %collective-permute-start.6) | collective-permute-done | bytes 557088 | tf_op jit(solution)/shard_map/ppermute | solution.py:34
  55.0 8.2 %attend_early.1 = (bf16[1,128,8192]{2,1,0:T(8,128)(2,1)}, bf16[128,2304]{1,0:T(8,128)(2,1)S(1)}) custom-call(s32[1]{0:T(128)} %bitcast.rank_ref, bf16[128,2176]{1,0:T(8,128)(2,1)S(1)} %get-tuple-element.19.refs_0_, bf16[128,2176]{1,0:T(8,128)(2,1)S(1)} %collective-permute-done.1.refs_1_, ...), custom_call_target="tpu_custom_call", output_to_operand_aliasing={{0}: (8, {})} | custom-call | tf_op jit(solution)/shard_map/attend_early/pallas_call | solution.py:119
  63.2 0.0 collective-permute-done.8.refs_7_
  63.2 4.8 %attend_late.1 = bf16[1,128,8192]{2,1,0:T(8,128)(2,1)} custom-call(s32[1]{0:T(128)} %bitcast.rank_ref, bf16[128,2176]{1,0:T(8,128)(2,1)S(1)} %get-tuple-element.19.refs_0_, bf16[128,2176]{1,0:T(8,128)(2,1)S(1)} %collective-permute-done.1.refs_1_, bf16[128,2176]{1,0:T(8,128)(2,1)S(1)} %collective-permute-done.3.refs_2_, ...), custom_call_target="tpu_custom_call", output_to_operand_aliasing={{}: (10, {})} | custom-call | tf_op jit(solution)/shard_map/attend_late/pallas_call | solution.py:119
  (3 shorter events, 0.1 us)
Async XLA Ops:
  0.0 8.8 %copy-start = (bf16[1,256,8192]{2,1,0:T(8,128)(2,1)S(1)}, bf16[1,256,8192]{2,1,0:T(8,128)(2,1)}, u32[]{:S(2)}) copy-start(bf16[1,256,8192]{2,1,0:T(8,128)(2,1)} %refs_6_.1) | copy-start | bytes 12582916
  0.0 17.0 %copy-start.1 = (s32[1,128]{1,0:T(1,128)S(1)}, s32[1,128]{1,0:T(1,128)}, u32[]{:S(2)}) copy-start(s32[1,128]{1,0:T(1,128)} %docs_ref.1) | copy-start | bytes 1540
  1.3 15.7 %collective-permute-start = (bf16[128,2048]{1,0:T(8,128)(2,1)S(1)}, bf16[128,2048]{1,0:T(8,128)(2,1)S(1)}, u32[]{:S(2)}, u32[]{:S(2)}) collective-permute-start(bf16[128,2048]{1,0:T(8,128)(2,1)S(1)} %pad_maximum_fusion), channel_id=1, source_target_pairs={{0,8},{8,16},{16,24},{1,9},{9,17},{17,25},{2,10},{10,18},{18,26},{... | collective-permute-start | bytes 1572872 | tf_op jit(solution)/shard_map/ppermute | solution.py:29
  9.8 21.2 %collective-permute-start.2 = (bf16[128,2560]{1,0:T(8,128)(2,1)S(1)}, bf16[128,2560]{1,0:T(8,128)(2,1)S(1)}, u32[]{:S(2)}, u32[]{:S(2)}) collective-permute-start(bf16[128,2560]{1,0:T(8,128)(2,1)S(1)} %add_bitcast_fusion.1), channel_id=1, source_target_pairs={{0,8},{8,16},{16,24},{1,9},{9,17},{17,25},{2,10},{10,18},{18,26},{... | collective-permute-start | bytes 1966088 | tf_op jit(solution)/shard_map/ppermute | solution.py:29
  17.8 14.5 %collective-permute-start.1 = (bf16[128,2176]{1,0:T(8,128)(2,1)S(1)}, bf16[128,2176]{1,0:T(8,128)(2,1)S(1)}, u32[]{:S(2)}, u32[]{:S(2)}) collective-permute-start(bf16[128,2176]{1,0:T(8,128)(2,1)S(1)} %get-tuple-element.19.refs_0_), channel_id=1, source_target_pairs={{0,2},{1,3},{2,4},{3,5},{4,6},{5,7},{8,10},{9,11},{10,12},{11,13},... | collective-permute-start | bytes 1671176 | tf_op jit(solution)/shard_map/ppermute | solution.py:29
  21.1 28.2 %collective-permute-start.5 = (bf16[128,3328]{1,0:T(8,128)(2,1)S(1)}, bf16[128,3328]{1,0:T(8,128)(2,1)S(1)}, u32[]{:S(2)}, u32[]{:S(2)}) collective-permute-start(bf16[128,3328]{1,0:T(8,128)(2,1)S(1)} %add_bitcast_fusion), channel_id=1, source_target_pairs={{0,8},{8,16},{16,24},{1,9},{9,17},{17,25},{2,10},{10,18},{18,26},{... | collective-permute-start | bytes 2555912 | tf_op jit(solution)/shard_map/ppermute | solution.py:29
  32.3 18.4 %collective-permute-start.4 = (bf16[128,2176]{1,0:T(8,128)(2,1)S(1)}, bf16[128,2176]{1,0:T(8,128)(2,1)S(1)}, u32[]{:S(2)}, u32[]{:S(2)}) collective-permute-start(bf16[128,2176]{1,0:T(8,128)(2,1)S(1)} %collective-permute-done.1.refs_1_), channel_id=1, source_target_pairs={{0,2},{1,3},{2,4},{3,5},{4,6},{5,7},{8,10},{9,11},{10,12},{11,13},... | collective-permute-start | bytes 1671176 | tf_op jit(solution)/shard_map/ppermute | solution.py:29
  35.5 27.7 %collective-permute-start.8 = (bf16[128,2304]{1,0:T(8,128)(2,1)}, bf16[128,2304]{1,0:T(8,128)(2,1)}, u32[]{:S(2)}, u32[]{:S(2)}) collective-permute-start(bf16[128,2304]{1,0:T(8,128)(2,1)} %add_bitcast_fusion.2), channel_id=1, source_target_pairs={{0,8},{8,16},{16,24},{1,9},{9,17},{17,25},{2,10},{10,18},{18,26},{... | collective-permute-start | bytes 1769480 | tf_op jit(solution)/shard_map/ppermute | solution.py:29
  37.7 15.7 %collective-permute-start.7 = (bf16[128,2176]{1,0:T(8,128)(2,1)S(1)}, bf16[128,2176]{1,0:T(8,128)(2,1)S(1)}, u32[]{:S(2)}, u32[]{:S(2)}) collective-permute-start(bf16[128,2176]{1,0:T(8,128)(2,1)S(1)} %get-tuple-element.19.refs_0_), channel_id=1, source_target_pairs={{0,1},{2,3},{4,5},{6,7},{8,9},{10,11},{12,13},{14,15},{16,17},{18,... | collective-permute-start | bytes 1671176 | tf_op jit(solution)/shard_map/ppermute | solution.py:34
  39.0 14.4 %collective-permute-start.3 = (bf16[128,2176]{1,0:T(8,128)(2,1)S(1)}, bf16[128,2176]{1,0:T(8,128)(2,1)S(1)}, u32[]{:S(2)}, u32[]{:S(2)}) collective-permute-start(bf16[128,2176]{1,0:T(8,128)(2,1)S(1)} %collective-permute-done.1.refs_1_), channel_id=1, source_target_pairs={{0,1},{1,0},{2,3},{3,2},{4,5},{5,4},{6,7},{7,6},{8,9},{9,8},{10,11... | collective-permute-start | bytes 1671176 | tf_op jit(solution)/shard_map/ppermute | solution.py:34
  50.7 4.3 %collective-permute-start.6 = (bf16[128,2176]{1,0:T(8,128)(2,1)S(1)}, bf16[128,2176]{1,0:T(8,128)(2,1)S(1)}, u32[]{:S(2)}, u32[]{:S(2)}) collective-permute-start(bf16[128,2176]{1,0:T(8,128)(2,1)S(1)} %collective-permute-done.4.refs_3_), channel_id=1, source_target_pairs={{0,1},{1,0},{2,3},{3,2},{4,5},{5,4},{6,7},{7,6},{8,9},{9,8},{10,11... | collective-permute-start | bytes 1671176 | tf_op jit(solution)/shard_map/ppermute | solution.py:34
